TPU v7x, 32 devices: a whole 2x2x4 slice. The times are simulated.
32 devices in a mesh: groups: 1, cells: 32 (over z, y, x, core).
Axes of the slice: x: 2, y: 2, z: 4, core: 2. Of those that a mesh axis runs over, the one named last changes fastest.
Arguments:
- rna_counts: bfloat16 [2048, 4096], P(('groups', 'cells')), may hold values from 1 to 30, as said below
- atac_counts: bfloat16 [2048, 16384], P(('groups', 'cells')), may hold values from 1 to 30, as said below
- cell_factor: float32 [64, 2048], P(None, ('groups', 'cells')), may hold values from 0.1 to 3, as said below
- gene_factor: float32 [64, 4096], P(None, ('groups', 'cells')), may hold values from 0.1 to 3, as said below
- peak_factor: float32 [64, 16384], P(None, ('groups', 'cells')), may hold values from 0.1 to 3, as said below
- link_gene: int32 [256], P(('groups', 'cells')), may hold values from 0 to 31
- link_peak: int32 [256], P(('groups', 'cells')), may hold values from 0 to 127
- link_weight: int32 [256], P(('groups', 'cells')), may hold values from 1 to 4
- link_count: int32 [32], P(('groups', 'cells')), may hold values from 1 to 8, as said below
Outputs:
- cell_out: float32 [64, 2048], P(None, ('groups', 'cells'))
- gene_out: float32 [64, 4096], P(None, ('groups', 'cells'))
- peak_out: float32 [64, 16384], P(None, ('groups', 'cells'))
Inputs may be any that keep to these rules, and one draw needn't show every extreme that they name: `rna_counts`: nonnegative counts. `atac_counts`: nonnegative counts. `cell_factor`: positive loadings. `gene_factor`: positive loadings. `peak_factor`: positive loadings. `link_count`: at least one live slot on every index, and some index has all 8 slots live.
All inputs are finite; a program needn't handle non-finite values.
Results may differ from a plain program's by a relative error of at most 0.00068.
Values may be sent and summed in bfloat16 or wider, within the bound.
No kernel may reach another device: no remote copies, remote signals or barrier semaphores. Data moves between devices by JAX's collectives and lax.ppermute only.
A program may use at most 64 MiB of HBM per device.

v0:
```python
import jax
import jax.numpy as jnp
from jax import lax
from jax.sharding import PartitionSpec as P

G = 4096
P_SIZE = 16384
BLOCK = 128
ROUNDS = 2


EPSILON = 1e-06


def own_table(link_gene, link_peak, link_weight, link_count, gene_blocks, peak_blocks):
    slot_ids = jnp.arange(link_gene.shape[0], dtype=jnp.int32)
    live_weight = jnp.where(slot_ids < link_count[0], link_weight, 0).astype(jnp.float32)
    gene_hot = (link_gene[:, None] == jnp.arange(gene_blocks, dtype=jnp.int32)[None, :]).astype(
        jnp.float32
    )
    peak_hot = (link_peak[:, None] == jnp.arange(peak_blocks, dtype=jnp.int32)[None, :]).astype(
        jnp.float32
    )
    return jnp.dot((gene_hot * live_weight[:, None]).T, peak_hot, precision=lax.Precision.HIGHEST)


def apply_links(link_table, source, out_width):
    rank = source.shape[0]
    blocked = source.reshape(rank, link_table.shape[1], -1)
    result = jnp.einsum(
        "kpc,gp->kgc", blocked, link_table.astype(jnp.bfloat16), preferred_element_type=jnp.float32
    )
    return result.reshape(rank, out_width)


def contract_features(loadings, counts):
    return lax.dot_general(
        loadings, counts, (((1,), (1,)), ((), ())), preferred_element_type=jnp.float32
    )


def shards(
    rna_counts,
    atac_counts,
    cell_factor,
    gene_factor,
    peak_factor,
    link_gene,
    link_peak,
    link_weight,
    link_count,
):
    device_count = lax.axis_size("cells")
    link_scale = rna_counts.shape[0] * device_count / 4.0
    link_table = own_table(
        link_gene, link_peak, link_weight, link_count, G // BLOCK, P_SIZE // BLOCK
    )
    gene_state = gene_factor
    gene_whole, peak_whole = (
        lax.all_gather(gene_factor.astype(jnp.bfloat16), "cells", axis=1, tiled=True),
        lax.all_gather(peak_factor.astype(jnp.bfloat16), "cells", axis=1, tiled=True),
    )
    peak_state = peak_factor
    for sweep_index in range(ROUNDS):
        cell_low = cell_factor.astype(jnp.bfloat16)
        gram_cells = lax.psum(
            jnp.dot(cell_factor, cell_factor.T, precision=lax.Precision.HIGHEST), "cells"
        )
        gene_term = jnp.dot(cell_low, rna_counts, preferred_element_type=jnp.float32)
        peak_term = jnp.dot(cell_low, atac_counts, preferred_element_type=jnp.float32)
        gene_term = gene_term + link_scale * apply_links(link_table, peak_whole, G)
        peak_term = peak_term + link_scale * apply_links(link_table.T, gene_whole, P_SIZE)
        gene_sum, peak_sum = (
            lax.psum_scatter(gene_term, "cells", scatter_dimension=1, tiled=True),
            lax.psum_scatter(peak_term, "cells", scatter_dimension=1, tiled=True),
        )
        gene_state = (
            gene_state
            * gene_sum
            / (jnp.dot(gram_cells, gene_state, precision=lax.Precision.HIGHEST) + EPSILON)
        )
        peak_state = (
            peak_state
            * peak_sum
            / (jnp.dot(gram_cells, peak_state, precision=lax.Precision.HIGHEST) + EPSILON)
        )
        peak_low = peak_state.astype(jnp.bfloat16)
        gene_mine = gene_state.astype(jnp.bfloat16)
        gene_whole, peak_whole = (
            lax.all_gather(gene_mine, "cells", axis=1, tiled=True),
            lax.all_gather(peak_low, "cells", axis=1, tiled=True),
        )
        gram_features = jnp.dot(
            gene_whole, gene_whole.T, preferred_element_type=jnp.float32
        ) + jnp.dot(peak_whole, peak_whole.T, preferred_element_type=jnp.float32)
        cell_num = contract_features(gene_whole, rna_counts) + contract_features(
            peak_whole, atac_counts
        )
        cell_factor = (
            cell_factor
            * cell_num
            / (jnp.dot(gram_features, cell_factor, precision=lax.Precision.HIGHEST) + EPSILON)
        )
    return (cell_factor, gene_state, peak_state)


def solution(mesh):
    in_specs = (
        P(("groups", "cells"), None),
        P(("groups", "cells"), None),
        P(None, ("groups", "cells")),
        P(None, ("groups", "cells")),
        P(None, ("groups", "cells")),
        P(("groups", "cells")),
        P(("groups", "cells")),
        P(("groups", "cells")),
        P(("groups", "cells")),
    )
    out_specs = (
        P(None, ("groups", "cells")),
        P(None, ("groups", "cells")),
        P(None, ("groups", "cells")),
    )
    return jax.shard_map(shards, mesh=mesh, in_specs=in_specs, out_specs=out_specs, check_vma=False)
```

profile of v0, /device:TPU:0, one launch (start us, length us, event | category | flops | bytes accessed | tf_op | source)
XLA Modules:
  0.0 747.7 jit_solution(7475219445144833741)
XLA Ops:
  7.2 1.7 convert_element_type.39
  9.6 0.8 convert_element_type.41
  10.4 44.8 %all_gather.20 = bf16[64,4096]{1,0:T(8,128)(2,1)S(1)} all-gather(bf16[64,128]{1,0:T(8,128)(2,1)S(1)} %convert_element_type.41), channel_id=1, replica_groups=mesh['groups'=1,'cells'=32] {'cells'}, dimensions={1}, use_global_device_ids=true | all-gather | bytes 540672 | tf_op jit(solution)/shard_map/all_gather | solution.py:60
  55.9 1.0 fusion.8
  56.9 0.7 convolution_multiply_fusion.1
  57.6 4.9 convolution_add_fusion.1
  62.6 7.0 all-gather.4.cloned.1.call-done
  69.6 2.2 copy.12
  72.8 1.7 convolution_add_fusion.3
  74.8 40.1 %psum.14 = f32[64,64]{1,0:T(8,128)S(1)} all-reduce(f32[64,64]{1,0:T(8,128)S(1)} %fusion.24), channel_id=1, replica_groups=mesh['groups'=1,'cells'=32] {'cells'}, use_global_device_ids=true, to_apply=%region_1.2 | all-reduce | flops 4096 | bytes 32768 | tf_op jit(solution)/shard_map/psum | solution.py:66
  114.8 97.4 %reduce-scatter.7.cloned.1.call-done = f32[64,512]{1,0:T(8,128)} async-done(((f32[64,16384]{1,0:T(8,128)}), f32[64,512]{1,0:T(8,128)}) %reduce-scatter.7.cloned.1.call-update) | async-done | bytes 131088 | tf_op jit(solution)/shard_map/reduce_scatter | solution.py:75
  212.3 1.8 fusion.21
  214.2 131.2 %reduce-scatter.5.cloned.1.call-done = f32[64,128]{1,0:T(8,128)} async-done(((f32[64,4096]{1,0:T(8,128)}), f32[64,128]{1,0:T(8,128)}) %reduce-scatter.5.cloned.1.call-update) | async-done | bytes 32784 | tf_op jit(solution)/shard_map/reduce_scatter | solution.py:74
  345.3 0.9 fusion.20
  346.3 38.0 %all_gather.19 = bf16[64,4096]{1,0:T(8,128)(2,1)S(1)} all-gather(bf16[64,128]{1,0:T(8,128)(2,1)S(1)} %get-tuple-element.3), channel_id=1, replica_groups=mesh['groups'=1,'cells'=32] {'cells'}, dimensions={1}, use_global_device_ids=true | all-gather | bytes 540672 | tf_op jit(solution)/shard_map/all_gather | solution.py:90
  384.9 2.8 convolution_multiply_fusion
  387.7 12.5 %all-gather.6.cloned.1.call-done = bf16[64,16384]{1,0:T(8,128)(2,1)} async-done(((bf16[64,512]{1,0:T(8,128)(2,1)}), bf16[64,16384]{1,0:T(8,128)(2,1)}) %all-gather.6.cloned.1.call-update) | async-done | bytes 2097168 | tf_op jit(solution)/shard_map/all_gather | solution.py:91
  400.2 2.4 fusion.6
  402.6 0.7 convolution_add_fusion.11
  403.5 1.3 copy-done.3
  404.8 5.0 convolution_add_fusion
  409.9 2.2 copy.16
  412.5 1.7 convolution_add_fusion.2
  414.4 40.2 %psum.15 = f32[64,64]{1,0:T(8,128)S(1)} all-reduce(f32[64,64]{1,0:T(8,128)S(1)} %fusion.27), channel_id=1, replica_groups=mesh['groups'=1,'cells'=32] {'cells'}, use_global_device_ids=true, to_apply=%region_4.5 | all-reduce | flops 4096 | bytes 32768 | tf_op jit(solution)/shard_map/psum | solution.py:66
  454.7 95.3 %reduce-scatter.11.cloned.1.call-done = f32[64,512]{1,0:T(8,128)} async-done(((f32[64,16384]{1,0:T(8,128)}), f32[64,512]{1,0:T(8,128)}) %reduce-scatter.11.cloned.1.call-update) | async-done | bytes 131088 | tf_op jit(solution)/shard_map/reduce_scatter | solution.py:75
  550.0 1.8 fusion.23
  551.9 131.1 %reduce-scatter.9.cloned.1.call-done = f32[64,128]{1,0:T(8,128)} async-done(((f32[64,4096]{1,0:T(8,128)}), f32[64,128]{1,0:T(8,128)}) %reduce-scatter.9.cloned.1.call-update) | async-done | bytes 32784 | tf_op jit(solution)/shard_map/reduce_scatter | solution.py:74
  683.0 1.5 fusion.22
  684.6 37.9 %all_gather.22 = bf16[64,4096]{1,0:T(8,128)(2,1)S(1)} all-gather(bf16[64,128]{1,0:T(8,128)(2,1)S(1)} %get-tuple-element.7), channel_id=1, replica_groups=mesh['groups'=1,'cells'=32] {'cells'}, dimensions={1}, use_global_device_ids=true | all-gather | bytes 540672 | tf_op jit(solution)/shard_map/all_gather | solution.py:90
  723.1 13.8 %all-gather.8.cloned.1.call-done = bf16[64,16384]{1,0:T(8,128)(2,1)} async-done(((bf16[64,512]{1,0:T(8,128)(2,1)}), bf16[64,16384]{1,0:T(8,128)(2,1)}) %all-gather.8.cloned.1.call-update) | async-done | bytes 2097168 | tf_op jit(solution)/shard_map/all_gather | solution.py:91
  736.9 2.4 fusion.3
  740.0 0.8 fusion.2
  (42 shorter events, 5.1 us)
Async XLA Ops:
  7.2 50.5 %copy-start = (bf16[64,16384]{1,0:T(8,128)(2,1)S(1)}, bf16[64,16384]{1,0:T(8,128)(2,1)}, u32[]{:S(2)}) copy-start(bf16[64,16384]{1,0:T(8,128)(2,1)} %param.10) | copy-start | bytes 6291460
  7.2 62.4 %all-gather.4.cloned.1.call-start = ((), (), s32[]{:S(2)}) async-start(), calls=%async_computation.4 | async-start | bytes 2162688 | tf_op jit(solution)/shard_map/all_gather | solution.py:61
  8.9 203.3 %reduce-scatter.7.cloned.1.call-start = ((), (), s32[]{:S(2)}) async-start(), calls=%async_computation.6 | async-start | bytes 4325376 | tf_op jit(solution)/shard_map/reduce_scatter | solution.py:75
  56.9 0.8 copy-start.5
  62.6 282.8 %reduce-scatter.5.cloned.1.call-start = ((), (), s32[]{:S(2)}) async-start(), calls=%async_computation.5 | async-start | bytes 1081344 | tf_op jit(solution)/shard_map/reduce_scatter | solution.py:74
  71.8 1.0 copy-start.4
  72.2 140.1 %copy-start.6 = (f32[64,512]{1,0:T(8,128)S(1)}, f32[64,512]{1,0:T(8,128)}, u32[]{:S(2)}) copy-start(f32[64,512]{1,0:T(8,128)} %param.13) | copy-start | bytes 393220
  72.8 272.5 %copy-start.7 = (f32[64,128]{1,0:T(8,128)S(1)}, f32[64,128]{1,0:T(8,128)}, u32[]{:S(2)}) copy-start(f32[64,128]{1,0:T(8,128)} %param.12) | copy-start | bytes 98308
  74.5 325.6 %all-gather.6.cloned.1.call-start = ((), (), s32[]{:S(2)}) async-start(), calls=%async_computation.7 | async-start | bytes 2162688 | tf_op jit(solution)/shard_map/all_gather | solution.py:91
  214.1 335.9 %reduce-scatter.11.cloned.1.call-start = ((), (), s32[]{:S(2)}) async-start(), calls=%async_computation.9 | async-start | bytes 4325376 | tf_op jit(solution)/shard_map/reduce_scatter | solution.py:75
  400.2 2.4 copy-start.1
  402.6 2.2 copy-start.3
  409.8 273.2 %reduce-scatter.9.cloned.1.call-start = ((), (), s32[]{:S(2)}) async-start(), calls=%async_computation.8 | async-start | bytes 1081344 | tf_op jit(solution)/shard_map/reduce_scatter | solution.py:74
  414.2 322.7 %all-gather.8.cloned.1.call-start = ((), (), s32[]{:S(2)}) async-start(), calls=%async_computation.10 | async-start | bytes 2162688 | tf_op jit(solution)/shard_map/all_gather | solution.py:91
  736.9 2.4 copy-start.2
Sparse Core Ops, SparseCore 0:
  11.5 58.0 all-gather.3
  71.9 140.3 reduce-scatter.6
  214.5 130.7 reduce-scatter.4
  349.0 51.0 all-gather.5
  409.9 140.0 reduce-scatter.10
  552.2 130.7 reduce-scatter.8
  685.9 50.9 all-gather.7
where the time goes:
time: 748 us
  waiting for transfers between devices  488 us (65%)
  blocking collectives  201 us (27%)
  matrix products  33.4 us (4%)
  between operations  15 us (2%)
    reduce_scatter x2, waiting for transfers between devices, shards(): lax.psum_scatter(gene_term, 'cells', scatter_dimension=1, tiled=True)  262 us
    reduce_scatter x2, waiting for transfers between devices, shards(): lax.psum_scatter(peak_term, 'cells', scatter_dimension=1, tiled=True)  193 us
    psum x2, blocking collectives, shards(): lax.psum(jnp.dot(cell_factor, cell_factor.T, precision=lax.Precision.HIGH...  80.3 us
    all_gather x2, blocking collectives, shards(): lax.all_gather(gene_mine, 'cells', axis=1, tiled=True)  75.9 us
    all_gather x1, blocking collectives, shards(): lax.all_gather(gene_factor.astype(jnp.bfloat16), 'cells', axis=1, tiled=T...  44.8 us
    all_gather x2, waiting for transfers between devices, shards(): lax.all_gather(peak_low, 'cells', axis=1, tiled=True)  26.3 us
  transfers between devices with their start and end apart: 7, of which 7 were waited for; matrix products, arithmetic and copies ran while one was open for 4% of the time, Pallas kernels for 0%

commit v1 on v0

v1 whole, which is shorter than its diff:
```python
import jax
import jax.numpy as jnp
from jax import lax
from jax.sharding import PartitionSpec as P

BLOCK = 128
ROUNDS = 2
EPSILON = 1e-06
AXIS = "cells"


def flip(value, bit):
    count = lax.axis_size(AXIS)
    return lax.ppermute(value, AXIS, [(i, i ^ bit) for i in range(count)])


def in_order(bit, mine, other):
    mine_first = (lax.axis_index(AXIS) & bit) == 0
    return jnp.where(mine_first, mine, other), jnp.where(mine_first, other, mine)


def bits_below(size):
    return [1 << b for b in range(size.bit_length() - 1)]


def own_table(link_gene, link_peak, link_weight, link_count, gene_blocks, peak_blocks):
    slot_ids = jnp.arange(link_gene.shape[0], dtype=jnp.int32)
    live_weight = jnp.where(slot_ids < link_count[0], link_weight, 0).astype(jnp.float32)
    gene_hot = (link_gene[:, None] == jnp.arange(gene_blocks, dtype=jnp.int32)[None, :]).astype(
        jnp.float32
    )
    peak_hot = (link_peak[:, None] == jnp.arange(peak_blocks, dtype=jnp.int32)[None, :]).astype(
        jnp.float32
    )
    return jnp.dot((gene_hot * live_weight[:, None]).T, peak_hot, precision=lax.Precision.HIGHEST)


def split_low(value):
    high = lax.reduce_precision(value, exponent_bits=8, mantissa_bits=7)
    return high.astype(jnp.bfloat16), (value - high).astype(jnp.bfloat16)


def gather_half(value, half):
    for bit in bits_below(half):
        value = jnp.concatenate(in_order(bit, value, flip(value, bit)), axis=1)
    return value


def scatter_half(value, half):
    for bit in reversed(bits_below(half)):
        low, high = jnp.split(value, 2, axis=1)
        clear = (lax.axis_index(AXIS) & bit) == 0
        value = jnp.where(clear, low, high) + flip(jnp.where(clear, high, low), bit)
    return value


def weigh(weights, source):
    rank = source.shape[0]
    blocks = source.astype(jnp.float32).reshape(rank, weights.shape[1], BLOCK)
    result = jnp.einsum("ksc,ts->ktc", blocks, weights, precision=lax.Precision.HIGHEST)
    return result.reshape(rank, weights.shape[0] * BLOCK)


def coupling(link_table, factors, widths):
    gene_width, peak_width = widths
    half = lax.axis_size(AXIS) // 2
    me = lax.axis_index(AXIS)
    side, place = me // half, me % half
    low = factors.astype(jnp.bfloat16)
    genes, peaks = low[:, : 2 * gene_width], low[:, 2 * gene_width :]
    own_gene = jnp.where(side == 0, genes[:, :gene_width], genes[:, gene_width:])
    side_blocks = half * gene_width // BLOCK
    peak_blocks = peak_width // BLOCK
    side_rows = lax.dynamic_slice_in_dim(link_table, side * side_blocks, side_blocks, 0)
    weights = jnp.concatenate(
        [
            lax.dynamic_slice_in_dim(side_rows, (place + s * half) * peak_blocks, peak_blocks, 1)
            for s in range(2)
        ],
        axis=1,
    )
    to_gene = scatter_half(weigh(weights, peaks), half)
    to_peak = weigh(weights.T, gather_half(own_gene, half))
    nothing = jnp.zeros_like(to_gene)
    return jnp.concatenate([*(jnp.where(side == s, to_gene, nothing) for s in range(2)), to_peak], axis=1)


def shards(
    rna_counts,
    atac_counts,
    cell_factor,
    gene_factor,
    peak_factor,
    link_gene,
    link_peak,
    link_weight,
    link_count,
):
    count = lax.axis_size(AXIS)
    half = count // 2
    me = lax.axis_index(AXIS)
    side = me // half
    rank, cells = cell_factor.shape
    gene_width, peak_width = gene_factor.shape[1], peak_factor.shape[1]
    features = 2 * (gene_width + peak_width)
    link_scale = cells * count / 4.0

    link_table = own_table(
        link_gene,
        link_peak,
        link_weight,
        link_count,
        rna_counts.shape[1] // BLOCK,
        atac_counts.shape[1] // BLOCK,
    )
    for bit in bits_below(count):
        link_table = link_table + flip(link_table, bit)

    def by_place(counts, width):
        return counts.reshape(cells, 2, half, width).transpose(2, 0, 1, 3).reshape(half, cells, 2 * width)

    cell_pair = jnp.concatenate([part.T for part in split_low(cell_factor)], axis=1)
    parcels = jnp.concatenate(
        [
            by_place(rna_counts, gene_width),
            by_place(atac_counts, peak_width),
            jnp.broadcast_to(cell_pair[None], (half, cells, 2 * rank)),
        ],
        axis=2,
    )
    halves = [list(range(half)), list(range(half, count))]
    received = lax.all_to_all(parcels, AXIS, 0, 0, axis_index_groups=halves, tiled=True)
    received = received.reshape(half * cells, features + 2 * rank)
    counts, cell_pair = received[:, :features], received[:, features:]

    gene_pair = in_order(half, gene_factor, flip(gene_factor, half))
    peak_pair = in_order(half, peak_factor, flip(peak_factor, half))
    factors = jnp.concatenate([*gene_pair, *peak_pair], axis=1)
    cell_low, cell_rest = cell_pair[:, :rank].T, cell_pair[:, rank:].T
    cell_state = cell_factor

    for sweep_index in range(ROUNDS):
        links = link_scale * coupling(link_table, factors, (gene_width, peak_width))
        pair = jnp.concatenate([cell_low, cell_rest], axis=0)
        squares = lax.dot_general(
            pair, pair, (((1,), (1,)), ((), ())), preferred_element_type=jnp.float32
        )
        gram_cells = (
            squares[:rank, :rank] + squares[:rank, rank:] + squares[rank:, :rank] + squares[rank:, rank:]
        )
        sums = jnp.dot(cell_low, counts, preferred_element_type=jnp.float32) + links
        groups = sums.reshape(rank, features // gene_width, gene_width)
        largest = jnp.max(groups, axis=2)
        scaled = (groups / largest[:, :, None]).astype(jnp.float16).reshape(rank, features)
        beside_other = flip(jnp.concatenate([gram_cells, largest], axis=1), half)
        groups_other = flip(scaled, half).astype(jnp.float32).reshape(groups.shape)
        gram_cells = gram_cells + beside_other[:, :rank]
        sums = sums + (groups_other * beside_other[:, rank:, None]).reshape(rank, features)
        factors = (
            factors
            * sums
            / (jnp.dot(gram_cells, factors, precision=lax.Precision.HIGHEST) + EPSILON)
        )
        low = factors.astype(jnp.bfloat16)
        gram_features = lax.dot_general(
            low, low, (((1,), (1,)), ((), ())), preferred_element_type=jnp.float32
        )
        cell_sums = lax.dot_general(
            low, counts, (((1,), (1,)), ((), ())), preferred_element_type=jnp.float32
        )
        last = sweep_index == ROUNDS - 1
        if last:
            for bit in reversed(bits_below(half)):
                left, right = jnp.split(cell_sums, 2, axis=1)
                clear = (me & bit) == 0
                sent = jnp.concatenate([jnp.where(clear, right, left), gram_features], axis=1)
                got = flip(sent, bit)
                kept = cell_sums.shape[1] // 2
                cell_sums = jnp.where(clear, left, right) + got[:, :kept]
                gram_features = gram_features + got[:, kept:]
        else:
            left, right = jnp.split(cell_sums, 2, axis=1)
            clear = (me & 1) == 0
            sent = jnp.concatenate([jnp.where(clear, right, left), gram_features], axis=1)
            kept = jnp.concatenate([jnp.where(clear, left, right), gram_features], axis=1)
            for bit in bits_below(half):
                kept = kept + flip(sent, bit)
                sent = kept
            width = cell_sums.shape[1] // 2
            cell_sums, gram_features = kept[:, :width], kept[:, width:]
            low_rest = [jnp.where(clear, *jnp.split(part, 2, axis=1)) for part in (cell_low, cell_rest)]
            cell_state = low_rest[0].astype(jnp.float32) + low_rest[1].astype(jnp.float32)
        cell_state = (
            cell_state
            * cell_sums
            / (jnp.dot(gram_features, cell_state, precision=lax.Precision.HIGHEST) + EPSILON)
        )
        if not last:
            pair = jnp.concatenate(split_low(cell_state), axis=0)
            pair = jnp.concatenate(in_order(1, pair, flip(pair, 1)), axis=1)
            cell_low, cell_rest = pair[:rank], pair[rank:]
            mine = lax.dynamic_slice_in_dim(pair, (me % half) * cells, cells, 1).astype(jnp.float32)
            cell_state = mine[:rank] + mine[rank:]

    def own(first, width):
        return jnp.where(side == 0, factors[:, first : first + width], factors[:, first + width : first + 2 * width])

    return cell_state, own(0, gene_width), own(2 * gene_width, peak_width)


def solution(mesh):
    columns = P(None, ("groups", "cells"))
    slots = P(("groups", "cells"))
    in_specs = (P(("groups", "cells"), None),) * 2 + (columns,) * 3 + (slots,) * 4
    return jax.shard_map(
        shards, mesh=mesh, in_specs=in_specs, out_specs=(columns,) * 3, check_vma=False
    )
```

time: 748 us -> 190 us (0.25)
  waiting for transfers between devices: 488 us -> 114 us
  blocking collectives: 201 us -> 0 us
  starting transfers between devices: 0.29 us -> 36.6 us
  matrix products: 33.4 us -> 11.3 us
  between operations: 15 us -> 2.29 us
  local copies, waits for them, and re-layouts: 6.45 us -> 16.2 us
    reduce_scatter x4 -> x0, waiting for transfers between devices: 455 us -> none  [the longest x2 262 us: shards(): lax.psum_scatter(gene_term, 'cells', scatter_dimension=1, tiled=True)]
    all_gather x3 -> x0, blocking collectives: 121 us -> none  [the longest x2 75.9 us: shards(): lax.all_gather(gene_mine, 'cells', axis=1, tiled=True)]
    ppermute x0 -> x36, waiting for transfers between devices: none -> 114 us  [flip(): return lax.ppermute(value, AXIS, [(i, i ^ bit) for i in range(count)])]
    psum x2 -> x0, blocking collectives: 80.3 us -> none  [shards(): lax.psum(jnp.dot(cell_factor, cell_factor.T, precision=lax.Precision.HIGH...]
    all_gather x3 -> x0, waiting for transfers between devices: 33.2 us -> none  [the longest x2 26.3 us: shards(): lax.all_gather(peak_low, 'cells', axis=1, tiled=True)]
    ppermute x0 -> x36, starting transfers between devices: none -> 30.2 us  [flip(): return lax.ppermute(value, AXIS, [(i, i ^ bit) for i in range(count)])]
    dot_general x24 -> x16, matrix products: 32.5 us -> 11 us  [the longest x2 2.92 us: shards(): jnp.dot(gram_cells, factors, precision=lax.Precision.HIGHEST) + EPSILON]
    reshape x0 -> x6, local copies, waits for them, and re-layouts: none -> 7.63 us  [the longest x4 5.73 us: by_place(): counts.reshape(cells, 2, half, width).transpose(2, 0, 1, 3)]
  transfers between devices with their start and end apart: 7 -> 37, of which waited for: 7 -> 27; matrix products, arithmetic and copies ran while one was open for 4% -> 4% of each run, Pallas kernels for 0% -> 0%
where the time goes in v1:
time: 190 us; the launch traced here: 189 us
  waiting for transfers between devices  114 us (60%)
  starting transfers between devices  36.6 us (19%)
  local copies, waits for them, and re-layouts  16.2 us (9%)
  matrix products  11.3 us (6%)
  other arithmetic  9 us (5%)
  between operations  2.29 us (1%)
    ppermute x36, waiting for transfers between devices, flip(): return lax.ppermute(value, AXIS, [(i, i ^ bit) for i in range(count)])  114 us
    ppermute x36, starting transfers between devices, flip(): return lax.ppermute(value, AXIS, [(i, i ^ bit) for i in range(count)])  30.2 us
    unnamed x53, local copies, waits for them, and re-layouts  7.46 us
    all_to_all x1, starting transfers between devices, shards(): lax.all_to_all(parcels, AXIS, 0, 0, axis_index_groups=halves, tiled=True)  6.44 us
    reshape x4, local copies, waits for them, and re-layouts, by_place(): counts.reshape(cells, 2, half, width).transpose(2, 0, 1, 3)  5.73 us
  transfers between devices with their start and end apart: 37, of which 27 were waited for; matrix products, arithmetic and copies ran while one was open for 4% of the time, Pallas kernels for 0%

profile of v1, /device:TPU:0, one launch (start us, length us, event | category | flops | bytes accessed | tf_op | source)
XLA Modules:
  0.0 189.4 jit_solution(2874629213619288907)
XLA Ops:
  1.5 2.4 %copy.38 = bf16[8,8,32,512]{3,2,1,0:T(8,128)(2,1)S(1)} copy(bf16[8,8,32,512]{3,1,2,0:T(8,128)(2,1)} %bitcast.109) | data formatting | bytes 4194304
  3.9 2.2 %copy.61 = bf16[64,2,16,512]{3,1,0,2:T(2,128)(2,1)S(1)} copy(bf16[64,2,16,512]{3,2,1,0:T(8,128)(2,1)S(1)} %bitcast.104) | data formatting | bytes 4194304 | tf_op jit(solution)/shard_map/reshape | solution.py:120
  6.0 2.7 %reshape.72 = bf16[16,64,1024]{2,1,0:T(8,128)(2,1)} reshape(bf16[16,64,2,512]{3,2,1,0:T(2,128)(2,1)S(1)} %bitcast.103) | data formatting | bytes 4194304 | tf_op jit(solution)/shard_map/reshape | solution.py:120
  10.4 1.8 pad_maximum_fusion
  12.2 6.4 %all-to-all-start = ((bf16[16,64,1408]{2,1,0:T(8,128)(2,1)}), bf16[16,64,1408]{2,1,0:T(8,128)(2,1)S(1)}, u32[]{:S(2)}, u32[]{:S(2)}) async-start(bf16[16,64,1408]{2,1,0:T(8,128)(2,1)} %pad_maximum_fusion), calls=%async_computation | async-start | bytes 5767168 | tf_op jit(solution)/shard_map/all_to_all | solution.py:132
  21.0 1.9 collective-permute-start.3
  22.8 37.2 %collective-permute-done.3 = f32[32,128]{1,0:T(8,128)S(1)} collective-permute-done((f32[32,128]{1,0:T(8,128)S(1)}, f32[32,128]{1,0:T(8,128)S(1)}, u32[]{:S(2)}, u32[]{:S(2)}) %collective-permute-start.3) | collective-permute-done | bytes 16416 | tf_op jit(solution)/shard_map/ppermute | solution.py:14
  60.1 2.7 %collective-permute-start = (f32[64,128]{1,0:T(8,128)S(1)}, f32[64,128]{1,0:T(8,128)S(1)}, u32[]{:S(2)}, u32[]{:S(2)}) collective-permute-start(f32[64,128]{1,0:T(8,128)S(1)} %copy-done.15), channel_id=1, source_target_pairs={{0,16},{1,17},{2,18},{3,19},{4,20},{5,21},{6,22},{7,23},{8,24},{9,... | collective-permute-start | bytes 98312 | tf_op jit(solution)/shard_map/ppermute | solution.py:14
  64.9 2.6 %collective-permute-start.1 = (f32[64,512]{1,0:T(8,128)S(1)}, f32[64,512]{1,0:T(8,128)S(1)}, u32[]{:S(2)}, u32[]{:S(2)}) collective-permute-start(f32[64,512]{1,0:T(8,128)S(1)} %copy-done.8), channel_id=1, source_target_pairs={{0,16},{1,17},{2,18},{3,19},{4,20},{5,21},{6,22},{7,23},{8,24},{9,... | collective-permute-start | bytes 393224 | tf_op jit(solution)/shard_map/ppermute | solution.py:14
  67.6 2.6 %collective-permute-start.6 = (f32[32,128]{1,0:T(8,128)S(1)}, f32[32,128]{1,0:T(8,128)S(1)}, u32[]{:S(2)}, u32[]{:S(2)}) collective-permute-start(f32[32,128]{1,0:T(8,128)S(1)} %add.169), channel_id=1, source_target_pairs={{0,16},{1,17},{2,18},{3,19},{4,20},{5,21},{6,22},{7,23},{8,24},{9,... | collective-permute-start | bytes 49160 | tf_op jit(solution)/shard_map/ppermute | solution.py:14
  70.2 3.0 %collective-permute-done.6 = f32[32,128]{1,0:T(8,128)S(1)} collective-permute-done((f32[32,128]{1,0:T(8,128)S(1)}, f32[32,128]{1,0:T(8,128)S(1)}, u32[]{:S(2)}, u32[]{:S(2)}) %collective-permute-start.6) | collective-permute-done | bytes 16416 | tf_op jit(solution)/shard_map/ppermute | solution.py:14
  76.2 2.5 %collective-permute-done.12 = bf16[64,256]{1,0:T(8,128)(2,1)S(1)} collective-permute-done((bf16[64,256]{1,0:T(8,128)(2,1)S(1)}, bf16[64,256]{1,0:T(8,128)(2,1)S(1)}, u32[]{:S(2)}, u32[]{:S(2)}) %collective-permute-start.12) | collective-permute-done | bytes 32800 | tf_op jit(solution)/shard_map/ppermute | solution.py:14
  80.4 2.7 %collective-permute-done.13 = bf16[64,512]{1,0:T(8,128)(2,1)S(1)} collective-permute-done((bf16[64,512]{1,0:T(8,128)(2,1)S(1)}, bf16[64,512]{1,0:T(8,128)(2,1)S(1)}, u32[]{:S(2)}, u32[]{:S(2)}) %collective-permute-start.13) | collective-permute-done | bytes 65568 | tf_op jit(solution)/shard_map/ppermute | solution.py:14
  83.4 5.4 %collective-permute-done.7 = f32[64,1024]{1,0:T(8,128)S(1)} collective-permute-done((f32[64,1024]{1,0:T(8,128)S(1)}, f32[64,1024]{1,0:T(8,128)S(1)}, u32[]{:S(2)}, u32[]{:S(2)}) %collective-permute-start.7) | collective-permute-done | bytes 262176 | tf_op jit(solution)/shard_map/ppermute | solution.py:14
  90.2 3.7 %collective-permute-done.8 = f32[64,512]{1,0:T(8,128)S(1)} collective-permute-done((f32[64,512]{1,0:T(8,128)S(1)}, f32[64,512]{1,0:T(8,128)S(1)}, u32[]{:S(2)}, u32[]{:S(2)}) %collective-permute-start.8) | collective-permute-done | bytes 131104 | tf_op jit(solution)/shard_map/ppermute | solution.py:14
  95.0 3.2 %collective-permute-done.9 = f32[64,256]{1,0:T(8,128)S(1)} collective-permute-done((f32[64,256]{1,0:T(8,128)S(1)}, f32[64,256]{1,0:T(8,128)S(1)}, u32[]{:S(2)}, u32[]{:S(2)}) %collective-permute-start.9) | collective-permute-done | bytes 65568 | tf_op jit(solution)/shard_map/ppermute | solution.py:14
  100.5 1.7 copy.36
  110.6 7.6 %collective-permute-done.16 = f32[64,74]{1,0:T(8,128)S(1)} collective-permute-done((f32[64,74]{1,0:T(8,128)S(1)}, f32[64,74]{1,0:T(8,128)S(1)}, u32[]{:S(2)}, u32[]{:S(2)}) %collective-permute-start.16) | collective-permute-done | bytes 18976 | tf_op jit(solution)/shard_map/ppermute | solution.py:14
  123.2 2.8 %collective-permute-done.27 = bf16[64,256]{1,0:T(8,128)(2,1)S(1)} collective-permute-done((bf16[64,256]{1,0:T(8,128)(2,1)S(1)}, bf16[64,256]{1,0:T(8,128)(2,1)S(1)}, u32[]{:S(2)}, u32[]{:S(2)}) %collective-permute-start.27) | collective-permute-done | bytes 32800 | tf_op jit(solution)/shard_map/ppermute | solution.py:14
  126.5 3.8 %collective-permute-done.28 = bf16[64,512]{1,0:T(8,128)(2,1)S(1)} collective-permute-done((bf16[64,512]{1,0:T(8,128)(2,1)S(1)}, bf16[64,512]{1,0:T(8,128)(2,1)S(1)}, u32[]{:S(2)}, u32[]{:S(2)}) %collective-permute-start.28) | collective-permute-done | bytes 65568 | tf_op jit(solution)/shard_map/ppermute | solution.py:14
  130.4 1.6 collective-permute-start.29
  133.6 1.7 collective-permute-done.29
  135.4 2.7 %collective-permute-done.23 = f32[64,512]{1,0:T(8,128)S(1)} collective-permute-done((f32[64,512]{1,0:T(8,128)S(1)}, f32[64,512]{1,0:T(8,128)S(1)}, u32[]{:S(2)}, u32[]{:S(2)}) %collective-permute-start.23) | collective-permute-done | bytes 131104 | tf_op jit(solution)/shard_map/ppermute | solution.py:14
  139.9 2.7 %collective-permute-done.24 = f32[64,256]{1,0:T(8,128)S(1)} collective-permute-done((f32[64,256]{1,0:T(8,128)S(1)}, f32[64,256]{1,0:T(8,128)S(1)}, u32[]{:S(2)}, u32[]{:S(2)}) %collective-permute-start.24) | collective-permute-done | bytes 65568 | tf_op jit(solution)/shard_map/ppermute | solution.py:14
  143.1 1.8 collective-permute-done.19
  145.4 4.8 %collective-permute-done.20 = f32[64,576]{1,0:T(8,128)S(1)} collective-permute-done((f32[64,576]{1,0:T(8,128)S(1)}, f32[64,576]{1,0:T(8,128)S(1)}, u32[]{:S(2)}, u32[]{:S(2)}) %collective-permute-start.20) | collective-permute-done | bytes 147488 | tf_op jit(solution)/shard_map/ppermute | solution.py:14
  156.6 1.8 collective-permute-start.30
  159.8 9.0 %collective-permute-done.31 = f32[64,74]{1,0:T(8,128)S(1)} collective-permute-done((f32[64,74]{1,0:T(8,128)S(1)}, f32[64,74]{1,0:T(8,128)S(1)}, u32[]{:S(2)}, u32[]{:S(2)}) %collective-permute-start.31) | collective-permute-done | bytes 18976 | tf_op jit(solution)/shard_map/ppermute | solution.py:14
  169.0 1.7 fusion.8
  171.9 6.0 %collective-permute-done.32 = f32[64,576]{1,0:T(8,128)S(1)} collective-permute-done((f32[64,576]{1,0:T(8,128)S(1)}, f32[64,576]{1,0:T(8,128)S(1)}, u32[]{:S(2)}, u32[]{:S(2)}) %collective-permute-start.32) | collective-permute-done | bytes 147488 | tf_op jit(solution)/shard_map/ppermute | solution.py:14
  179.4 3.3 %collective-permute-done.33 = f32[64,320]{1,0:T(8,128)S(1)} collective-permute-done((f32[64,320]{1,0:T(8,128)S(1)}, f32[64,320]{1,0:T(8,128)S(1)}, u32[]{:S(2)}, u32[]{:S(2)}) %collective-permute-start.33) | collective-permute-done | bytes 81952 | tf_op jit(solution)/shard_map/ppermute | solution.py:14
  184.1 3.1 %collective-permute-done.34 = f32[64,192]{1,0:T(8,128)S(1)} collective-permute-done((f32[64,192]{1,0:T(8,128)S(1)}, f32[64,192]{1,0:T(8,128)S(1)}, u32[]{:S(2)}, u32[]{:S(2)}) %collective-permute-start.34) | collective-permute-done | bytes 49184 | tf_op jit(solution)/shard_map/ppermute | solution.py:14
  (208 shorter events, 48.0 us)
Async XLA Ops:
  12.2 87.4 %all-to-all-start = ((bf16[16,64,1408]{2,1,0:T(8,128)(2,1)}), bf16[16,64,1408]{2,1,0:T(8,128)(2,1)S(1)}, u32[]{:S(2)}, u32[]{:S(2)}) async-start(bf16[16,64,1408]{2,1,0:T(8,128)(2,1)} %pad_maximum_fusion), calls=%async_computation | async-start | bytes 5767168 | tf_op jit(solution)/shard_map/all_to_all | solution.py:132
  21.0 39.1 %collective-permute-start.3 = (f32[32,128]{1,0:T(8,128)S(1)}, f32[32,128]{1,0:T(8,128)S(1)}, u32[]{:S(2)}, u32[]{:S(2)}) collective-permute-start(f32[32,128]{1,0:T(8,128)S(1)} %add.166), channel_id=1, source_target_pairs={{0,2},{1,3},{2,0},{3,1},{4,6},{5,7},{6,4},{7,5},{8,10},{9,11},{10,... | collective-permute-start | bytes 49160 | tf_op jit(solution)/shard_map/ppermute | solution.py:14
  60.1 3.7 %collective-permute-start.4 = (f32[32,128]{1,0:T(8,128)S(1)}, f32[32,128]{1,0:T(8,128)S(1)}, u32[]{:S(2)}, u32[]{:S(2)}) collective-permute-start(f32[32,128]{1,0:T(8,128)S(1)} %add.167), channel_id=1, source_target_pairs={{0,4},{1,5},{2,6},{3,7},{4,0},{5,1},{6,2},{7,3},{8,12},{9,13},{10,... | collective-permute-start | bytes 49160 | tf_op jit(solution)/shard_map/ppermute | solution.py:14
  60.1 10.1 %collective-permute-start = (f32[64,128]{1,0:T(8,128)S(1)}, f32[64,128]{1,0:T(8,128)S(1)}, u32[]{:S(2)}, u32[]{:S(2)}) collective-permute-start(f32[64,128]{1,0:T(8,128)S(1)} %copy-done.15), channel_id=1, source_target_pairs={{0,16},{1,17},{2,18},{3,19},{4,20},{5,21},{6,22},{7,23},{8,24},{9,... | collective-permute-start | bytes 98312 | tf_op jit(solution)/shard_map/ppermute | solution.py:14
  63.8 3.8 %collective-permute-start.5 = (f32[32,128]{1,0:T(8,128)S(1)}, f32[32,128]{1,0:T(8,128)S(1)}, u32[]{:S(2)}, u32[]{:S(2)}) collective-permute-start(f32[32,128]{1,0:T(8,128)S(1)} %add.168), channel_id=1, source_target_pairs={{0,8},{1,9},{2,10},{3,11},{4,12},{5,13},{6,14},{7,15},{8,0},{9,1},... | collective-permute-start | bytes 49160 | tf_op jit(solution)/shard_map/ppermute | solution.py:14
  64.9 8.4 %collective-permute-start.1 = (f32[64,512]{1,0:T(8,128)S(1)}, f32[64,512]{1,0:T(8,128)S(1)}, u32[]{:S(2)}, u32[]{:S(2)}) collective-permute-start(f32[64,512]{1,0:T(8,128)S(1)} %copy-done.8), channel_id=1, source_target_pairs={{0,16},{1,17},{2,18},{3,19},{4,20},{5,21},{6,22},{7,23},{8,24},{9,... | collective-permute-start | bytes 393224 | tf_op jit(solution)/shard_map/ppermute | solution.py:14
  67.6 5.6 %collective-permute-start.6 = (f32[32,128]{1,0:T(8,128)S(1)}, f32[32,128]{1,0:T(8,128)S(1)}, u32[]{:S(2)}, u32[]{:S(2)}) collective-permute-start(f32[32,128]{1,0:T(8,128)S(1)} %add.169), channel_id=1, source_target_pairs={{0,16},{1,17},{2,18},{3,19},{4,20},{5,21},{6,22},{7,23},{8,24},{9,... | collective-permute-start | bytes 49160 | tf_op jit(solution)/shard_map/ppermute | solution.py:14
  74.7 4.0 %collective-permute-start.12 = (bf16[64,256]{1,0:T(8,128)(2,1)S(1)}, bf16[64,256]{1,0:T(8,128)(2,1)S(1)}, u32[]{:S(2)}, u32[]{:S(2)}) collective-permute-start(bf16[64,256]{1,0:T(8,128)(2,1)S(1)} %pad_maximum_fusion.16), channel_id=1, source_target_pairs={{0,2},{1,3},{2,0},{3,1},{4,6},{5,7},{6,4},{7,5},{8,10},{9,11},{10,... | collective-permute-start | bytes 98312 | tf_op jit(solution)/shard_map/ppermute | solution.py:14
  78.8 4.3 %collective-permute-start.13 = (bf16[64,512]{1,0:T(8,128)(2,1)S(1)}, bf16[64,512]{1,0:T(8,128)(2,1)S(1)}, u32[]{:S(2)}, u32[]{:S(2)}) collective-permute-start(bf16[64,512]{1,0:T(8,128)(2,1)S(1)} %pad_maximum_fusion.12), channel_id=1, source_target_pairs={{0,4},{1,5},{2,6},{3,7},{4,0},{5,1},{6,2},{7,3},{8,12},{9,13},{10,... | collective-permute-start | bytes 196616 | tf_op jit(solution)/shard_map/ppermute | solution.py:14
  80.4 8.4 %collective-permute-start.7 = (f32[64,1024]{1,0:T(8,128)S(1)}, f32[64,1024]{1,0:T(8,128)S(1)}, u32[]{:S(2)}, u32[]{:S(2)}) collective-permute-start(f32[64,1024]{1,0:T(8,128)S(1)} %slice_select_fusion.1), channel_id=1, source_target_pairs={{0,8},{1,9},{2,10},{3,11},{4,12},{5,13},{6,14},{7,15},{8,0},{9,1},... | collective-permute-start | bytes 786440 | tf_op jit(solution)/shard_map/ppermute | solution.py:14
  83.1 7.0 %collective-permute-start.14 = (bf16[64,1024]{1,0:T(8,128)(2,1)S(1)}, bf16[64,1024]{1,0:T(8,128)(2,1)S(1)}, u32[]{:S(2)}, u32[]{:S(2)}) collective-permute-start(bf16[64,1024]{1,0:T(8,128)(2,1)S(1)} %pad_maximum_fusion.8), channel_id=1, source_target_pairs={{0,8},{1,9},{2,10},{3,11},{4,12},{5,13},{6,14},{7,15},{8,0},{9,1},... | collective-permute-start | bytes 393224 | tf_op jit(solution)/shard_map/ppermute | solution.py:14
  88.9 5.0 %collective-permute-start.8 = (f32[64,512]{1,0:T(8,128)S(1)}, f32[64,512]{1,0:T(8,128)S(1)}, u32[]{:S(2)}, u32[]{:S(2)}) collective-permute-start(f32[64,512]{1,0:T(8,128)S(1)} %slice_select_fusion.7), channel_id=1, source_target_pairs={{0,4},{1,5},{2,6},{3,7},{4,0},{5,1},{6,2},{7,3},{8,12},{9,13},{10,... | collective-permute-start | bytes 393224 | tf_op jit(solution)/shard_map/ppermute | solution.py:14
  93.9 4.3 %collective-permute-start.9 = (f32[64,256]{1,0:T(8,128)S(1)}, f32[64,256]{1,0:T(8,128)S(1)}, u32[]{:S(2)}, u32[]{:S(2)}) collective-permute-start(f32[64,256]{1,0:T(8,128)S(1)} %slice_select_fusion.14), channel_id=1, source_target_pairs={{0,2},{1,3},{2,0},{3,1},{4,6},{5,7},{6,4},{7,5},{8,10},{9,11},{10,... | collective-permute-start | bytes 196616 | tf_op jit(solution)/shard_map/ppermute | solution.py:14
  106.1 12.2 %collective-permute-start.15 = (f16[64,1280]{1,0:T(8,128)(2,1)S(1)}, f16[64,1280]{1,0:T(8,128)(2,1)S(1)}, u32[]{:S(2)}, u32[]{:S(2)}) collective-permute-start(f16[64,1280]{1,0:T(8,128)(2,1)S(1)} %fusion.13), channel_id=1, source_target_pairs={{0,16},{1,17},{2,18},{3,19},{4,20},{5,21},{6,22},{7,23},{8,24},{9,... | collective-permute-start | bytes 491528 | tf_op jit(solution)/shard_map/ppermute | solution.py:14
  109.1 9.1 %collective-permute-start.16 = (f32[64,74]{1,0:T(8,128)S(1)}, f32[64,74]{1,0:T(8,128)S(1)}, u32[]{:S(2)}, u32[]{:S(2)}) collective-permute-start(f32[64,74]{1,0:T(8,128)S(1)} %pad_maximum_fusion.17), channel_id=1, source_target_pairs={{0,16},{1,17},{2,18},{3,19},{4,20},{5,21},{6,22},{7,23},{8,24},{9,... | collective-permute-start | bytes 56840 | tf_op jit(solution)/shard_map/ppermute | solution.py:14
  121.4 11.7 %collective-permute-start.22 = (f32[64,1024]{1,0:T(8,128)S(1)}, f32[64,1024]{1,0:T(8,128)S(1)}, u32[]{:S(2)}, u32[]{:S(2)}) collective-permute-start(f32[64,1024]{1,0:T(8,128)S(1)} %slice_select_fusion), channel_id=1, source_target_pairs={{0,8},{1,9},{2,10},{3,11},{4,12},{5,13},{6,14},{7,15},{8,0},{9,1},... | collective-permute-start | bytes 786440 | tf_op jit(solution)/shard_map/ppermute | solution.py:14
  122.0 4.0 %collective-permute-start.27 = (bf16[64,256]{1,0:T(8,128)(2,1)S(1)}, bf16[64,256]{1,0:T(8,128)(2,1)S(1)}, u32[]{:S(2)}, u32[]{:S(2)}) collective-permute-start(bf16[64,256]{1,0:T(8,128)(2,1)S(1)} %pad_maximum_fusion.18), channel_id=1, source_target_pairs={{0,2},{1,3},{2,0},{3,1},{4,6},{5,7},{6,4},{7,5},{8,10},{9,11},{10,... | collective-permute-start | bytes 98312 | tf_op jit(solution)/shard_map/ppermute | solution.py:14
  126.0 4.3 %collective-permute-start.28 = (bf16[64,512]{1,0:T(8,128)(2,1)S(1)}, bf16[64,512]{1,0:T(8,128)(2,1)S(1)}, u32[]{:S(2)}, u32[]{:S(2)}) collective-permute-start(bf16[64,512]{1,0:T(8,128)(2,1)S(1)} %pad_maximum_fusion.13), channel_id=1, source_target_pairs={{0,4},{1,5},{2,6},{3,7},{4,0},{5,1},{6,2},{7,3},{8,12},{9,13},{10,... | collective-permute-start | bytes 196616 | tf_op jit(solution)/shard_map/ppermute | solution.py:14
  126.4 5.6 %collective-permute-start.17 = (f32[64,576]{1,0:T(8,128)S(1)}, f32[64,576]{1,0:T(8,128)S(1)}, u32[]{:S(2)}, u32[]{:S(2)}) collective-permute-start(f32[64,576]{1,0:T(8,128)S(1)} %pad_maximum_fusion.4), channel_id=1, source_target_pairs={{0,1},{1,0},{2,3},{3,2},{4,5},{5,4},{6,7},{7,6},{8,9},{9,8},{10,11... | collective-permute-start | bytes 442376 | tf_op jit(solution)/shard_map/ppermute | solution.py:14
  130.4 5.0 %collective-permute-start.29 = (bf16[64,1024]{1,0:T(8,128)(2,1)S(1)}, bf16[64,1024]{1,0:T(8,128)(2,1)S(1)}, u32[]{:S(2)}, u32[]{:S(2)}) collective-permute-start(bf16[64,1024]{1,0:T(8,128)(2,1)S(1)} %pad_maximum_fusion.10), channel_id=1, source_target_pairs={{0,8},{1,9},{2,10},{3,11},{4,12},{5,13},{6,14},{7,15},{8,0},{9,1},... | collective-permute-start | bytes 393224 | tf_op jit(solution)/shard_map/ppermute | solution.py:14
  132.0 7.4 %collective-permute-start.18 = (f32[64,576]{1,0:T(8,128)S(1)}, f32[64,576]{1,0:T(8,128)S(1)}, u32[]{:S(2)}, u32[]{:S(2)}) collective-permute-start(f32[64,576]{1,0:T(8,128)S(1)} %fusion.19), channel_id=1, source_target_pairs={{0,2},{1,3},{2,0},{3,1},{4,6},{5,7},{6,4},{7,5},{8,10},{9,11},{10,... | collective-permute-start | bytes 442376 | tf_op jit(solution)/shard_map/ppermute | solution.py:14
  133.1 5.0 %collective-permute-start.23 = (f32[64,512]{1,0:T(8,128)S(1)}, f32[64,512]{1,0:T(8,128)S(1)}, u32[]{:S(2)}, u32[]{:S(2)}) collective-permute-start(f32[64,512]{1,0:T(8,128)S(1)} %slice_select_fusion.4), channel_id=1, source_target_pairs={{0,4},{1,5},{2,6},{3,7},{4,0},{5,1},{6,2},{7,3},{8,12},{9,13},{10,... | collective-permute-start | bytes 393224 | tf_op jit(solution)/shard_map/ppermute | solution.py:14
  138.2 4.3 %collective-permute-start.24 = (f32[64,256]{1,0:T(8,128)S(1)}, f32[64,256]{1,0:T(8,128)S(1)}, u32[]{:S(2)}, u32[]{:S(2)}) collective-permute-start(f32[64,256]{1,0:T(8,128)S(1)} %slice_select_fusion.13), channel_id=1, source_target_pairs={{0,2},{1,3},{2,0},{3,1},{4,6},{5,7},{6,4},{7,5},{8,10},{9,11},{10,... | collective-permute-start | bytes 196616 | tf_op jit(solution)/shard_map/ppermute | solution.py:14
  139.4 5.4 %collective-permute-start.19 = (f32[64,576]{1,0:T(8,128)S(1)}, f32[64,576]{1,0:T(8,128)S(1)}, u32[]{:S(2)}, u32[]{:S(2)}) collective-permute-start(f32[64,576]{1,0:T(8,128)S(1)} %add.188), channel_id=1, source_target_pairs={{0,4},{1,5},{2,6},{3,7},{4,0},{5,1},{6,2},{7,3},{8,12},{9,13},{10,... | collective-permute-start | bytes 442376 | tf_op jit(solution)/shard_map/ppermute | solution.py:14
  142.6 2.8 %collective-permute-start.25 = (f32[64,128]{1,0:T(8,128)S(1)}, f32[64,128]{1,0:T(8,128)S(1)}, u32[]{:S(2)}, u32[]{:S(2)}) collective-permute-start(f32[64,128]{1,0:T(8,128)S(1)} %slice_select_fusion.18), channel_id=1, source_target_pairs={{0,1},{1,0},{2,3},{3,2},{4,5},{5,4},{6,7},{7,6},{8,9},{9,8},{10,11... | collective-permute-start | bytes 98312 | tf_op jit(solution)/shard_map/ppermute | solution.py:14
  144.9 5.4 %collective-permute-start.20 = (f32[64,576]{1,0:T(8,128)S(1)}, f32[64,576]{1,0:T(8,128)S(1)}, u32[]{:S(2)}, u32[]{:S(2)}) collective-permute-start(f32[64,576]{1,0:T(8,128)S(1)} %add.189), channel_id=1, source_target_pairs={{0,8},{1,9},{2,10},{3,11},{4,12},{5,13},{6,14},{7,15},{8,0},{9,1},... | collective-permute-start | bytes 442376 | tf_op jit(solution)/shard_map/ppermute | solution.py:14
  150.6 1.4 collective-permute-start.21
  156.6 12.2 %collective-permute-start.30 = (f16[64,1280]{1,0:T(8,128)(2,1)S(1)}, f16[64,1280]{1,0:T(8,128)(2,1)S(1)}, u32[]{:S(2)}, u32[]{:S(2)}) collective-permute-start(f16[64,1280]{1,0:T(8,128)(2,1)S(1)} %fusion.9), channel_id=1, source_target_pairs={{0,16},{1,17},{2,18},{3,19},{4,20},{5,21},{6,22},{7,23},{8,24},{9,... | collective-permute-start | bytes 491528 | tf_op jit(solution)/shard_map/ppermute | solution.py:14
  158.6 10.2 %collective-permute-start.31 = (f32[64,74]{1,0:T(8,128)S(1)}, f32[64,74]{1,0:T(8,128)S(1)}, u32[]{:S(2)}, u32[]{:S(2)}) collective-permute-start(f32[64,74]{1,0:T(8,128)S(1)} %pad_maximum_fusion.19), channel_id=1, source_target_pairs={{0,16},{1,17},{2,18},{3,19},{4,20},{5,21},{6,22},{7,23},{8,24},{9,... | collective-permute-start | bytes 56840 | tf_op jit(solution)/shard_map/ppermute | solution.py:14
  171.9 6.1 %collective-permute-start.32 = (f32[64,576]{1,0:T(8,128)S(1)}, f32[64,576]{1,0:T(8,128)S(1)}, u32[]{:S(2)}, u32[]{:S(2)}) collective-permute-start(f32[64,576]{1,0:T(8,128)S(1)} %pad_maximum_fusion.6), channel_id=1, source_target_pairs={{0,8},{1,9},{2,10},{3,11},{4,12},{5,13},{6,14},{7,15},{8,0},{9,1},... | collective-permute-start | bytes 442376 | tf_op jit(solution)/shard_map/ppermute | solution.py:14
  178.0 4.7 %collective-permute-start.33 = (f32[64,320]{1,0:T(8,128)S(1)}, f32[64,320]{1,0:T(8,128)S(1)}, u32[]{:S(2)}, u32[]{:S(2)}) collective-permute-start(f32[64,320]{1,0:T(8,128)S(1)} %pad_maximum_fusion.11), channel_id=1, source_target_pairs={{0,4},{1,5},{2,6},{3,7},{4,0},{5,1},{6,2},{7,3},{8,12},{9,13},{10,... | collective-permute-start | bytes 245768 | tf_op jit(solution)/shard_map/ppermute | solution.py:14
  182.8 4.3 %collective-permute-start.34 = (f32[64,192]{1,0:T(8,128)S(1)}, f32[64,192]{1,0:T(8,128)S(1)}, u32[]{:S(2)}, u32[]{:S(2)}) collective-permute-start(f32[64,192]{1,0:T(8,128)S(1)} %pad_maximum_fusion.14), channel_id=1, source_target_pairs={{0,2},{1,3},{2,0},{3,1},{4,6},{5,7},{6,4},{7,5},{8,10},{9,11},{10,... | collective-permute-start | bytes 147464 | tf_op jit(solution)/shard_map/ppermute | solution.py:14
  (24 other events, 268.4 us)

commit v2 on v1

--- a/solution.py
+++ b/solution.py
@@ -1,12 +1,20 @@
+import functools
+
 import jax
 import jax.numpy as jnp
 from jax import lax
+from jax.experimental import pallas as pl
+from jax.experimental.pallas import tpu as pltpu
 from jax.sharding import PartitionSpec as P
 
 BLOCK = 128
 ROUNDS = 2
 EPSILON = 1e-06
+TINY = 1e-30
 AXIS = "cells"
+PARAMS = pltpu.CompilerParams(vmem_limit_bytes=32 * 1024 * 1024)
+SMEM = pl.BlockSpec(memory_space=pltpu.SMEM)
+VMEM = pl.BlockSpec(memory_space=pltpu.VMEM)
 
 
 def flip(value, bit):
@@ -85,7 +93,7 @@
     return jnp.concatenate([*(jnp.where(side == s, to_gene, nothing) for s in range(2)), to_peak], axis=1)
 
 
-def shards(
+def shards_any(
     rna_counts,
     atac_counts,
     cell_factor,
@@ -208,6 +216,450 @@
     return cell_state, own(0, gene_width), own(2 * gene_width, peak_width)
 
 
+def layout(bits):
+    size = 1 << len(bits)
+    return [
+        sum(bit for i, bit in enumerate(bits) if position >> (len(bits) - 1 - i) & 1)
+        for position in range(size)
+    ]
+
+
+def turned(bits, by):
+    return bits[by:] + bits[:by]
+
+
+def across(left, right):
+    return lax.dot_general(left, right, (((1,), (1,)), ((), ())), preferred_element_type=jnp.float32)
+
+
+def exact(left, right):
+    return lax.dot_general(
+        left,
+        right,
+        (((1,), (0,)), ((), ())),
+        precision=lax.Precision.HIGHEST,
+        preferred_element_type=jnp.float32,
+    )
+
+
+def halved(value):
+    high = value.astype(jnp.bfloat16)
+    return high, (value - high.astype(jnp.float32)).astype(jnp.bfloat16)
+
+
+def struct(*shape, dtype=jnp.float32):
+    return jax.ShapeDtypeStruct(shape, dtype)
+
+
+def gram_of(high, rest):
+    pair = jnp.concatenate([high, rest], axis=0)
+    squares = across(pair, pair)
+    rank = high.shape[0]
+    return (squares[:rank, :rank] + squares[rank:, rank:]) + (squares[:rank, rank:] + squares[rank:, :rank])
+
+
+def parcels_kernel(rna_0, rna_1, atac_0, atac_1, cell, gene, peak, slots, out):
+    rank = cell.shape[0]
+    cells = rna_0.shape[0]
+    gene_width, peak_width = gene.shape[1], peak.shape[1]
+    width = gene_width + peak_width
+    cell_pair = jnp.concatenate(halved(cell[...]), axis=1)
+    gene_low = gene[...].astype(jnp.bfloat16)
+    peak_low = peak[...].astype(jnp.bfloat16)
+    part = rank // 4
+    for j in range(out.shape[0]):
+        at = 0
+        for source, size in ((rna_0, gene_width), (rna_1, gene_width), (atac_0, peak_width), (atac_1, peak_width)):
+            out[j, 0:cells, at : at + size] = source[:, j * size : (j + 1) * size]
+            at += size
+        out[j, 0:cells, at:] = cell_pair
+        for s in range(2):
+            row = (2 * (j % 2) + s) * part
+            out[j, cells:, s * width : s * width + gene_width] = gene_low[row : row + part]
+            out[j, cells:, s * width + gene_width : (s + 1) * width] = peak_low[row : row + part]
+        out[j, cells:, 2 * width :] = slots[...]
+
+
+def parcels(rna_counts, atac_counts, cell_factor, gene_factor, peak_factor, slots, half):
+    cells = rna_counts.shape[0]
+    rank = cell_factor.shape[0]
+    gene_width, peak_width = gene_factor.shape[1], peak_factor.shape[1]
+    rows, lanes = cells + rank // 4, 2 * (gene_width + peak_width) + 2 * rank
+    each = 4
+    steps = half // each
+
+    def columns(width, side):
+        return pl.BlockSpec((cells, each * width), lambda i: (0, i + side * steps))
+
+    def whole(array):
+        return pl.BlockSpec(array.shape, lambda i: (0, 0))
+
+    return pl.pallas_call(
+        parcels_kernel,
+        grid=(steps,),
+        in_specs=[columns(gene_width, 0), columns(gene_width, 1), columns(peak_width, 0), columns(peak_width, 1)]
+        + [whole(a) for a in (cell_factor, gene_factor, peak_factor, slots)],
+        out_specs=pl.BlockSpec((each, rows, lanes), lambda i: (i, 0, 0)),
+        out_shape=struct(half, rows, lanes, dtype=jnp.bfloat16),
+        compiler_params=PARAMS,
+    )(rna_counts, rna_counts, atac_counts, atac_counts, cell_factor, gene_factor, peak_factor, slots)
+
+
+def first_sums_kernel(received, sums, gram):
+    half, cells, features = received.shape[0], received.shape[1] - sums.shape[0] // 4, sums.shape[1]
+    rank = sums.shape[0]
+    high = jnp.concatenate([received[j, 0:cells, features : features + rank] for j in range(half)], axis=1)
+    rest = jnp.concatenate([received[j, 0:cells, features + rank :] for j in range(half)], axis=1)
+    counts = jnp.concatenate([received[j, 0:cells, 0:features] for j in range(half)], axis=0)
+    sums[...] = jnp.dot(high, counts, preferred_element_type=jnp.float32)
+    gram[...] = gram_of(high, rest)
+
+
+def finish_sums(sums_value, gram_value, widths, sums, scaled, beside):
+    rank, features = sums_value.shape
+    largest = []
+    for b in range(features // BLOCK):
+        group = sums_value[:, b * BLOCK : (b + 1) * BLOCK]
+        top = jnp.maximum(jnp.max(group, axis=1, keepdims=True), TINY)
+        sums[:, b * BLOCK : (b + 1) * BLOCK] = group
+        scaled[:, b * BLOCK : (b + 1) * BLOCK] = group / top
+        largest.append(top)
+    pad = jnp.zeros((rank, beside.shape[1] - rank - len(largest)), jnp.float32)
+    beside[...] = jnp.concatenate([gram_value, *largest, pad], axis=1)
+
+
+def first_links_kernel(
+    link_scale, widths, spot, mine, other, sums_in, gram, sums, scaled, beside, table, table_sem, table_smem
+):
+    half = mine.shape[0]
+    rank, features = sums_in.shape
+    gene_width, peak_width = widths
+    gene_blocks, peak_blocks = gene_width // BLOCK, peak_width // BLOCK
+    width = gene_width + peak_width
+    slots = mine[:, :, 2 * width :].reshape(half * mine.shape[1], 2 * rank).astype(jnp.float32)
+
+    def hot(column, size, value):
+        ids = lax.broadcasted_iota(jnp.int32, (slots.shape[0], size), 1).astype(jnp.float32)
+        return jnp.where(slots[:, column : column + 1] == ids, value, 0.0).astype(jnp.bfloat16)
+
+    table[...] = lax.dot_general(
+        hot(0, table.shape[0], slots[:, 2:3]),
+        hot(1, table.shape[1], 1.0),
+        (((0,), (0,)), ((), ())),
+        preferred_element_type=jnp.float32,
+    )
+    copy = pltpu.make_async_copy(table, table_smem, table_sem)
+    copy.start()
+    copy.wait()
+    side, place, core = spot[0], spot[1], spot[2]
+    total = [None] * (features // BLOCK)
+
+    def add(target, weight, block):
+        term = weight * block
+        total[target] = term if total[target] is None else total[target] + term
+
+    for j in range(half):
+        blocks = []
+        for b in range(width // BLOCK):
+            pieces = [
+                ref[j, :, s * width + b * BLOCK : s * width + (b + 1) * BLOCK] for ref in (mine, other) for s in range(2)
+            ]
+            blocks.append(jnp.concatenate(pieces, axis=0).astype(jnp.float32))
+        for b in range(gene_blocks):
+            row = (side * half + j) * gene_blocks + b
+            for u in range(2 * peak_blocks):
+                column = (place + u // peak_blocks * half) * peak_blocks + u % peak_blocks
+                add(2 * gene_blocks + u, table_smem[row, column], blocks[b])
+        for b in range(peak_blocks):
+            column = (side * half + j) * peak_blocks + b
+            for t in range(2 * gene_blocks):
+                row = (place + t // gene_blocks * half) * gene_blocks + t % gene_blocks
+                add(t, table_smem[row, column], blocks[gene_blocks + b])
+    links = jnp.concatenate(total, axis=1)
+    ahead, behind = links[: rank // 2], links[rank // 2 :]
+    first = core == 0
+    links = jnp.concatenate([jnp.where(first, ahead, behind), jnp.where(first, behind, ahead)], axis=0)
+    finish_sums(sums_in[...] + link_scale * links, gram[...], widths, sums, scaled, beside)
+
+
+def next_sums_kernel(
+    link_scale, widths, orders, spot, table, mine, other, received, to_gene, genes, sums, scaled, beside
+):
+    half = received.shape[0]
+    rank, features = sums.shape
+    cells = mine.shape[1] * 2 // (2 * half)
+    gene_width, peak_width = widths
+    gene_blocks, peak_blocks = gene_width // BLOCK, peak_width // BLOCK
+    side, place, core = spot[0], spot[1], spot[2]
+    first = core == 0
+    left, right = mine[...], other[...]
+    even, odd = jnp.where(first, left, right), jnp.where(first, right, left)
+    kept = half // 2 * cells
+    high = jnp.concatenate([even[:, :kept], odd[:, :kept]], axis=1)
+    rest = jnp.concatenate([even[:, kept:], odd[:, kept:]], axis=1)
+    counts = jnp.concatenate([received[j, 0:cells, 0:features] for j in orders[0]], axis=0)
+    products = jnp.dot(high, counts, preferred_element_type=jnp.float32)
+    total = [None] * (2 * peak_blocks)
+    for position, j in enumerate(orders[1]):
+        for b in range(gene_blocks):
+            at = (position * gene_blocks + b) * BLOCK
+            block = genes[:, at : at + BLOCK].astype(jnp.float32)
+            row = (side * half + j) * gene_blocks + b
+            for u in range(2 * peak_blocks):
+                column = (place + u // peak_blocks * half) * peak_blocks + u % peak_blocks
+                term = table[row, column] * block
+                total[u] = term if total[u] is None else total[u] + term
+    gene_links = to_gene[...]
+    nothing = jnp.zeros_like(gene_links)
+    links = jnp.concatenate(
+        [jnp.where(side == 0, gene_links, nothing), jnp.where(side == 0, nothing, gene_links), *total], axis=1
+    )
+    finish_sums(products + link_scale * links, gram_of(high, rest), widths, sums, scaled, beside)
+
+
+def update_kernel(last, widths, orders, spot, table, sums, other, beside, beside_other, factors, received, *outs):
+    half = received.shape[0]
+    rank, features = sums.shape
+    cells = received.shape[1] - rank // 4
+    gene_width, peak_width = widths
+    gene_blocks, peak_blocks = gene_width // BLOCK, peak_width // BLOCK
+    side, place, core = spot[0], spot[1], spot[2]
+    first = core == 0
+    gram = beside[:, 0:rank] + beside_other[:, 0:rank]
+    old = factors[...]
+    below = exact(gram, old) + EPSILON
+    whole = jnp.concatenate(
+        [
+            sums[:, b * BLOCK : (b + 1) * BLOCK]
+            + other[:, b * BLOCK : (b + 1) * BLOCK] * beside_other[:, rank + b : rank + b + 1]
+            for b in range(features // BLOCK)
+        ],
+        axis=1,
+    )
+    new = old * whole / below
+    low = new.astype(jnp.bfloat16)
+    cell_sums = jnp.concatenate([across(low, received[j, 0:cells, 0:features]) for j in orders[0]], axis=1)
+    gram_features = across(low, low)
+    kept, sent, *outs = outs
+    split = half // 2 * cells
+    left, right = cell_sums[:, :split], cell_sums[:, split:]
+    for ref, value in ((kept, jnp.where(first, left, right)), (sent, jnp.where(first, right, left))):
+        ref[:, :split] = value
+        ref[:, split : split + rank] = gram_features
+        ref[:, split + rank :] = jnp.zeros((rank, ref.shape[1] - split - rank), jnp.float32)
+
+    def own(at, width):
+        return jnp.where(side == 0, new[:, at : at + width], new[:, at + width : at + 2 * width])
+
+    if last:
+        gene_out, peak_out = outs
+        gene_out[...] = own(0, gene_width)
+        peak_out[...] = own(2 * gene_width, peak_width)
+        return
+    factors_out, links_kept, links_sent, gene_low = outs
+    factors_out[...] = new
+    gene_low[...] = own(0, gene_width).astype(jnp.bfloat16)
+    peaks = low[:, 2 * gene_width :].astype(jnp.float32)
+    peaks = [peaks[:, u * BLOCK : (u + 1) * BLOCK] for u in range(2 * peak_blocks)]
+    for position in range(half // 2):
+        pair = []
+        for j in (orders[1][position], orders[1][position + half // 2]):
+            parts = []
+            for b in range(gene_blocks):
+                row = (side * half + j) * gene_blocks + b
+                part = None
+                for u, block in enumerate(peaks):
+                    column = (place + u // peak_blocks * half) * peak_blocks + u % peak_blocks
+                    term = table[row, column] * block
+                    part = term if part is None else part + term
+                parts.append(part)
+            pair.append(jnp.concatenate(parts, axis=1))
+        at = position * gene_width
+        links_kept[:, at : at + gene_width] = jnp.where(first, *pair)
+        links_sent[:, at : at + gene_width] = jnp.where(first, pair[1], pair[0])
+
+
+def cells_kernel(order, spot, totals, received_cells, pair, own):
+    rank = totals.shape[0]
+    cells = own.shape[1]
+    kept = cells * len(order) // 2
+    place, core = spot[1], spot[2]
+    first = core == 0
+
+    def state(j):
+        terms = received_cells[j].astype(jnp.float32)
+        return terms[:, :rank] + terms[:, rank:]
+
+    old = jnp.concatenate(
+        [
+            jnp.where(first, state(order[s]), state(order[s + len(order) // 2]))
+            for s in range(len(order) // 2)
+        ],
+        axis=1,
+    )
+    new = old * totals[:, :kept] / (exact(totals[:, kept : kept + rank], old) + EPSILON)
+    pair[...] = jnp.concatenate(halved(new), axis=1)
+    mine = new[:, :cells]
+    for s in range(1, len(order) // 2):
+        mine = jnp.where(place // 2 == order[s] // 2, new[:, s * cells : (s + 1) * cells], mine)
+    own[...] = mine
+
+
+def shards_blocks(
+    rna_counts,
+    atac_counts,
+    cell_factor,
+    gene_factor,
+    peak_factor,
+    link_gene,
+    link_peak,
+    link_weight,
+    link_count,
+):
+    count = lax.axis_size(AXIS)
+    half = count // 2
+    me = lax.axis_index(AXIS)
+    side, place, core = me // half, me % half, me % 2
+    spot = jnp.stack([side, place, core]).astype(jnp.int32)
+    rank, cells = cell_factor.shape
+    gene_width, peak_width = gene_factor.shape[1], peak_factor.shape[1]
+    widths = (gene_width, peak_width)
+    width = gene_width + peak_width
+    features = 2 * width
+    link_scale = cells * count / 4.0
+    table_shape = (rna_counts.shape[1] // BLOCK, atac_counts.shape[1] // BLOCK)
+    chip_bits = bits_below(half)[1:]
+    cell_bits, link_bits, gene_bits = (turned(chip_bits, i % len(chip_bits)) for i in range(3))
+    cell_order = layout([1] + cell_bits)
+    link_order = layout([1] + link_bits)
+    gene_order = layout([1] + gene_bits[::-1])
+
+    live = jnp.arange(link_gene.shape[0], dtype=jnp.int32) < link_count[0]
+    slots = jnp.stack([link_gene, link_peak, jnp.where(live, link_weight, 0)], axis=1).astype(jnp.float32)
+    slots = jnp.pad(slots, ((0, 0), (0, 2 * rank - slots.shape[1])))
+    slots_other = flip(slots, half)
+    state = jnp.concatenate([gene_factor, peak_factor], axis=1)
+    state_other = flip(state, half)
+    slots = jnp.concatenate([slots, slots_other], axis=0)
+    slots = jnp.pad(slots, ((0, rank // 4 - slots.shape[0]), (0, 0))).astype(jnp.bfloat16)
+    sent = parcels(rna_counts, atac_counts, cell_factor, gene_factor, peak_factor, slots, half)
+    halves = [list(range(half)), list(range(half, count))]
+    received = lax.all_to_all(sent, AXIS, 0, 0, axis_index_groups=halves, tiled=True)
+    low, high = in_order(half, state, state_other)
+    factors = jnp.concatenate(
+        [low[:, :gene_width], high[:, :gene_width], low[:, gene_width:], high[:, gene_width:]], axis=1
+    )
+
+    sums_shapes = (struct(rank, features), struct(rank, features), struct(rank, 2 * rank))
+    rows_other = flip(received[:, cells:, :features], 1)
+    sums, gram = pl.pallas_call(
+        first_sums_kernel,
+        in_specs=[VMEM],
+        out_specs=[VMEM] * 2,
+        out_shape=(struct(rank, features), struct(rank, rank)),
+        compiler_params=PARAMS,
+    )(received)
+    rows = rank // 4
+    sums, scaled, beside, link_table = pl.pallas_call(
+        functools.partial(first_links_kernel, link_scale, widths),
+        grid=(1,),
+        in_specs=[
+            SMEM,
+            pl.BlockSpec((half, rows, features + 2 * rank), lambda i: (0, cells // rows, 0)),
+            VMEM,
+            VMEM,
+            VMEM,
+        ],
+        out_specs=[VMEM] * 4,
+        out_shape=(*sums_shapes, struct(*table_shape)),
+        scratch_shapes=[pltpu.SemaphoreType.DMA, pltpu.SMEM(table_shape, jnp.float32)],
+        compiler_params=PARAMS,
+    )(spot, received, rows_other, sums, gram)
+
+    split = half // 2 * cells
+    for sweep_index in range(ROUNDS):
+        last = sweep_index == ROUNDS - 1
+        beside_other = flip(beside, half)
+        other = flip(scaled.astype(jnp.float16), half).astype(jnp.float32)
+        lanes = -(-(split + rank) // BLOCK) * BLOCK
+        outs = [struct(rank, lanes)] * 2
+        if last:
+            outs += [struct(rank, gene_width), struct(rank, peak_width)]
+        else:
+            outs += [struct(rank, features)] + [struct(rank, half // 2 * gene_width)] * 2
+            outs += [struct(rank, gene_width, dtype=jnp.bfloat16)]
+        kept, sent, *outs = pl.pallas_call(
+            functools.partial(update_kernel, last, widths, (cell_order, link_order)),
+            in_specs=[SMEM] * 2 + [VMEM] * 6,
+            out_specs=[VMEM] * len(outs),
+            out_shape=outs,
+            compiler_params=PARAMS,
+        )(spot, link_table, sums, other, beside, beside_other, factors, received)
+        if last:
+            gene_out, peak_out = outs
+            totals = kept + flip(sent, 1)
+            cell_sums, gram_features = totals[:, :split], totals[:, split : split + rank]
+            for bit in cell_bits:
+                left, right = jnp.split(cell_sums, 2, axis=1)
+                clear = (me & bit) == 0
+                got = flip(jnp.concatenate([jnp.where(clear, right, left), gram_features], axis=1), bit)
+                cell_sums = jnp.where(clear, left, right) + got[:, : left.shape[1]]
+                gram_features = gram_features + got[:, left.shape[1] :]
+            cell_out = own_cells * cell_sums / (exact(gram_features, own_cells) + EPSILON)
+            return cell_out, gene_out, peak_out
+        factors, links_kept, links_sent, genes = outs
+        totals = kept + flip(sent, 1)
+        to_gene = links_kept + flip(links_sent, 1)
+        for cell_bit, link_bit, gene_bit in zip(cell_bits, link_bits, gene_bits):
+            totals_other = flip(totals, cell_bit)
+            left, right = jnp.split(to_gene, 2, axis=1)
+            clear = (me & link_bit) == 0
+            to_gene_other = flip(jnp.where(clear, right, left), link_bit)
+            genes_other = flip(genes, gene_bit)
+            totals = totals + totals_other
+            to_gene = jnp.where(clear, left, right) + to_gene_other
+            genes = jnp.concatenate(in_order(gene_bit, genes, genes_other), axis=1)
+        genes = jnp.concatenate(in_order(1, genes, flip(genes, 1)), axis=1)
+        pair, own_cells = pl.pallas_call(
+            functools.partial(cells_kernel, cell_order),
+            grid=(1,),
+            in_specs=[
+                SMEM,
+                VMEM,
+                pl.BlockSpec((half, cells, 2 * rank), lambda i: (0, 0, features // (2 * rank))),
+            ],
+            out_specs=[VMEM] * 2,
+            out_shape=(struct(rank, 2 * split, dtype=jnp.bfloat16), struct(rank, cells)),
+            compiler_params=PARAMS,
+        )(spot, totals, received)
+        sums, scaled, beside = pl.pallas_call(
+            functools.partial(next_sums_kernel, link_scale, widths, (cell_order, gene_order)),
+            in_specs=[SMEM] * 2 + [VMEM] * 5,
+            out_specs=[VMEM] * 3,
+            out_shape=sums_shapes,
+            compiler_params=PARAMS,
+        )(spot, link_table, pair, flip(pair, 1), received, to_gene, genes)
+
+
+def shards(rna_counts, atac_counts, cell_factor, gene_factor, peak_factor, link_gene, *links):
+    half = lax.axis_size(AXIS) // 2
+    rank, cells = cell_factor.shape
+    gene_width, peak_width = gene_factor.shape[1], peak_factor.shape[1]
+    features = 2 * (gene_width + peak_width)
+    in_blocks = (
+        half % 8 == 0
+        and rank == cells
+        and 2 * rank == BLOCK
+        and gene_width % BLOCK == 0
+        and peak_width % BLOCK == 0
+        and features // BLOCK <= rank
+        and 2 * link_gene.shape[0] <= rank // 4
+        and max(rna_counts.shape[1], atac_counts.shape[1]) // BLOCK <= 256
+    )
+    run = shards_blocks if in_blocks else shards_any
+    return run(rna_counts, atac_counts, cell_factor, gene_factor, peak_factor, link_gene, *links)
+
+
 def solution(mesh):
     columns = P(None, ("groups", "cells"))
     slots = P(("groups", "cells"))

time: 190 us -> 161 us (0.85)
  blocking collectives: 0 us -> 48.5 us
  waiting for transfers between devices: 114 us -> 67.3 us
  starting transfers between devices: 36.6 us -> 18.2 us
  Pallas kernels: 0 us -> 11.9 us
  matrix products: 11.3 us -> 0.85 us
  other arithmetic: 9 us -> 1.55 us
  local copies, waits for them, and re-layouts: 16.2 us -> 10.5 us
    all_to_all x0 -> x1, blocking collectives: none -> 48.5 us  [shards_blocks(): lax.all_to_all(sent, AXIS, 0, 0, axis_index_groups=halves, tiled=True)]
    ppermute x36 -> x24, waiting for transfers between devices: 114 us -> 67.3 us  [flip(): return lax.ppermute(value, AXIS, [(i, i ^ bit) for i in range(count)])]
    ppermute x36 -> x24, starting transfers between devices: 30.2 us -> 18.2 us  [flip(): return lax.ppermute(value, AXIS, [(i, i ^ bit) for i in range(count)])]
    pallas_call x0 -> x7, Pallas kernels: none -> 11.9 us  [the longest x2 4.6 us: shards_blocks(): pl.pallas_call(functools.partial(update_kernel, last, widths, (cell_order...]
    dot_general x17 -> x1, matrix products: 11.3 us -> 0.85 us  [exact(): lax.dot_general(left, right, (((1,), (0,)), ((), ())), precision=lax.Prec...]
    reshape x6 -> x0, local copies, waits for them, and re-layouts: 7.63 us -> none  [the longest x4 5.73 us: by_place(): counts.reshape(cells, 2, half, width).transpose(2, 0, 1, 3)]
    all_to_all x1 -> x0, starting transfers between devices: 6.44 us -> none  [shards(): lax.all_to_all(parcels, AXIS, 0, 0, axis_index_groups=halves, tiled=True)]
    concatenate x17 -> x9, other arithmetic: 2.27 us -> 0.17 us  [the longest x3 0.1 us: shards_blocks(): jnp.concatenate([jnp.where(clear, right, left), gram_features], axis=1)]
  transfers between devices with their start and end apart: 37 -> 24, of which waited for: 27 -> 18; matrix products, arithmetic and copies ran while one was open for 4% -> 0% of each run, Pallas kernels for 0% -> 1%
where the time goes in v2:
time: 161 us
  waiting for transfers between devices  67.3 us (42%)
  blocking collectives  48.5 us (30%)
  starting transfers between devices  18.2 us (11%)
  Pallas kernels  11.9 us (7%)
  local copies, waits for them, and re-layouts  10.5 us (7%)
  between operations  1.72 us (1%)
    ppermute x24, waiting for transfers between devices, flip(): return lax.ppermute(value, AXIS, [(i, i ^ bit) for i in range(count)])  67.3 us
    all_to_all x1, blocking collectives, shards_blocks(): lax.all_to_all(sent, AXIS, 0, 0, axis_index_groups=halves, tiled=True)  48.5 us
    ppermute x24, starting transfers between devices, flip(): return lax.ppermute(value, AXIS, [(i, i ^ bit) for i in range(count)])  18.2 us
    unnamed x17, local copies, waits for them, and re-layouts  8.83 us
    pallas_call x2, Pallas kernels, shards_blocks(): pl.pallas_call(functools.partial(update_kernel, last, widths, (cell_order...  4.6 us
  transfers between devices with their start and end apart: 24, of which 18 were waited for; matrix products, arithmetic and copies ran while one was open for 0% of the time, Pallas kernels for 1%

profile of v2, /device:TPU:0, one launch (start us, length us, event | category | flops | bytes accessed | tf_op | source)
XLA Modules:
  0.0 160.5 jit_solution(10716101903176702579)
XLA Ops:
  3.6 4.1 %collective-permute-start = (bf16[8,128]{1,0:T(8,128)(2,1)S(1)}, bf16[8,128]{1,0:T(8,128)(2,1)S(1)}, u32[]{:S(2)}, u32[]{:S(2)}) collective-permute-start(bf16[8,128]{1,0:T(8,128)(2,1)S(1)} %fusion.3), channel_id=1, source_target_pairs={{0,16},{1,17},{2,18},{3,19},{4,20},{5,21},{6,22},{7,23},{8,24},{9,... | collective-permute-start | bytes 6152 | tf_op jit(solution)/shard_map/ppermute | solution.py:22
  7.6 1.6 collective-permute-done
  9.2 1.6 copy-done.3
  10.8 1.0 copy-done.4
  14.9 48.5 %all_to_all.5.received.mine.received_cells = bf16[16,80,1408]{2,1,0:T(8,128)(2,1)S(1)} all-to-all(bf16[16,80,1408]{2,1,0:T(8,128)(2,1)S(1)} %shard_map.112), channel_id=1, replica_groups={{0,1,2,3,4,5,6,7,8,9,10,11,12,13,14,15},{16,17,18,19,20,21,22,23,24,25,..., dimensions={0} | all-to-all | bytes 7208960 | tf_op jit(solution)/shard_map/all_to_all | solution.py:547
  63.5 1.8 %copy-done = bf16[16,80,1408]{2,1,0:T(8,128)(2,1)} copy-done((bf16[16,80,1408]{2,1,0:T(8,128)(2,1)}, bf16[16,80,1408]{2,1,0:T(8,128)(2,1)S(1)}, u32[]{:S(2)}) %copy-start) | copy-done | bytes 3604504
  65.2 2.7 %collective-permute-start.4 = (f32[64,640]{1,0:T(8,128)S(1)}, f32[64,640]{1,0:T(8,128)S(1)}, u32[]{:S(2)}, u32[]{:S(2)}) collective-permute-start(f32[64,640]{1,0:T(8,128)S(1)} %constant_dynamic-update-slice_fusion), channel_id=1, source_target_pairs={{0,16},{1,17},{2,18},{3,19},{4,20},{5,21},{6,22},{7,23},{8,24},{9,... | collective-permute-start | bytes 491528 | tf_op jit(solution)/shard_map/ppermute | solution.py:22
  68.0 8.4 %collective-permute-done.4 = f32[64,640]{1,0:T(8,128)S(1)} collective-permute-done((f32[64,640]{1,0:T(8,128)S(1)}, f32[64,640]{1,0:T(8,128)S(1)}, u32[]{:S(2)}, u32[]{:S(2)}) %collective-permute-start.4) | collective-permute-done | bytes 163872 | tf_op jit(solution)/shard_map/ppermute | solution.py:22
  76.4 2.0 %copy-done.1 = bf16[16,80,1408]{2,1,0:T(8,128)(2,1)S(1)} copy-done((bf16[16,80,1408]{2,1,0:T(8,128)(2,1)S(1)}, bf16[16,80,1408]{2,1,0:T(8,128)(2,1)}, u32[]{:S(2)}) %copy-start.1) | copy-done | bytes 3604504
  79.3 2.6 %shard_map.114 = (f32[64,1280]{1,0:T(8,128)S(1)}, f32[64,1280]{1,0:T(8,128)S(1)}, f32[64,128]{1,0:T(8,128)S(1)}, f32[32,128]{1,0:T(8,128)S(1)}) custom-call(s32[3]{0:T(128)S(1)} %pad_add_fusion.spot, bf16[16,80,1408]{2,1,0:T(8,128)(2,1)S(1)} %copy-done.1, bf16[16,16,1280]{2,1,0:T(8,128)(2,1)S(1)} %collective-permute-done.1.other, ...), custom_call_target="tpu_custom_call" | custom-call | tf_op jit(solution)/shard_map/pallas_call | solution.py:563
  82.0 2.9 %collective-permute-start.3 = (f32[64,128]{1,0:T(8,128)S(1)}, f32[64,128]{1,0:T(8,128)S(1)}, u32[]{:S(2)}, u32[]{:S(2)}) collective-permute-start(f32[64,128]{1,0:T(8,128)S(1)} %get-tuple-element.29.beside), channel_id=1, source_target_pairs={{0,16},{1,17},{2,18},{3,19},{4,20},{5,21},{6,22},{7,23},{8,24},{9,... | collective-permute-start | bytes 98312 | tf_op jit(solution)/shard_map/ppermute | solution.py:22
  84.9 8.0 %collective-permute-done.2 = f16[64,1280]{1,0:T(8,128)(2,1)S(1)} collective-permute-done((f16[64,1280]{1,0:T(8,128)(2,1)S(1)}, f16[64,1280]{1,0:T(8,128)(2,1)S(1)}, u32[]{:S(2)}, u32[]{:S(2)}) %collective-permute-start.2) | collective-permute-done | bytes 163872 | tf_op jit(solution)/shard_map/ppermute | solution.py:22
  93.6 2.5 %shard_map.115 = (f32[64,640]{1,0:T(8,128)S(1)}, f32[64,640]{1,0:T(8,128)S(1)}, f32[64,1280]{1,0:T(8,128)S(1)}, f32[64,1024]{1,0:T(8,128)S(1)}, f32[64,1024]{1,0:T(8,128)S(1)}, /*index=5*/bf16[64,128]{1,0:T(8,128)(2,1)S(1)}) custom-call(s32[3]{0:T(128)S(1)} %pad_add_fusion.spot, f32[32,128]{1,0:T(8,128)S(1)} %get-tuple-element.26.table, ...), custom_call_target="tpu_custom_call" | custom-call | tf_op jit(solution)/shard_map/pallas_call | solution.py:591
  96.1 3.7 %collective-permute-done.14 = bf16[64,128]{1,0:T(8,128)(2,1)S(1)} collective-permute-done((bf16[64,128]{1,0:T(8,128)(2,1)S(1)}, bf16[64,128]{1,0:T(8,128)(2,1)S(1)}, u32[]{:S(2)}, u32[]{:S(2)}) %collective-permute-start.14) | collective-permute-done | bytes 16416 | tf_op jit(solution)/shard_map/ppermute | solution.py:22
  100.5 3.3 %collective-permute-done.15 = bf16[64,256]{1,0:T(8,128)(2,1)S(1)} collective-permute-done((bf16[64,256]{1,0:T(8,128)(2,1)S(1)}, bf16[64,256]{1,0:T(8,128)(2,1)S(1)}, u32[]{:S(2)}, u32[]{:S(2)}) %collective-permute-start.15) | collective-permute-done | bytes 32800 | tf_op jit(solution)/shard_map/ppermute | solution.py:22
  104.0 2.1 %collective-permute-start.11 = (f32[64,512]{1,0:T(8,128)S(1)}, f32[64,512]{1,0:T(8,128)S(1)}, u32[]{:S(2)}, u32[]{:S(2)}) collective-permute-start(f32[64,512]{1,0:T(8,128)S(1)} %slice_select_fusion), channel_id=1, source_target_pairs={{0,4},{1,5},{2,6},{3,7},{4,0},{5,1},{6,2},{7,3},{8,12},{9,13},{10,... | collective-permute-start | bytes 393224 | tf_op jit(solution)/shard_map/ppermute | solution.py:22
  106.1 2.1 %collective-permute-done.16 = bf16[64,512]{1,0:T(8,128)(2,1)S(1)} collective-permute-done((bf16[64,512]{1,0:T(8,128)(2,1)S(1)}, bf16[64,512]{1,0:T(8,128)(2,1)S(1)}, u32[]{:S(2)}, u32[]{:S(2)}) %collective-permute-start.16) | collective-permute-done | bytes 65568 | tf_op jit(solution)/shard_map/ppermute | solution.py:22
  108.7 0.9 collective-permute-done.11
  109.8 5.2 %collective-permute-done.6 = f32[64,640]{1,0:T(8,128)S(1)} collective-permute-done((f32[64,640]{1,0:T(8,128)S(1)}, f32[64,640]{1,0:T(8,128)S(1)}, u32[]{:S(2)}, u32[]{:S(2)}) %collective-permute-start.6) | collective-permute-done | bytes 163872 | tf_op jit(solution)/shard_map/ppermute | solution.py:22
  115.2 1.0 collective-permute-start.13
  116.2 4.8 %collective-permute-done.7 = f32[64,640]{1,0:T(8,128)S(1)} collective-permute-done((f32[64,640]{1,0:T(8,128)S(1)}, f32[64,640]{1,0:T(8,128)S(1)}, u32[]{:S(2)}, u32[]{:S(2)}) %collective-permute-start.7) | collective-permute-done | bytes 163872 | tf_op jit(solution)/shard_map/ppermute | solution.py:22
  121.1 5.3 %collective-permute-done.8 = f32[64,640]{1,0:T(8,128)S(1)} collective-permute-done((f32[64,640]{1,0:T(8,128)S(1)}, f32[64,640]{1,0:T(8,128)S(1)}, u32[]{:S(2)}, u32[]{:S(2)}) %collective-permute-start.8) | collective-permute-done | bytes 163872 | tf_op jit(solution)/shard_map/ppermute | solution.py:22
  126.4 1.5 shard_map.116
  127.9 1.3 collective-permute-done.9.other
  129.2 1.8 %shard_map.117 = (f32[64,1280]{1,0:T(8,128)S(1)}, f32[64,1280]{1,0:T(8,128)S(1)}, f32[64,128]{1,0:T(8,128)S(1)}) custom-call(s32[3]{0:T(128)S(1)} %pad_add_fusion.spot, f32[32,128]{1,0:T(8,128)S(1)} %get-tuple-element.26.table, bf16[64,1024]{1,0:T(8,128)(2,1)S(1)} %get-tuple-element.33.mine, bf16[64,1024]{1,0:T(8,128)(2,1)S(1)} %collective-permute-done.9.other, ...), custom_call_target="tpu_custom_call" | custom-call | tf_op jit(solution)/shard_map/pallas_call | solution.py:635
  131.2 2.9 %collective-permute-start.19 = (f32[64,128]{1,0:T(8,128)S(1)}, f32[64,128]{1,0:T(8,128)S(1)}, u32[]{:S(2)}, u32[]{:S(2)}) collective-permute-start(f32[64,128]{1,0:T(8,128)S(1)} %get-tuple-element.39.beside), channel_id=1, source_target_pairs={{0,16},{1,17},{2,18},{3,19},{4,20},{5,21},{6,22},{7,23},{8,24},{9,... | collective-permute-start | bytes 98312 | tf_op jit(solution)/shard_map/ppermute | solution.py:22
  134.0 8.0 %collective-permute-done.18 = f16[64,1280]{1,0:T(8,128)(2,1)S(1)} collective-permute-done((f16[64,1280]{1,0:T(8,128)(2,1)S(1)}, f16[64,1280]{1,0:T(8,128)(2,1)S(1)}, u32[]{:S(2)}, u32[]{:S(2)}) %collective-permute-start.18) | collective-permute-done | bytes 163872 | tf_op jit(solution)/shard_map/ppermute | solution.py:22
  142.6 2.1 %shard_map.118 = (f32[64,640]{1,0:T(8,128)S(1)}, f32[64,640]{1,0:T(8,128)S(1)}, f32[64,128]{1,0:T(8,128)}, f32[64,512]{1,0:T(8,128)}) custom-call(s32[3]{0:T(128)S(1)} %pad_add_fusion.spot, f32[32,128]{1,0:T(8,128)S(1)} %get-tuple-element.26.table, f32[64,1280]{1,0:T(8,128)S(1)} %get-tuple-element.37.sums, f32[64,1280]{1,0:T(8,128)S(1)} %convert_element_type.22.other, ...), custom_call_target="tpu_custom_call" | custom-call | tf_op jit(solution)/shard_map/pallas_call | solution.py:591
  144.9 1.4 collective-permute-done.20
  146.7 4.5 %collective-permute-done.21 = f32[64,320]{1,0:T(8,128)S(1)} collective-permute-done((f32[64,320]{1,0:T(8,128)S(1)}, f32[64,320]{1,0:T(8,128)S(1)}, u32[]{:S(2)}, u32[]{:S(2)}) %collective-permute-start.21) | collective-permute-done | bytes 81952 | tf_op jit(solution)/shard_map/ppermute | solution.py:22
  151.8 3.8 %collective-permute-done.22 = f32[64,192]{1,0:T(8,128)S(1)} collective-permute-done((f32[64,192]{1,0:T(8,128)S(1)}, f32[64,192]{1,0:T(8,128)S(1)}, u32[]{:S(2)}, u32[]{:S(2)}) %collective-permute-start.22) | collective-permute-done | bytes 49184 | tf_op jit(solution)/shard_map/ppermute | solution.py:22
  155.8 3.9 %collective-permute-done.23 = f32[64,128]{1,0:T(8,128)S(1)} collective-permute-done((f32[64,128]{1,0:T(8,128)S(1)}, f32[64,128]{1,0:T(8,128)S(1)}, u32[]{:S(2)}, u32[]{:S(2)}) %collective-permute-start.23) | collective-permute-done | bytes 32800 | tf_op jit(solution)/shard_map/ppermute | solution.py:22
  (92 shorter events, 11.8 us)
Async XLA Ops:
  3.6 5.6 %collective-permute-start = (bf16[8,128]{1,0:T(8,128)(2,1)S(1)}, bf16[8,128]{1,0:T(8,128)(2,1)S(1)}, u32[]{:S(2)}, u32[]{:S(2)}) collective-permute-start(bf16[8,128]{1,0:T(8,128)(2,1)S(1)} %fusion.3), channel_id=1, source_target_pairs={{0,16},{1,17},{2,18},{3,19},{4,20},{5,21},{6,22},{7,23},{8,24},{9,... | collective-permute-start | bytes 6152 | tf_op jit(solution)/shard_map/ppermute | solution.py:22
  9.2 1.6 copy-start.3
  10.8 1.0 copy-start.4
  11.8 0.9 copy-start.5
  12.7 0.8 copy-start.6
  13.5 0.8 copy-start.7
  63.4 1.8 %copy-start = (bf16[16,80,1408]{2,1,0:T(8,128)(2,1)}, bf16[16,80,1408]{2,1,0:T(8,128)(2,1)S(1)}, u32[]{:S(2)}) copy-start(bf16[16,80,1408]{2,1,0:T(8,128)(2,1)S(1)} %all_to_all.5.received.mine.received_cells) | copy-start | bytes 10813444
  65.2 14.1 %collective-permute-start.1 = (bf16[16,16,1280]{2,1,0:T(8,128)(2,1)S(1)}, bf16[16,16,1280]{2,1,0:T(8,128)(2,1)S(1)}, u32[]{:S(2)}, u32[]{:S(2)}) collective-permute-start(bf16[16,16,1280]{2,1,0:T(8,128)(2,1)S(1)} %slice.51), channel_id=1, source_target_pairs={{0,1},{1,0},{2,3},{3,2},{4,5},{5,4},{6,7},{7,6},{8,9},{9,8},{10,11... | collective-permute-start | bytes 1966088 | tf_op jit(solution)/shard_map/ppermute | solution.py:22
  65.2 11.1 %collective-permute-start.4 = (f32[64,640]{1,0:T(8,128)S(1)}, f32[64,640]{1,0:T(8,128)S(1)}, u32[]{:S(2)}, u32[]{:S(2)}) collective-permute-start(f32[64,640]{1,0:T(8,128)S(1)} %constant_dynamic-update-slice_fusion), channel_id=1, source_target_pairs={{0,16},{1,17},{2,18},{3,19},{4,20},{5,21},{6,22},{7,23},{8,24},{9,... | collective-permute-start | bytes 491528 | tf_op jit(solution)/shard_map/ppermute | solution.py:22
  76.4 2.0 %copy-start.1 = (bf16[16,80,1408]{2,1,0:T(8,128)(2,1)S(1)}, bf16[16,80,1408]{2,1,0:T(8,128)(2,1)}, u32[]{:S(2)}) copy-start(bf16[16,80,1408]{2,1,0:T(8,128)(2,1)} %copy-done) | copy-start | bytes 10813444
  81.9 11.0 %collective-permute-start.2 = (f16[64,1280]{1,0:T(8,128)(2,1)S(1)}, f16[64,1280]{1,0:T(8,128)(2,1)S(1)}, u32[]{:S(2)}, u32[]{:S(2)}) collective-permute-start(f16[64,1280]{1,0:T(8,128)(2,1)S(1)} %convert_element_type.19), channel_id=1, source_target_pairs={{0,16},{1,17},{2,18},{3,19},{4,20},{5,21},{6,22},{7,23},{8,24},{9,... | collective-permute-start | bytes 491528 | tf_op jit(solution)/shard_map/ppermute | solution.py:22
  82.0 11.6 %collective-permute-start.3 = (f32[64,128]{1,0:T(8,128)S(1)}, f32[64,128]{1,0:T(8,128)S(1)}, u32[]{:S(2)}, u32[]{:S(2)}) collective-permute-start(f32[64,128]{1,0:T(8,128)S(1)} %get-tuple-element.29.beside), channel_id=1, source_target_pairs={{0,16},{1,17},{2,18},{3,19},{4,20},{5,21},{6,22},{7,23},{8,24},{9,... | collective-permute-start | bytes 98312 | tf_op jit(solution)/shard_map/ppermute | solution.py:22
  96.0 3.8 %collective-permute-start.14 = (bf16[64,128]{1,0:T(8,128)(2,1)S(1)}, bf16[64,128]{1,0:T(8,128)(2,1)S(1)}, u32[]{:S(2)}, u32[]{:S(2)}) collective-permute-start(bf16[64,128]{1,0:T(8,128)(2,1)S(1)} %get-tuple-element.36), channel_id=1, source_target_pairs={{0,8},{1,9},{2,10},{3,11},{4,12},{5,13},{6,14},{7,15},{8,0},{9,1},... | collective-permute-start | bytes 49160 | tf_op jit(solution)/shard_map/ppermute | solution.py:22
  99.9 4.0 %collective-permute-start.15 = (bf16[64,256]{1,0:T(8,128)(2,1)S(1)}, bf16[64,256]{1,0:T(8,128)(2,1)S(1)}, u32[]{:S(2)}, u32[]{:S(2)}) collective-permute-start(bf16[64,256]{1,0:T(8,128)(2,1)S(1)} %pad_maximum_fusion.6), channel_id=1, source_target_pairs={{0,2},{1,3},{2,0},{3,1},{4,6},{5,7},{6,4},{7,5},{8,10},{9,11},{10,... | collective-permute-start | bytes 98312 | tf_op jit(solution)/shard_map/ppermute | solution.py:22
  100.0 26.4 %copy-start.2 = (bf16[16,80,1408]{2,1,0:T(8,128)(2,1)S(1)}, bf16[16,80,1408]{2,1,0:T(8,128)(2,1)}, u32[]{:S(2)}) copy-start(bf16[16,80,1408]{2,1,0:T(8,128)(2,1)} %copy-done) | copy-start | bytes 10813444
  100.0 4.0 %collective-permute-start.10 = (f32[64,1024]{1,0:T(8,128)S(1)}, f32[64,1024]{1,0:T(8,128)S(1)}, u32[]{:S(2)}, u32[]{:S(2)}) collective-permute-start(f32[64,1024]{1,0:T(8,128)S(1)} %get-tuple-element.35), channel_id=1, source_target_pairs={{0,1},{1,0},{2,3},{3,2},{4,5},{5,4},{6,7},{7,6},{8,9},{9,8},{10,11... | collective-permute-start | bytes 786440 | tf_op jit(solution)/shard_map/ppermute | solution.py:22
  100.0 8.3 %collective-permute-start.5 = (f32[64,640]{1,0:T(8,128)S(1)}, f32[64,640]{1,0:T(8,128)S(1)}, u32[]{:S(2)}, u32[]{:S(2)}) collective-permute-start(f32[64,640]{1,0:T(8,128)S(1)} %get-tuple-element.31), channel_id=1, source_target_pairs={{0,1},{1,0},{2,3},{3,2},{4,5},{5,4},{6,7},{7,6},{8,9},{9,8},{10,11... | collective-permute-start | bytes 491528 | tf_op jit(solution)/shard_map/ppermute | solution.py:22
  103.9 4.3 %collective-permute-start.16 = (bf16[64,512]{1,0:T(8,128)(2,1)S(1)}, bf16[64,512]{1,0:T(8,128)(2,1)S(1)}, u32[]{:S(2)}, u32[]{:S(2)}) collective-permute-start(bf16[64,512]{1,0:T(8,128)(2,1)S(1)} %pad_maximum_fusion.4), channel_id=1, source_target_pairs={{0,4},{1,5},{2,6},{3,7},{4,0},{5,1},{6,2},{7,3},{8,12},{9,13},{10,... | collective-permute-start | bytes 196616 | tf_op jit(solution)/shard_map/ppermute | solution.py:22
  104.0 5.6 %collective-permute-start.11 = (f32[64,512]{1,0:T(8,128)S(1)}, f32[64,512]{1,0:T(8,128)S(1)}, u32[]{:S(2)}, u32[]{:S(2)}) collective-permute-start(f32[64,512]{1,0:T(8,128)S(1)} %slice_select_fusion), channel_id=1, source_target_pairs={{0,4},{1,5},{2,6},{3,7},{4,0},{5,1},{6,2},{7,3},{8,12},{9,13},{10,... | collective-permute-start | bytes 393224 | tf_op jit(solution)/shard_map/ppermute | solution.py:22
  108.3 1.5 collective-permute-start.17
  108.4 6.7 %collective-permute-start.6 = (f32[64,640]{1,0:T(8,128)S(1)}, f32[64,640]{1,0:T(8,128)S(1)}, u32[]{:S(2)}, u32[]{:S(2)}) collective-permute-start(f32[64,640]{1,0:T(8,128)S(1)} %add.63), channel_id=1, source_target_pairs={{0,2},{1,3},{2,0},{3,1},{4,6},{5,7},{6,4},{7,5},{8,10},{9,11},{10,... | collective-permute-start | bytes 491528 | tf_op jit(solution)/shard_map/ppermute | solution.py:22
  109.7 5.5 %collective-permute-start.12 = (f32[64,256]{1,0:T(8,128)S(1)}, f32[64,256]{1,0:T(8,128)S(1)}, u32[]{:S(2)}, u32[]{:S(2)}) collective-permute-start(f32[64,256]{1,0:T(8,128)S(1)} %slice_select_fusion.2), channel_id=1, source_target_pairs={{0,8},{1,9},{2,10},{3,11},{4,12},{5,13},{6,14},{7,15},{8,0},{9,1},... | collective-permute-start | bytes 196616 | tf_op jit(solution)/shard_map/ppermute | solution.py:22
  115.1 5.9 %collective-permute-start.7 = (f32[64,640]{1,0:T(8,128)S(1)}, f32[64,640]{1,0:T(8,128)S(1)}, u32[]{:S(2)}, u32[]{:S(2)}) collective-permute-start(f32[64,640]{1,0:T(8,128)S(1)} %add.64), channel_id=1, source_target_pairs={{0,4},{1,5},{2,6},{3,7},{4,0},{5,1},{6,2},{7,3},{8,12},{9,13},{10,... | collective-permute-start | bytes 491528 | tf_op jit(solution)/shard_map/ppermute | solution.py:22
  115.2 12.7 %collective-permute-start.13 = (f32[64,128]{1,0:T(8,128)S(1)}, f32[64,128]{1,0:T(8,128)S(1)}, u32[]{:S(2)}, u32[]{:S(2)}) collective-permute-start(f32[64,128]{1,0:T(8,128)S(1)} %slice_select_fusion.5), channel_id=1, source_target_pairs={{0,2},{1,3},{2,0},{3,1},{4,6},{5,7},{6,4},{7,5},{8,10},{9,11},{10,... | collective-permute-start | bytes 98312 | tf_op jit(solution)/shard_map/ppermute | solution.py:22
  121.0 5.4 %collective-permute-start.8 = (f32[64,640]{1,0:T(8,128)S(1)}, f32[64,640]{1,0:T(8,128)S(1)}, u32[]{:S(2)}, u32[]{:S(2)}) collective-permute-start(f32[64,640]{1,0:T(8,128)S(1)} %add.65), channel_id=1, source_target_pairs={{0,8},{1,9},{2,10},{3,11},{4,12},{5,13},{6,14},{7,15},{8,0},{9,1},... | collective-permute-start | bytes 491528 | tf_op jit(solution)/shard_map/ppermute | solution.py:22
  127.8 1.4 collective-permute-start.9
  131.0 10.9 %collective-permute-start.18 = (f16[64,1280]{1,0:T(8,128)(2,1)S(1)}, f16[64,1280]{1,0:T(8,128)(2,1)S(1)}, u32[]{:S(2)}, u32[]{:S(2)}) collective-permute-start(f16[64,1280]{1,0:T(8,128)(2,1)S(1)} %convert_element_type.21), channel_id=1, source_target_pairs={{0,16},{1,17},{2,18},{3,19},{4,20},{5,21},{6,22},{7,23},{8,24},{9,... | collective-permute-start | bytes 491528 | tf_op jit(solution)/shard_map/ppermute | solution.py:22
  131.2 11.4 %collective-permute-start.19 = (f32[64,128]{1,0:T(8,128)S(1)}, f32[64,128]{1,0:T(8,128)S(1)}, u32[]{:S(2)}, u32[]{:S(2)}) collective-permute-start(f32[64,128]{1,0:T(8,128)S(1)} %get-tuple-element.39.beside), channel_id=1, source_target_pairs={{0,16},{1,17},{2,18},{3,19},{4,20},{5,21},{6,22},{7,23},{8,24},{9,... | collective-permute-start | bytes 98312 | tf_op jit(solution)/shard_map/ppermute | solution.py:22
  144.8 1.5 collective-permute-start.20
  146.3 4.9 %collective-permute-start.21 = (f32[64,320]{1,0:T(8,128)S(1)}, f32[64,320]{1,0:T(8,128)S(1)}, u32[]{:S(2)}, u32[]{:S(2)}) collective-permute-start(f32[64,320]{1,0:T(8,128)S(1)} %pad_maximum_fusion.3), channel_id=1, source_target_pairs={{0,2},{1,3},{2,0},{3,1},{4,6},{5,7},{6,4},{7,5},{8,10},{9,11},{10,... | collective-permute-start | bytes 245768 | tf_op jit(solution)/shard_map/ppermute | solution.py:22
  151.3 4.3 %collective-permute-start.22 = (f32[64,192]{1,0:T(8,128)S(1)}, f32[64,192]{1,0:T(8,128)S(1)}, u32[]{:S(2)}, u32[]{:S(2)}) collective-permute-start(f32[64,192]{1,0:T(8,128)S(1)} %pad_maximum_fusion.5), channel_id=1, source_target_pairs={{0,4},{1,5},{2,6},{3,7},{4,0},{5,1},{6,2},{7,3},{8,12},{9,13},{10,... | collective-permute-start | bytes 147464 | tf_op jit(solution)/shard_map/ppermute | solution.py:22
  155.8 3.9 %collective-permute-start.23 = (f32[64,128]{1,0:T(8,128)S(1)}, f32[64,128]{1,0:T(8,128)S(1)}, u32[]{:S(2)}, u32[]{:S(2)}) collective-permute-start(f32[64,128]{1,0:T(8,128)S(1)} %pad_maximum_fusion.7), channel_id=1, source_target_pairs={{0,8},{1,9},{2,10},{3,11},{4,12},{5,13},{6,14},{7,15},{8,0},{9,1},... | collective-permute-start | bytes 98312 | tf_op jit(solution)/shard_map/ppermute | solution.py:22

commit v3 on v2

--- a/solution.py
+++ b/solution.py
@@ -10,9 +10,9 @@
 BLOCK = 128
 ROUNDS = 2
 EPSILON = 1e-06
-TINY = 1e-30
+CODES = 65535.0
 AXIS = "cells"
-PARAMS = pltpu.CompilerParams(vmem_limit_bytes=32 * 1024 * 1024)
+PARAMS = pltpu.CompilerParams(vmem_limit_bytes=14 * 1024 * 1024)
 SMEM = pl.BlockSpec(memory_space=pltpu.SMEM)
 VMEM = pl.BlockSpec(memory_space=pltpu.VMEM)
 
@@ -157,13 +157,8 @@
             squares[:rank, :rank] + squares[:rank, rank:] + squares[rank:, :rank] + squares[rank:, rank:]
         )
         sums = jnp.dot(cell_low, counts, preferred_element_type=jnp.float32) + links
-        groups = sums.reshape(rank, features // gene_width, gene_width)
-        largest = jnp.max(groups, axis=2)
-        scaled = (groups / largest[:, :, None]).astype(jnp.float16).reshape(rank, features)
-        beside_other = flip(jnp.concatenate([gram_cells, largest], axis=1), half)
-        groups_other = flip(scaled, half).astype(jnp.float32).reshape(groups.shape)
-        gram_cells = gram_cells + beside_other[:, :rank]
-        sums = sums + (groups_other * beside_other[:, rank:, None]).reshape(rank, features)
+        gram_cells = gram_cells + flip(gram_cells, half)
+        sums = sums + flip(sums, half)
         factors = (
             factors
             * sums
@@ -258,7 +253,7 @@
     return (squares[:rank, :rank] + squares[rank:, rank:]) + (squares[:rank, rank:] + squares[rank:, :rank])
 
 
-def parcels_kernel(rna_0, rna_1, atac_0, atac_1, cell, gene, peak, slots, out):
+def parcels_kernel(rna_0, rna_1, atac_0, atac_1, cell, gene, peak, out):
     rank = cell.shape[0]
     cells = rna_0.shape[0]
     gene_width, peak_width = gene.shape[1], peak.shape[1]
@@ -277,10 +272,52 @@
             row = (2 * (j % 2) + s) * part
             out[j, cells:, s * width : s * width + gene_width] = gene_low[row : row + part]
             out[j, cells:, s * width + gene_width : (s + 1) * width] = peak_low[row : row + part]
-        out[j, cells:, 2 * width :] = slots[...]
-
-
-def parcels(rna_counts, atac_counts, cell_factor, gene_factor, peak_factor, slots, half):
+
+
+def slots_kernel(spot, link_gene, link_peak, link_weight, link_count, out):
+    slots = link_gene.shape[0]
+    lane = lax.broadcasted_iota(jnp.int32, out.shape, 1) - spot[1] * slots
+    row = lax.broadcasted_iota(jnp.int32, out.shape, 0)
+    value = jnp.zeros(out.shape, jnp.float32)
+    for s in range(slots):
+        weight = jnp.where(s < link_count[0], link_weight[s], 0)
+        for r, entry in enumerate((link_gene[s], link_peak[s], weight)):
+            value = jnp.where((lane == s) & (row == r), entry.astype(jnp.float32), value)
+    out[...] = value
+
+
+def put_slots_kernel(mine, other, parcels_in, out, block, sems):
+    block[...] = jnp.concatenate([mine[...], other[...]], axis=0).astype(jnp.bfloat16)
+    half, rows, lanes = out.shape
+    copies = [
+        pltpu.make_async_copy(
+            block, out.at[j, rows - block.shape[0] : rows, lanes - block.shape[1] : lanes], sems.at[j]
+        )
+        for j in range(half)
+    ]
+    for copy in copies:
+        copy.start()
+    for copy in copies:
+        copy.wait()
+
+
+def put_slots(mine, other, parcels_value):
+    anywhere = pl.BlockSpec(memory_space=pl.ANY)
+    return pl.pallas_call(
+        put_slots_kernel,
+        in_specs=[VMEM, VMEM, anywhere],
+        out_specs=anywhere,
+        out_shape=struct(*parcels_value.shape, dtype=parcels_value.dtype),
+        scratch_shapes=[
+            pltpu.VMEM((2 * mine.shape[0], mine.shape[1]), jnp.bfloat16),
+            pltpu.SemaphoreType.DMA((parcels_value.shape[0],)),
+        ],
+        input_output_aliases={2: 0},
+        compiler_params=PARAMS,
+    )(mine, other, parcels_value)
+
+
+def parcels(rna_counts, atac_counts, cell_factor, gene_factor, peak_factor, half):
     cells = rna_counts.shape[0]
     rank = cell_factor.shape[0]
     gene_width, peak_width = gene_factor.shape[1], peak_factor.shape[1]
@@ -298,11 +335,11 @@
         parcels_kernel,
         grid=(steps,),
         in_specs=[columns(gene_width, 0), columns(gene_width, 1), columns(peak_width, 0), columns(peak_width, 1)]
-        + [whole(a) for a in (cell_factor, gene_factor, peak_factor, slots)],
+        + [whole(a) for a in (cell_factor, gene_factor, peak_factor)],
         out_specs=pl.BlockSpec((each, rows, lanes), lambda i: (i, 0, 0)),
         out_shape=struct(half, rows, lanes, dtype=jnp.bfloat16),
         compiler_params=PARAMS,
-    )(rna_counts, rna_counts, atac_counts, atac_counts, cell_factor, gene_factor, peak_factor, slots)
+    )(rna_counts, rna_counts, atac_counts, atac_counts, cell_factor, gene_factor, peak_factor)
 
 
 def first_sums_kernel(received, sums, gram):
@@ -315,38 +352,40 @@
     gram[...] = gram_of(high, rest)
 
 
-def finish_sums(sums_value, gram_value, widths, sums, scaled, beside):
+def finish_sums(sums_value, gram_value, sums, coded, beside):
     rank, features = sums_value.shape
-    largest = []
+    least, step = [], []
     for b in range(features // BLOCK):
         group = sums_value[:, b * BLOCK : (b + 1) * BLOCK]
-        top = jnp.maximum(jnp.max(group, axis=1, keepdims=True), TINY)
         sums[:, b * BLOCK : (b + 1) * BLOCK] = group
-        scaled[:, b * BLOCK : (b + 1) * BLOCK] = group / top
-        largest.append(top)
-    pad = jnp.zeros((rank, beside.shape[1] - rank - len(largest)), jnp.float32)
-    beside[...] = jnp.concatenate([gram_value, *largest, pad], axis=1)
+        low = jnp.min(group, axis=1, keepdims=True)
+        spread = jnp.max(group, axis=1, keepdims=True) - low
+        per = jnp.where(spread > 0.0, CODES / spread, 0.0)
+        code = jnp.minimum(jnp.floor((group - low) * per + 0.5), CODES) - (CODES + 1) / 2
+        coded[:, b * BLOCK : (b + 1) * BLOCK] = code.astype(jnp.int32).astype(jnp.int16)
+        least.append(low)
+        step.append(spread / CODES)
+    pad = jnp.zeros((rank, beside.shape[1] - rank - 2 * len(least)), jnp.float32)
+    beside[...] = jnp.concatenate([gram_value, *least, *step, pad], axis=1)
 
 
 def first_links_kernel(
-    link_scale, widths, spot, mine, other, sums_in, gram, sums, scaled, beside, table, table_sem, table_smem
+    link_scale, widths, spot, mine, other, sums_in, gram, sums, coded, beside, table, table_sem, table_smem
 ):
     half = mine.shape[0]
     rank, features = sums_in.shape
     gene_width, peak_width = widths
     gene_blocks, peak_blocks = gene_width // BLOCK, peak_width // BLOCK
     width = gene_width + peak_width
-    slots = mine[:, :, 2 * width :].reshape(half * mine.shape[1], 2 * rank).astype(jnp.float32)
-
-    def hot(column, size, value):
-        ids = lax.broadcasted_iota(jnp.int32, (slots.shape[0], size), 1).astype(jnp.float32)
-        return jnp.where(slots[:, column : column + 1] == ids, value, 0.0).astype(jnp.bfloat16)
-
-    table[...] = lax.dot_general(
-        hot(0, table.shape[0], slots[:, 2:3]),
-        hot(1, table.shape[1], 1.0),
-        (((0,), (0,)), ((), ())),
-        preferred_element_type=jnp.float32,
+    slots = sum(mine[j, :, 2 * width :].astype(jnp.float32) for j in range(half))
+
+    def hot(row, size, value):
+        ids = lax.broadcasted_iota(jnp.int32, (size, slots.shape[1]), 0).astype(jnp.float32)
+        return jnp.where(slots[row : row + 1] == ids, value, 0.0).astype(jnp.bfloat16)
+
+    table[...] = sum(
+        across(hot(row, table.shape[0], slots[row + 2 : row + 3]), hot(row + 1, table.shape[1], 1.0))
+        for row in (0, slots.shape[0] // 2)
     )
     copy = pltpu.make_async_copy(table, table_smem, table_sem)
     copy.start()
@@ -379,11 +418,11 @@
     ahead, behind = links[: rank // 2], links[rank // 2 :]
     first = core == 0
     links = jnp.concatenate([jnp.where(first, ahead, behind), jnp.where(first, behind, ahead)], axis=0)
-    finish_sums(sums_in[...] + link_scale * links, gram[...], widths, sums, scaled, beside)
+    finish_sums(sums_in[...] + link_scale * links, gram[...], sums, coded, beside)
 
 
 def next_sums_kernel(
-    link_scale, widths, orders, spot, table, mine, other, received, to_gene, genes, sums, scaled, beside
+    link_scale, widths, orders, spot, table, mine, other, received, to_gene, genes, sums, coded, beside
 ):
     half = received.shape[0]
     rank, features = sums.shape
@@ -414,7 +453,7 @@
     links = jnp.concatenate(
         [jnp.where(side == 0, gene_links, nothing), jnp.where(side == 0, nothing, gene_links), *total], axis=1
     )
-    finish_sums(products + link_scale * links, gram_of(high, rest), widths, sums, scaled, beside)
+    finish_sums(products + link_scale * links, gram_of(high, rest), sums, coded, beside)
 
 
 def update_kernel(last, widths, orders, spot, table, sums, other, beside, beside_other, factors, received, *outs):
@@ -428,14 +467,14 @@
     gram = beside[:, 0:rank] + beside_other[:, 0:rank]
     old = factors[...]
     below = exact(gram, old) + EPSILON
-    whole = jnp.concatenate(
-        [
-            sums[:, b * BLOCK : (b + 1) * BLOCK]
-            + other[:, b * BLOCK : (b + 1) * BLOCK] * beside_other[:, rank + b : rank + b + 1]
-            for b in range(features // BLOCK)
-        ],
-        axis=1,
-    )
+    groups = features // BLOCK
+    whole = []
+    for b in range(groups):
+        code = other[:, b * BLOCK : (b + 1) * BLOCK].astype(jnp.int32).astype(jnp.float32) + (CODES + 1) / 2
+        least = beside_other[:, rank + b : rank + b + 1]
+        step = beside_other[:, rank + groups + b : rank + groups + b + 1]
+        whole.append(sums[:, b * BLOCK : (b + 1) * BLOCK] + (least + code * step))
+    whole = jnp.concatenate(whole, axis=1)
     new = old * whole / below
     low = new.astype(jnp.bfloat16)
     cell_sums = jnp.concatenate([across(low, received[j, 0:cells, 0:features]) for j in orders[0]], axis=1)
@@ -534,23 +573,34 @@
     link_order = layout([1] + link_bits)
     gene_order = layout([1] + gene_bits[::-1])
 
-    live = jnp.arange(link_gene.shape[0], dtype=jnp.int32) < link_count[0]
-    slots = jnp.stack([link_gene, link_peak, jnp.where(live, link_weight, 0)], axis=1).astype(jnp.float32)
-    slots = jnp.pad(slots, ((0, 0), (0, 2 * rank - slots.shape[1])))
+    slots = pl.pallas_call(
+        slots_kernel,
+        in_specs=[SMEM] * 5,
+        out_specs=VMEM,
+        out_shape=struct(rank // 8, 2 * rank),
+        compiler_params=PARAMS,
+    )(spot, link_gene, link_peak, link_weight, link_count)
     slots_other = flip(slots, half)
     state = jnp.concatenate([gene_factor, peak_factor], axis=1)
     state_other = flip(state, half)
-    slots = jnp.concatenate([slots, slots_other], axis=0)
-    slots = jnp.pad(slots, ((0, rank // 4 - slots.shape[0]), (0, 0))).astype(jnp.bfloat16)
-    sent = parcels(rna_counts, atac_counts, cell_factor, gene_factor, peak_factor, slots, half)
+    sent = parcels(
+        pltpu.with_memory_space_constraint(rna_counts, pltpu.HBM),
+        pltpu.with_memory_space_constraint(atac_counts, pltpu.HBM),
+        cell_factor,
+        gene_factor,
+        peak_factor,
+        half,
+    )
+    sent = put_slots(slots, slots_other, sent)
     halves = [list(range(half)), list(range(half, count))]
     received = lax.all_to_all(sent, AXIS, 0, 0, axis_index_groups=halves, tiled=True)
+    received, state_other = lax.optimization_barrier((received, state_other))
     low, high = in_order(half, state, state_other)
     factors = jnp.concatenate(
         [low[:, :gene_width], high[:, :gene_width], low[:, gene_width:], high[:, gene_width:]], axis=1
     )
 
-    sums_shapes = (struct(rank, features), struct(rank, features), struct(rank, 2 * rank))
+    sums_shapes = (struct(rank, features), struct(rank, features, dtype=jnp.int16), struct(rank, 2 * rank))
     rows_other = flip(received[:, cells:, :features], 1)
     sums, gram = pl.pallas_call(
         first_sums_kernel,
@@ -560,7 +610,7 @@
         compiler_params=PARAMS,
     )(received)
     rows = rank // 4
-    sums, scaled, beside, link_table = pl.pallas_call(
+    sums, coded, beside, link_table = pl.pallas_call(
         functools.partial(first_links_kernel, link_scale, widths),
         grid=(1,),
         in_specs=[
@@ -580,7 +630,7 @@
     for sweep_index in range(ROUNDS):
         last = sweep_index == ROUNDS - 1
         beside_other = flip(beside, half)
-        other = flip(scaled.astype(jnp.float16), half).astype(jnp.float32)
+        other = flip(coded, half)
         lanes = -(-(split + rank) // BLOCK) * BLOCK
         outs = [struct(rank, lanes)] * 2
         if last:
@@ -611,15 +661,15 @@
         totals = kept + flip(sent, 1)
         to_gene = links_kept + flip(links_sent, 1)
         for cell_bit, link_bit, gene_bit in zip(cell_bits, link_bits, gene_bits):
-            totals_other = flip(totals, cell_bit)
             left, right = jnp.split(to_gene, 2, axis=1)
             clear = (me & link_bit) == 0
-            to_gene_other = flip(jnp.where(clear, right, left), link_bit)
-            genes_other = flip(genes, gene_bit)
-            totals = totals + totals_other
-            to_gene = jnp.where(clear, left, right) + to_gene_other
-            genes = jnp.concatenate(in_order(gene_bit, genes, genes_other), axis=1)
-        genes = jnp.concatenate(in_order(1, genes, flip(genes, 1)), axis=1)
+            leaving, staying = jnp.where(clear, right, left), jnp.where(clear, left, right)
+            totals, leaving, genes = lax.optimization_barrier((totals, leaving, genes))
+            got = flip(totals, cell_bit), flip(leaving, link_bit), flip(genes, gene_bit)
+            got = lax.optimization_barrier(got)
+            totals = totals + got[0]
+            to_gene = staying + got[1]
+            genes = jnp.concatenate(in_order(gene_bit, genes, got[2]), axis=1)
         pair, own_cells = pl.pallas_call(
             functools.partial(cells_kernel, cell_order),
             grid=(1,),
@@ -632,7 +682,8 @@
             out_shape=(struct(rank, 2 * split, dtype=jnp.bfloat16), struct(rank, cells)),
             compiler_params=PARAMS,
         )(spot, totals, received)
-        sums, scaled, beside = pl.pallas_call(
+        genes = jnp.concatenate(in_order(1, genes, flip(genes, 1)), axis=1)
+        sums, coded, beside = pl.pallas_call(
             functools.partial(next_sums_kernel, link_scale, widths, (cell_order, gene_order)),
             in_specs=[SMEM] * 2 + [VMEM] * 5,
             out_specs=[VMEM] * 3,
@@ -652,8 +703,9 @@
         and 2 * rank == BLOCK
         and gene_width % BLOCK == 0
         and peak_width % BLOCK == 0
-        and features // BLOCK <= rank
-        and 2 * link_gene.shape[0] <= rank // 4
+        and 2 * (features // BLOCK) <= rank
+        and half * link_gene.shape[0] <= 2 * rank
+        and rank % 64 == 0
         and max(rna_counts.shape[1], atac_counts.shape[1]) // BLOCK <= 256
     )
     run = shards_blocks if in_blocks else shards_any

time: 161 us -> 160 us (level)
  blocking collectives: 48.5 us -> 0 us
  waiting for transfers between devices: 67.3 us -> 100 us
  Pallas kernels: 11.9 us -> 21.7 us
  starting transfers between devices: 18.2 us -> 26.2 us
  local copies, waits for them, and re-layouts: 10.5 us -> 7.36 us
    all_to_all x1 -> x0, blocking collectives: 48.5 us -> none  [shards_blocks(): lax.all_to_all(sent, AXIS, 0, 0, axis_index_groups=halves, tiled=True)]
    ppermute x24, waiting for transfers between devices: 67.3 us -> 100 us  [flip(): return lax.ppermute(value, AXIS, [(i, i ^ bit) for i in range(count)])]
    all_to_all x0 -> x1, starting transfers between devices: none -> 5.02 us  [shards_blocks(): lax.all_to_all(sent, AXIS, 0, 0, axis_index_groups=halves, tiled=True)]
    ppermute x24, starting transfers between devices: 18.2 us -> 21.2 us  [flip(): return lax.ppermute(value, AXIS, [(i, i ^ bit) for i in range(count)])]
    pallas_call x2, Pallas kernels: 4.6 us -> 7.35 us  [shards_blocks(): pl.pallas_call(functools.partial(update_kernel, last, widths, (cell_order...]
    unnamed x17 -> x19, local copies, waits for them, and re-layouts: 8.83 us -> 6.18 us
    pallas_call x1, Pallas kernels: 0.61 us -> 2.64 us  [parcels(): pl.pallas_call(parcels_kernel, grid=(steps,), in_specs=[columns(gene_widt...]
    pallas_call x1, Pallas kernels: 0.83 us -> 2.86 us  [shards_blocks(): pl.pallas_call(first_sums_kernel, in_specs=[VMEM], out_specs=[VMEM] * 2,...]
  transfers between devices with their start and end apart: 24 -> 25, of which waited for: 18 -> 16; matrix products, arithmetic and copies ran while one was open for 0% -> 0% of each run, Pallas kernels for 1% -> 5%
where the time goes in v3:
time: 160 us; the launch traced here: 159 us
  waiting for transfers between devices  100 us (62%)
  starting transfers between devices  26.2 us (16%)
  Pallas kernels  21.7 us (14%)
  local copies, waits for them, and re-layouts  7.36 us (5%)
  between operations  1.7 us (1%)
    ppermute x24, waiting for transfers between devices, flip(): return lax.ppermute(value, AXIS, [(i, i ^ bit) for i in range(count)])  100 us
    ppermute x24, starting transfers between devices, flip(): return lax.ppermute(value, AXIS, [(i, i ^ bit) for i in range(count)])  21.2 us
    pallas_call x2, Pallas kernels, shards_blocks(): pl.pallas_call(functools.partial(update_kernel, last, widths, (cell_order...  7.35 us
    unnamed x19, local copies, waits for them, and re-layouts  6.18 us
    all_to_all x1, starting transfers between devices, shards_blocks(): lax.all_to_all(sent, AXIS, 0, 0, axis_index_groups=halves, tiled=True)  5.02 us
  transfers between devices with their start and end apart: 25, of which 16 were waited for; matrix products, arithmetic and copies ran while one was open for 0% of the time, Pallas kernels for 5%

profile of v3, /device:TPU:0, one launch (start us, length us, event | category | flops | bytes accessed | tf_op | source)
XLA Modules:
  0.0 159.0 jit_solution(13853373943305498782)
XLA Ops:
  3.9 4.1 %collective-permute-start = (f32[8,128]{1,0:T(8,128)S(1)}, f32[8,128]{1,0:T(8,128)S(1)}, u32[]{:S(2)}, u32[]{:S(2)}) collective-permute-start(f32[8,128]{1,0:T(8,128)S(1)} %shard_map.112.mine), channel_id=1, source_target_pairs={{0,16},{1,17},{2,18},{3,19},{4,20},{5,21},{6,22},{7,23},{8,24},{9,... | collective-permute-start | bytes 12296 | tf_op jit(solution)/shard_map/ppermute | solution.py:22
  8.1 0.9 copy-done.1
  10.5 2.6 %shard_map.113.parcels_in = bf16[16,80,1408]{2,1,0:T(8,128)(2,1)S(1)} custom-call(bf16[64,4096]{1,0:T(8,128)(2,1)} %rna_1.1, bf16[64,4096]{1,0:T(8,128)(2,1)} %rna_1.1, bf16[64,16384]{1,0:T(8,128)(2,1)} %atac_1.1, bf16[64,16384]{1,0:T(8,128)(2,1)} %atac_1.1, f32[64,64]{1,0:T(8,128)S(1)} %copy-done.5, f32[64,128]{1,0:T(8,128)S(1)} %copy-done.3, ...), custom_call_target="tpu_custom_call" | custom-call | tf_op jit(solution)/shard_map/pallas_call | solution.py:334
  13.3 1.8 %copy-done = bf16[16,80,1408]{2,1,0:T(8,128)(2,1)} copy-done((bf16[16,80,1408]{2,1,0:T(8,128)(2,1)}, bf16[16,80,1408]{2,1,0:T(8,128)(2,1)S(1)}, u32[]{:S(2)}) %copy-start) | copy-done | bytes 3604504
  15.1 5.0 %all-to-all-start = ((bf16[16,80,1408]{2,1,0:T(8,128)(2,1)}), bf16[16,80,1408]{2,1,0:T(8,128)(2,1)}, u32[]{:S(2)}, u32[]{:S(2)}) async-start(bf16[16,80,1408]{2,1,0:T(8,128)(2,1)} %copy-done), calls=%async_computation | async-start | bytes 7208960 | tf_op jit(solution)/shard_map/all_to_all | solution.py:596
  20.6 55.4 %collective-permute-done.1 = f32[64,640]{1,0:T(8,128)S(1)} collective-permute-done((f32[64,640]{1,0:T(8,128)S(1)}, f32[64,640]{1,0:T(8,128)S(1)}, u32[]{:S(2)}, u32[]{:S(2)}) %collective-permute-start.1) | collective-permute-done | bytes 163872 | tf_op jit(solution)/shard_map/ppermute | solution.py:22
  76.1 1.1 slice.39
  77.4 2.9 %shard_map.115 = (f32[64,1280]{1,0:T(8,128)S(1)}, f32[64,64]{1,0:T(8,128)S(1)}) custom-call(bf16[16,80,1408]{2,1,0:T(8,128)(2,1)} %all-to-all-done.received.mine.received_cells), custom_call_target="tpu_custom_call" | custom-call | tf_op jit(solution)/shard_map/pallas_call | solution.py:605
  80.2 3.2 %shard_map.116 = (f32[64,1280]{1,0:T(8,128)S(1)}, s16[64,1280]{1,0:T(8,128)(2,1)S(1)}, f32[64,128]{1,0:T(8,128)S(1)}, f32[32,128]{1,0:T(8,128)S(1)}) custom-call(s32[3]{0:T(128)S(1)} %pad_add_fusion.spot, bf16[16,80,1408]{2,1,0:T(8,128)(2,1)} %all-to-all-done.received.mine.received_cells, bf16[16,16,1280]{2,1,0:T(8,128)(2,1)S(1)} %collective-permute-done.2.other, ...), custom_call_target="tpu_custom_call" | custom-call | tf_op jit(solution)/shard_map/pallas_call | solution.py:613
  83.4 3.4 %collective-permute-start.3 = (s16[64,1280]{1,0:T(8,128)(2,1)S(1)}, s16[64,1280]{1,0:T(8,128)(2,1)S(1)}, u32[]{:S(2)}, u32[]{:S(2)}) collective-permute-start(s16[64,1280]{1,0:T(8,128)(2,1)S(1)} %get-tuple-element.49), channel_id=1, source_target_pairs={{0,16},{1,17},{2,18},{3,19},{4,20},{5,21},{6,22},{7,23},{8,24},{9,... | collective-permute-start | bytes 491528 | tf_op jit(solution)/shard_map/ppermute | solution.py:22
  87.0 9.7 %collective-permute-done.4.beside_other = f32[64,128]{1,0:T(8,128)S(1)} collective-permute-done((f32[64,128]{1,0:T(8,128)S(1)}, f32[64,128]{1,0:T(8,128)S(1)}, u32[]{:S(2)}, u32[]{:S(2)}) %collective-permute-start.4) | collective-permute-done | bytes 32800 | tf_op jit(solution)/shard_map/ppermute | solution.py:22
  96.6 3.6 %shard_map.117 = (f32[64,640]{1,0:T(8,128)S(1)}, f32[64,640]{1,0:T(8,128)S(1)}, f32[64,1280]{1,0:T(8,128)S(1)}, f32[64,1024]{1,0:T(8,128)S(1)}, f32[64,1024]{1,0:T(8,128)S(1)}, /*index=5*/bf16[64,128]{1,0:T(8,128)(2,1)S(1)}) custom-call(s32[3]{0:T(128)S(1)} %pad_add_fusion.spot, f32[32,128]{1,0:T(8,128)S(1)} %get-tuple-element.47.table, ...), custom_call_target="tpu_custom_call" | custom-call | tf_op jit(solution)/shard_map/pallas_call | solution.py:641
  100.8 1.3 collective-permute-done.5
  102.3 1.5 collective-permute-start.8
  103.8 3.7 %collective-permute-done.9 = bf16[64,128]{1,0:T(8,128)(2,1)S(1)} collective-permute-done((bf16[64,128]{1,0:T(8,128)(2,1)S(1)}, bf16[64,128]{1,0:T(8,128)(2,1)S(1)}, u32[]{:S(2)}, u32[]{:S(2)}) %collective-permute-start.9) | collective-permute-done | bytes 16416 | tf_op jit(solution)/shard_map/ppermute | solution.py:22
  109.2 1.0 collective-permute-start.12
  110.2 2.9 %collective-permute-done.12 = bf16[64,256]{1,0:T(8,128)(2,1)S(1)} collective-permute-done((bf16[64,256]{1,0:T(8,128)(2,1)S(1)}, bf16[64,256]{1,0:T(8,128)(2,1)S(1)}, u32[]{:S(2)}, u32[]{:S(2)}) %collective-permute-start.12) | collective-permute-done | bytes 32800 | tf_op jit(solution)/shard_map/ppermute | solution.py:22
  114.2 1.1 collective-permute-start.13
  115.3 1.5 collective-permute-start.15
  116.8 1.0 collective-permute-start.14
  117.9 2.9 %collective-permute-done.14 = f32[64,128]{1,0:T(8,128)S(1)} collective-permute-done((f32[64,128]{1,0:T(8,128)S(1)}, f32[64,128]{1,0:T(8,128)S(1)}, u32[]{:S(2)}, u32[]{:S(2)}) %collective-permute-start.14) | collective-permute-done | bytes 32800 | tf_op jit(solution)/shard_map/ppermute | solution.py:22
  120.9 1.9 %shard_map.118 = (bf16[64,1024]{1,0:T(8,128)(2,1)S(1)}, f32[64,64]{1,0:T(8,128)S(1)}) custom-call(s32[3]{0:T(128)S(1)} %pad_add_fusion.spot, f32[64,640]{1,0:T(8,128)S(1)} %add.67.totals, bf16[16,80,1408]{2,1,0:T(8,128)(2,1)} %all-to-all-done.received.mine.received_cells), custom_call_target="tpu_custom_call" | custom-call | tf_op jit(solution)/shard_map/pallas_call | solution.py:673
  123.4 0.9 collective-permute-done.16.other
  124.3 3.0 %shard_map.119 = (f32[64,1280]{1,0:T(8,128)S(1)}, s16[64,1280]{1,0:T(8,128)(2,1)S(1)}, f32[64,128]{1,0:T(8,128)S(1)}) custom-call(s32[3]{0:T(128)S(1)} %pad_add_fusion.spot, f32[32,128]{1,0:T(8,128)S(1)} %get-tuple-element.47.table, bf16[64,1024]{1,0:T(8,128)(2,1)S(1)} %get-tuple-element.74.mine, bf16[64,1024]{1,0:T(8,128)(2,1)S(1)} %collective-permute-done.16.other, ...), custom_call_target="tpu_custom_call" | custom-call | tf_op jit(solution)/shard_map/pallas_call | solution.py:686
  127.5 2.9 %collective-permute-start.19 = (f32[64,128]{1,0:T(8,128)S(1)}, f32[64,128]{1,0:T(8,128)S(1)}, u32[]{:S(2)}, u32[]{:S(2)}) collective-permute-start(f32[64,128]{1,0:T(8,128)S(1)} %get-tuple-element.79.beside), channel_id=1, source_target_pairs={{0,16},{1,17},{2,18},{3,19},{4,20},{5,21},{6,22},{7,23},{8,24},{9,... | collective-permute-start | bytes 98312 | tf_op jit(solution)/shard_map/ppermute | solution.py:22
  130.4 9.1 %collective-permute-done.19.beside_other = f32[64,128]{1,0:T(8,128)S(1)} collective-permute-done((f32[64,128]{1,0:T(8,128)S(1)}, f32[64,128]{1,0:T(8,128)S(1)}, u32[]{:S(2)}, u32[]{:S(2)}) %collective-permute-start.19) | collective-permute-done | bytes 32800 | tf_op jit(solution)/shard_map/ppermute | solution.py:22
  139.5 3.7 %shard_map.120 = (f32[64,640]{1,0:T(8,128)S(1)}, f32[64,640]{1,0:T(8,128)S(1)}, f32[64,128]{1,0:T(8,128)}, f32[64,512]{1,0:T(8,128)}) custom-call(s32[3]{0:T(128)S(1)} %pad_add_fusion.spot, f32[32,128]{1,0:T(8,128)S(1)} %get-tuple-element.47.table, f32[64,1280]{1,0:T(8,128)S(1)} %get-tuple-element.77.sums, ...), custom_call_target="tpu_custom_call" | custom-call | tf_op jit(solution)/shard_map/pallas_call | solution.py:641
  143.3 1.3 collective-permute-done.20
  144.7 1.1 collective-permute-start.21
  145.8 3.8 %collective-permute-done.21 = f32[64,320]{1,0:T(8,128)S(1)} collective-permute-done((f32[64,320]{1,0:T(8,128)S(1)}, f32[64,320]{1,0:T(8,128)S(1)}, u32[]{:S(2)}, u32[]{:S(2)}) %collective-permute-start.21) | collective-permute-done | bytes 81952 | tf_op jit(solution)/shard_map/ppermute | solution.py:22
  150.5 3.5 %collective-permute-done.22 = f32[64,192]{1,0:T(8,128)S(1)} collective-permute-done((f32[64,192]{1,0:T(8,128)S(1)}, f32[64,192]{1,0:T(8,128)S(1)}, u32[]{:S(2)}, u32[]{:S(2)}) %collective-permute-start.22) | collective-permute-done | bytes 49184 | tf_op jit(solution)/shard_map/ppermute | solution.py:22
  154.2 3.9 %collective-permute-done.23 = f32[64,128]{1,0:T(8,128)S(1)} collective-permute-done((f32[64,128]{1,0:T(8,128)S(1)}, f32[64,128]{1,0:T(8,128)S(1)}, u32[]{:S(2)}, u32[]{:S(2)}) %collective-permute-start.23) | collective-permute-done | bytes 32800 | tf_op jit(solution)/shard_map/ppermute | solution.py:22
  (86 shorter events, 11.3 us)
Async XLA Ops:
  1.4 0.7 copy-start.6
  3.9 9.2 %collective-permute-start = (f32[8,128]{1,0:T(8,128)S(1)}, f32[8,128]{1,0:T(8,128)S(1)}, u32[]{:S(2)}, u32[]{:S(2)}) collective-permute-start(f32[8,128]{1,0:T(8,128)S(1)} %shard_map.112.mine), channel_id=1, source_target_pairs={{0,16},{1,17},{2,18},{3,19},{4,20},{5,21},{6,22},{7,23},{8,24},{9,... | collective-permute-start | bytes 12296 | tf_op jit(solution)/shard_map/ppermute | solution.py:22
  8.0 0.9 copy-start.1
  9.0 0.8 copy-start.3
  9.7 0.8 copy-start.5
  13.3 1.8 %copy-start = (bf16[16,80,1408]{2,1,0:T(8,128)(2,1)}, bf16[16,80,1408]{2,1,0:T(8,128)(2,1)S(1)}, u32[]{:S(2)}) copy-start(bf16[16,80,1408]{2,1,0:T(8,128)(2,1)S(1)} %shard_map.114) | copy-start | bytes 10813444
  15.1 5.0 %copy-start.4 = (f32[64,128]{1,0:T(8,128)S(1)}, f32[64,128]{1,0:T(8,128)}, u32[]{:S(2)}) copy-start(f32[64,128]{1,0:T(8,128)} %gene.1) | copy-start | bytes 98308
  15.1 5.1 %copy-start.2 = (f32[64,512]{1,0:T(8,128)S(1)}, f32[64,512]{1,0:T(8,128)}, u32[]{:S(2)}) copy-start(f32[64,512]{1,0:T(8,128)} %peak.1) | copy-start | bytes 393220
  15.1 60.9 %all-to-all-start = ((bf16[16,80,1408]{2,1,0:T(8,128)(2,1)}), bf16[16,80,1408]{2,1,0:T(8,128)(2,1)}, u32[]{:S(2)}, u32[]{:S(2)}) async-start(bf16[16,80,1408]{2,1,0:T(8,128)(2,1)} %copy-done), calls=%async_computation | async-start | bytes 7208960 | tf_op jit(solution)/shard_map/all_to_all | solution.py:596
  20.2 55.9 %collective-permute-start.1 = (f32[64,640]{1,0:T(8,128)S(1)}, f32[64,640]{1,0:T(8,128)S(1)}, u32[]{:S(2)}, u32[]{:S(2)}) collective-permute-start(f32[64,640]{1,0:T(8,128)S(1)} %constant_dynamic-update-slice_fusion), channel_id=1, source_target_pairs={{0,16},{1,17},{2,18},{3,19},{4,20},{5,21},{6,22},{7,23},{8,24},{9,... | collective-permute-start | bytes 491528 | tf_op jit(solution)/shard_map/ppermute | solution.py:22
  77.2 3.0 %collective-permute-start.2 = (bf16[16,16,1280]{2,1,0:T(8,128)(2,1)S(1)}, bf16[16,16,1280]{2,1,0:T(8,128)(2,1)S(1)}, u32[]{:S(2)}, u32[]{:S(2)}) collective-permute-start(bf16[16,16,1280]{2,1,0:T(8,128)(2,1)S(1)} %slice.39), channel_id=1, source_target_pairs={{0,1},{1,0},{2,3},{3,2},{4,5},{5,4},{6,7},{7,6},{8,9},{9,8},{10,11... | collective-permute-start | bytes 1966088 | tf_op jit(solution)/shard_map/ppermute | solution.py:22
  83.4 13.2 %collective-permute-start.3 = (s16[64,1280]{1,0:T(8,128)(2,1)S(1)}, s16[64,1280]{1,0:T(8,128)(2,1)S(1)}, u32[]{:S(2)}, u32[]{:S(2)}) collective-permute-start(s16[64,1280]{1,0:T(8,128)(2,1)S(1)} %get-tuple-element.49), channel_id=1, source_target_pairs={{0,16},{1,17},{2,18},{3,19},{4,20},{5,21},{6,22},{7,23},{8,24},{9,... | collective-permute-start | bytes 491528 | tf_op jit(solution)/shard_map/ppermute | solution.py:22
  86.9 9.8 %collective-permute-start.4 = (f32[64,128]{1,0:T(8,128)S(1)}, f32[64,128]{1,0:T(8,128)S(1)}, u32[]{:S(2)}, u32[]{:S(2)}) collective-permute-start(f32[64,128]{1,0:T(8,128)S(1)} %get-tuple-element.50.beside), channel_id=1, source_target_pairs={{0,16},{1,17},{2,18},{3,19},{4,20},{5,21},{6,22},{7,23},{8,24},{9,... | collective-permute-start | bytes 98312 | tf_op jit(solution)/shard_map/ppermute | solution.py:22
  100.3 1.9 %collective-permute-start.6 = (f32[64,1024]{1,0:T(8,128)S(1)}, f32[64,1024]{1,0:T(8,128)S(1)}, u32[]{:S(2)}, u32[]{:S(2)}) collective-permute-start(f32[64,1024]{1,0:T(8,128)S(1)} %get-tuple-element.55), channel_id=1, source_target_pairs={{0,1},{1,0},{2,3},{3,2},{4,5},{5,4},{6,7},{7,6},{8,9},{9,8},{10,11... | collective-permute-start | bytes 786440 | tf_op jit(solution)/shard_map/ppermute | solution.py:22
  100.3 1.8 %collective-permute-start.5 = (f32[64,640]{1,0:T(8,128)S(1)}, f32[64,640]{1,0:T(8,128)S(1)}, u32[]{:S(2)}, u32[]{:S(2)}) collective-permute-start(f32[64,640]{1,0:T(8,128)S(1)} %get-tuple-element.53), channel_id=1, source_target_pairs={{0,1},{1,0},{2,3},{3,2},{4,5},{5,4},{6,7},{7,6},{8,9},{9,8},{10,11... | collective-permute-start | bytes 491528 | tf_op jit(solution)/shard_map/ppermute | solution.py:22
  102.2 6.3 %collective-permute-start.7 = (f32[64,640]{1,0:T(8,128)S(1)}, f32[64,640]{1,0:T(8,128)S(1)}, u32[]{:S(2)}, u32[]{:S(2)}) collective-permute-start(f32[64,640]{1,0:T(8,128)S(1)} %add.61), channel_id=1, source_target_pairs={{0,2},{1,3},{2,0},{3,1},{4,6},{5,7},{6,4},{7,5},{8,10},{9,11},{10,... | collective-permute-start | bytes 491528 | tf_op jit(solution)/shard_map/ppermute | solution.py:22
  102.3 5.6 %collective-permute-start.8 = (f32[64,512]{1,0:T(8,128)S(1)}, f32[64,512]{1,0:T(8,128)S(1)}, u32[]{:S(2)}, u32[]{:S(2)}) collective-permute-start(f32[64,512]{1,0:T(8,128)S(1)} %slice_select_fusion), channel_id=1, source_target_pairs={{0,4},{1,5},{2,6},{3,7},{4,0},{5,1},{6,2},{7,3},{8,12},{9,13},{10,... | collective-permute-start | bytes 393224 | tf_op jit(solution)/shard_map/ppermute | solution.py:22
  103.8 3.7 %collective-permute-start.9 = (bf16[64,128]{1,0:T(8,128)(2,1)S(1)}, bf16[64,128]{1,0:T(8,128)(2,1)S(1)}, u32[]{:S(2)}, u32[]{:S(2)}) collective-permute-start(bf16[64,128]{1,0:T(8,128)(2,1)S(1)} %get-tuple-element.59), channel_id=1, source_target_pairs={{0,8},{1,9},{2,10},{3,11},{4,12},{5,13},{6,14},{7,15},{8,0},{9,1},... | collective-permute-start | bytes 49160 | tf_op jit(solution)/shard_map/ppermute | solution.py:22
  108.6 5.5 %collective-permute-start.10 = (f32[64,640]{1,0:T(8,128)S(1)}, f32[64,640]{1,0:T(8,128)S(1)}, u32[]{:S(2)}, u32[]{:S(2)}) collective-permute-start(f32[64,640]{1,0:T(8,128)S(1)} %add.63), channel_id=1, source_target_pairs={{0,4},{1,5},{2,6},{3,7},{4,0},{5,1},{6,2},{7,3},{8,12},{9,13},{10,... | collective-permute-start | bytes 491528 | tf_op jit(solution)/shard_map/ppermute | solution.py:22
  109.2 4.3 %collective-permute-start.11 = (f32[64,256]{1,0:T(8,128)S(1)}, f32[64,256]{1,0:T(8,128)S(1)}, u32[]{:S(2)}, u32[]{:S(2)}) collective-permute-start(f32[64,256]{1,0:T(8,128)S(1)} %slice_select_fusion.2), channel_id=1, source_target_pairs={{0,8},{1,9},{2,10},{3,11},{4,12},{5,13},{6,14},{7,15},{8,0},{9,1},... | collective-permute-start | bytes 196616 | tf_op jit(solution)/shard_map/ppermute | solution.py:22
  109.2 3.9 %collective-permute-start.12 = (bf16[64,256]{1,0:T(8,128)(2,1)S(1)}, bf16[64,256]{1,0:T(8,128)(2,1)S(1)}, u32[]{:S(2)}, u32[]{:S(2)}) collective-permute-start(bf16[64,256]{1,0:T(8,128)(2,1)S(1)} %pad_maximum_fusion.6), channel_id=1, source_target_pairs={{0,2},{1,3},{2,0},{3,1},{4,6},{5,7},{6,4},{7,5},{8,10},{9,11},{10,... | collective-permute-start | bytes 98312 | tf_op jit(solution)/shard_map/ppermute | solution.py:22
  114.2 6.5 %collective-permute-start.13 = (f32[64,640]{1,0:T(8,128)S(1)}, f32[64,640]{1,0:T(8,128)S(1)}, u32[]{:S(2)}, u32[]{:S(2)}) collective-permute-start(f32[64,640]{1,0:T(8,128)S(1)} %add.65), channel_id=1, source_target_pairs={{0,8},{1,9},{2,10},{3,11},{4,12},{5,13},{6,14},{7,15},{8,0},{9,1},... | collective-permute-start | bytes 491528 | tf_op jit(solution)/shard_map/ppermute | solution.py:22
  115.3 5.4 %collective-permute-start.15 = (bf16[64,512]{1,0:T(8,128)(2,1)S(1)}, bf16[64,512]{1,0:T(8,128)(2,1)S(1)}, u32[]{:S(2)}, u32[]{:S(2)}) collective-permute-start(bf16[64,512]{1,0:T(8,128)(2,1)S(1)} %pad_maximum_fusion.4), channel_id=1, source_target_pairs={{0,4},{1,5},{2,6},{3,7},{4,0},{5,1},{6,2},{7,3},{8,12},{9,13},{10,... | collective-permute-start | bytes 196616 | tf_op jit(solution)/shard_map/ppermute | solution.py:22
  116.8 3.9 %collective-permute-start.14 = (f32[64,128]{1,0:T(8,128)S(1)}, f32[64,128]{1,0:T(8,128)S(1)}, u32[]{:S(2)}, u32[]{:S(2)}) collective-permute-start(f32[64,128]{1,0:T(8,128)S(1)} %slice_select_fusion.5), channel_id=1, source_target_pairs={{0,2},{1,3},{2,0},{3,1},{4,6},{5,7},{6,4},{7,5},{8,10},{9,11},{10,... | collective-permute-start | bytes 98312 | tf_op jit(solution)/shard_map/ppermute | solution.py:22
  120.8 2.6 %collective-permute-start.17 = (bf16[64,1024]{1,0:T(8,128)(2,1)S(1)}, bf16[64,1024]{1,0:T(8,128)(2,1)S(1)}, u32[]{:S(2)}, u32[]{:S(2)}) collective-permute-start(bf16[64,1024]{1,0:T(8,128)(2,1)S(1)} %pad_maximum_fusion.2), channel_id=1, source_target_pairs={{0,1},{1,0},{2,3},{3,2},{4,5},{5,4},{6,7},{7,6},{8,9},{9,8},{10,11... | collective-permute-start | bytes 393224 | tf_op jit(solution)/shard_map/ppermute | solution.py:22
  122.8 1.5 collective-permute-start.16
  127.4 12.1 %collective-permute-start.18 = (s16[64,1280]{1,0:T(8,128)(2,1)S(1)}, s16[64,1280]{1,0:T(8,128)(2,1)S(1)}, u32[]{:S(2)}, u32[]{:S(2)}) collective-permute-start(s16[64,1280]{1,0:T(8,128)(2,1)S(1)} %get-tuple-element.78), channel_id=1, source_target_pairs={{0,16},{1,17},{2,18},{3,19},{4,20},{5,21},{6,22},{7,23},{8,24},{9,... | collective-permute-start | bytes 491528 | tf_op jit(solution)/shard_map/ppermute | solution.py:22
  127.5 12.0 %collective-permute-start.19 = (f32[64,128]{1,0:T(8,128)S(1)}, f32[64,128]{1,0:T(8,128)S(1)}, u32[]{:S(2)}, u32[]{:S(2)}) collective-permute-start(f32[64,128]{1,0:T(8,128)S(1)} %get-tuple-element.79.beside), channel_id=1, source_target_pairs={{0,16},{1,17},{2,18},{3,19},{4,20},{5,21},{6,22},{7,23},{8,24},{9,... | collective-permute-start | bytes 98312 | tf_op jit(solution)/shard_map/ppermute | solution.py:22
  143.2 1.4 collective-permute-start.20
  144.7 4.9 %collective-permute-start.21 = (f32[64,320]{1,0:T(8,128)S(1)}, f32[64,320]{1,0:T(8,128)S(1)}, u32[]{:S(2)}, u32[]{:S(2)}) collective-permute-start(f32[64,320]{1,0:T(8,128)S(1)} %pad_maximum_fusion.3), channel_id=1, source_target_pairs={{0,2},{1,3},{2,0},{3,1},{4,6},{5,7},{6,4},{7,5},{8,10},{9,11},{10,... | collective-permute-start | bytes 245768 | tf_op jit(solution)/shard_map/ppermute | solution.py:22
  149.7 4.3 %collective-permute-start.22 = (f32[64,192]{1,0:T(8,128)S(1)}, f32[64,192]{1,0:T(8,128)S(1)}, u32[]{:S(2)}, u32[]{:S(2)}) collective-permute-start(f32[64,192]{1,0:T(8,128)S(1)} %pad_maximum_fusion.5), channel_id=1, source_target_pairs={{0,4},{1,5},{2,6},{3,7},{4,0},{5,1},{6,2},{7,3},{8,12},{9,13},{10,... | collective-permute-start | bytes 147464 | tf_op jit(solution)/shard_map/ppermute | solution.py:22
  154.2 3.9 %collective-permute-start.23 = (f32[64,128]{1,0:T(8,128)S(1)}, f32[64,128]{1,0:T(8,128)S(1)}, u32[]{:S(2)}, u32[]{:S(2)}) collective-permute-start(f32[64,128]{1,0:T(8,128)S(1)} %pad_maximum_fusion.7), channel_id=1, source_target_pairs={{0,8},{1,9},{2,10},{3,11},{4,12},{5,13},{6,14},{7,15},{8,0},{9,1},... | collective-permute-start | bytes 98312 | tf_op jit(solution)/shard_map/ppermute | solution.py:22
  (2 other events, 1.3 us)

commit v4 on v3

--- a/solution.py
+++ b/solution.py
@@ -274,20 +274,88 @@
             out[j, cells:, s * width + gene_width : (s + 1) * width] = peak_low[row : row + part]
 
 
-def slots_kernel(spot, link_gene, link_peak, link_weight, link_count, out):
+def encode(group):
+    least = jnp.min(group, axis=1, keepdims=True)
+    spread = jnp.max(group, axis=1, keepdims=True) - least
+    per = jnp.where(spread > 0.0, CODES / spread, 0.0)
+    code = jnp.minimum(jnp.floor((group - least) * per + 0.5), CODES) - (CODES + 1) / 2
+    return code.astype(jnp.int32).astype(jnp.int16), least, spread / CODES
+
+
+def decode(code, least, step):
+    return least + (code.astype(jnp.int32).astype(jnp.float32) + (CODES + 1) / 2) * step
+
+
+def ahead_kernel(spot, gene, peak, *refs):
+    links, (codes, beside), copied, sems = refs[:4], refs[4:6], refs[6:10], refs[10]
+    copies = [pltpu.make_async_copy(link, to, sems.at[i]) for i, (link, to) in enumerate(zip(links, copied))]
+    for copy in copies:
+        copy.start()
+    rank, width = codes.shape
+    gene_width = gene.shape[1]
+    least, step = [], []
+    for b in range(width // BLOCK):
+        ref, at = (gene, b * BLOCK) if b * BLOCK < gene_width else (peak, b * BLOCK - gene_width)
+        code, low, per = encode(ref[:, at : at + BLOCK])
+        codes[:, b * BLOCK : (b + 1) * BLOCK] = code
+        least.append(low)
+        step.append(per)
+    pad = jnp.zeros((rank, beside.shape[1] - 2 * len(least)), jnp.float32)
+    beside[:rank] = jnp.concatenate([*least, *step, pad], axis=1)
+    for copy in copies:
+        copy.wait()
+    link_gene, link_peak, link_weight, link_count = copied
     slots = link_gene.shape[0]
-    lane = lax.broadcasted_iota(jnp.int32, out.shape, 1) - spot[1] * slots
-    row = lax.broadcasted_iota(jnp.int32, out.shape, 0)
-    value = jnp.zeros(out.shape, jnp.float32)
+    shape = (beside.shape[0] - rank, beside.shape[1])
+    lane = lax.broadcasted_iota(jnp.int32, shape, 1) - spot[1] * slots
+    row = lax.broadcasted_iota(jnp.int32, shape, 0)
+    value = jnp.zeros(shape, jnp.float32)
     for s in range(slots):
         weight = jnp.where(s < link_count[0], link_weight[s], 0)
         for r, entry in enumerate((link_gene[s], link_peak[s], weight)):
             value = jnp.where((lane == s) & (row == r), entry.astype(jnp.float32), value)
-    out[...] = value
+    beside[rank:] = value
+
+
+def ahead(spot, gene_factor, peak_factor, links):
+    rank = gene_factor.shape[0]
+    width = gene_factor.shape[1] + peak_factor.shape[1]
+    anywhere = pl.BlockSpec(memory_space=pl.ANY)
+    return pl.pallas_call(
+        ahead_kernel,
+        grid=(1,),
+        in_specs=[SMEM] + [pl.BlockSpec(f.shape, lambda i: (0, 0)) for f in (gene_factor, peak_factor)] + [anywhere] * 4,
+        out_specs=[VMEM, VMEM],
+        out_shape=(struct(rank, width, dtype=jnp.int16), struct(rank + rank // 8, 2 * rank)),
+        scratch_shapes=[pltpu.SMEM(link.shape, jnp.int32) for link in links] + [pltpu.SemaphoreType.DMA((4,))],
+        compiler_params=PARAMS,
+    )(spot, in_hbm(gene_factor), in_hbm(peak_factor), *links)
+
+
+def twins_kernel(spot, gene, peak, codes, beside, out):
+    gene_width, peak_width = gene.shape[1], peak.shape[1]
+    groups = (gene_width + peak_width) // BLOCK
+    at = 0
+    first = spot[0] == 0
+    for ref, start in ((gene, 0), (peak, gene_width)):
+        size = ref.shape[1]
+        for b in range(size // BLOCK):
+            g = start // BLOCK + b
+            mine = ref[:, b * BLOCK : (b + 1) * BLOCK]
+            code = codes[:, g * BLOCK : (g + 1) * BLOCK]
+            other = decode(code, beside[: mine.shape[0], g : g + 1], beside[: mine.shape[0], groups + g : groups + g + 1])
+            out[:, at + b * BLOCK : at + (b + 1) * BLOCK] = jnp.where(first, mine, other)
+            out[:, at + size + b * BLOCK : at + size + (b + 1) * BLOCK] = jnp.where(first, other, mine)
+        at += 2 * size
+
+
+def in_hbm(value):
+    return pltpu.with_memory_space_constraint(value, pltpu.HBM)
 
 
 def put_slots_kernel(mine, other, parcels_in, out, block, sems):
-    block[...] = jnp.concatenate([mine[...], other[...]], axis=0).astype(jnp.bfloat16)
+    first = mine.shape[0] - block.shape[0] // 2
+    block[...] = jnp.concatenate([mine[first:], other[first:]], axis=0).astype(jnp.bfloat16)
     half, rows, lanes = out.shape
     copies = [
         pltpu.make_async_copy(
@@ -302,14 +370,14 @@
 
 
 def put_slots(mine, other, parcels_value):
-    anywhere = pl.BlockSpec(memory_space=pl.ANY)
+    rank = mine.shape[1] // 2
     return pl.pallas_call(
         put_slots_kernel,
-        in_specs=[VMEM, VMEM, anywhere],
-        out_specs=anywhere,
+        in_specs=[VMEM] * 3,
+        out_specs=VMEM,
         out_shape=struct(*parcels_value.shape, dtype=parcels_value.dtype),
         scratch_shapes=[
-            pltpu.VMEM((2 * mine.shape[0], mine.shape[1]), jnp.bfloat16),
+            pltpu.VMEM((rank // 4, 2 * rank), jnp.bfloat16),
             pltpu.SemaphoreType.DMA((parcels_value.shape[0],)),
         ],
         input_output_aliases={2: 0},
@@ -339,7 +407,7 @@
         out_specs=pl.BlockSpec((each, rows, lanes), lambda i: (i, 0, 0)),
         out_shape=struct(half, rows, lanes, dtype=jnp.bfloat16),
         compiler_params=PARAMS,
-    )(rna_counts, rna_counts, atac_counts, atac_counts, cell_factor, gene_factor, peak_factor)
+    )(*(in_hbm(a) for a in (rna_counts, rna_counts, atac_counts, atac_counts, cell_factor, gene_factor, peak_factor)))
 
 
 def first_sums_kernel(received, sums, gram):
@@ -358,13 +426,10 @@
     for b in range(features // BLOCK):
         group = sums_value[:, b * BLOCK : (b + 1) * BLOCK]
         sums[:, b * BLOCK : (b + 1) * BLOCK] = group
-        low = jnp.min(group, axis=1, keepdims=True)
-        spread = jnp.max(group, axis=1, keepdims=True) - low
-        per = jnp.where(spread > 0.0, CODES / spread, 0.0)
-        code = jnp.minimum(jnp.floor((group - low) * per + 0.5), CODES) - (CODES + 1) / 2
-        coded[:, b * BLOCK : (b + 1) * BLOCK] = code.astype(jnp.int32).astype(jnp.int16)
+        code, low, per = encode(group)
+        coded[:, b * BLOCK : (b + 1) * BLOCK] = code
         least.append(low)
-        step.append(spread / CODES)
+        step.append(per)
     pad = jnp.zeros((rank, beside.shape[1] - rank - 2 * len(least)), jnp.float32)
     beside[...] = jnp.concatenate([gram_value, *least, *step, pad], axis=1)
 
@@ -470,10 +535,10 @@
     groups = features // BLOCK
     whole = []
     for b in range(groups):
-        code = other[:, b * BLOCK : (b + 1) * BLOCK].astype(jnp.int32).astype(jnp.float32) + (CODES + 1) / 2
+        code = other[:, b * BLOCK : (b + 1) * BLOCK]
         least = beside_other[:, rank + b : rank + b + 1]
         step = beside_other[:, rank + groups + b : rank + groups + b + 1]
-        whole.append(sums[:, b * BLOCK : (b + 1) * BLOCK] + (least + code * step))
+        whole.append(sums[:, b * BLOCK : (b + 1) * BLOCK] + decode(code, least, step))
     whole = jnp.concatenate(whole, axis=1)
     new = old * whole / below
     low = new.astype(jnp.bfloat16)
@@ -573,35 +638,25 @@
     link_order = layout([1] + link_bits)
     gene_order = layout([1] + gene_bits[::-1])
 
-    slots = pl.pallas_call(
-        slots_kernel,
-        in_specs=[SMEM] * 5,
-        out_specs=VMEM,
-        out_shape=struct(rank // 8, 2 * rank),
-        compiler_params=PARAMS,
-    )(spot, link_gene, link_peak, link_weight, link_count)
-    slots_other = flip(slots, half)
-    state = jnp.concatenate([gene_factor, peak_factor], axis=1)
-    state_other = flip(state, half)
-    sent = parcels(
-        pltpu.with_memory_space_constraint(rna_counts, pltpu.HBM),
-        pltpu.with_memory_space_constraint(atac_counts, pltpu.HBM),
-        cell_factor,
-        gene_factor,
-        peak_factor,
-        half,
-    )
-    sent = put_slots(slots, slots_other, sent)
+    codes, aside = ahead(spot, gene_factor, peak_factor, (link_gene, link_peak, link_weight, link_count))
+    aside_other = flip(aside, half)
+    codes_other = flip(codes, half)
+    sent = parcels(rna_counts, atac_counts, cell_factor, gene_factor, peak_factor, half)
+    sent = put_slots(aside, aside_other, sent)
+    sent, codes_other = lax.optimization_barrier((sent, codes_other))
     halves = [list(range(half)), list(range(half, count))]
     received = lax.all_to_all(sent, AXIS, 0, 0, axis_index_groups=halves, tiled=True)
-    received, state_other = lax.optimization_barrier((received, state_other))
-    low, high = in_order(half, state, state_other)
-    factors = jnp.concatenate(
-        [low[:, :gene_width], high[:, :gene_width], low[:, gene_width:], high[:, gene_width:]], axis=1
-    )
+    factors = pl.pallas_call(
+        twins_kernel,
+        in_specs=[SMEM] + [VMEM] * 4,
+        out_specs=VMEM,
+        out_shape=struct(rank, features),
+        compiler_params=PARAMS,
+    )(spot, gene_factor, peak_factor, codes_other, aside_other)
 
     sums_shapes = (struct(rank, features), struct(rank, features, dtype=jnp.int16), struct(rank, 2 * rank))
     rows_other = flip(received[:, cells:, :features], 1)
+    received = pltpu.with_memory_space_constraint(received, pltpu.VMEM)
     sums, gram = pl.pallas_call(
         first_sums_kernel,
         in_specs=[VMEM],
@@ -649,7 +704,25 @@
             gene_out, peak_out = outs
             totals = kept + flip(sent, 1)
             cell_sums, gram_features = totals[:, :split], totals[:, split : split + rank]
-            for bit in cell_bits:
+            first, second = cell_bits[:2]
+            quarters = jnp.split(cell_sums, 4, axis=1)
+            is_first, is_second = (me & first) != 0, (me & second) != 0
+
+            def quarter(flip_first, flip_second):
+                low, high = (
+                    jnp.where(is_second ^ flip_second, quarters[2 * i + 1], quarters[2 * i]) for i in range(2)
+                )
+                return jnp.where(is_first ^ flip_first, high, low)
+
+            leaving = [
+                jnp.concatenate([quarter(*which), gram_features], axis=1)
+                for which in ((True, False), (False, True), (True, True))
+            ]
+            got = [flip(value, bit) for value, bit in zip(leaving, (first, second, first | second))]
+            size = quarters[0].shape[1]
+            cell_sums = quarter(False, False) + (got[0][:, :size] + got[1][:, :size] + got[2][:, :size])
+            gram_features = gram_features + (got[0][:, size:] + got[1][:, size:] + got[2][:, size:])
+            for bit in cell_bits[2:]:
                 left, right = jnp.split(cell_sums, 2, axis=1)
                 clear = (me & bit) == 0
                 got = flip(jnp.concatenate([jnp.where(clear, right, left), gram_features], axis=1), bit)

time: 160 us -> 138 us (0.86)
  waiting for transfers between devices: 100 us -> 44.3 us
  blocking collectives: 0 us -> 47.8 us
  Pallas kernels: 21.7 us -> 16.6 us
  starting transfers between devices: 26.2 us -> 22 us
  local copies, waits for them, and re-layouts: 7.36 us -> 4.04 us
    ppermute x24 -> x25, waiting for transfers between devices: 100 us -> 44.3 us  [flip(): return lax.ppermute(value, AXIS, [(i, i ^ bit) for i in range(count)])]
    all_to_all x0 -> x1, blocking collectives: none -> 47.8 us  [shards_blocks(): lax.all_to_all(sent, AXIS, 0, 0, axis_index_groups=halves, tiled=True)]
    all_to_all x1 -> x0, starting transfers between devices: 5.02 us -> none  [shards_blocks(): lax.all_to_all(sent, AXIS, 0, 0, axis_index_groups=halves, tiled=True)]
    pallas_call x2, Pallas kernels: 7.35 us -> 4.6 us  [shards_blocks(): pl.pallas_call(functools.partial(update_kernel, last, widths, (cell_order...]
    unnamed x19 -> x14, local copies, waits for them, and re-layouts: 6.18 us -> 4 us
    pallas_call x1, Pallas kernels: 2.86 us -> 0.84 us  [shards_blocks(): pl.pallas_call(first_sums_kernel, in_specs=[VMEM], out_specs=[VMEM] * 2,...]
    pallas_call x2 -> x3, Pallas kernels: 0.79 us -> 2.46 us  [the longest x1 1.57 us: ahead(): pl.pallas_call(ahead_kernel, grid=(1,), in_specs=[SMEM] + [pl.BlockSpec(f...]
    ppermute x24 -> x25, starting transfers between devices: 21.2 us -> 22 us  [flip(): return lax.ppermute(value, AXIS, [(i, i ^ bit) for i in range(count)])]
  transfers between devices with their start and end apart: 25 -> 25, of which waited for: 16 -> 17; matrix products, arithmetic and copies ran while one was open for 0% -> 0% of each run, Pallas kernels for 5% -> 4%
where the time goes in v4:
time: 138 us
  blocking collectives  47.8 us (35%)
  waiting for transfers between devices  44.3 us (32%)
  starting transfers between devices  22 us (16%)
  Pallas kernels  16.6 us (12%)
  local copies, waits for them, and re-layouts  4.04 us (3%)
  between operations  1.62 us (1%)
    all_to_all x1, blocking collectives, shards_blocks(): lax.all_to_all(sent, AXIS, 0, 0, axis_index_groups=halves, tiled=True)  47.8 us
    ppermute x25, waiting for transfers between devices, flip(): return lax.ppermute(value, AXIS, [(i, i ^ bit) for i in range(count)])  44.3 us
    ppermute x25, starting transfers between devices, flip(): return lax.ppermute(value, AXIS, [(i, i ^ bit) for i in range(count)])  22 us
    pallas_call x2, Pallas kernels, shards_blocks(): pl.pallas_call(functools.partial(update_kernel, last, widths, (cell_order...  4.6 us
    unnamed x14, local copies, waits for them, and re-layouts  4 us
  transfers between devices with their start and end apart: 25, of which 17 were waited for; matrix products, arithmetic and copies ran while one was open for 0% of the time, Pallas kernels for 4%

profile of v4, /device:TPU:0, one launch (start us, length us, event | category | flops | bytes accessed | tf_op | source)
XLA Modules:
  0.0 137.8 jit_solution(3267682265300363956)
XLA Ops:
  3.4 1.6 %shard_map.112 = (s16[64,640]{1,0:T(8,128)(2,1)S(1)}, f32[72,128]{1,0:T(8,128)S(1)}) custom-call(s32[3]{0:T(128)S(1)} %pad_add_fusion.spot, f32[64,128]{1,0:T(8,128)} %gene.5, f32[64,512]{1,0:T(8,128)} %peak.5, s32[8]{0:T(128)S(1)} %copy-done.4, s32[8]{0:T(128)S(1)} %copy-done.5, s32[8]{0:T(128)S(1)} %copy-done.6, s32[1]{0:T(128)S(6)} %copy.14.refs_3_), custom_call_target="tpu_custom_call" | custom-call | tf_op jit(solution)/shard_map/pallas_call | solution.py:324
  4.9 4.1 %collective-permute-start.1 = (s16[64,640]{1,0:T(8,128)(2,1)S(1)}, s16[64,640]{1,0:T(8,128)(2,1)S(1)}, u32[]{:S(2)}, u32[]{:S(2)}) collective-permute-start(s16[64,640]{1,0:T(8,128)(2,1)S(1)} %get-tuple-element.47), channel_id=1, source_target_pairs={{0,16},{1,17},{2,18},{3,19},{4,20},{5,21},{6,22},{7,23},{8,24},{9,... | collective-permute-start | bytes 245768 | tf_op jit(solution)/shard_map/ppermute | solution.py:22
  9.1 2.7 %shard_map.113.parcels_in = bf16[16,80,1408]{2,1,0:T(8,128)(2,1)S(1)} custom-call(bf16[64,4096]{1,0:T(8,128)(2,1)} %rna_1.1, bf16[64,4096]{1,0:T(8,128)(2,1)} %rna_1.1, bf16[64,16384]{1,0:T(8,128)(2,1)} %atac_1.1, bf16[64,16384]{1,0:T(8,128)(2,1)} %atac_1.1, f32[64,64]{1,0:T(8,128)} %cell.1, f32[64,128]{1,0:T(8,128)} %gene.5, f32[64,512]{1,0:T(8,128)} %peak.5), custom_call_target="tpu_custom_call" | custom-call | tf_op jit(solution)/shard_map/pallas_call | solution.py:402
  11.9 2.6 %collective-permute-done.other.beside = f32[72,128]{1,0:T(8,128)S(1)} collective-permute-done((f32[72,128]{1,0:T(8,128)S(1)}, f32[72,128]{1,0:T(8,128)S(1)}, u32[]{:S(2)}, u32[]{:S(2)}) %collective-permute-start) | collective-permute-done | bytes 36896 | tf_op jit(solution)/shard_map/ppermute | solution.py:22
  14.6 47.8 %all_to_all.5.received.mine.received_cells = bf16[16,80,1408]{2,1,0:T(8,128)(2,1)S(1)} all-to-all(bf16[16,80,1408]{2,1,0:T(8,128)(2,1)S(1)} %shard_map.114), channel_id=1, replica_groups={{0,1,2,3,4,5,6,7,8,9,10,11,12,13,14,15},{16,17,18,19,20,21,22,23,24,25,..., dimensions={0} | all-to-all | bytes 7208960 | tf_op jit(solution)/shard_map/all_to_all | solution.py:648
  63.4 1.2 collective-permute-done.2.other
  64.6 2.6 %shard_map.116 = (f32[64,1280]{1,0:T(8,128)S(1)}, s16[64,1280]{1,0:T(8,128)(2,1)S(1)}, f32[64,128]{1,0:T(8,128)S(1)}, f32[32,128]{1,0:T(8,128)S(1)}) custom-call(s32[3]{0:T(128)S(1)} %pad_add_fusion.spot, bf16[16,80,1408]{2,1,0:T(8,128)(2,1)S(1)} %all_to_all.5.received.mine.received_cells, bf16[16,16,1280]{2,1,0:T(8,128)(2,1)S(1)} %collective-permute-done.2.other, ...), custom_call_target="tpu_custom_call" | custom-call | tf_op jit(solution)/shard_map/pallas_call | solution.py:668
  67.2 3.4 %collective-permute-start.3 = (s16[64,1280]{1,0:T(8,128)(2,1)S(1)}, s16[64,1280]{1,0:T(8,128)(2,1)S(1)}, u32[]{:S(2)}, u32[]{:S(2)}) collective-permute-start(s16[64,1280]{1,0:T(8,128)(2,1)S(1)} %get-tuple-element.53), channel_id=1, source_target_pairs={{0,16},{1,17},{2,18},{3,19},{4,20},{5,21},{6,22},{7,23},{8,24},{9,... | collective-permute-start | bytes 491528 | tf_op jit(solution)/shard_map/ppermute | solution.py:22
  71.5 8.6 %collective-permute-done.4.beside_other = f32[64,128]{1,0:T(8,128)S(1)} collective-permute-done((f32[64,128]{1,0:T(8,128)S(1)}, f32[64,128]{1,0:T(8,128)S(1)}, u32[]{:S(2)}, u32[]{:S(2)}) %collective-permute-start.4) | collective-permute-done | bytes 32800 | tf_op jit(solution)/shard_map/ppermute | solution.py:22
  80.1 2.5 %shard_map.118 = (f32[64,640]{1,0:T(8,128)S(1)}, f32[64,640]{1,0:T(8,128)S(1)}, f32[64,1280]{1,0:T(8,128)S(1)}, f32[64,1024]{1,0:T(8,128)S(1)}, f32[64,1024]{1,0:T(8,128)S(1)}, /*index=5*/bf16[64,128]{1,0:T(8,128)(2,1)S(1)}) custom-call(s32[3]{0:T(128)S(1)} %pad_add_fusion.spot, f32[32,128]{1,0:T(8,128)S(1)} %get-tuple-element.51.table, ...), custom_call_target="tpu_custom_call" | custom-call | tf_op jit(solution)/shard_map/pallas_call | solution.py:696
  83.1 1.3 collective-permute-done.5
  84.6 1.0 collective-permute-start.8
  85.6 3.7 %collective-permute-done.9 = bf16[64,128]{1,0:T(8,128)(2,1)S(1)} collective-permute-done((bf16[64,128]{1,0:T(8,128)(2,1)S(1)}, bf16[64,128]{1,0:T(8,128)(2,1)S(1)}, u32[]{:S(2)}, u32[]{:S(2)}) %collective-permute-start.9) | collective-permute-done | bytes 16416 | tf_op jit(solution)/shard_map/ppermute | solution.py:22
  91.3 1.2 collective-permute-start.12
  92.5 2.7 %collective-permute-done.12 = bf16[64,256]{1,0:T(8,128)(2,1)S(1)} collective-permute-done((bf16[64,256]{1,0:T(8,128)(2,1)S(1)}, bf16[64,256]{1,0:T(8,128)(2,1)S(1)}, u32[]{:S(2)}, u32[]{:S(2)}) %collective-permute-start.12) | collective-permute-done | bytes 32800 | tf_op jit(solution)/shard_map/ppermute | solution.py:22
  95.3 1.1 collective-permute-done.10
  97.2 1.9 %collective-permute-start.15 = (bf16[64,512]{1,0:T(8,128)(2,1)S(1)}, bf16[64,512]{1,0:T(8,128)(2,1)S(1)}, u32[]{:S(2)}, u32[]{:S(2)}) collective-permute-start(bf16[64,512]{1,0:T(8,128)(2,1)S(1)} %pad_maximum_fusion.5), channel_id=1, source_target_pairs={{0,4},{1,5},{2,6},{3,7},{4,0},{5,1},{6,2},{7,3},{8,12},{9,13},{10,... | collective-permute-start | bytes 196616 | tf_op jit(solution)/shard_map/ppermute | solution.py:22
  99.1 1.0 collective-permute-start.14
  100.2 2.9 %collective-permute-done.14 = f32[64,128]{1,0:T(8,128)S(1)} collective-permute-done((f32[64,128]{1,0:T(8,128)S(1)}, f32[64,128]{1,0:T(8,128)S(1)}, u32[]{:S(2)}, u32[]{:S(2)}) %collective-permute-start.14) | collective-permute-done | bytes 32800 | tf_op jit(solution)/shard_map/ppermute | solution.py:22
  103.2 2.0 %copy-done.1 = bf16[16,80,1408]{2,1,0:T(8,128)(2,1)S(1)} copy-done((bf16[16,80,1408]{2,1,0:T(8,128)(2,1)S(1)}, bf16[16,80,1408]{2,1,0:T(8,128)(2,1)}, u32[]{:S(2)}) %copy-start.1) | copy-done | bytes 3604504
  105.2 1.5 %shard_map.119 = (bf16[64,1024]{1,0:T(8,128)(2,1)S(1)}, f32[64,64]{1,0:T(8,128)S(1)}) custom-call(s32[3]{0:T(128)S(1)} %pad_add_fusion.spot, f32[64,640]{1,0:T(8,128)S(1)} %add.73.totals, bf16[16,80,1408]{2,1,0:T(8,128)(2,1)S(1)} %copy-done.1), custom_call_target="tpu_custom_call" | custom-call | tf_op jit(solution)/shard_map/pallas_call | solution.py:746
  107.3 0.9 collective-permute-done.16.other
  108.2 1.9 %shard_map.120 = (f32[64,1280]{1,0:T(8,128)S(1)}, s16[64,1280]{1,0:T(8,128)(2,1)S(1)}, f32[64,128]{1,0:T(8,128)S(1)}) custom-call(s32[3]{0:T(128)S(1)} %pad_add_fusion.spot, f32[32,128]{1,0:T(8,128)S(1)} %get-tuple-element.51.table, bf16[64,1024]{1,0:T(8,128)(2,1)S(1)} %get-tuple-element.78.mine, bf16[64,1024]{1,0:T(8,128)(2,1)S(1)} %collective-permute-done.16.other, ...), custom_call_target="tpu_custom_call" | custom-call | tf_op jit(solution)/shard_map/pallas_call | solution.py:759
  110.0 1.6 %collective-permute-start.18 = (s16[64,1280]{1,0:T(8,128)(2,1)S(1)}, s16[64,1280]{1,0:T(8,128)(2,1)S(1)}, u32[]{:S(2)}, u32[]{:S(2)}) collective-permute-start(s16[64,1280]{1,0:T(8,128)(2,1)S(1)} %get-tuple-element.82), channel_id=1, source_target_pairs={{0,16},{1,17},{2,18},{3,19},{4,20},{5,21},{6,22},{7,23},{8,24},{9,... | collective-permute-start | bytes 491528 | tf_op jit(solution)/shard_map/ppermute | solution.py:22
  111.6 1.4 %collective-permute-start.19 = (f32[64,128]{1,0:T(8,128)S(1)}, f32[64,128]{1,0:T(8,128)S(1)}, u32[]{:S(2)}, u32[]{:S(2)}) collective-permute-start(f32[64,128]{1,0:T(8,128)S(1)} %get-tuple-element.83.beside), channel_id=1, source_target_pairs={{0,16},{1,17},{2,18},{3,19},{4,20},{5,21},{6,22},{7,23},{8,24},{9,... | collective-permute-start | bytes 98312 | tf_op jit(solution)/shard_map/ppermute | solution.py:22
  113.0 9.3 %collective-permute-done.19.beside_other = f32[64,128]{1,0:T(8,128)S(1)} collective-permute-done((f32[64,128]{1,0:T(8,128)S(1)}, f32[64,128]{1,0:T(8,128)S(1)}, u32[]{:S(2)}, u32[]{:S(2)}) %collective-permute-start.19) | collective-permute-done | bytes 32800 | tf_op jit(solution)/shard_map/ppermute | solution.py:22
  122.4 2.2 %shard_map.121 = (f32[64,640]{1,0:T(8,128)S(1)}, f32[64,640]{1,0:T(8,128)S(1)}, f32[64,128]{1,0:T(8,128)}, f32[64,512]{1,0:T(8,128)}) custom-call(s32[3]{0:T(128)S(1)} %pad_add_fusion.spot, f32[32,128]{1,0:T(8,128)S(1)} %get-tuple-element.51.table, f32[64,1280]{1,0:T(8,128)S(1)} %get-tuple-element.81.sums, ...), custom_call_target="tpu_custom_call" | custom-call | tf_op jit(solution)/shard_map/pallas_call | solution.py:696
  124.6 1.4 collective-permute-done.20
  126.1 1.1 collective-permute-start.21
  127.7 1.9 %collective-permute-start.23 = (f32[64,192]{1,0:T(8,128)S(1)}, f32[64,192]{1,0:T(8,128)S(1)}, u32[]{:S(2)}, u32[]{:S(2)}) collective-permute-start(f32[64,192]{1,0:T(8,128)S(1)} %get-tuple-element.99), channel_id=1, source_target_pairs={{0,6},{1,7},{2,4},{3,5},{4,2},{5,3},{6,0},{7,1},{8,14},{9,15},{10,... | collective-permute-start | bytes 147464 | tf_op jit(solution)/shard_map/ppermute | solution.py:22
  130.4 1.7 %collective-permute-done.22 = f32[64,192]{1,0:T(8,128)S(1)} collective-permute-done((f32[64,192]{1,0:T(8,128)S(1)}, f32[64,192]{1,0:T(8,128)S(1)}, u32[]{:S(2)}, u32[]{:S(2)}) %collective-permute-start.22) | collective-permute-done | bytes 49184 | tf_op jit(solution)/shard_map/ppermute | solution.py:22
  133.1 3.9 %collective-permute-done.24 = f32[64,128]{1,0:T(8,128)S(1)} collective-permute-done((f32[64,128]{1,0:T(8,128)S(1)}, f32[64,128]{1,0:T(8,128)S(1)}, u32[]{:S(2)}, u32[]{:S(2)}) %collective-permute-start.24) | collective-permute-done | bytes 32800 | tf_op jit(solution)/shard_map/ppermute | solution.py:22
  (72 shorter events, 11.5 us)
Async XLA Ops:
  1.4 0.7 copy-start.4
  2.0 0.7 copy-start.5
  2.7 0.7 copy-start.6
  4.9 9.7 %collective-permute-start.1 = (s16[64,640]{1,0:T(8,128)(2,1)S(1)}, s16[64,640]{1,0:T(8,128)(2,1)S(1)}, u32[]{:S(2)}, u32[]{:S(2)}) collective-permute-start(s16[64,640]{1,0:T(8,128)(2,1)S(1)} %get-tuple-element.47), channel_id=1, source_target_pairs={{0,16},{1,17},{2,18},{3,19},{4,20},{5,21},{6,22},{7,23},{8,24},{9,... | collective-permute-start | bytes 245768 | tf_op jit(solution)/shard_map/ppermute | solution.py:22
  9.0 5.4 %collective-permute-start = (f32[72,128]{1,0:T(8,128)S(1)}, f32[72,128]{1,0:T(8,128)S(1)}, u32[]{:S(2)}, u32[]{:S(2)}) collective-permute-start(f32[72,128]{1,0:T(8,128)S(1)} %get-tuple-element.46.mine), channel_id=1, source_target_pairs={{0,16},{1,17},{2,18},{3,19},{4,20},{5,21},{6,22},{7,23},{8,24},{9,... | collective-permute-start | bytes 110600 | tf_op jit(solution)/shard_map/ppermute | solution.py:22
  62.4 17.7 %copy-start = (bf16[16,80,1408]{2,1,0:T(8,128)(2,1)}, bf16[16,80,1408]{2,1,0:T(8,128)(2,1)S(1)}, u32[]{:S(2)}) copy-start(bf16[16,80,1408]{2,1,0:T(8,128)(2,1)S(1)} %all_to_all.5.received.mine.received_cells) | copy-start | bytes 10813444
  62.4 8.3 %copy-start.2 = (f32[64,512]{1,0:T(8,128)S(1)}, f32[64,512]{1,0:T(8,128)}, u32[]{:S(2)}) copy-start(f32[64,512]{1,0:T(8,128)} %peak.5) | copy-start | bytes 393220
  62.4 8.3 %copy-start.3 = (f32[64,128]{1,0:T(8,128)S(1)}, f32[64,128]{1,0:T(8,128)}, u32[]{:S(2)}) copy-start(f32[64,128]{1,0:T(8,128)} %gene.5) | copy-start | bytes 98308
  62.5 2.2 %collective-permute-start.2 = (bf16[16,16,1280]{2,1,0:T(8,128)(2,1)S(1)}, bf16[16,16,1280]{2,1,0:T(8,128)(2,1)S(1)}, u32[]{:S(2)}, u32[]{:S(2)}) collective-permute-start(bf16[16,16,1280]{2,1,0:T(8,128)(2,1)S(1)} %slice.45), channel_id=1, source_target_pairs={{0,1},{1,0},{2,3},{3,2},{4,5},{5,4},{6,7},{7,6},{8,9},{9,8},{10,11... | collective-permute-start | bytes 1966088 | tf_op jit(solution)/shard_map/ppermute | solution.py:22
  67.2 12.8 %collective-permute-start.3 = (s16[64,1280]{1,0:T(8,128)(2,1)S(1)}, s16[64,1280]{1,0:T(8,128)(2,1)S(1)}, u32[]{:S(2)}, u32[]{:S(2)}) collective-permute-start(s16[64,1280]{1,0:T(8,128)(2,1)S(1)} %get-tuple-element.53), channel_id=1, source_target_pairs={{0,16},{1,17},{2,18},{3,19},{4,20},{5,21},{6,22},{7,23},{8,24},{9,... | collective-permute-start | bytes 491528 | tf_op jit(solution)/shard_map/ppermute | solution.py:22
  70.7 9.4 %collective-permute-start.4 = (f32[64,128]{1,0:T(8,128)S(1)}, f32[64,128]{1,0:T(8,128)S(1)}, u32[]{:S(2)}, u32[]{:S(2)}) collective-permute-start(f32[64,128]{1,0:T(8,128)S(1)} %get-tuple-element.54.beside), channel_id=1, source_target_pairs={{0,16},{1,17},{2,18},{3,19},{4,20},{5,21},{6,22},{7,23},{8,24},{9,... | collective-permute-start | bytes 98312 | tf_op jit(solution)/shard_map/ppermute | solution.py:22
  82.5 1.9 %collective-permute-start.6 = (f32[64,1024]{1,0:T(8,128)S(1)}, f32[64,1024]{1,0:T(8,128)S(1)}, u32[]{:S(2)}, u32[]{:S(2)}) collective-permute-start(f32[64,1024]{1,0:T(8,128)S(1)} %get-tuple-element.59), channel_id=1, source_target_pairs={{0,1},{1,0},{2,3},{3,2},{4,5},{5,4},{6,7},{7,6},{8,9},{9,8},{10,11... | collective-permute-start | bytes 786440 | tf_op jit(solution)/shard_map/ppermute | solution.py:22
  82.6 1.8 %collective-permute-start.5 = (f32[64,640]{1,0:T(8,128)S(1)}, f32[64,640]{1,0:T(8,128)S(1)}, u32[]{:S(2)}, u32[]{:S(2)}) collective-permute-start(f32[64,640]{1,0:T(8,128)S(1)} %get-tuple-element.57), channel_id=1, source_target_pairs={{0,1},{1,0},{2,3},{3,2},{4,5},{5,4},{6,7},{7,6},{8,9},{9,8},{10,11... | collective-permute-start | bytes 491528 | tf_op jit(solution)/shard_map/ppermute | solution.py:22
  84.5 6.3 %collective-permute-start.7 = (f32[64,640]{1,0:T(8,128)S(1)}, f32[64,640]{1,0:T(8,128)S(1)}, u32[]{:S(2)}, u32[]{:S(2)}) collective-permute-start(f32[64,640]{1,0:T(8,128)S(1)} %add.67), channel_id=1, source_target_pairs={{0,2},{1,3},{2,0},{3,1},{4,6},{5,7},{6,4},{7,5},{8,10},{9,11},{10,... | collective-permute-start | bytes 491528 | tf_op jit(solution)/shard_map/ppermute | solution.py:22
  84.6 5.6 %collective-permute-start.8 = (f32[64,512]{1,0:T(8,128)S(1)}, f32[64,512]{1,0:T(8,128)S(1)}, u32[]{:S(2)}, u32[]{:S(2)}) collective-permute-start(f32[64,512]{1,0:T(8,128)S(1)} %slice_select_fusion), channel_id=1, source_target_pairs={{0,4},{1,5},{2,6},{3,7},{4,0},{5,1},{6,2},{7,3},{8,12},{9,13},{10,... | collective-permute-start | bytes 393224 | tf_op jit(solution)/shard_map/ppermute | solution.py:22
  85.6 3.7 %collective-permute-start.9 = (bf16[64,128]{1,0:T(8,128)(2,1)S(1)}, bf16[64,128]{1,0:T(8,128)(2,1)S(1)}, u32[]{:S(2)}, u32[]{:S(2)}) collective-permute-start(bf16[64,128]{1,0:T(8,128)(2,1)S(1)} %get-tuple-element.63), channel_id=1, source_target_pairs={{0,8},{1,9},{2,10},{3,11},{4,12},{5,13},{6,14},{7,15},{8,0},{9,1},... | collective-permute-start | bytes 49160 | tf_op jit(solution)/shard_map/ppermute | solution.py:22
  90.9 5.5 %collective-permute-start.10 = (f32[64,640]{1,0:T(8,128)S(1)}, f32[64,640]{1,0:T(8,128)S(1)}, u32[]{:S(2)}, u32[]{:S(2)}) collective-permute-start(f32[64,640]{1,0:T(8,128)S(1)} %add.69), channel_id=1, source_target_pairs={{0,4},{1,5},{2,6},{3,7},{4,0},{5,1},{6,2},{7,3},{8,12},{9,13},{10,... | collective-permute-start | bytes 491528 | tf_op jit(solution)/shard_map/ppermute | solution.py:22
  91.0 4.3 %collective-permute-start.11 = (f32[64,256]{1,0:T(8,128)S(1)}, f32[64,256]{1,0:T(8,128)S(1)}, u32[]{:S(2)}, u32[]{:S(2)}) collective-permute-start(f32[64,256]{1,0:T(8,128)S(1)} %slice_select_fusion.1), channel_id=1, source_target_pairs={{0,8},{1,9},{2,10},{3,11},{4,12},{5,13},{6,14},{7,15},{8,0},{9,1},... | collective-permute-start | bytes 196616 | tf_op jit(solution)/shard_map/ppermute | solution.py:22
  91.3 3.9 %collective-permute-start.12 = (bf16[64,256]{1,0:T(8,128)(2,1)S(1)}, bf16[64,256]{1,0:T(8,128)(2,1)S(1)}, u32[]{:S(2)}, u32[]{:S(2)}) collective-permute-start(bf16[64,256]{1,0:T(8,128)(2,1)S(1)} %pad_maximum_fusion.6), channel_id=1, source_target_pairs={{0,2},{1,3},{2,0},{3,1},{4,6},{5,7},{6,4},{7,5},{8,10},{9,11},{10,... | collective-permute-start | bytes 98312 | tf_op jit(solution)/shard_map/ppermute | solution.py:22
  96.5 6.5 %collective-permute-start.13 = (f32[64,640]{1,0:T(8,128)S(1)}, f32[64,640]{1,0:T(8,128)S(1)}, u32[]{:S(2)}, u32[]{:S(2)}) collective-permute-start(f32[64,640]{1,0:T(8,128)S(1)} %add.71), channel_id=1, source_target_pairs={{0,8},{1,9},{2,10},{3,11},{4,12},{5,13},{6,14},{7,15},{8,0},{9,1},... | collective-permute-start | bytes 491528 | tf_op jit(solution)/shard_map/ppermute | solution.py:22
  97.2 5.9 %collective-permute-start.15 = (bf16[64,512]{1,0:T(8,128)(2,1)S(1)}, bf16[64,512]{1,0:T(8,128)(2,1)S(1)}, u32[]{:S(2)}, u32[]{:S(2)}) collective-permute-start(bf16[64,512]{1,0:T(8,128)(2,1)S(1)} %pad_maximum_fusion.5), channel_id=1, source_target_pairs={{0,4},{1,5},{2,6},{3,7},{4,0},{5,1},{6,2},{7,3},{8,12},{9,13},{10,... | collective-permute-start | bytes 196616 | tf_op jit(solution)/shard_map/ppermute | solution.py:22
  99.1 3.9 %collective-permute-start.14 = (f32[64,128]{1,0:T(8,128)S(1)}, f32[64,128]{1,0:T(8,128)S(1)}, u32[]{:S(2)}, u32[]{:S(2)}) collective-permute-start(f32[64,128]{1,0:T(8,128)S(1)} %slice_select_fusion.7), channel_id=1, source_target_pairs={{0,2},{1,3},{2,0},{3,1},{4,6},{5,7},{6,4},{7,5},{8,10},{9,11},{10,... | collective-permute-start | bytes 98312 | tf_op jit(solution)/shard_map/ppermute | solution.py:22
  103.1 4.1 %collective-permute-start.17 = (bf16[64,1024]{1,0:T(8,128)(2,1)S(1)}, bf16[64,1024]{1,0:T(8,128)(2,1)S(1)}, u32[]{:S(2)}, u32[]{:S(2)}) collective-permute-start(bf16[64,1024]{1,0:T(8,128)(2,1)S(1)} %pad_maximum_fusion.1), channel_id=1, source_target_pairs={{0,1},{1,0},{2,3},{3,2},{4,5},{5,4},{6,7},{7,6},{8,9},{9,8},{10,11... | collective-permute-start | bytes 393224 | tf_op jit(solution)/shard_map/ppermute | solution.py:22
  103.2 2.0 %copy-start.1 = (bf16[16,80,1408]{2,1,0:T(8,128)(2,1)S(1)}, bf16[16,80,1408]{2,1,0:T(8,128)(2,1)}, u32[]{:S(2)}) copy-start(bf16[16,80,1408]{2,1,0:T(8,128)(2,1)} %copy-done) | copy-start | bytes 10813444
  106.7 1.5 %collective-permute-start.16 = (bf16[64,1024]{1,0:T(8,128)(2,1)S(1)}, bf16[64,1024]{1,0:T(8,128)(2,1)S(1)}, u32[]{:S(2)}, u32[]{:S(2)}) collective-permute-start(bf16[64,1024]{1,0:T(8,128)(2,1)S(1)} %get-tuple-element.78.mine), channel_id=1, source_target_pairs={{0,1},{1,0},{2,3},{3,2},{4,5},{5,4},{6,7},{7,6},{8,9},{9,8},{10,11... | collective-permute-start | bytes 393224 | tf_op jit(solution)/shard_map/ppermute | solution.py:22
  110.0 12.4 %collective-permute-start.18 = (s16[64,1280]{1,0:T(8,128)(2,1)S(1)}, s16[64,1280]{1,0:T(8,128)(2,1)S(1)}, u32[]{:S(2)}, u32[]{:S(2)}) collective-permute-start(s16[64,1280]{1,0:T(8,128)(2,1)S(1)} %get-tuple-element.82), channel_id=1, source_target_pairs={{0,16},{1,17},{2,18},{3,19},{4,20},{5,21},{6,22},{7,23},{8,24},{9,... | collective-permute-start | bytes 491528 | tf_op jit(solution)/shard_map/ppermute | solution.py:22
  111.6 10.7 %collective-permute-start.19 = (f32[64,128]{1,0:T(8,128)S(1)}, f32[64,128]{1,0:T(8,128)S(1)}, u32[]{:S(2)}, u32[]{:S(2)}) collective-permute-start(f32[64,128]{1,0:T(8,128)S(1)} %get-tuple-element.83.beside), channel_id=1, source_target_pairs={{0,16},{1,17},{2,18},{3,19},{4,20},{5,21},{6,22},{7,23},{8,24},{9,... | collective-permute-start | bytes 98312 | tf_op jit(solution)/shard_map/ppermute | solution.py:22
  124.5 1.5 %collective-permute-start.20 = (f32[64,640]{1,0:T(8,128)S(1)}, f32[64,640]{1,0:T(8,128)S(1)}, u32[]{:S(2)}, u32[]{:S(2)}) collective-permute-start(f32[64,640]{1,0:T(8,128)S(1)} %get-tuple-element.86), channel_id=1, source_target_pairs={{0,1},{1,0},{2,3},{3,2},{4,5},{5,4},{6,7},{7,6},{8,9},{9,8},{10,11... | collective-permute-start | bytes 491528 | tf_op jit(solution)/shard_map/ppermute | solution.py:22
  126.1 4.3 %collective-permute-start.21 = (f32[64,192]{1,0:T(8,128)S(1)}, f32[64,192]{1,0:T(8,128)S(1)}, u32[]{:S(2)}, u32[]{:S(2)}) collective-permute-start(f32[64,192]{1,0:T(8,128)S(1)} %get-tuple-element.98), channel_id=1, source_target_pairs={{0,2},{1,3},{2,0},{3,1},{4,6},{5,7},{6,4},{7,5},{8,10},{9,11},{10,... | collective-permute-start | bytes 147464 | tf_op jit(solution)/shard_map/ppermute | solution.py:22
  127.2 5.0 %collective-permute-start.22 = (f32[64,192]{1,0:T(8,128)S(1)}, f32[64,192]{1,0:T(8,128)S(1)}, u32[]{:S(2)}, u32[]{:S(2)}) collective-permute-start(f32[64,192]{1,0:T(8,128)S(1)} %get-tuple-element.100), channel_id=1, source_target_pairs={{0,4},{1,5},{2,6},{3,7},{4,0},{5,1},{6,2},{7,3},{8,12},{9,13},{10,... | collective-permute-start | bytes 147464 | tf_op jit(solution)/shard_map/ppermute | solution.py:22
  127.7 5.2 %collective-permute-start.23 = (f32[64,192]{1,0:T(8,128)S(1)}, f32[64,192]{1,0:T(8,128)S(1)}, u32[]{:S(2)}, u32[]{:S(2)}) collective-permute-start(f32[64,192]{1,0:T(8,128)S(1)} %get-tuple-element.99), channel_id=1, source_target_pairs={{0,6},{1,7},{2,4},{3,5},{4,2},{5,3},{6,0},{7,1},{8,14},{9,15},{10,... | collective-permute-start | bytes 147464 | tf_op jit(solution)/shard_map/ppermute | solution.py:22
  133.1 3.9 %collective-permute-start.24 = (f32[64,128]{1,0:T(8,128)S(1)}, f32[64,128]{1,0:T(8,128)S(1)}, u32[]{:S(2)}, u32[]{:S(2)}) collective-permute-start(f32[64,128]{1,0:T(8,128)S(1)} %pad_maximum_fusion.7), channel_id=1, source_target_pairs={{0,8},{1,9},{2,10},{3,11},{4,12},{5,13},{6,14},{7,15},{8,0},{9,1},... | collective-permute-start | bytes 98312 | tf_op jit(solution)/shard_map/ppermute | solution.py:22

commit v5 on v4

--- a/solution.py
+++ b/solution.py
@@ -253,7 +253,27 @@
     return (squares[:rank, :rank] + squares[rank:, rank:]) + (squares[:rank, rank:] + squares[rank:, :rank])
 
 
-def parcels_kernel(rna_0, rna_1, atac_0, atac_1, cell, gene, peak, out):
+def parcels_kernel(spot, rna_0, rna_1, atac_0, atac_1, cell, gene, peak, *refs):
+    links, out, copied, slots, sems = refs[:4], refs[4], refs[5:9], refs[9], refs[10]
+
+    @pl.when(pl.program_id(0) == 0)
+    def _():
+        copies = [pltpu.make_async_copy(link, to, sems.at[i]) for i, (link, to) in enumerate(zip(links, copied))]
+        for copy in copies:
+            copy.start()
+        for copy in copies:
+            copy.wait()
+        link_gene, link_peak, link_weight, link_count = copied
+        count = link_gene.shape[0]
+        lane = lax.broadcasted_iota(jnp.int32, slots.shape, 1) - spot[1] * count
+        row = lax.broadcasted_iota(jnp.int32, slots.shape, 0)
+        value = jnp.zeros(slots.shape, jnp.float32)
+        for s in range(count):
+            weight = jnp.where(s < link_count[0], link_weight[s], 0)
+            for r, entry in enumerate((link_gene[s], link_peak[s], weight)):
+                value = jnp.where((lane == s) & (row == r), entry.astype(jnp.float32), value)
+        slots[...] = value.astype(jnp.bfloat16)
+
     rank = cell.shape[0]
     cells = rna_0.shape[0]
     gene_width, peak_width = gene.shape[1], peak.shape[1]
@@ -272,6 +292,7 @@
             row = (2 * (j % 2) + s) * part
             out[j, cells:, s * width : s * width + gene_width] = gene_low[row : row + part]
             out[j, cells:, s * width + gene_width : (s + 1) * width] = peak_low[row : row + part]
+        out[j, cells:, 2 * width :] = slots[...]
 
 
 def encode(group):
@@ -286,11 +307,7 @@
     return least + (code.astype(jnp.int32).astype(jnp.float32) + (CODES + 1) / 2) * step
 
 
-def ahead_kernel(spot, gene, peak, *refs):
-    links, (codes, beside), copied, sems = refs[:4], refs[4:6], refs[6:10], refs[10]
-    copies = [pltpu.make_async_copy(link, to, sems.at[i]) for i, (link, to) in enumerate(zip(links, copied))]
-    for copy in copies:
-        copy.start()
+def codes_kernel(gene, peak, codes, bounds):
     rank, width = codes.shape
     gene_width = gene.shape[1]
     least, step = [], []
@@ -300,36 +317,20 @@
         codes[:, b * BLOCK : (b + 1) * BLOCK] = code
         least.append(low)
         step.append(per)
-    pad = jnp.zeros((rank, beside.shape[1] - 2 * len(least)), jnp.float32)
-    beside[:rank] = jnp.concatenate([*least, *step, pad], axis=1)
-    for copy in copies:
-        copy.wait()
-    link_gene, link_peak, link_weight, link_count = copied
-    slots = link_gene.shape[0]
-    shape = (beside.shape[0] - rank, beside.shape[1])
-    lane = lax.broadcasted_iota(jnp.int32, shape, 1) - spot[1] * slots
-    row = lax.broadcasted_iota(jnp.int32, shape, 0)
-    value = jnp.zeros(shape, jnp.float32)
-    for s in range(slots):
-        weight = jnp.where(s < link_count[0], link_weight[s], 0)
-        for r, entry in enumerate((link_gene[s], link_peak[s], weight)):
-            value = jnp.where((lane == s) & (row == r), entry.astype(jnp.float32), value)
-    beside[rank:] = value
-
-
-def ahead(spot, gene_factor, peak_factor, links):
-    rank = gene_factor.shape[0]
-    width = gene_factor.shape[1] + peak_factor.shape[1]
-    anywhere = pl.BlockSpec(memory_space=pl.ANY)
-    return pl.pallas_call(
-        ahead_kernel,
-        grid=(1,),
-        in_specs=[SMEM] + [pl.BlockSpec(f.shape, lambda i: (0, 0)) for f in (gene_factor, peak_factor)] + [anywhere] * 4,
-        out_specs=[VMEM, VMEM],
-        out_shape=(struct(rank, width, dtype=jnp.int16), struct(rank + rank // 8, 2 * rank)),
-        scratch_shapes=[pltpu.SMEM(link.shape, jnp.int32) for link in links] + [pltpu.SemaphoreType.DMA((4,))],
-        compiler_params=PARAMS,
-    )(spot, in_hbm(gene_factor), in_hbm(peak_factor), *links)
+    pad = jnp.zeros((rank, bounds.shape[1] - 2 * len(least)), jnp.float32)
+    bounds[...] = jnp.concatenate([*least, *step, pad], axis=1)
+
+
+def table_kernel(received_slots, bounds, out):
+    rank = bounds.shape[0]
+    out[:rank] = bounds[...]
+    slots = sum(received_slots[j].astype(jnp.float32) for j in range(received_slots.shape[0]))
+
+    def hot(row, size, value):
+        ids = lax.broadcasted_iota(jnp.int32, (size, slots.shape[1]), 0).astype(jnp.float32)
+        return jnp.where(slots[row : row + 1] == ids, value, 0.0).astype(jnp.bfloat16)
+
+    out[rank:] = across(hot(0, out.shape[0] - rank, slots[2:3]), hot(1, out.shape[1], 1.0))
 
 
 def twins_kernel(spot, gene, peak, codes, beside, out):
@@ -353,39 +354,7 @@
     return pltpu.with_memory_space_constraint(value, pltpu.HBM)
 
 
-def put_slots_kernel(mine, other, parcels_in, out, block, sems):
-    first = mine.shape[0] - block.shape[0] // 2
-    block[...] = jnp.concatenate([mine[first:], other[first:]], axis=0).astype(jnp.bfloat16)
-    half, rows, lanes = out.shape
-    copies = [
-        pltpu.make_async_copy(
-            block, out.at[j, rows - block.shape[0] : rows, lanes - block.shape[1] : lanes], sems.at[j]
-        )
-        for j in range(half)
-    ]
-    for copy in copies:
-        copy.start()
-    for copy in copies:
-        copy.wait()
-
-
-def put_slots(mine, other, parcels_value):
-    rank = mine.shape[1] // 2
-    return pl.pallas_call(
-        put_slots_kernel,
-        in_specs=[VMEM] * 3,
-        out_specs=VMEM,
-        out_shape=struct(*parcels_value.shape, dtype=parcels_value.dtype),
-        scratch_shapes=[
-            pltpu.VMEM((rank // 4, 2 * rank), jnp.bfloat16),
-            pltpu.SemaphoreType.DMA((parcels_value.shape[0],)),
-        ],
-        input_output_aliases={2: 0},
-        compiler_params=PARAMS,
-    )(mine, other, parcels_value)
-
-
-def parcels(rna_counts, atac_counts, cell_factor, gene_factor, peak_factor, half):
+def parcels(spot, rna_counts, atac_counts, cell_factor, gene_factor, peak_factor, links, half):
     cells = rna_counts.shape[0]
     rank = cell_factor.shape[0]
     gene_width, peak_width = gene_factor.shape[1], peak_factor.shape[1]
@@ -402,22 +371,31 @@
     return pl.pallas_call(
         parcels_kernel,
         grid=(steps,),
-        in_specs=[columns(gene_width, 0), columns(gene_width, 1), columns(peak_width, 0), columns(peak_width, 1)]
-        + [whole(a) for a in (cell_factor, gene_factor, peak_factor)],
+        in_specs=[SMEM, columns(gene_width, 0), columns(gene_width, 1), columns(peak_width, 0), columns(peak_width, 1)]
+        + [whole(a) for a in (cell_factor, gene_factor, peak_factor)]
+        + [pl.BlockSpec(memory_space=pl.ANY)] * 4,
         out_specs=pl.BlockSpec((each, rows, lanes), lambda i: (i, 0, 0)),
         out_shape=struct(half, rows, lanes, dtype=jnp.bfloat16),
+        scratch_shapes=[pltpu.SMEM(link.shape, jnp.int32) for link in links]
+        + [pltpu.VMEM((rank // 4, 2 * rank), jnp.bfloat16), pltpu.SemaphoreType.DMA((4,))],
         compiler_params=PARAMS,
-    )(*(in_hbm(a) for a in (rna_counts, rna_counts, atac_counts, atac_counts, cell_factor, gene_factor, peak_factor)))
-
-
-def first_sums_kernel(received, sums, gram):
-    half, cells, features = received.shape[0], received.shape[1] - sums.shape[0] // 4, sums.shape[1]
-    rank = sums.shape[0]
-    high = jnp.concatenate([received[j, 0:cells, features : features + rank] for j in range(half)], axis=1)
-    rest = jnp.concatenate([received[j, 0:cells, features + rank :] for j in range(half)], axis=1)
-    counts = jnp.concatenate([received[j, 0:cells, 0:features] for j in range(half)], axis=0)
+    )(
+        spot,
+        *(in_hbm(a) for a in (rna_counts, rna_counts, atac_counts, atac_counts, cell_factor, gene_factor, peak_factor)),
+        *(in_hbm(a) for a in links[:-1]),
+        links[-1],
+    )
+
+
+def first_sums_kernel(order, received, sums, gram, state):
+    rank, features = sums.shape
+    cells = received.shape[1] - rank // 4
+    high = jnp.concatenate([received[j, 0:cells, features : features + rank] for j in order], axis=1)
+    rest = jnp.concatenate([received[j, 0:cells, features + rank :] for j in order], axis=1)
+    counts = jnp.concatenate([received[j, 0:cells, 0:features] for j in order], axis=0)
     sums[...] = jnp.dot(high, counts, preferred_element_type=jnp.float32)
     gram[...] = gram_of(high, rest)
+    state[...] = high.astype(jnp.float32) + rest.astype(jnp.float32)
 
 
 def finish_sums(sums_value, gram_value, sums, coded, beside):
@@ -435,24 +413,15 @@
 
 
 def first_links_kernel(
-    link_scale, widths, spot, mine, other, sums_in, gram, sums, coded, beside, table, table_sem, table_smem
+    link_scale, widths, spot, mine, other, aside, aside_other, sums_in, gram, sums, coded, beside, table, sem, table_smem
 ):
     half = mine.shape[0]
     rank, features = sums_in.shape
     gene_width, peak_width = widths
     gene_blocks, peak_blocks = gene_width // BLOCK, peak_width // BLOCK
     width = gene_width + peak_width
-    slots = sum(mine[j, :, 2 * width :].astype(jnp.float32) for j in range(half))
-
-    def hot(row, size, value):
-        ids = lax.broadcasted_iota(jnp.int32, (size, slots.shape[1]), 0).astype(jnp.float32)
-        return jnp.where(slots[row : row + 1] == ids, value, 0.0).astype(jnp.bfloat16)
-
-    table[...] = sum(
-        across(hot(row, table.shape[0], slots[row + 2 : row + 3]), hot(row + 1, table.shape[1], 1.0))
-        for row in (0, slots.shape[0] // 2)
-    )
-    copy = pltpu.make_async_copy(table, table_smem, table_sem)
+    table[...] = aside[rank:] + aside_other[rank:]
+    copy = pltpu.make_async_copy(table, table_smem, sem)
     copy.start()
     copy.wait()
     side, place, core = spot[0], spot[1], spot[2]
@@ -486,21 +455,39 @@
     finish_sums(sums_in[...] + link_scale * links, gram[...], sums, coded, beside)
 
 
+def gram_rows(gram, lanes):
+    rank = gram.shape[0]
+    rows = rank * rank // lanes
+    return jnp.concatenate([gram[b * rows : (b + 1) * rows] for b in range(rank // rows)], axis=1)
+
+
+def gram_back(rows_value, rank):
+    return jnp.concatenate(
+        [rows_value[:, b * rank : (b + 1) * rank] for b in range(rows_value.shape[1] // rank)], axis=0
+    )
+
+
 def next_sums_kernel(
-    link_scale, widths, orders, spot, table, mine, other, received, to_gene, genes, sums, coded, beside
+    link_scale, widths, orders, spot, table, mine, other, state, received, to_gene, genes, sums, coded, beside, state_out, own
 ):
     half = received.shape[0]
     rank, features = sums.shape
-    cells = mine.shape[1] * 2 // (2 * half)
+    cells = own.shape[1]
     gene_width, peak_width = widths
     gene_blocks, peak_blocks = gene_width // BLOCK, peak_width // BLOCK
     side, place, core = spot[0], spot[1], spot[2]
     first = core == 0
-    left, right = mine[...], other[...]
-    even, odd = jnp.where(first, left, right), jnp.where(first, right, left)
-    kept = half // 2 * cells
-    high = jnp.concatenate([even[:, :kept], odd[:, :kept]], axis=1)
-    rest = jnp.concatenate([even[:, kept:], odd[:, kept:]], axis=1)
+    old = state[...]
+    left, right = mine[:rank], other[:rank]
+    products = jnp.concatenate([jnp.where(first, left, right), jnp.where(first, right, left)], axis=1)
+    new = old * products / (exact(gram_back(mine[rank:], rank), old) + EPSILON)
+    state_out[...] = new
+    mine_now = new[:, :cells]
+    for position in range(1, half):
+        at = position * cells
+        mine_now = jnp.where(place == orders[0][position], new[:, at : at + cells], mine_now)
+    own[...] = mine_now
+    high, rest = halved(new)
     counts = jnp.concatenate([received[j, 0:cells, 0:features] for j in orders[0]], axis=0)
     products = jnp.dot(high, counts, preferred_element_type=jnp.float32)
     total = [None] * (2 * peak_blocks)
@@ -548,9 +535,8 @@
     split = half // 2 * cells
     left, right = cell_sums[:, :split], cell_sums[:, split:]
     for ref, value in ((kept, jnp.where(first, left, right)), (sent, jnp.where(first, right, left))):
-        ref[:, :split] = value
-        ref[:, split : split + rank] = gram_features
-        ref[:, split + rank :] = jnp.zeros((rank, ref.shape[1] - split - rank), jnp.float32)
+        ref[:rank] = value
+        ref[rank:] = gram_rows(gram_features, split)
 
     def own(at, width):
         return jnp.where(side == 0, new[:, at : at + width], new[:, at + width : at + 2 * width])
@@ -583,30 +569,20 @@
         links_sent[:, at : at + gene_width] = jnp.where(first, pair[1], pair[0])
 
 
-def cells_kernel(order, spot, totals, received_cells, pair, own):
-    rank = totals.shape[0]
-    cells = own.shape[1]
-    kept = cells * len(order) // 2
-    place, core = spot[1], spot[2]
-    first = core == 0
-
-    def state(j):
-        terms = received_cells[j].astype(jnp.float32)
-        return terms[:, :rank] + terms[:, rank:]
-
-    old = jnp.concatenate(
-        [
-            jnp.where(first, state(order[s]), state(order[s + len(order) // 2]))
-            for s in range(len(order) // 2)
-        ],
-        axis=1,
-    )
-    new = old * totals[:, :kept] / (exact(totals[:, kept : kept + rank], old) + EPSILON)
-    pair[...] = jnp.concatenate(halved(new), axis=1)
-    mine = new[:, :cells]
-    for s in range(1, len(order) // 2):
-        mine = jnp.where(place // 2 == order[s] // 2, new[:, s * cells : (s + 1) * cells], mine)
-    own[...] = mine
+def last_cells_kernel(spot, mine, other, old, out):
+    rank, cells = out.shape
+    totals = mine[:rank] + other[:rank]
+    gram = mine[rank:] + other[rank:]
+    lanes = totals.shape[1]
+    rows = rank * rank // (4 * lanes)
+    gram = jnp.concatenate(
+        [gram[i * rows : (i + 1) * rows, b * rank : (b + 1) * rank] for i in range(4) for b in range(lanes // rank)],
+        axis=0,
+    )
+    own = totals[:, :cells]
+    for position in range(1, lanes // cells):
+        own = jnp.where(spot[3] == position, totals[:, position * cells : (position + 1) * cells], own)
+    out[...] = old[...] * own / (exact(gram, old[...]) + EPSILON)
 
 
 def shards_blocks(
@@ -624,7 +600,12 @@
     half = count // 2
     me = lax.axis_index(AXIS)
     side, place, core = me // half, me % half, me % 2
-    spot = jnp.stack([side, place, core]).astype(jnp.int32)
+    chip_bits = bits_below(half)[1:]
+    cell_bits, link_bits, gene_bits = (turned(chip_bits, i % len(chip_bits)) for i in range(3))
+    tail = sum(
+        jnp.where((me & bit) != 0, 1 << i, 0) for i, bit in enumerate(reversed(cell_bits[2:]))
+    )
+    spot = jnp.stack([side, place, core, tail]).astype(jnp.int32)
     rank, cells = cell_factor.shape
     gene_width, peak_width = gene_factor.shape[1], peak_factor.shape[1]
     widths = (gene_width, peak_width)
@@ -632,39 +613,45 @@
     features = 2 * width
     link_scale = cells * count / 4.0
     table_shape = (rna_counts.shape[1] // BLOCK, atac_counts.shape[1] // BLOCK)
-    chip_bits = bits_below(half)[1:]
-    cell_bits, link_bits, gene_bits = (turned(chip_bits, i % len(chip_bits)) for i in range(3))
     cell_order = layout([1] + cell_bits)
     link_order = layout([1] + link_bits)
     gene_order = layout([1] + gene_bits[::-1])
 
-    codes, aside = ahead(spot, gene_factor, peak_factor, (link_gene, link_peak, link_weight, link_count))
+    links = (link_gene, link_peak, link_weight, link_count)
+    sent = parcels(spot, rna_counts, atac_counts, cell_factor, gene_factor, peak_factor, links, half)
+    halves = [list(range(half)), list(range(half, count))]
+    received = lax.all_to_all(sent, AXIS, 0, 0, axis_index_groups=halves, tiled=True)
+    rows_other = flip(received[:, cells:, :features], 1)
+    received = pltpu.with_memory_space_constraint(received, pltpu.VMEM)
+    codes, bounds = pl.pallas_call(
+        codes_kernel,
+        in_specs=[VMEM] * 2,
+        out_specs=[VMEM] * 2,
+        out_shape=(struct(rank, width, dtype=jnp.int16), struct(rank, 2 * rank)),
+        compiler_params=PARAMS,
+    )(gene_factor, peak_factor)
+    rows = rank // 4
+    aside = pl.pallas_call(
+        table_kernel,
+        grid=(1,),
+        in_specs=[
+            pl.BlockSpec((half, rows, 2 * rank), lambda i: (0, cells // rows, features // (2 * rank))),
+            VMEM,
+        ],
+        out_specs=VMEM,
+        out_shape=struct(rank + table_shape[0], table_shape[1]),
+        compiler_params=PARAMS,
+    )(received, bounds)
     aside_other = flip(aside, half)
     codes_other = flip(codes, half)
-    sent = parcels(rna_counts, atac_counts, cell_factor, gene_factor, peak_factor, half)
-    sent = put_slots(aside, aside_other, sent)
-    sent, codes_other = lax.optimization_barrier((sent, codes_other))
-    halves = [list(range(half)), list(range(half, count))]
-    received = lax.all_to_all(sent, AXIS, 0, 0, axis_index_groups=halves, tiled=True)
-    factors = pl.pallas_call(
-        twins_kernel,
-        in_specs=[SMEM] + [VMEM] * 4,
-        out_specs=VMEM,
-        out_shape=struct(rank, features),
-        compiler_params=PARAMS,
-    )(spot, gene_factor, peak_factor, codes_other, aside_other)
-
     sums_shapes = (struct(rank, features), struct(rank, features, dtype=jnp.int16), struct(rank, 2 * rank))
-    rows_other = flip(received[:, cells:, :features], 1)
-    received = pltpu.with_memory_space_constraint(received, pltpu.VMEM)
-    sums, gram = pl.pallas_call(
-        first_sums_kernel,
+    sums, gram, state = pl.pallas_call(
+        functools.partial(first_sums_kernel, cell_order),
         in_specs=[VMEM],
-        out_specs=[VMEM] * 2,
-        out_shape=(struct(rank, features), struct(rank, rank)),
+        out_specs=[VMEM] * 3,
+        out_shape=(struct(rank, features), struct(rank, rank), struct(rank, half * cells)),
         compiler_params=PARAMS,
     )(received)
-    rows = rank // 4
     sums, coded, beside, link_table = pl.pallas_call(
         functools.partial(first_links_kernel, link_scale, widths),
         grid=(1,),
@@ -674,20 +661,30 @@
             VMEM,
             VMEM,
             VMEM,
+            VMEM,
+            VMEM,
         ],
         out_specs=[VMEM] * 4,
         out_shape=(*sums_shapes, struct(*table_shape)),
         scratch_shapes=[pltpu.SemaphoreType.DMA, pltpu.SMEM(table_shape, jnp.float32)],
         compiler_params=PARAMS,
-    )(spot, received, rows_other, sums, gram)
+    )(spot, received, rows_other, aside, aside_other, sums, gram)
+
+    beside, codes_other = lax.optimization_barrier((beside, codes_other))
+    factors = pl.pallas_call(
+        twins_kernel,
+        in_specs=[SMEM] + [VMEM] * 4,
+        out_specs=VMEM,
+        out_shape=struct(rank, features),
+        compiler_params=PARAMS,
+    )(spot, gene_factor, peak_factor, codes_other, aside_other)
 
     split = half // 2 * cells
     for sweep_index in range(ROUNDS):
         last = sweep_index == ROUNDS - 1
         beside_other = flip(beside, half)
         other = flip(coded, half)
-        lanes = -(-(split + rank) // BLOCK) * BLOCK
-        outs = [struct(rank, lanes)] * 2
+        outs = [struct(rank + rank * rank // split, split)] * 2
         if last:
             outs += [struct(rank, gene_width), struct(rank, peak_width)]
         else:
@@ -703,32 +700,31 @@
         if last:
             gene_out, peak_out = outs
             totals = kept + flip(sent, 1)
-            cell_sums, gram_features = totals[:, :split], totals[:, split : split + rank]
             first, second = cell_bits[:2]
-            quarters = jnp.split(cell_sums, 4, axis=1)
+            quarters = jnp.split(totals[:rank], 4, axis=1)
+            gram_part = jnp.concatenate(jnp.split(totals[rank:], 4, axis=1), axis=0)
             is_first, is_second = (me & first) != 0, (me & second) != 0
 
             def quarter(flip_first, flip_second):
                 low, high = (
                     jnp.where(is_second ^ flip_second, quarters[2 * i + 1], quarters[2 * i]) for i in range(2)
                 )
-                return jnp.where(is_first ^ flip_first, high, low)
-
-            leaving = [
-                jnp.concatenate([quarter(*which), gram_features], axis=1)
-                for which in ((True, False), (False, True), (True, True))
+                return jnp.concatenate([jnp.where(is_first ^ flip_first, high, low), gram_part], axis=0)
+
+            got = [
+                flip(quarter(*which), bit)
+                for which, bit in (((True, False), first), ((False, True), second), ((True, True), first | second))
             ]
-            got = [flip(value, bit) for value, bit in zip(leaving, (first, second, first | second))]
-            size = quarters[0].shape[1]
-            cell_sums = quarter(False, False) + (got[0][:, :size] + got[1][:, :size] + got[2][:, :size])
-            gram_features = gram_features + (got[0][:, size:] + got[1][:, size:] + got[2][:, size:])
-            for bit in cell_bits[2:]:
-                left, right = jnp.split(cell_sums, 2, axis=1)
-                clear = (me & bit) == 0
-                got = flip(jnp.concatenate([jnp.where(clear, right, left), gram_features], axis=1), bit)
-                cell_sums = jnp.where(clear, left, right) + got[:, : left.shape[1]]
-                gram_features = gram_features + got[:, left.shape[1] :]
-            cell_out = own_cells * cell_sums / (exact(gram_features, own_cells) + EPSILON)
+            totals = quarter(False, False) + (got[0] + got[1] + got[2])
+            for bit in cell_bits[2:-1]:
+                totals = totals + flip(totals, bit)
+            cell_out = pl.pallas_call(
+                last_cells_kernel,
+                in_specs=[SMEM] + [VMEM] * 3,
+                out_specs=VMEM,
+                out_shape=struct(rank, cells),
+                compiler_params=PARAMS,
+            )(spot, totals, flip(totals, cell_bits[-1]), own_cells)
             return cell_out, gene_out, peak_out
         factors, links_kept, links_sent, genes = outs
         totals = kept + flip(sent, 1)
@@ -743,26 +739,14 @@
             totals = totals + got[0]
             to_gene = staying + got[1]
             genes = jnp.concatenate(in_order(gene_bit, genes, got[2]), axis=1)
-        pair, own_cells = pl.pallas_call(
-            functools.partial(cells_kernel, cell_order),
-            grid=(1,),
-            in_specs=[
-                SMEM,
-                VMEM,
-                pl.BlockSpec((half, cells, 2 * rank), lambda i: (0, 0, features // (2 * rank))),
-            ],
-            out_specs=[VMEM] * 2,
-            out_shape=(struct(rank, 2 * split, dtype=jnp.bfloat16), struct(rank, cells)),
+        genes = jnp.concatenate(in_order(1, genes, flip(genes, 1)), axis=1)
+        sums, coded, beside, state, own_cells = pl.pallas_call(
+            functools.partial(next_sums_kernel, link_scale, widths, (cell_order, gene_order)),
+            in_specs=[SMEM] * 2 + [VMEM] * 6,
+            out_specs=[VMEM] * 5,
+            out_shape=(*sums_shapes, struct(rank, half * cells), struct(rank, cells)),
             compiler_params=PARAMS,
-        )(spot, totals, received)
-        genes = jnp.concatenate(in_order(1, genes, flip(genes, 1)), axis=1)
-        sums, coded, beside = pl.pallas_call(
-            functools.partial(next_sums_kernel, link_scale, widths, (cell_order, gene_order)),
-            in_specs=[SMEM] * 2 + [VMEM] * 5,
-            out_specs=[VMEM] * 3,
-            out_shape=sums_shapes,
-            compiler_params=PARAMS,
-        )(spot, link_table, pair, flip(pair, 1), received, to_gene, genes)
+        )(spot, link_table, totals, flip(totals, 1), state, received, to_gene, genes)
 
 
 def shards(rna_counts, atac_counts, cell_factor, gene_factor, peak_factor, link_gene, *links):
@@ -771,7 +755,7 @@
     gene_width, peak_width = gene_factor.shape[1], peak_factor.shape[1]
     features = 2 * (gene_width + peak_width)
     in_blocks = (
-        half % 8 == 0
+        half % 16 == 0
         and rank == cells
         and 2 * rank == BLOCK
         and gene_width % BLOCK == 0
@@ -779,6 +763,7 @@
         and 2 * (features // BLOCK) <= rank
         and half * link_gene.shape[0] <= 2 * rank
         and rank % 64 == 0
+        and atac_counts.shape[1] // BLOCK == 2 * rank
         and max(rna_counts.shape[1], atac_counts.shape[1]) // BLOCK <= 256
     )
     run = shards_blocks if in_blocks else shards_any

time: 138 us -> 139 us (level)
  waiting for transfers between devices: 44.3 us -> 46.5 us
  blocking collectives: 47.8 us -> 49.8 us
  local copies, waits for them, and re-layouts: 4.04 us -> 2.11 us
    ppermute x25, waiting for transfers between devices: 44.3 us -> 46.5 us  [flip(): return lax.ppermute(value, AXIS, [(i, i ^ bit) for i in range(count)])]
    all_to_all x1, blocking collectives: 47.8 us -> 49.8 us  [shards_blocks(): lax.all_to_all(sent, AXIS, 0, 0, axis_index_groups=halves, tiled=True)]
    unnamed x14, local copies, waits for them, and re-layouts: 4 us -> 2.06 us
  transfers between devices with their start and end apart: 25 -> 25, of which waited for: 17 -> 18; matrix products, arithmetic and copies ran while one was open for 0% -> 0% of each run, Pallas kernels for 4% -> 1%
where the time goes in v5:
time: 139 us
  blocking collectives  49.8 us (36%)
  waiting for transfers between devices  46.5 us (33%)
  starting transfers between devices  20.8 us (15%)
  Pallas kernels  17.3 us (12%)
  local copies, waits for them, and re-layouts  2.11 us (2%)
  between operations  1.66 us (1%)
    all_to_all x1, blocking collectives, shards_blocks(): lax.all_to_all(sent, AXIS, 0, 0, axis_index_groups=halves, tiled=True)  49.8 us
    ppermute x25, waiting for transfers between devices, flip(): return lax.ppermute(value, AXIS, [(i, i ^ bit) for i in range(count)])  46.5 us
    ppermute x25, starting transfers between devices, flip(): return lax.ppermute(value, AXIS, [(i, i ^ bit) for i in range(count)])  20.8 us
    pallas_call x2, Pallas kernels, shards_blocks(): pl.pallas_call(functools.partial(update_kernel, last, widths, (cell_order...  5.02 us
    pallas_call x1, Pallas kernels, parcels(): pl.pallas_call(parcels_kernel, grid=(steps,), in_specs=[SMEM, columns(gen...  3.53 us
    pallas_call x1, Pallas kernels, shards_blocks(): pl.pallas_call(functools.partial(next_sums_kernel, link_scale, widths, (c...  3.02 us
  transfers between devices with their start and end apart: 25, of which 18 were waited for; matrix products, arithmetic and copies ran while one was open for 0% of the time, Pallas kernels for 1%

profile of v5, /device:TPU:0, one launch (start us, length us, event | category | flops | bytes accessed | tf_op | source)
XLA Modules:
  0.0 138.6 jit_solution(6581485325261748028)
XLA Ops:
  1.4 3.5 %shard_map.112 = bf16[16,80,1408]{2,1,0:T(8,128)(2,1)S(1)} custom-call(s32[4]{0:T(128)S(1)} %pad_add_fusion.spot, bf16[64,4096]{1,0:T(8,128)(2,1)} %rna_1.1, bf16[64,4096]{1,0:T(8,128)(2,1)} %rna_1.1, bf16[64,16384]{1,0:T(8,128)(2,1)} %atac_1.1, bf16[64,16384]{1,0:T(8,128)(2,1)} %atac_1.1, f32[64,64]{1,0:T(8,128)} %cell.1, f32[64,128]{1,0:T(8,128)} %gene.5, ...), custom_call_target="tpu_custom_call" | custom-call | tf_op jit(solution)/shard_map/pallas_call | solution.py:371
  4.9 49.8 %all_to_all.5.received_slots.received.mine = bf16[16,80,1408]{2,1,0:T(8,128)(2,1)S(1)} all-to-all(bf16[16,80,1408]{2,1,0:T(8,128)(2,1)S(1)} %shard_map.112), channel_id=1, replica_groups={{0,1,2,3,4,5,6,7,8,9,10,11,12,13,14,15},{16,17,18,19,20,21,22,23,24,25,..., dimensions={0} | all-to-all | bytes 7208960 | tf_op jit(solution)/shard_map/all_to_all | solution.py:623
  55.2 2.6 %collective-permute-start.1 = (f32[96,128]{1,0:T(8,128)S(1)}, f32[96,128]{1,0:T(8,128)S(1)}, u32[]{:S(2)}, u32[]{:S(2)}) collective-permute-start(f32[96,128]{1,0:T(8,128)S(1)} %shard_map.114.aside), channel_id=1, source_target_pairs={{0,16},{1,17},{2,18},{3,19},{4,20},{5,21},{6,22},{7,23},{8,24},{9,... | collective-permute-start | bytes 147464 | tf_op jit(solution)/shard_map/ppermute | solution.py:22
  57.8 0.8 shard_map.115
  58.7 2.6 %collective-permute-done.1.aside_other.beside = f32[96,128]{1,0:T(8,128)S(1)} collective-permute-done((f32[96,128]{1,0:T(8,128)S(1)}, f32[96,128]{1,0:T(8,128)S(1)}, u32[]{:S(2)}, u32[]{:S(2)}) %collective-permute-start.1) | collective-permute-done | bytes 49184 | tf_op jit(solution)/shard_map/ppermute | solution.py:22
  61.3 2.4 %shard_map.116 = (f32[64,1280]{1,0:T(8,128)S(1)}, s16[64,1280]{1,0:T(8,128)(2,1)S(1)}, f32[64,128]{1,0:T(8,128)S(1)}, f32[32,128]{1,0:T(8,128)S(1)}) custom-call(s32[4]{0:T(128)S(1)} %pad_add_fusion.spot, bf16[16,80,1408]{2,1,0:T(8,128)(2,1)S(1)} %all_to_all.5.received_slots.received.mine, bf16[16,16,1280]{2,1,0:T(8,128)(2,1)S(1)} %collective-permute-done.other, ...), custom_call_target="tpu_custom_call" | custom-call | tf_op jit(solution)/shard_map/pallas_call | solution.py:655
  63.8 1.7 %collective-permute-start.2 = (s16[64,1280]{1,0:T(8,128)(2,1)S(1)}, s16[64,1280]{1,0:T(8,128)(2,1)S(1)}, u32[]{:S(2)}, u32[]{:S(2)}) collective-permute-start(s16[64,1280]{1,0:T(8,128)(2,1)S(1)} %get-tuple-element.51), channel_id=1, source_target_pairs={{0,16},{1,17},{2,18},{3,19},{4,20},{5,21},{6,22},{7,23},{8,24},{9,... | collective-permute-start | bytes 491528 | tf_op jit(solution)/shard_map/ppermute | solution.py:22
  65.5 1.3 collective-permute-start.3
  66.7 9.7 %collective-permute-done.3.codes = s16[64,640]{1,0:T(8,128)(2,1)S(1)} collective-permute-done((s16[64,640]{1,0:T(8,128)(2,1)S(1)}, s16[64,640]{1,0:T(8,128)(2,1)S(1)}, u32[]{:S(2)}, u32[]{:S(2)}) %collective-permute-start.3) | collective-permute-done | bytes 81952 | tf_op jit(solution)/shard_map/ppermute | solution.py:22
  77.2 4.1 %collective-permute-done.4.beside_other = f32[64,128]{1,0:T(8,128)S(1)} collective-permute-done((f32[64,128]{1,0:T(8,128)S(1)}, f32[64,128]{1,0:T(8,128)S(1)}, u32[]{:S(2)}, u32[]{:S(2)}) %collective-permute-start.4) | collective-permute-done | bytes 32800 | tf_op jit(solution)/shard_map/ppermute | solution.py:22
  81.3 2.5 %shard_map.118 = (f32[72,512]{1,0:T(8,128)S(1)}, f32[72,512]{1,0:T(8,128)S(1)}, f32[64,1280]{1,0:T(8,128)S(1)}, f32[64,1024]{1,0:T(8,128)S(1)}, f32[64,1024]{1,0:T(8,128)S(1)}, /*index=5*/bf16[64,128]{1,0:T(8,128)(2,1)S(1)}) custom-call(s32[4]{0:T(128)S(1)} %pad_add_fusion.spot, f32[32,128]{1,0:T(8,128)S(1)} %get-tuple-element.49.table, ...), custom_call_target="tpu_custom_call" | custom-call | tf_op jit(solution)/shard_map/pallas_call | solution.py:693
  84.4 1.2 collective-permute-done.5
  86.6 3.5 %collective-permute-done.9 = bf16[64,128]{1,0:T(8,128)(2,1)S(1)} collective-permute-done((bf16[64,128]{1,0:T(8,128)(2,1)S(1)}, bf16[64,128]{1,0:T(8,128)(2,1)S(1)}, u32[]{:S(2)}, u32[]{:S(2)}) %collective-permute-start.9) | collective-permute-done | bytes 16416 | tf_op jit(solution)/shard_map/ppermute | solution.py:22
  90.1 1.3 collective-permute-done.8
  92.5 1.4 %collective-permute-start.12 = (bf16[64,256]{1,0:T(8,128)(2,1)S(1)}, bf16[64,256]{1,0:T(8,128)(2,1)S(1)}, u32[]{:S(2)}, u32[]{:S(2)}) collective-permute-start(bf16[64,256]{1,0:T(8,128)(2,1)S(1)} %pad_maximum_fusion.3), channel_id=1, source_target_pairs={{0,2},{1,3},{2,0},{3,1},{4,6},{5,7},{6,4},{7,5},{8,10},{9,11},{10,... | collective-permute-start | bytes 98312 | tf_op jit(solution)/shard_map/ppermute | solution.py:22
  94.0 2.5 %collective-permute-done.12 = bf16[64,256]{1,0:T(8,128)(2,1)S(1)} collective-permute-done((bf16[64,256]{1,0:T(8,128)(2,1)S(1)}, bf16[64,256]{1,0:T(8,128)(2,1)S(1)}, u32[]{:S(2)}, u32[]{:S(2)}) %collective-permute-start.12) | collective-permute-done | bytes 32800 | tf_op jit(solution)/shard_map/ppermute | solution.py:22
  97.1 1.1 collective-permute-start.13
  98.1 1.8 %collective-permute-start.15 = (bf16[64,512]{1,0:T(8,128)(2,1)S(1)}, bf16[64,512]{1,0:T(8,128)(2,1)S(1)}, u32[]{:S(2)}, u32[]{:S(2)}) collective-permute-start(bf16[64,512]{1,0:T(8,128)(2,1)S(1)} %pad_maximum_fusion.2), channel_id=1, source_target_pairs={{0,4},{1,5},{2,6},{3,7},{4,0},{5,1},{6,2},{7,3},{8,12},{9,13},{10,... | collective-permute-start | bytes 196616 | tf_op jit(solution)/shard_map/ppermute | solution.py:22
  100.0 1.4 %collective-permute-start.14 = (f32[64,128]{1,0:T(8,128)S(1)}, f32[64,128]{1,0:T(8,128)S(1)}, u32[]{:S(2)}, u32[]{:S(2)}) collective-permute-start(f32[64,128]{1,0:T(8,128)S(1)} %slice_select_fusion.6), channel_id=1, source_target_pairs={{0,2},{1,3},{2,0},{3,1},{4,6},{5,7},{6,4},{7,5},{8,10},{9,11},{10,... | collective-permute-start | bytes 98312 | tf_op jit(solution)/shard_map/ppermute | solution.py:22
  101.4 2.5 %collective-permute-done.14 = f32[64,128]{1,0:T(8,128)S(1)} collective-permute-done((f32[64,128]{1,0:T(8,128)S(1)}, f32[64,128]{1,0:T(8,128)S(1)}, u32[]{:S(2)}, u32[]{:S(2)}) %collective-permute-start.14) | collective-permute-done | bytes 32800 | tf_op jit(solution)/shard_map/ppermute | solution.py:22
  105.6 2.0 %copy-done.1 = bf16[16,80,1408]{2,1,0:T(8,128)(2,1)S(1)} copy-done((bf16[16,80,1408]{2,1,0:T(8,128)(2,1)S(1)}, bf16[16,80,1408]{2,1,0:T(8,128)(2,1)}, u32[]{:S(2)}) %copy-start.1) | copy-done | bytes 3604504
  107.6 3.0 %shard_map.119 = (f32[64,1280]{1,0:T(8,128)S(1)}, s16[64,1280]{1,0:T(8,128)(2,1)S(1)}, f32[64,128]{1,0:T(8,128)S(1)}, f32[64,1024]{1,0:T(8,128)}, f32[64,64]{1,0:T(8,128)S(1)}) custom-call(s32[4]{0:T(128)S(1)} %pad_add_fusion.spot, f32[32,128]{1,0:T(8,128)S(1)} %get-tuple-element.49.table, f32[72,512]{1,0:T(8,128)S(1)} %add.52.mine, ...), custom_call_target="tpu_custom_call" | custom-call | tf_op jit(solution)/shard_map/pallas_call | solution.py:743
  110.7 1.5 %collective-permute-start.18 = (s16[64,1280]{1,0:T(8,128)(2,1)S(1)}, s16[64,1280]{1,0:T(8,128)(2,1)S(1)}, u32[]{:S(2)}, u32[]{:S(2)}) collective-permute-start(s16[64,1280]{1,0:T(8,128)(2,1)S(1)} %get-tuple-element.81), channel_id=1, source_target_pairs={{0,16},{1,17},{2,18},{3,19},{4,20},{5,21},{6,22},{7,23},{8,24},{9,... | collective-permute-start | bytes 491528 | tf_op jit(solution)/shard_map/ppermute | solution.py:22
  112.1 1.5 %collective-permute-start.19 = (f32[64,128]{1,0:T(8,128)S(1)}, f32[64,128]{1,0:T(8,128)S(1)}, u32[]{:S(2)}, u32[]{:S(2)}) collective-permute-start(f32[64,128]{1,0:T(8,128)S(1)} %get-tuple-element.82.beside), channel_id=1, source_target_pairs={{0,16},{1,17},{2,18},{3,19},{4,20},{5,21},{6,22},{7,23},{8,24},{9,... | collective-permute-start | bytes 98312 | tf_op jit(solution)/shard_map/ppermute | solution.py:22
  113.6 9.3 %collective-permute-done.19.beside_other = f32[64,128]{1,0:T(8,128)S(1)} collective-permute-done((f32[64,128]{1,0:T(8,128)S(1)}, f32[64,128]{1,0:T(8,128)S(1)}, u32[]{:S(2)}, u32[]{:S(2)}) %collective-permute-start.19) | collective-permute-done | bytes 32800 | tf_op jit(solution)/shard_map/ppermute | solution.py:22
  122.9 2.6 %shard_map.120 = (f32[72,512]{1,0:T(8,128)S(1)}, f32[72,512]{1,0:T(8,128)S(1)}, f32[64,128]{1,0:T(8,128)}, f32[64,512]{1,0:T(8,128)}) custom-call(s32[4]{0:T(128)S(1)} %pad_add_fusion.spot, f32[32,128]{1,0:T(8,128)S(1)} %get-tuple-element.49.table, f32[64,1280]{1,0:T(8,128)S(1)} %get-tuple-element.80.sums, ...), custom_call_target="tpu_custom_call" | custom-call | tf_op jit(solution)/shard_map/pallas_call | solution.py:693
  125.5 1.3 collective-permute-done.20
  127.0 1.5 %collective-permute-start.23 = (f32[96,128]{1,0:T(8,128)S(1)}, f32[96,128]{1,0:T(8,128)S(1)}, u32[]{:S(2)}, u32[]{:S(2)}) collective-permute-start(f32[96,128]{1,0:T(8,128)S(1)} %constant_dynamic-update-slice_fusion.15), channel_id=1, source_target_pairs={{0,6},{1,7},{2,4},{3,5},{4,2},{5,3},{6,0},{7,1},{8,14},{9,15},{10,... | collective-permute-start | bytes 147464 | tf_op jit(solution)/shard_map/ppermute | solution.py:22
  128.9 1.6 %collective-permute-start.22 = (f32[96,128]{1,0:T(8,128)S(1)}, f32[96,128]{1,0:T(8,128)S(1)}, u32[]{:S(2)}, u32[]{:S(2)}) collective-permute-start(f32[96,128]{1,0:T(8,128)S(1)} %get-tuple-element.91), channel_id=1, source_target_pairs={{0,4},{1,5},{2,6},{3,7},{4,0},{5,1},{6,2},{7,3},{8,12},{9,13},{10,... | collective-permute-start | bytes 147464 | tf_op jit(solution)/shard_map/ppermute | solution.py:22
  130.5 1.7 %collective-permute-done.23 = f32[96,128]{1,0:T(8,128)S(1)} collective-permute-done((f32[96,128]{1,0:T(8,128)S(1)}, f32[96,128]{1,0:T(8,128)S(1)}, u32[]{:S(2)}, u32[]{:S(2)}) %collective-permute-start.23) | collective-permute-done | bytes 49184 | tf_op jit(solution)/shard_map/ppermute | solution.py:22
  133.1 4.1 %collective-permute-done.24.other = f32[96,128]{1,0:T(8,128)S(1)} collective-permute-done((f32[96,128]{1,0:T(8,128)S(1)}, f32[96,128]{1,0:T(8,128)S(1)}, u32[]{:S(2)}, u32[]{:S(2)}) %collective-permute-start.24) | collective-permute-done | bytes 49184 | tf_op jit(solution)/shard_map/ppermute | solution.py:22
  137.2 1.4 %shard_map.121 = f32[64,64]{1,0:T(8,128)} custom-call(s32[4]{0:T(128)S(1)} %pad_add_fusion.spot, f32[96,128]{1,0:T(8,128)S(1)} %add_add_fusion.mine, f32[96,128]{1,0:T(8,128)S(1)} %collective-permute-done.24.other, f32[64,64]{1,0:T(8,128)S(1)} %get-tuple-element.86.old), custom_call_target="tpu_custom_call" | custom-call | tf_op jit(solution)/shard_map/pallas_call | solution.py:721
  (71 shorter events, 7.6 us)
Async XLA Ops:
  4.9 49.9 %copy-start.2 = (f32[64,512]{1,0:T(8,128)S(1)}, f32[64,512]{1,0:T(8,128)}, u32[]{:S(2)}) copy-start(f32[64,512]{1,0:T(8,128)} %peak.5) | copy-start | bytes 393220
  4.9 49.9 %copy-start.3 = (f32[64,128]{1,0:T(8,128)S(1)}, f32[64,128]{1,0:T(8,128)}, u32[]{:S(2)}) copy-start(f32[64,128]{1,0:T(8,128)} %gene.5) | copy-start | bytes 98308
  54.7 26.6 %copy-start = (bf16[16,80,1408]{2,1,0:T(8,128)(2,1)}, bf16[16,80,1408]{2,1,0:T(8,128)(2,1)S(1)}, u32[]{:S(2)}) copy-start(bf16[16,80,1408]{2,1,0:T(8,128)(2,1)S(1)} %all_to_all.5.received_slots.received.mine) | copy-start | bytes 10813444
  54.8 6.6 %collective-permute-start = (bf16[16,16,1280]{2,1,0:T(8,128)(2,1)S(1)}, bf16[16,16,1280]{2,1,0:T(8,128)(2,1)S(1)}, u32[]{:S(2)}, u32[]{:S(2)}) collective-permute-start(bf16[16,16,1280]{2,1,0:T(8,128)(2,1)S(1)} %slice.14), channel_id=1, source_target_pairs={{0,1},{1,0},{2,3},{3,2},{4,5},{5,4},{6,7},{7,6},{8,9},{9,8},{10,11... | collective-permute-start | bytes 1966088 | tf_op jit(solution)/shard_map/ppermute | solution.py:22
  55.2 6.1 %collective-permute-start.1 = (f32[96,128]{1,0:T(8,128)S(1)}, f32[96,128]{1,0:T(8,128)S(1)}, u32[]{:S(2)}, u32[]{:S(2)}) collective-permute-start(f32[96,128]{1,0:T(8,128)S(1)} %shard_map.114.aside), channel_id=1, source_target_pairs={{0,16},{1,17},{2,18},{3,19},{4,20},{5,21},{6,22},{7,23},{8,24},{9,... | collective-permute-start | bytes 147464 | tf_op jit(solution)/shard_map/ppermute | solution.py:22
  63.8 17.6 %collective-permute-start.2 = (s16[64,1280]{1,0:T(8,128)(2,1)S(1)}, s16[64,1280]{1,0:T(8,128)(2,1)S(1)}, u32[]{:S(2)}, u32[]{:S(2)}) collective-permute-start(s16[64,1280]{1,0:T(8,128)(2,1)S(1)} %get-tuple-element.51), channel_id=1, source_target_pairs={{0,16},{1,17},{2,18},{3,19},{4,20},{5,21},{6,22},{7,23},{8,24},{9,... | collective-permute-start | bytes 491528 | tf_op jit(solution)/shard_map/ppermute | solution.py:22
  65.5 11.0 %collective-permute-start.3 = (s16[64,640]{1,0:T(8,128)(2,1)S(1)}, s16[64,640]{1,0:T(8,128)(2,1)S(1)}, u32[]{:S(2)}, u32[]{:S(2)}) collective-permute-start(s16[64,640]{1,0:T(8,128)(2,1)S(1)} %get-tuple-element.53), channel_id=1, source_target_pairs={{0,16},{1,17},{2,18},{3,19},{4,20},{5,21},{6,22},{7,23},{8,24},{9,... | collective-permute-start | bytes 245768 | tf_op jit(solution)/shard_map/ppermute | solution.py:22
  76.5 4.8 %collective-permute-start.4 = (f32[64,128]{1,0:T(8,128)S(1)}, f32[64,128]{1,0:T(8,128)S(1)}, u32[]{:S(2)}, u32[]{:S(2)}) collective-permute-start(f32[64,128]{1,0:T(8,128)S(1)} %get-tuple-element.54.beside), channel_id=1, source_target_pairs={{0,16},{1,17},{2,18},{3,19},{4,20},{5,21},{6,22},{7,23},{8,24},{9,... | collective-permute-start | bytes 98312 | tf_op jit(solution)/shard_map/ppermute | solution.py:22
  83.8 1.8 %collective-permute-start.6 = (f32[64,1024]{1,0:T(8,128)S(1)}, f32[64,1024]{1,0:T(8,128)S(1)}, u32[]{:S(2)}, u32[]{:S(2)}) collective-permute-start(f32[64,1024]{1,0:T(8,128)S(1)} %get-tuple-element.59), channel_id=1, source_target_pairs={{0,1},{1,0},{2,3},{3,2},{4,5},{5,4},{6,7},{7,6},{8,9},{9,8},{10,11... | collective-permute-start | bytes 786440 | tf_op jit(solution)/shard_map/ppermute | solution.py:22
  83.9 1.7 %collective-permute-start.5 = (f32[72,512]{1,0:T(8,128)S(1)}, f32[72,512]{1,0:T(8,128)S(1)}, u32[]{:S(2)}, u32[]{:S(2)}) collective-permute-start(f32[72,512]{1,0:T(8,128)S(1)} %get-tuple-element.57), channel_id=1, source_target_pairs={{0,1},{1,0},{2,3},{3,2},{4,5},{5,4},{6,7},{7,6},{8,9},{9,8},{10,11... | collective-permute-start | bytes 442376 | tf_op jit(solution)/shard_map/ppermute | solution.py:22
  85.7 6.0 %collective-permute-start.7 = (f32[72,512]{1,0:T(8,128)S(1)}, f32[72,512]{1,0:T(8,128)S(1)}, u32[]{:S(2)}, u32[]{:S(2)}) collective-permute-start(f32[72,512]{1,0:T(8,128)S(1)} %add.46), channel_id=1, source_target_pairs={{0,2},{1,3},{2,0},{3,1},{4,6},{5,7},{6,4},{7,5},{8,10},{9,11},{10,... | collective-permute-start | bytes 442376 | tf_op jit(solution)/shard_map/ppermute | solution.py:22
  85.8 5.6 %collective-permute-start.8 = (f32[64,512]{1,0:T(8,128)S(1)}, f32[64,512]{1,0:T(8,128)S(1)}, u32[]{:S(2)}, u32[]{:S(2)}) collective-permute-start(f32[64,512]{1,0:T(8,128)S(1)} %slice_select_fusion), channel_id=1, source_target_pairs={{0,4},{1,5},{2,6},{3,7},{4,0},{5,1},{6,2},{7,3},{8,12},{9,13},{10,... | collective-permute-start | bytes 393224 | tf_op jit(solution)/shard_map/ppermute | solution.py:22
  86.3 3.7 %collective-permute-start.9 = (bf16[64,128]{1,0:T(8,128)(2,1)S(1)}, bf16[64,128]{1,0:T(8,128)(2,1)S(1)}, u32[]{:S(2)}, u32[]{:S(2)}) collective-permute-start(bf16[64,128]{1,0:T(8,128)(2,1)S(1)} %get-tuple-element.63), channel_id=1, source_target_pairs={{0,8},{1,9},{2,10},{3,11},{4,12},{5,13},{6,14},{7,15},{8,0},{9,1},... | collective-permute-start | bytes 49160 | tf_op jit(solution)/shard_map/ppermute | solution.py:22
  91.8 5.2 %collective-permute-start.10 = (f32[72,512]{1,0:T(8,128)S(1)}, f32[72,512]{1,0:T(8,128)S(1)}, u32[]{:S(2)}, u32[]{:S(2)}) collective-permute-start(f32[72,512]{1,0:T(8,128)S(1)} %add.48), channel_id=1, source_target_pairs={{0,4},{1,5},{2,6},{3,7},{4,0},{5,1},{6,2},{7,3},{8,12},{9,13},{10,... | collective-permute-start | bytes 442376 | tf_op jit(solution)/shard_map/ppermute | solution.py:22
  92.0 4.4 %collective-permute-start.11 = (f32[64,256]{1,0:T(8,128)S(1)}, f32[64,256]{1,0:T(8,128)S(1)}, u32[]{:S(2)}, u32[]{:S(2)}) collective-permute-start(f32[64,256]{1,0:T(8,128)S(1)} %slice_select_fusion.1), channel_id=1, source_target_pairs={{0,8},{1,9},{2,10},{3,11},{4,12},{5,13},{6,14},{7,15},{8,0},{9,1},... | collective-permute-start | bytes 196616 | tf_op jit(solution)/shard_map/ppermute | solution.py:22
  92.5 3.9 %collective-permute-start.12 = (bf16[64,256]{1,0:T(8,128)(2,1)S(1)}, bf16[64,256]{1,0:T(8,128)(2,1)S(1)}, u32[]{:S(2)}, u32[]{:S(2)}) collective-permute-start(bf16[64,256]{1,0:T(8,128)(2,1)S(1)} %pad_maximum_fusion.3), channel_id=1, source_target_pairs={{0,2},{1,3},{2,0},{3,1},{4,6},{5,7},{6,4},{7,5},{8,10},{9,11},{10,... | collective-permute-start | bytes 98312 | tf_op jit(solution)/shard_map/ppermute | solution.py:22
  97.1 6.8 %collective-permute-start.13 = (f32[72,512]{1,0:T(8,128)S(1)}, f32[72,512]{1,0:T(8,128)S(1)}, u32[]{:S(2)}, u32[]{:S(2)}) collective-permute-start(f32[72,512]{1,0:T(8,128)S(1)} %add.50), channel_id=1, source_target_pairs={{0,8},{1,9},{2,10},{3,11},{4,12},{5,13},{6,14},{7,15},{8,0},{9,1},... | collective-permute-start | bytes 442376 | tf_op jit(solution)/shard_map/ppermute | solution.py:22
  98.1 5.8 %collective-permute-start.15 = (bf16[64,512]{1,0:T(8,128)(2,1)S(1)}, bf16[64,512]{1,0:T(8,128)(2,1)S(1)}, u32[]{:S(2)}, u32[]{:S(2)}) collective-permute-start(bf16[64,512]{1,0:T(8,128)(2,1)S(1)} %pad_maximum_fusion.2), channel_id=1, source_target_pairs={{0,4},{1,5},{2,6},{3,7},{4,0},{5,1},{6,2},{7,3},{8,12},{9,13},{10,... | collective-permute-start | bytes 196616 | tf_op jit(solution)/shard_map/ppermute | solution.py:22
  100.0 3.9 %collective-permute-start.14 = (f32[64,128]{1,0:T(8,128)S(1)}, f32[64,128]{1,0:T(8,128)S(1)}, u32[]{:S(2)}, u32[]{:S(2)}) collective-permute-start(f32[64,128]{1,0:T(8,128)S(1)} %slice_select_fusion.6), channel_id=1, source_target_pairs={{0,2},{1,3},{2,0},{3,1},{4,6},{5,7},{6,4},{7,5},{8,10},{9,11},{10,... | collective-permute-start | bytes 98312 | tf_op jit(solution)/shard_map/ppermute | solution.py:22
  103.9 1.4 %collective-permute-start.17 = (bf16[64,1024]{1,0:T(8,128)(2,1)S(1)}, bf16[64,1024]{1,0:T(8,128)(2,1)S(1)}, u32[]{:S(2)}, u32[]{:S(2)}) collective-permute-start(bf16[64,1024]{1,0:T(8,128)(2,1)S(1)} %pad_maximum_fusion.1), channel_id=1, source_target_pairs={{0,1},{1,0},{2,3},{3,2},{4,5},{5,4},{6,7},{7,6},{8,9},{9,8},{10,11... | collective-permute-start | bytes 393224 | tf_op jit(solution)/shard_map/ppermute | solution.py:22
  104.0 1.6 %collective-permute-start.16 = (f32[72,512]{1,0:T(8,128)S(1)}, f32[72,512]{1,0:T(8,128)S(1)}, u32[]{:S(2)}, u32[]{:S(2)}) collective-permute-start(f32[72,512]{1,0:T(8,128)S(1)} %add.52.mine), channel_id=1, source_target_pairs={{0,1},{1,0},{2,3},{3,2},{4,5},{5,4},{6,7},{7,6},{8,9},{9,8},{10,11... | collective-permute-start | bytes 442376 | tf_op jit(solution)/shard_map/ppermute | solution.py:22
  105.6 2.0 %copy-start.1 = (bf16[16,80,1408]{2,1,0:T(8,128)(2,1)S(1)}, bf16[16,80,1408]{2,1,0:T(8,128)(2,1)}, u32[]{:S(2)}) copy-start(bf16[16,80,1408]{2,1,0:T(8,128)(2,1)} %copy-done) | copy-start | bytes 10813444
  110.7 12.2 %collective-permute-start.18 = (s16[64,1280]{1,0:T(8,128)(2,1)S(1)}, s16[64,1280]{1,0:T(8,128)(2,1)S(1)}, u32[]{:S(2)}, u32[]{:S(2)}) collective-permute-start(s16[64,1280]{1,0:T(8,128)(2,1)S(1)} %get-tuple-element.81), channel_id=1, source_target_pairs={{0,16},{1,17},{2,18},{3,19},{4,20},{5,21},{6,22},{7,23},{8,24},{9,... | collective-permute-start | bytes 491528 | tf_op jit(solution)/shard_map/ppermute | solution.py:22
  112.1 10.7 %collective-permute-start.19 = (f32[64,128]{1,0:T(8,128)S(1)}, f32[64,128]{1,0:T(8,128)S(1)}, u32[]{:S(2)}, u32[]{:S(2)}) collective-permute-start(f32[64,128]{1,0:T(8,128)S(1)} %get-tuple-element.82.beside), channel_id=1, source_target_pairs={{0,16},{1,17},{2,18},{3,19},{4,20},{5,21},{6,22},{7,23},{8,24},{9,... | collective-permute-start | bytes 98312 | tf_op jit(solution)/shard_map/ppermute | solution.py:22
  125.4 1.4 collective-permute-start.20
  127.0 5.3 %collective-permute-start.23 = (f32[96,128]{1,0:T(8,128)S(1)}, f32[96,128]{1,0:T(8,128)S(1)}, u32[]{:S(2)}, u32[]{:S(2)}) collective-permute-start(f32[96,128]{1,0:T(8,128)S(1)} %constant_dynamic-update-slice_fusion.15), channel_id=1, source_target_pairs={{0,6},{1,7},{2,4},{3,5},{4,2},{5,3},{6,0},{7,1},{8,14},{9,15},{10,... | collective-permute-start | bytes 147464 | tf_op jit(solution)/shard_map/ppermute | solution.py:22
  128.5 4.1 %collective-permute-start.21 = (f32[96,128]{1,0:T(8,128)S(1)}, f32[96,128]{1,0:T(8,128)S(1)}, u32[]{:S(2)}, u32[]{:S(2)}) collective-permute-start(f32[96,128]{1,0:T(8,128)S(1)} %get-tuple-element.104), channel_id=1, source_target_pairs={{0,2},{1,3},{2,0},{3,1},{4,6},{5,7},{6,4},{7,5},{8,10},{9,11},{10,... | collective-permute-start | bytes 147464 | tf_op jit(solution)/shard_map/ppermute | solution.py:22
  128.9 4.1 %collective-permute-start.22 = (f32[96,128]{1,0:T(8,128)S(1)}, f32[96,128]{1,0:T(8,128)S(1)}, u32[]{:S(2)}, u32[]{:S(2)}) collective-permute-start(f32[96,128]{1,0:T(8,128)S(1)} %get-tuple-element.91), channel_id=1, source_target_pairs={{0,4},{1,5},{2,6},{3,7},{4,0},{5,1},{6,2},{7,3},{8,12},{9,13},{10,... | collective-permute-start | bytes 147464 | tf_op jit(solution)/shard_map/ppermute | solution.py:22
  133.0 4.2 %collective-permute-start.24 = (f32[96,128]{1,0:T(8,128)S(1)}, f32[96,128]{1,0:T(8,128)S(1)}, u32[]{:S(2)}, u32[]{:S(2)}) collective-permute-start(f32[96,128]{1,0:T(8,128)S(1)} %add_add_fusion.mine), channel_id=1, source_target_pairs={{0,8},{1,9},{2,10},{3,11},{4,12},{5,13},{6,14},{7,15},{8,0},{9,1},... | collective-permute-start | bytes 147464 | tf_op jit(solution)/shard_map/ppermute | solution.py:22

commit v6 on v5

--- a/solution.py
+++ b/solution.py
@@ -256,23 +256,12 @@
 def parcels_kernel(spot, rna_0, rna_1, atac_0, atac_1, cell, gene, peak, *refs):
     links, out, copied, slots, sems = refs[:4], refs[4], refs[5:9], refs[9], refs[10]
 
+    copies = [pltpu.make_async_copy(link, to, sems.at[i]) for i, (link, to) in enumerate(zip(links, copied))]
+
     @pl.when(pl.program_id(0) == 0)
     def _():
-        copies = [pltpu.make_async_copy(link, to, sems.at[i]) for i, (link, to) in enumerate(zip(links, copied))]
         for copy in copies:
             copy.start()
-        for copy in copies:
-            copy.wait()
-        link_gene, link_peak, link_weight, link_count = copied
-        count = link_gene.shape[0]
-        lane = lax.broadcasted_iota(jnp.int32, slots.shape, 1) - spot[1] * count
-        row = lax.broadcasted_iota(jnp.int32, slots.shape, 0)
-        value = jnp.zeros(slots.shape, jnp.float32)
-        for s in range(count):
-            weight = jnp.where(s < link_count[0], link_weight[s], 0)
-            for r, entry in enumerate((link_gene[s], link_peak[s], weight)):
-                value = jnp.where((lane == s) & (row == r), entry.astype(jnp.float32), value)
-        slots[...] = value.astype(jnp.bfloat16)
 
     rank = cell.shape[0]
     cells = rna_0.shape[0]
@@ -292,6 +281,23 @@
             row = (2 * (j % 2) + s) * part
             out[j, cells:, s * width : s * width + gene_width] = gene_low[row : row + part]
             out[j, cells:, s * width + gene_width : (s + 1) * width] = peak_low[row : row + part]
+
+    @pl.when(pl.program_id(0) == 0)
+    def _():
+        for copy in copies:
+            copy.wait()
+        link_gene, link_peak, link_weight, link_count = copied
+        count = link_gene.shape[0]
+        lane = lax.broadcasted_iota(jnp.int32, slots.shape, 1) - spot[1] * count
+        row = lax.broadcasted_iota(jnp.int32, slots.shape, 0)
+        value = jnp.zeros(slots.shape, jnp.float32)
+        for s in range(count):
+            weight = jnp.where(s < link_count[0], link_weight[s], 0)
+            for r, entry in enumerate((link_gene[s], link_peak[s], weight)):
+                value = jnp.where((lane == s) & (row == r), entry.astype(jnp.float32), value)
+        slots[...] = value.astype(jnp.bfloat16)
+
+    for j in range(out.shape[0]):
         out[j, cells:, 2 * width :] = slots[...]
 
 
@@ -455,6 +461,19 @@
     finish_sums(sums_in[...] + link_scale * links, gram[...], sums, coded, beside)
 
 
+def fetch(received, order, counts, sems):
+    cells, features = counts.shape[0] // len(order), counts.shape[1]
+    copies = [
+        pltpu.make_async_copy(
+            received.at[j, pl.ds(0, cells), pl.ds(0, features)], counts.at[pl.ds(i * cells, cells)], sems.at[i]
+        )
+        for i, j in enumerate(order)
+    ]
+    for copy in copies:
+        copy.start()
+    return copies
+
+
 def gram_rows(gram, lanes):
     rank = gram.shape[0]
     rows = rank * rank // lanes
@@ -468,8 +487,10 @@
 
 
 def next_sums_kernel(
-    link_scale, widths, orders, spot, table, mine, other, state, received, to_gene, genes, sums, coded, beside, state_out, own
+    link_scale, widths, orders, spot, table, mine, other, state, received, to_gene, genes, *refs
 ):
+    sums, coded, beside, state_out, own, counts, sems = refs
+    copies = fetch(received, orders[0], counts, sems)
     half = received.shape[0]
     rank, features = sums.shape
     cells = own.shape[1]
@@ -488,8 +509,6 @@
         mine_now = jnp.where(place == orders[0][position], new[:, at : at + cells], mine_now)
     own[...] = mine_now
     high, rest = halved(new)
-    counts = jnp.concatenate([received[j, 0:cells, 0:features] for j in orders[0]], axis=0)
-    products = jnp.dot(high, counts, preferred_element_type=jnp.float32)
     total = [None] * (2 * peak_blocks)
     for position, j in enumerate(orders[1]):
         for b in range(gene_blocks):
@@ -505,13 +524,20 @@
     links = jnp.concatenate(
         [jnp.where(side == 0, gene_links, nothing), jnp.where(side == 0, nothing, gene_links), *total], axis=1
     )
-    finish_sums(products + link_scale * links, gram_of(high, rest), sums, coded, beside)
+    gram = gram_of(high, rest)
+    for copy in copies:
+        copy.wait()
+    products = jnp.dot(high, counts[...], preferred_element_type=jnp.float32)
+    finish_sums(products + link_scale * links, gram, sums, coded, beside)
 
 
 def update_kernel(last, widths, orders, spot, table, sums, other, beside, beside_other, factors, received, *outs):
     half = received.shape[0]
     rank, features = sums.shape
     cells = received.shape[1] - rank // 4
+    if last:
+        *outs, counts, sems = outs
+        copies = fetch(received, orders[0], counts, sems)
     gene_width, peak_width = widths
     gene_blocks, peak_blocks = gene_width // BLOCK, peak_width // BLOCK
     side, place, core = spot[0], spot[1], spot[2]
@@ -529,7 +555,12 @@
     whole = jnp.concatenate(whole, axis=1)
     new = old * whole / below
     low = new.astype(jnp.bfloat16)
-    cell_sums = jnp.concatenate([across(low, received[j, 0:cells, 0:features]) for j in orders[0]], axis=1)
+    if last:
+        for copy in copies:
+            copy.wait()
+        cell_sums = across(low, counts[...])
+    else:
+        cell_sums = jnp.concatenate([across(low, received[j, 0:cells, 0:features]) for j in orders[0]], axis=1)
     gram_features = across(low, low)
     kept, sent, *outs = outs
     split = half // 2 * cells
@@ -622,7 +653,7 @@
     halves = [list(range(half)), list(range(half, count))]
     received = lax.all_to_all(sent, AXIS, 0, 0, axis_index_groups=halves, tiled=True)
     rows_other = flip(received[:, cells:, :features], 1)
-    received = pltpu.with_memory_space_constraint(received, pltpu.VMEM)
+    received_here = pltpu.with_memory_space_constraint(received, pltpu.VMEM)
     codes, bounds = pl.pallas_call(
         codes_kernel,
         in_specs=[VMEM] * 2,
@@ -641,9 +672,10 @@
         out_specs=VMEM,
         out_shape=struct(rank + table_shape[0], table_shape[1]),
         compiler_params=PARAMS,
-    )(received, bounds)
+    )(received_here, bounds)
     aside_other = flip(aside, half)
     codes_other = flip(codes, half)
+    aside_other, codes_other = lax.optimization_barrier((aside_other, codes_other))
     sums_shapes = (struct(rank, features), struct(rank, features, dtype=jnp.int16), struct(rank, 2 * rank))
     sums, gram, state = pl.pallas_call(
         functools.partial(first_sums_kernel, cell_order),
@@ -651,7 +683,7 @@
         out_specs=[VMEM] * 3,
         out_shape=(struct(rank, features), struct(rank, rank), struct(rank, half * cells)),
         compiler_params=PARAMS,
-    )(received)
+    )(received_here)
     sums, coded, beside, link_table = pl.pallas_call(
         functools.partial(first_links_kernel, link_scale, widths),
         grid=(1,),
@@ -668,9 +700,8 @@
         out_shape=(*sums_shapes, struct(*table_shape)),
         scratch_shapes=[pltpu.SemaphoreType.DMA, pltpu.SMEM(table_shape, jnp.float32)],
         compiler_params=PARAMS,
-    )(spot, received, rows_other, aside, aside_other, sums, gram)
-
-    beside, codes_other = lax.optimization_barrier((beside, codes_other))
+    )(spot, received_here, rows_other, aside, aside_other, sums, gram)
+
     factors = pl.pallas_call(
         twins_kernel,
         in_specs=[SMEM] + [VMEM] * 4,
@@ -680,6 +711,8 @@
     )(spot, gene_factor, peak_factor, codes_other, aside_other)
 
     split = half // 2 * cells
+    anywhere = pl.BlockSpec(memory_space=pl.ANY)
+    fetched = [pltpu.VMEM((half * cells, features), jnp.bfloat16), pltpu.SemaphoreType.DMA((half,))]
     for sweep_index in range(ROUNDS):
         last = sweep_index == ROUNDS - 1
         beside_other = flip(beside, half)
@@ -692,11 +725,12 @@
             outs += [struct(rank, gene_width, dtype=jnp.bfloat16)]
         kept, sent, *outs = pl.pallas_call(
             functools.partial(update_kernel, last, widths, (cell_order, link_order)),
-            in_specs=[SMEM] * 2 + [VMEM] * 6,
+            in_specs=[SMEM] * 2 + [VMEM] * 5 + [anywhere if last else VMEM],
             out_specs=[VMEM] * len(outs),
             out_shape=outs,
+            scratch_shapes=fetched if last else [],
             compiler_params=PARAMS,
-        )(spot, link_table, sums, other, beside, beside_other, factors, received)
+        )(spot, link_table, sums, other, beside, beside_other, factors, in_hbm(received) if last else received_here)
         if last:
             gene_out, peak_out = outs
             totals = kept + flip(sent, 1)
@@ -742,11 +776,12 @@
         genes = jnp.concatenate(in_order(1, genes, flip(genes, 1)), axis=1)
         sums, coded, beside, state, own_cells = pl.pallas_call(
             functools.partial(next_sums_kernel, link_scale, widths, (cell_order, gene_order)),
-            in_specs=[SMEM] * 2 + [VMEM] * 6,
+            in_specs=[SMEM] * 2 + [VMEM] * 3 + [anywhere] + [VMEM] * 2,
             out_specs=[VMEM] * 5,
+            scratch_shapes=fetched,
             out_shape=(*sums_shapes, struct(rank, half * cells), struct(rank, cells)),
             compiler_params=PARAMS,
-        )(spot, link_table, totals, flip(totals, 1), state, received, to_gene, genes)
+        )(spot, link_table, totals, flip(totals, 1), state, in_hbm(received), to_gene, genes)
 
 
 def shards(rna_counts, atac_counts, cell_factor, gene_factor, peak_factor, link_gene, *links):

time: 139 us -> 138 us (level)
  Pallas kernels: 17.3 us -> 20.8 us
  waiting for transfers between devices: 46.5 us -> 44 us
  local copies, waits for them, and re-layouts: 2.11 us -> 0.09 us
    ppermute x25, waiting for transfers between devices: 46.5 us -> 44 us  [flip(): return lax.ppermute(value, AXIS, [(i, i ^ bit) for i in range(count)])]
    pallas_call x2, Pallas kernels: 5.02 us -> 7.07 us  [shards_blocks(): pl.pallas_call(functools.partial(update_kernel, last, widths, (cell_order...]
    unnamed x14 -> x12, local copies, waits for them, and re-layouts: 2.06 us -> 0.04 us
    pallas_call x1, Pallas kernels: 3.02 us -> 4.63 us  [shards_blocks(): pl.pallas_call(functools.partial(next_sums_kernel, link_scale, widths, (c...]
  transfers between devices with their start and end apart: 25 -> 25, of which waited for: 18 -> 19; matrix products, arithmetic and copies ran while one was open for 0% -> 0% of each run, Pallas kernels for 1% -> 1%
where the time goes in v6:
time: 138 us
  blocking collectives  49.8 us (36%)
  waiting for transfers between devices  44 us (32%)
  starting transfers between devices  20.9 us (15%)
  Pallas kernels  20.8 us (15%)
  between operations  1.67 us (1%)
    all_to_all x1, blocking collectives, shards_blocks(): lax.all_to_all(sent, AXIS, 0, 0, axis_index_groups=halves, tiled=True)  49.8 us
    ppermute x25, waiting for transfers between devices, flip(): return lax.ppermute(value, AXIS, [(i, i ^ bit) for i in range(count)])  44 us
    ppermute x25, starting transfers between devices, flip(): return lax.ppermute(value, AXIS, [(i, i ^ bit) for i in range(count)])  20.9 us
    pallas_call x2, Pallas kernels, shards_blocks(): pl.pallas_call(functools.partial(update_kernel, last, widths, (cell_order...  7.07 us
    pallas_call x1, Pallas kernels, shards_blocks(): pl.pallas_call(functools.partial(next_sums_kernel, link_scale, widths, (c...  4.63 us
    pallas_call x1, Pallas kernels, parcels(): pl.pallas_call(parcels_kernel, grid=(steps,), in_specs=[SMEM, columns(gen...  3.45 us
  transfers between devices with their start and end apart: 25, of which 19 were waited for; matrix products, arithmetic and copies ran while one was open for 0% of the time, Pallas kernels for 1%

profile of v6, /device:TPU:0, one launch (start us, length us, event | category | flops | bytes accessed | tf_op | source)
XLA Modules:
  0.0 137.7 jit_solution(16666848171003650751)
XLA Ops:
  1.4 3.4 %shard_map.112 = bf16[16,80,1408]{2,1,0:T(8,128)(2,1)S(1)} custom-call(s32[4]{0:T(128)S(1)} %pad_add_fusion.spot, bf16[64,4096]{1,0:T(8,128)(2,1)} %rna_1.1, bf16[64,4096]{1,0:T(8,128)(2,1)} %rna_1.1, bf16[64,16384]{1,0:T(8,128)(2,1)} %atac_1.1, bf16[64,16384]{1,0:T(8,128)(2,1)} %atac_1.1, f32[64,64]{1,0:T(8,128)} %cell.1, f32[64,128]{1,0:T(8,128)} %gene.5, ...), custom_call_target="tpu_custom_call" | custom-call | tf_op jit(solution)/shard_map/pallas_call | solution.py:377
  4.9 49.8 %all_to_all.5.received_slots.received.mine = bf16[16,80,1408]{2,1,0:T(8,128)(2,1)S(1)} all-to-all(bf16[16,80,1408]{2,1,0:T(8,128)(2,1)S(1)} %shard_map.112), channel_id=1, replica_groups={{0,1,2,3,4,5,6,7,8,9,10,11,12,13,14,15},{16,17,18,19,20,21,22,23,24,25,..., dimensions={0} | all-to-all | bytes 7208960 | tf_op jit(solution)/shard_map/all_to_all | solution.py:654
  55.0 2.7 %collective-permute-start.2 = (s16[64,640]{1,0:T(8,128)(2,1)S(1)}, s16[64,640]{1,0:T(8,128)(2,1)S(1)}, u32[]{:S(2)}, u32[]{:S(2)}) collective-permute-start(s16[64,640]{1,0:T(8,128)(2,1)S(1)} %get-tuple-element.47), channel_id=1, source_target_pairs={{0,16},{1,17},{2,18},{3,19},{4,20},{5,21},{6,22},{7,23},{8,24},{9,... | collective-permute-start | bytes 245768 | tf_op jit(solution)/shard_map/ppermute | solution.py:22
  58.2 0.8 shard_map.115
  59.0 4.7 %collective-permute-done.2.codes = s16[64,640]{1,0:T(8,128)(2,1)S(1)} collective-permute-done((s16[64,640]{1,0:T(8,128)(2,1)S(1)}, s16[64,640]{1,0:T(8,128)(2,1)S(1)}, u32[]{:S(2)}, u32[]{:S(2)}) %collective-permute-start.2) | collective-permute-done | bytes 81952 | tf_op jit(solution)/shard_map/ppermute | solution.py:22
  63.7 1.0 collective-permute-done.1.aside_other.beside
  64.6 2.4 %shard_map.116 = (f32[64,1280]{1,0:T(8,128)S(1)}, s16[64,1280]{1,0:T(8,128)(2,1)S(1)}, f32[64,128]{1,0:T(8,128)S(1)}, f32[32,128]{1,0:T(8,128)S(1)}) custom-call(s32[4]{0:T(128)S(1)} %pad_add_fusion.spot, bf16[16,80,1408]{2,1,0:T(8,128)(2,1)S(1)} %all_to_all.5.received_slots.received.mine, bf16[16,16,1280]{2,1,0:T(8,128)(2,1)S(1)} %collective-permute-done.other, ...), custom_call_target="tpu_custom_call" | custom-call | tf_op jit(solution)/shard_map/pallas_call | solution.py:687
  67.1 2.9 %collective-permute-start.4 = (f32[64,128]{1,0:T(8,128)S(1)}, f32[64,128]{1,0:T(8,128)S(1)}, u32[]{:S(2)}, u32[]{:S(2)}) collective-permute-start(f32[64,128]{1,0:T(8,128)S(1)} %get-tuple-element.54.beside), channel_id=1, source_target_pairs={{0,16},{1,17},{2,18},{3,19},{4,20},{5,21},{6,22},{7,23},{8,24},{9,... | collective-permute-start | bytes 98312 | tf_op jit(solution)/shard_map/ppermute | solution.py:22
  70.1 0.7 shard_map.117.factors
  70.8 7.9 %collective-permute-done.4.beside_other = f32[64,128]{1,0:T(8,128)S(1)} collective-permute-done((f32[64,128]{1,0:T(8,128)S(1)}, f32[64,128]{1,0:T(8,128)S(1)}, u32[]{:S(2)}, u32[]{:S(2)}) %collective-permute-start.4) | collective-permute-done | bytes 32800 | tf_op jit(solution)/shard_map/ppermute | solution.py:22
  78.7 2.5 %shard_map.118 = (f32[72,512]{1,0:T(8,128)S(1)}, f32[72,512]{1,0:T(8,128)S(1)}, f32[64,1280]{1,0:T(8,128)S(1)}, f32[64,1024]{1,0:T(8,128)S(1)}, f32[64,1024]{1,0:T(8,128)S(1)}, /*index=5*/bf16[64,128]{1,0:T(8,128)(2,1)S(1)}) custom-call(s32[4]{0:T(128)S(1)} %pad_add_fusion.spot, f32[32,128]{1,0:T(8,128)S(1)} %get-tuple-element.51.table, ...), custom_call_target="tpu_custom_call" | custom-call | tf_op jit(solution)/shard_map/pallas_call | solution.py:726
  81.7 1.2 collective-permute-done.5
  83.7 3.7 %collective-permute-done.9 = bf16[64,128]{1,0:T(8,128)(2,1)S(1)} collective-permute-done((bf16[64,128]{1,0:T(8,128)(2,1)S(1)}, bf16[64,128]{1,0:T(8,128)(2,1)S(1)}, u32[]{:S(2)}, u32[]{:S(2)}) %collective-permute-start.9) | collective-permute-done | bytes 16416 | tf_op jit(solution)/shard_map/ppermute | solution.py:22
  87.4 1.3 collective-permute-done.8
  89.3 1.8 %collective-permute-start.12 = (bf16[64,256]{1,0:T(8,128)(2,1)S(1)}, bf16[64,256]{1,0:T(8,128)(2,1)S(1)}, u32[]{:S(2)}, u32[]{:S(2)}) collective-permute-start(bf16[64,256]{1,0:T(8,128)(2,1)S(1)} %pad_maximum_fusion.3), channel_id=1, source_target_pairs={{0,2},{1,3},{2,0},{3,1},{4,6},{5,7},{6,4},{7,5},{8,10},{9,11},{10,... | collective-permute-start | bytes 98312 | tf_op jit(solution)/shard_map/ppermute | solution.py:22
  91.1 2.2 %collective-permute-done.12 = bf16[64,256]{1,0:T(8,128)(2,1)S(1)} collective-permute-done((bf16[64,256]{1,0:T(8,128)(2,1)S(1)}, bf16[64,256]{1,0:T(8,128)(2,1)S(1)}, u32[]{:S(2)}, u32[]{:S(2)}) %collective-permute-start.12) | collective-permute-done | bytes 32800 | tf_op jit(solution)/shard_map/ppermute | solution.py:22
  93.6 0.8 collective-permute-done.10
  94.5 1.0 collective-permute-start.13
  95.4 1.9 %collective-permute-start.15 = (bf16[64,512]{1,0:T(8,128)(2,1)S(1)}, bf16[64,512]{1,0:T(8,128)(2,1)S(1)}, u32[]{:S(2)}, u32[]{:S(2)}) collective-permute-start(bf16[64,512]{1,0:T(8,128)(2,1)S(1)} %pad_maximum_fusion.2), channel_id=1, source_target_pairs={{0,4},{1,5},{2,6},{3,7},{4,0},{5,1},{6,2},{7,3},{8,12},{9,13},{10,... | collective-permute-start | bytes 196616 | tf_op jit(solution)/shard_map/ppermute | solution.py:22
  97.4 1.4 %collective-permute-start.14 = (f32[64,128]{1,0:T(8,128)S(1)}, f32[64,128]{1,0:T(8,128)S(1)}, u32[]{:S(2)}, u32[]{:S(2)}) collective-permute-start(f32[64,128]{1,0:T(8,128)S(1)} %slice_select_fusion.6), channel_id=1, source_target_pairs={{0,2},{1,3},{2,0},{3,1},{4,6},{5,7},{6,4},{7,5},{8,10},{9,11},{10,... | collective-permute-start | bytes 98312 | tf_op jit(solution)/shard_map/ppermute | solution.py:22
  98.8 2.5 %collective-permute-done.14 = f32[64,128]{1,0:T(8,128)S(1)} collective-permute-done((f32[64,128]{1,0:T(8,128)S(1)}, f32[64,128]{1,0:T(8,128)S(1)}, u32[]{:S(2)}, u32[]{:S(2)}) %collective-permute-start.14) | collective-permute-done | bytes 32800 | tf_op jit(solution)/shard_map/ppermute | solution.py:22
  102.0 0.7 collective-permute-done.17
  103.0 4.6 %shard_map.119 = (f32[64,1280]{1,0:T(8,128)S(1)}, s16[64,1280]{1,0:T(8,128)(2,1)S(1)}, f32[64,128]{1,0:T(8,128)S(1)}, f32[64,1024]{1,0:T(8,128)}, f32[64,64]{1,0:T(8,128)S(1)}) custom-call(s32[4]{0:T(128)S(1)} %pad_add_fusion.spot, f32[32,128]{1,0:T(8,128)S(1)} %get-tuple-element.51.table, f32[72,512]{1,0:T(8,128)S(1)} %add.52.mine, ...), custom_call_target="tpu_custom_call" | custom-call | tf_op jit(solution)/shard_map/pallas_call | solution.py:777
  108.1 2.5 %collective-permute-start.19 = (f32[64,128]{1,0:T(8,128)S(1)}, f32[64,128]{1,0:T(8,128)S(1)}, u32[]{:S(2)}, u32[]{:S(2)}) collective-permute-start(f32[64,128]{1,0:T(8,128)S(1)} %get-tuple-element.82.beside), channel_id=1, source_target_pairs={{0,16},{1,17},{2,18},{3,19},{4,20},{5,21},{6,22},{7,23},{8,24},{9,... | collective-permute-start | bytes 98312 | tf_op jit(solution)/shard_map/ppermute | solution.py:22
  110.6 9.1 %collective-permute-done.19.beside_other = f32[64,128]{1,0:T(8,128)S(1)} collective-permute-done((f32[64,128]{1,0:T(8,128)S(1)}, f32[64,128]{1,0:T(8,128)S(1)}, u32[]{:S(2)}, u32[]{:S(2)}) %collective-permute-start.19) | collective-permute-done | bytes 32800 | tf_op jit(solution)/shard_map/ppermute | solution.py:22
  119.8 4.6 %shard_map.120 = (f32[72,512]{1,0:T(8,128)S(1)}, f32[72,512]{1,0:T(8,128)S(1)}, f32[64,128]{1,0:T(8,128)}, f32[64,512]{1,0:T(8,128)}) custom-call(s32[4]{0:T(128)S(1)} %pad_add_fusion.spot, f32[32,128]{1,0:T(8,128)S(1)} %get-tuple-element.51.table, f32[64,1280]{1,0:T(8,128)S(1)} %get-tuple-element.80.sums, ...), custom_call_target="tpu_custom_call" | custom-call | tf_op jit(solution)/shard_map/pallas_call | solution.py:726
  124.5 1.3 collective-permute-done.20
  126.0 1.6 %collective-permute-start.23 = (f32[96,128]{1,0:T(8,128)S(1)}, f32[96,128]{1,0:T(8,128)S(1)}, u32[]{:S(2)}, u32[]{:S(2)}) collective-permute-start(f32[96,128]{1,0:T(8,128)S(1)} %constant_dynamic-update-slice_fusion.15), channel_id=1, source_target_pairs={{0,6},{1,7},{2,4},{3,5},{4,2},{5,3},{6,0},{7,1},{8,14},{9,15},{10,... | collective-permute-start | bytes 147464 | tf_op jit(solution)/shard_map/ppermute | solution.py:22
  128.1 1.5 %collective-permute-start.22 = (f32[96,128]{1,0:T(8,128)S(1)}, f32[96,128]{1,0:T(8,128)S(1)}, u32[]{:S(2)}, u32[]{:S(2)}) collective-permute-start(f32[96,128]{1,0:T(8,128)S(1)} %get-tuple-element.91), channel_id=1, source_target_pairs={{0,4},{1,5},{2,6},{3,7},{4,0},{5,1},{6,2},{7,3},{8,12},{9,13},{10,... | collective-permute-start | bytes 147464 | tf_op jit(solution)/shard_map/ppermute | solution.py:22
  129.5 1.7 %collective-permute-done.23 = f32[96,128]{1,0:T(8,128)S(1)} collective-permute-done((f32[96,128]{1,0:T(8,128)S(1)}, f32[96,128]{1,0:T(8,128)S(1)}, u32[]{:S(2)}, u32[]{:S(2)}) %collective-permute-start.23) | collective-permute-done | bytes 49184 | tf_op jit(solution)/shard_map/ppermute | solution.py:22
  132.3 4.1 %collective-permute-done.24.other = f32[96,128]{1,0:T(8,128)S(1)} collective-permute-done((f32[96,128]{1,0:T(8,128)S(1)}, f32[96,128]{1,0:T(8,128)S(1)}, u32[]{:S(2)}, u32[]{:S(2)}) %collective-permute-start.24) | collective-permute-done | bytes 49184 | tf_op jit(solution)/shard_map/ppermute | solution.py:22
  136.3 1.4 %shard_map.121 = f32[64,64]{1,0:T(8,128)} custom-call(s32[4]{0:T(128)S(1)} %pad_add_fusion.spot, f32[96,128]{1,0:T(8,128)S(1)} %add_add_fusion.mine, f32[96,128]{1,0:T(8,128)S(1)} %collective-permute-done.24.other, f32[64,64]{1,0:T(8,128)S(1)} %get-tuple-element.86.old), custom_call_target="tpu_custom_call" | custom-call | tf_op jit(solution)/shard_map/pallas_call | solution.py:755
  (69 shorter events, 6.2 us)
Async XLA Ops:
  4.8 49.9 %copy-start.1 = (f32[64,512]{1,0:T(8,128)S(1)}, f32[64,512]{1,0:T(8,128)}, u32[]{:S(2)}) copy-start(f32[64,512]{1,0:T(8,128)} %peak.5) | copy-start | bytes 393220
  4.9 49.9 %copy-start.2 = (f32[64,128]{1,0:T(8,128)S(1)}, f32[64,128]{1,0:T(8,128)}, u32[]{:S(2)}) copy-start(f32[64,128]{1,0:T(8,128)} %gene.5) | copy-start | bytes 98308
  54.6 24.1 %copy-start = (bf16[16,80,1408]{2,1,0:T(8,128)(2,1)}, bf16[16,80,1408]{2,1,0:T(8,128)(2,1)S(1)}, u32[]{:S(2)}) copy-start(bf16[16,80,1408]{2,1,0:T(8,128)(2,1)S(1)} %all_to_all.5.received_slots.received.mine) | copy-start | bytes 10813444
  54.7 10.0 %collective-permute-start = (bf16[16,16,1280]{2,1,0:T(8,128)(2,1)S(1)}, bf16[16,16,1280]{2,1,0:T(8,128)(2,1)S(1)}, u32[]{:S(2)}, u32[]{:S(2)}) collective-permute-start(bf16[16,16,1280]{2,1,0:T(8,128)(2,1)S(1)} %slice.14), channel_id=1, source_target_pairs={{0,1},{1,0},{2,3},{3,2},{4,5},{5,4},{6,7},{7,6},{8,9},{9,8},{10,11... | collective-permute-start | bytes 1966088 | tf_op jit(solution)/shard_map/ppermute | solution.py:22
  55.0 8.7 %collective-permute-start.2 = (s16[64,640]{1,0:T(8,128)(2,1)S(1)}, s16[64,640]{1,0:T(8,128)(2,1)S(1)}, u32[]{:S(2)}, u32[]{:S(2)}) collective-permute-start(s16[64,640]{1,0:T(8,128)(2,1)S(1)} %get-tuple-element.47), channel_id=1, source_target_pairs={{0,16},{1,17},{2,18},{3,19},{4,20},{5,21},{6,22},{7,23},{8,24},{9,... | collective-permute-start | bytes 245768 | tf_op jit(solution)/shard_map/ppermute | solution.py:22
  57.8 6.8 %collective-permute-start.1 = (f32[96,128]{1,0:T(8,128)S(1)}, f32[96,128]{1,0:T(8,128)S(1)}, u32[]{:S(2)}, u32[]{:S(2)}) collective-permute-start(f32[96,128]{1,0:T(8,128)S(1)} %shard_map.114.aside), channel_id=1, source_target_pairs={{0,16},{1,17},{2,18},{3,19},{4,20},{5,21},{6,22},{7,23},{8,24},{9,... | collective-permute-start | bytes 147464 | tf_op jit(solution)/shard_map/ppermute | solution.py:22
  67.1 11.6 %collective-permute-start.3 = (s16[64,1280]{1,0:T(8,128)(2,1)S(1)}, s16[64,1280]{1,0:T(8,128)(2,1)S(1)}, u32[]{:S(2)}, u32[]{:S(2)}) collective-permute-start(s16[64,1280]{1,0:T(8,128)(2,1)S(1)} %get-tuple-element.53), channel_id=1, source_target_pairs={{0,16},{1,17},{2,18},{3,19},{4,20},{5,21},{6,22},{7,23},{8,24},{9,... | collective-permute-start | bytes 491528 | tf_op jit(solution)/shard_map/ppermute | solution.py:22
  67.1 11.5 %collective-permute-start.4 = (f32[64,128]{1,0:T(8,128)S(1)}, f32[64,128]{1,0:T(8,128)S(1)}, u32[]{:S(2)}, u32[]{:S(2)}) collective-permute-start(f32[64,128]{1,0:T(8,128)S(1)} %get-tuple-element.54.beside), channel_id=1, source_target_pairs={{0,16},{1,17},{2,18},{3,19},{4,20},{5,21},{6,22},{7,23},{8,24},{9,... | collective-permute-start | bytes 98312 | tf_op jit(solution)/shard_map/ppermute | solution.py:22
  81.2 1.8 %collective-permute-start.6 = (f32[64,1024]{1,0:T(8,128)S(1)}, f32[64,1024]{1,0:T(8,128)S(1)}, u32[]{:S(2)}, u32[]{:S(2)}) collective-permute-start(f32[64,1024]{1,0:T(8,128)S(1)} %get-tuple-element.59), channel_id=1, source_target_pairs={{0,1},{1,0},{2,3},{3,2},{4,5},{5,4},{6,7},{7,6},{8,9},{9,8},{10,11... | collective-permute-start | bytes 786440 | tf_op jit(solution)/shard_map/ppermute | solution.py:22
  81.2 1.7 %collective-permute-start.5 = (f32[72,512]{1,0:T(8,128)S(1)}, f32[72,512]{1,0:T(8,128)S(1)}, u32[]{:S(2)}, u32[]{:S(2)}) collective-permute-start(f32[72,512]{1,0:T(8,128)S(1)} %get-tuple-element.57), channel_id=1, source_target_pairs={{0,1},{1,0},{2,3},{3,2},{4,5},{5,4},{6,7},{7,6},{8,9},{9,8},{10,11... | collective-permute-start | bytes 442376 | tf_op jit(solution)/shard_map/ppermute | solution.py:22
  83.1 6.0 %collective-permute-start.7 = (f32[72,512]{1,0:T(8,128)S(1)}, f32[72,512]{1,0:T(8,128)S(1)}, u32[]{:S(2)}, u32[]{:S(2)}) collective-permute-start(f32[72,512]{1,0:T(8,128)S(1)} %add.46), channel_id=1, source_target_pairs={{0,2},{1,3},{2,0},{3,1},{4,6},{5,7},{6,4},{7,5},{8,10},{9,11},{10,... | collective-permute-start | bytes 442376 | tf_op jit(solution)/shard_map/ppermute | solution.py:22
  83.2 5.6 %collective-permute-start.8 = (f32[64,512]{1,0:T(8,128)S(1)}, f32[64,512]{1,0:T(8,128)S(1)}, u32[]{:S(2)}, u32[]{:S(2)}) collective-permute-start(f32[64,512]{1,0:T(8,128)S(1)} %slice_select_fusion), channel_id=1, source_target_pairs={{0,4},{1,5},{2,6},{3,7},{4,0},{5,1},{6,2},{7,3},{8,12},{9,13},{10,... | collective-permute-start | bytes 393224 | tf_op jit(solution)/shard_map/ppermute | solution.py:22
  83.7 3.7 %collective-permute-start.9 = (bf16[64,128]{1,0:T(8,128)(2,1)S(1)}, bf16[64,128]{1,0:T(8,128)(2,1)S(1)}, u32[]{:S(2)}, u32[]{:S(2)}) collective-permute-start(bf16[64,128]{1,0:T(8,128)(2,1)S(1)} %get-tuple-element.63), channel_id=1, source_target_pairs={{0,8},{1,9},{2,10},{3,11},{4,12},{5,13},{6,14},{7,15},{8,0},{9,1},... | collective-permute-start | bytes 49160 | tf_op jit(solution)/shard_map/ppermute | solution.py:22
  89.2 5.2 %collective-permute-start.10 = (f32[72,512]{1,0:T(8,128)S(1)}, f32[72,512]{1,0:T(8,128)S(1)}, u32[]{:S(2)}, u32[]{:S(2)}) collective-permute-start(f32[72,512]{1,0:T(8,128)S(1)} %add.48), channel_id=1, source_target_pairs={{0,4},{1,5},{2,6},{3,7},{4,0},{5,1},{6,2},{7,3},{8,12},{9,13},{10,... | collective-permute-start | bytes 442376 | tf_op jit(solution)/shard_map/ppermute | solution.py:22
  89.2 4.3 %collective-permute-start.11 = (f32[64,256]{1,0:T(8,128)S(1)}, f32[64,256]{1,0:T(8,128)S(1)}, u32[]{:S(2)}, u32[]{:S(2)}) collective-permute-start(f32[64,256]{1,0:T(8,128)S(1)} %slice_select_fusion.1), channel_id=1, source_target_pairs={{0,8},{1,9},{2,10},{3,11},{4,12},{5,13},{6,14},{7,15},{8,0},{9,1},... | collective-permute-start | bytes 196616 | tf_op jit(solution)/shard_map/ppermute | solution.py:22
  89.3 4.0 %collective-permute-start.12 = (bf16[64,256]{1,0:T(8,128)(2,1)S(1)}, bf16[64,256]{1,0:T(8,128)(2,1)S(1)}, u32[]{:S(2)}, u32[]{:S(2)}) collective-permute-start(bf16[64,256]{1,0:T(8,128)(2,1)S(1)} %pad_maximum_fusion.3), channel_id=1, source_target_pairs={{0,2},{1,3},{2,0},{3,1},{4,6},{5,7},{6,4},{7,5},{8,10},{9,11},{10,... | collective-permute-start | bytes 98312 | tf_op jit(solution)/shard_map/ppermute | solution.py:22
  94.5 6.8 %collective-permute-start.13 = (f32[72,512]{1,0:T(8,128)S(1)}, f32[72,512]{1,0:T(8,128)S(1)}, u32[]{:S(2)}, u32[]{:S(2)}) collective-permute-start(f32[72,512]{1,0:T(8,128)S(1)} %add.50), channel_id=1, source_target_pairs={{0,8},{1,9},{2,10},{3,11},{4,12},{5,13},{6,14},{7,15},{8,0},{9,1},... | collective-permute-start | bytes 442376 | tf_op jit(solution)/shard_map/ppermute | solution.py:22
  95.4 5.9 %collective-permute-start.15 = (bf16[64,512]{1,0:T(8,128)(2,1)S(1)}, bf16[64,512]{1,0:T(8,128)(2,1)S(1)}, u32[]{:S(2)}, u32[]{:S(2)}) collective-permute-start(bf16[64,512]{1,0:T(8,128)(2,1)S(1)} %pad_maximum_fusion.2), channel_id=1, source_target_pairs={{0,4},{1,5},{2,6},{3,7},{4,0},{5,1},{6,2},{7,3},{8,12},{9,13},{10,... | collective-permute-start | bytes 196616 | tf_op jit(solution)/shard_map/ppermute | solution.py:22
  97.4 3.9 %collective-permute-start.14 = (f32[64,128]{1,0:T(8,128)S(1)}, f32[64,128]{1,0:T(8,128)S(1)}, u32[]{:S(2)}, u32[]{:S(2)}) collective-permute-start(f32[64,128]{1,0:T(8,128)S(1)} %slice_select_fusion.6), channel_id=1, source_target_pairs={{0,2},{1,3},{2,0},{3,1},{4,6},{5,7},{6,4},{7,5},{8,10},{9,11},{10,... | collective-permute-start | bytes 98312 | tf_op jit(solution)/shard_map/ppermute | solution.py:22
  101.3 1.4 %collective-permute-start.17 = (bf16[64,1024]{1,0:T(8,128)(2,1)S(1)}, bf16[64,1024]{1,0:T(8,128)(2,1)S(1)}, u32[]{:S(2)}, u32[]{:S(2)}) collective-permute-start(bf16[64,1024]{1,0:T(8,128)(2,1)S(1)} %pad_maximum_fusion.1), channel_id=1, source_target_pairs={{0,1},{1,0},{2,3},{3,2},{4,5},{5,4},{6,7},{7,6},{8,9},{9,8},{10,11... | collective-permute-start | bytes 393224 | tf_op jit(solution)/shard_map/ppermute | solution.py:22
  101.4 1.6 %collective-permute-start.16 = (f32[72,512]{1,0:T(8,128)S(1)}, f32[72,512]{1,0:T(8,128)S(1)}, u32[]{:S(2)}, u32[]{:S(2)}) collective-permute-start(f32[72,512]{1,0:T(8,128)S(1)} %add.52.mine), channel_id=1, source_target_pairs={{0,1},{1,0},{2,3},{3,2},{4,5},{5,4},{6,7},{7,6},{8,9},{9,8},{10,11... | collective-permute-start | bytes 442376 | tf_op jit(solution)/shard_map/ppermute | solution.py:22
  107.6 12.1 %collective-permute-start.18 = (s16[64,1280]{1,0:T(8,128)(2,1)S(1)}, s16[64,1280]{1,0:T(8,128)(2,1)S(1)}, u32[]{:S(2)}, u32[]{:S(2)}) collective-permute-start(s16[64,1280]{1,0:T(8,128)(2,1)S(1)} %get-tuple-element.81), channel_id=1, source_target_pairs={{0,16},{1,17},{2,18},{3,19},{4,20},{5,21},{6,22},{7,23},{8,24},{9,... | collective-permute-start | bytes 491528 | tf_op jit(solution)/shard_map/ppermute | solution.py:22
  108.1 11.6 %collective-permute-start.19 = (f32[64,128]{1,0:T(8,128)S(1)}, f32[64,128]{1,0:T(8,128)S(1)}, u32[]{:S(2)}, u32[]{:S(2)}) collective-permute-start(f32[64,128]{1,0:T(8,128)S(1)} %get-tuple-element.82.beside), channel_id=1, source_target_pairs={{0,16},{1,17},{2,18},{3,19},{4,20},{5,21},{6,22},{7,23},{8,24},{9,... | collective-permute-start | bytes 98312 | tf_op jit(solution)/shard_map/ppermute | solution.py:22
  124.4 1.4 %collective-permute-start.20 = (f32[72,512]{1,0:T(8,128)S(1)}, f32[72,512]{1,0:T(8,128)S(1)}, u32[]{:S(2)}, u32[]{:S(2)}) collective-permute-start(f32[72,512]{1,0:T(8,128)S(1)} %get-tuple-element.85), channel_id=1, source_target_pairs={{0,1},{1,0},{2,3},{3,2},{4,5},{5,4},{6,7},{7,6},{8,9},{9,8},{10,11... | collective-permute-start | bytes 442376 | tf_op jit(solution)/shard_map/ppermute | solution.py:22
  126.0 5.3 %collective-permute-start.23 = (f32[96,128]{1,0:T(8,128)S(1)}, f32[96,128]{1,0:T(8,128)S(1)}, u32[]{:S(2)}, u32[]{:S(2)}) collective-permute-start(f32[96,128]{1,0:T(8,128)S(1)} %constant_dynamic-update-slice_fusion.15), channel_id=1, source_target_pairs={{0,6},{1,7},{2,4},{3,5},{4,2},{5,3},{6,0},{7,1},{8,14},{9,15},{10,... | collective-permute-start | bytes 147464 | tf_op jit(solution)/shard_map/ppermute | solution.py:22
  127.6 4.1 %collective-permute-start.21 = (f32[96,128]{1,0:T(8,128)S(1)}, f32[96,128]{1,0:T(8,128)S(1)}, u32[]{:S(2)}, u32[]{:S(2)}) collective-permute-start(f32[96,128]{1,0:T(8,128)S(1)} %get-tuple-element.104), channel_id=1, source_target_pairs={{0,2},{1,3},{2,0},{3,1},{4,6},{5,7},{6,4},{7,5},{8,10},{9,11},{10,... | collective-permute-start | bytes 147464 | tf_op jit(solution)/shard_map/ppermute | solution.py:22
  128.1 4.1 %collective-permute-start.22 = (f32[96,128]{1,0:T(8,128)S(1)}, f32[96,128]{1,0:T(8,128)S(1)}, u32[]{:S(2)}, u32[]{:S(2)}) collective-permute-start(f32[96,128]{1,0:T(8,128)S(1)} %get-tuple-element.91), channel_id=1, source_target_pairs={{0,4},{1,5},{2,6},{3,7},{4,0},{5,1},{6,2},{7,3},{8,12},{9,13},{10,... | collective-permute-start | bytes 147464 | tf_op jit(solution)/shard_map/ppermute | solution.py:22
  132.2 4.2 %collective-permute-start.24 = (f32[96,128]{1,0:T(8,128)S(1)}, f32[96,128]{1,0:T(8,128)S(1)}, u32[]{:S(2)}, u32[]{:S(2)}) collective-permute-start(f32[96,128]{1,0:T(8,128)S(1)} %add_add_fusion.mine), channel_id=1, source_target_pairs={{0,8},{1,9},{2,10},{3,11},{4,12},{5,13},{6,14},{7,15},{8,0},{9,1},... | collective-permute-start | bytes 147464 | tf_op jit(solution)/shard_map/ppermute | solution.py:22

commit v7 on v6

--- a/solution.py
+++ b/solution.py
@@ -323,25 +323,31 @@
         codes[:, b * BLOCK : (b + 1) * BLOCK] = code
         least.append(low)
         step.append(per)
-    pad = jnp.zeros((rank, bounds.shape[1] - 2 * len(least)), jnp.float32)
-    bounds[...] = jnp.concatenate([*least, *step, pad], axis=1)
+    pad = jnp.zeros((rank, 2 * rank - 2 * len(least)), jnp.float32)
+    columns = jnp.concatenate([*least, *step, pad], axis=1)
+    square = jnp.concatenate([columns, jnp.zeros_like(columns)], axis=0)
+    bounds[...] = square.T[: bounds.shape[0]]
 
 
 def table_kernel(received_slots, bounds, out):
-    rank = bounds.shape[0]
-    out[:rank] = bounds[...]
+    above = bounds.shape[0]
+    out[:above] = bounds[...]
     slots = sum(received_slots[j].astype(jnp.float32) for j in range(received_slots.shape[0]))
 
     def hot(row, size, value):
         ids = lax.broadcasted_iota(jnp.int32, (size, slots.shape[1]), 0).astype(jnp.float32)
         return jnp.where(slots[row : row + 1] == ids, value, 0.0).astype(jnp.bfloat16)
 
-    out[rank:] = across(hot(0, out.shape[0] - rank, slots[2:3]), hot(1, out.shape[1], 1.0))
+    out[above:] = across(hot(0, out.shape[0] - above, slots[2:3]), hot(1, out.shape[1], 1.0))
 
 
 def twins_kernel(spot, gene, peak, codes, beside, out):
     gene_width, peak_width = gene.shape[1], peak.shape[1]
     groups = (gene_width + peak_width) // BLOCK
+    lanes = beside.shape[1]
+    above = -(-2 * groups // 8) * 8
+    square = jnp.concatenate([beside[:above], jnp.zeros((lanes - above, lanes), jnp.float32)], axis=0)
+    bounds = square.T[: gene.shape[0]]
     at = 0
     first = spot[0] == 0
     for ref, start in ((gene, 0), (peak, gene_width)):
@@ -350,7 +356,7 @@
             g = start // BLOCK + b
             mine = ref[:, b * BLOCK : (b + 1) * BLOCK]
             code = codes[:, g * BLOCK : (g + 1) * BLOCK]
-            other = decode(code, beside[: mine.shape[0], g : g + 1], beside[: mine.shape[0], groups + g : groups + g + 1])
+            other = decode(code, bounds[:, g : g + 1], bounds[:, groups + g : groups + g + 1])
             out[:, at + b * BLOCK : at + (b + 1) * BLOCK] = jnp.where(first, mine, other)
             out[:, at + size + b * BLOCK : at + size + (b + 1) * BLOCK] = jnp.where(first, other, mine)
         at += 2 * size
@@ -426,7 +432,8 @@
     gene_width, peak_width = widths
     gene_blocks, peak_blocks = gene_width // BLOCK, peak_width // BLOCK
     width = gene_width + peak_width
-    table[...] = aside[rank:] + aside_other[rank:]
+    above = aside.shape[0] - table.shape[0]
+    table[...] = aside[above:] + aside_other[above:]
     copy = pltpu.make_async_copy(table, table_smem, sem)
     copy.start()
     copy.wait()
@@ -461,19 +468,6 @@
     finish_sums(sums_in[...] + link_scale * links, gram[...], sums, coded, beside)
 
 
-def fetch(received, order, counts, sems):
-    cells, features = counts.shape[0] // len(order), counts.shape[1]
-    copies = [
-        pltpu.make_async_copy(
-            received.at[j, pl.ds(0, cells), pl.ds(0, features)], counts.at[pl.ds(i * cells, cells)], sems.at[i]
-        )
-        for i, j in enumerate(order)
-    ]
-    for copy in copies:
-        copy.start()
-    return copies
-
-
 def gram_rows(gram, lanes):
     rank = gram.shape[0]
     rows = rank * rank // lanes
@@ -486,11 +480,49 @@
     )
 
 
+def step_kernel(link_bit, gene_bit, spot, totals, totals_got, staying, staying_got, *refs):
+    if gene_bit:
+        genes, genes_got, *refs = refs
+    received, totals_out, *outs = refs
+    totals_out[...] = totals[...] + totals_got[...]
+    to_gene = staying[...] + staying_got[...]
+    if gene_bit:
+        genes_out, *outs = outs
+        width = genes.shape[1]
+        clear = (spot[1] // gene_bit) % 2 == 0
+        left, right = genes[...].astype(jnp.float32), genes_got[...].astype(jnp.float32)
+        genes_out[:, :width] = jnp.where(clear, left, right).astype(jnp.bfloat16)
+        genes_out[:, width:] = jnp.where(clear, right, left).astype(jnp.bfloat16)
+    if link_bit:
+        clear = (spot[1] // link_bit) % 2 == 0
+        width = to_gene.shape[1] // 2
+        left, right = to_gene[:, :width], to_gene[:, width:]
+        outs[0][...] = jnp.where(clear, left, right)
+        outs[1][...] = jnp.where(clear, right, left)
+    else:
+        outs[0][...] = to_gene
+
+
+def step(spot, received, link_bit, gene_bit, totals, staying, genes=None):
+    rank, width = staying[0].shape
+    outs = [struct(*totals[0].shape)]
+    if gene_bit:
+        outs += [struct(rank, 2 * genes[0].shape[1], dtype=jnp.bfloat16)]
+    outs += [struct(rank, width // 2)] * 2 if link_bit else [struct(rank, width)]
+    values = [*totals, *staying, *(genes if gene_bit else ()), received]
+    return pl.pallas_call(
+        functools.partial(step_kernel, link_bit, gene_bit),
+        in_specs=[SMEM] + [VMEM] * len(values),
+        out_specs=[VMEM] * len(outs),
+        out_shape=outs,
+        compiler_params=PARAMS,
+    )(spot, *values)
+
+
 def next_sums_kernel(
-    link_scale, widths, orders, spot, table, mine, other, state, received, to_gene, genes, *refs
+    link_scale, widths, orders, spot, table, mine, other, state, received, to_gene, genes_mine, genes_other, *refs
 ):
-    sums, coded, beside, state_out, own, counts, sems = refs
-    copies = fetch(received, orders[0], counts, sems)
+    sums, coded, beside, state_out, own = refs
     half = received.shape[0]
     rank, features = sums.shape
     cells = own.shape[1]
@@ -509,11 +541,15 @@
         mine_now = jnp.where(place == orders[0][position], new[:, at : at + cells], mine_now)
     own[...] = mine_now
     high, rest = halved(new)
+    mine_low, other_low = genes_mine[...].astype(jnp.float32), genes_other[...].astype(jnp.float32)
+    genes = jnp.concatenate(
+        [jnp.where(first, mine_low, other_low), jnp.where(first, other_low, mine_low)], axis=1
+    )
     total = [None] * (2 * peak_blocks)
     for position, j in enumerate(orders[1]):
         for b in range(gene_blocks):
             at = (position * gene_blocks + b) * BLOCK
-            block = genes[:, at : at + BLOCK].astype(jnp.float32)
+            block = genes[:, at : at + BLOCK]
             row = (side * half + j) * gene_blocks + b
             for u in range(2 * peak_blocks):
                 column = (place + u // peak_blocks * half) * peak_blocks + u % peak_blocks
@@ -524,20 +560,15 @@
     links = jnp.concatenate(
         [jnp.where(side == 0, gene_links, nothing), jnp.where(side == 0, nothing, gene_links), *total], axis=1
     )
-    gram = gram_of(high, rest)
-    for copy in copies:
-        copy.wait()
-    products = jnp.dot(high, counts[...], preferred_element_type=jnp.float32)
-    finish_sums(products + link_scale * links, gram, sums, coded, beside)
+    counts = jnp.concatenate([received[j, 0:cells, 0:features] for j in orders[0]], axis=0)
+    products = jnp.dot(high, counts, preferred_element_type=jnp.float32)
+    finish_sums(products + link_scale * links, gram_of(high, rest), sums, coded, beside)
 
 
 def update_kernel(last, widths, orders, spot, table, sums, other, beside, beside_other, factors, received, *outs):
     half = received.shape[0]
     rank, features = sums.shape
     cells = received.shape[1] - rank // 4
-    if last:
-        *outs, counts, sems = outs
-        copies = fetch(received, orders[0], counts, sems)
     gene_width, peak_width = widths
     gene_blocks, peak_blocks = gene_width // BLOCK, peak_width // BLOCK
     side, place, core = spot[0], spot[1], spot[2]
@@ -555,12 +586,7 @@
     whole = jnp.concatenate(whole, axis=1)
     new = old * whole / below
     low = new.astype(jnp.bfloat16)
-    if last:
-        for copy in copies:
-            copy.wait()
-        cell_sums = across(low, counts[...])
-    else:
-        cell_sums = jnp.concatenate([across(low, received[j, 0:cells, 0:features]) for j in orders[0]], axis=1)
+    cell_sums = jnp.concatenate([across(low, received[j, 0:cells, 0:features]) for j in orders[0]], axis=1)
     gram_features = across(low, low)
     kept, sent, *outs = outs
     split = half // 2 * cells
@@ -654,11 +680,12 @@
     received = lax.all_to_all(sent, AXIS, 0, 0, axis_index_groups=halves, tiled=True)
     rows_other = flip(received[:, cells:, :features], 1)
     received_here = pltpu.with_memory_space_constraint(received, pltpu.VMEM)
+    above = -(-2 * width // BLOCK // 8) * 8
     codes, bounds = pl.pallas_call(
         codes_kernel,
         in_specs=[VMEM] * 2,
         out_specs=[VMEM] * 2,
-        out_shape=(struct(rank, width, dtype=jnp.int16), struct(rank, 2 * rank)),
+        out_shape=(struct(rank, width, dtype=jnp.int16), struct(above, 2 * rank)),
         compiler_params=PARAMS,
     )(gene_factor, peak_factor)
     rows = rank // 4
@@ -670,12 +697,10 @@
             VMEM,
         ],
         out_specs=VMEM,
-        out_shape=struct(rank + table_shape[0], table_shape[1]),
+        out_shape=struct(above + table_shape[0], table_shape[1]),
         compiler_params=PARAMS,
     )(received_here, bounds)
     aside_other = flip(aside, half)
-    codes_other = flip(codes, half)
-    aside_other, codes_other = lax.optimization_barrier((aside_other, codes_other))
     sums_shapes = (struct(rank, features), struct(rank, features, dtype=jnp.int16), struct(rank, 2 * rank))
     sums, gram, state = pl.pallas_call(
         functools.partial(first_sums_kernel, cell_order),
@@ -684,6 +709,8 @@
         out_shape=(struct(rank, features), struct(rank, rank), struct(rank, half * cells)),
         compiler_params=PARAMS,
     )(received_here)
+    codes, sums = lax.optimization_barrier((codes, sums))
+    codes_other = flip(codes, half)
     sums, coded, beside, link_table = pl.pallas_call(
         functools.partial(first_links_kernel, link_scale, widths),
         grid=(1,),
@@ -702,6 +729,7 @@
         compiler_params=PARAMS,
     )(spot, received_here, rows_other, aside, aside_other, sums, gram)
 
+    coded, beside, codes_other = lax.optimization_barrier((coded, beside, codes_other))
     factors = pl.pallas_call(
         twins_kernel,
         in_specs=[SMEM] + [VMEM] * 4,
@@ -711,8 +739,6 @@
     )(spot, gene_factor, peak_factor, codes_other, aside_other)
 
     split = half // 2 * cells
-    anywhere = pl.BlockSpec(memory_space=pl.ANY)
-    fetched = [pltpu.VMEM((half * cells, features), jnp.bfloat16), pltpu.SemaphoreType.DMA((half,))]
     for sweep_index in range(ROUNDS):
         last = sweep_index == ROUNDS - 1
         beside_other = flip(beside, half)
@@ -725,12 +751,11 @@
             outs += [struct(rank, gene_width, dtype=jnp.bfloat16)]
         kept, sent, *outs = pl.pallas_call(
             functools.partial(update_kernel, last, widths, (cell_order, link_order)),
-            in_specs=[SMEM] * 2 + [VMEM] * 5 + [anywhere if last else VMEM],
+            in_specs=[SMEM] * 2 + [VMEM] * 6,
             out_specs=[VMEM] * len(outs),
             out_shape=outs,
-            scratch_shapes=fetched if last else [],
             compiler_params=PARAMS,
-        )(spot, link_table, sums, other, beside, beside_other, factors, in_hbm(received) if last else received_here)
+        )(spot, link_table, sums, other, beside, beside_other, factors, received_here)
         if last:
             gene_out, peak_out = outs
             totals = kept + flip(sent, 1)
@@ -761,27 +786,25 @@
             )(spot, totals, flip(totals, cell_bits[-1]), own_cells)
             return cell_out, gene_out, peak_out
         factors, links_kept, links_sent, genes = outs
-        totals = kept + flip(sent, 1)
-        to_gene = links_kept + flip(links_sent, 1)
-        for cell_bit, link_bit, gene_bit in zip(cell_bits, link_bits, gene_bits):
-            left, right = jnp.split(to_gene, 2, axis=1)
-            clear = (me & link_bit) == 0
-            leaving, staying = jnp.where(clear, right, left), jnp.where(clear, left, right)
-            totals, leaving, genes = lax.optimization_barrier((totals, leaving, genes))
-            got = flip(totals, cell_bit), flip(leaving, link_bit), flip(genes, gene_bit)
-            got = lax.optimization_barrier(got)
-            totals = totals + got[0]
-            to_gene = staying + got[1]
-            genes = jnp.concatenate(in_order(gene_bit, genes, got[2]), axis=1)
-        genes = jnp.concatenate(in_order(1, genes, flip(genes, 1)), axis=1)
+        totals, staying, leaving = step(
+            spot, received_here, link_bits[0], 0, (kept, flip(sent, 1)), (links_kept, flip(links_sent, 1))
+        )
+        for i, bits in enumerate(zip(cell_bits, link_bits, gene_bits)):
+            going = lax.optimization_barrier((totals, leaving, genes))
+            got = lax.optimization_barrier(tuple(flip(value, bit) for value, bit in zip(going, bits)))
+            next_bit = link_bits[i + 1] if i + 1 < len(link_bits) else 0
+            totals, genes, staying, *leaving = step(
+                spot, received_here, next_bit, bits[2], (totals, got[0]), (staying, got[1]), (genes, got[2])
+            )
+            leaving = leaving[0] if next_bit else None
+        to_gene = staying
         sums, coded, beside, state, own_cells = pl.pallas_call(
             functools.partial(next_sums_kernel, link_scale, widths, (cell_order, gene_order)),
-            in_specs=[SMEM] * 2 + [VMEM] * 3 + [anywhere] + [VMEM] * 2,
+            in_specs=[SMEM] * 2 + [VMEM] * 7,
             out_specs=[VMEM] * 5,
-            scratch_shapes=fetched,
             out_shape=(*sums_shapes, struct(rank, half * cells), struct(rank, cells)),
             compiler_params=PARAMS,
-        )(spot, link_table, totals, flip(totals, 1), state, in_hbm(received), to_gene, genes)
+        )(spot, link_table, totals, flip(totals, 1), state, received_here, to_gene, genes, flip(genes, 1))
 
 
 def shards(rna_counts, atac_counts, cell_factor, gene_factor, peak_factor, link_gene, *links):

time: 138 us -> 136 us (0.986)
    pallas_call x0 -> x4, Pallas kernels: none -> 2.32 us  [step(): pl.pallas_call(functools.partial(step_kernel, link_bit, gene_bit), in_spe...]
    pallas_call x2, Pallas kernels: 7.07 us -> 5.02 us  [shards_blocks(): pl.pallas_call(functools.partial(update_kernel, last, widths, (cell_order...]
    pallas_call x1, Pallas kernels: 4.63 us -> 3.05 us  [shards_blocks(): pl.pallas_call(functools.partial(next_sums_kernel, link_scale, widths, (c...]
  transfers between devices with their start and end apart: 25 -> 25, of which waited for: 19 -> 17; matrix products, arithmetic and copies ran while one was open for 0% -> 0% of each run, Pallas kernels for 1% -> 3%
where the time goes in v7:
time: 136 us
  blocking collectives  49.8 us (37%)
  waiting for transfers between devices  43.8 us (32%)
  starting transfers between devices  20.7 us (15%)
  Pallas kernels  19.7 us (14%)
  between operations  1.58 us (1%)
    all_to_all x1, blocking collectives, shards_blocks(): lax.all_to_all(sent, AXIS, 0, 0, axis_index_groups=halves, tiled=True)  49.8 us
    ppermute x25, waiting for transfers between devices, flip(): return lax.ppermute(value, AXIS, [(i, i ^ bit) for i in range(count)])  43.8 us
    ppermute x25, starting transfers between devices, flip(): return lax.ppermute(value, AXIS, [(i, i ^ bit) for i in range(count)])  20.7 us
    pallas_call x2, Pallas kernels, shards_blocks(): pl.pallas_call(functools.partial(update_kernel, last, widths, (cell_order...  5.02 us
    pallas_call x1, Pallas kernels, parcels(): pl.pallas_call(parcels_kernel, grid=(steps,), in_specs=[SMEM, columns(gen...  3.45 us
    pallas_call x1, Pallas kernels, shards_blocks(): pl.pallas_call(functools.partial(next_sums_kernel, link_scale, widths, (c...  3.05 us
  transfers between devices with their start and end apart: 25, of which 17 were waited for; matrix products, arithmetic and copies ran while one was open for 0% of the time, Pallas kernels for 3%

profile of v7, /device:TPU:0, one launch (start us, length us, event | category | flops | bytes accessed | tf_op | source)
XLA Modules:
  0.0 135.8 jit_solution(9547013353868579345)
XLA Ops:
  1.4 3.4 %shard_map.112 = bf16[16,80,1408]{2,1,0:T(8,128)(2,1)S(1)} custom-call(s32[4]{0:T(128)S(1)} %pad_add_fusion.spot, bf16[64,4096]{1,0:T(8,128)(2,1)} %rna_1.1, bf16[64,4096]{1,0:T(8,128)(2,1)} %rna_1.1, bf16[64,16384]{1,0:T(8,128)(2,1)} %atac_1.1, bf16[64,16384]{1,0:T(8,128)(2,1)} %atac_1.1, f32[64,64]{1,0:T(8,128)} %cell.1, f32[64,128]{1,0:T(8,128)} %gene.5, ...), custom_call_target="tpu_custom_call" | custom-call | tf_op jit(solution)/shard_map/pallas_call | solution.py:383
  4.9 49.8 %all_to_all.5.received_slots.received.mine.refs_0_.refs_2_ = bf16[16,80,1408]{2,1,0:T(8,128)(2,1)S(1)} all-to-all(bf16[16,80,1408]{2,1,0:T(8,128)(2,1)S(1)} %shard_map.112), channel_id=1, replica_groups={{0,1,2,3,4,5,6,7,8,9,10,11,12,13,14,15},{16,17,18,19,20,21,22,23,24,25,..., dimensions={0} | all-to-all | bytes 7208960 | tf_op jit(solution)/shard_map/all_to_all | solution.py:680
  55.0 0.8 shard_map.115
  55.9 2.7 %collective-permute-start.2 = (s16[64,640]{1,0:T(8,128)(2,1)S(1)}, s16[64,640]{1,0:T(8,128)(2,1)S(1)}, u32[]{:S(2)}, u32[]{:S(2)}) collective-permute-start(s16[64,640]{1,0:T(8,128)(2,1)S(1)} %get-tuple-element.72), channel_id=1, source_target_pairs={{0,16},{1,17},{2,18},{3,19},{4,20},{5,21},{6,22},{7,23},{8,24},{9,... | collective-permute-start | bytes 245768 | tf_op jit(solution)/shard_map/ppermute | solution.py:22
  59.0 5.4 %collective-permute-done.1.aside_other.beside = f32[48,128]{1,0:T(8,128)S(1)} collective-permute-done((f32[48,128]{1,0:T(8,128)S(1)}, f32[48,128]{1,0:T(8,128)S(1)}, u32[]{:S(2)}, u32[]{:S(2)}) %collective-permute-start.1) | collective-permute-done | bytes 24608 | tf_op jit(solution)/shard_map/ppermute | solution.py:22
  64.5 2.5 %shard_map.116 = (f32[64,1280]{1,0:T(8,128)S(1)}, s16[64,1280]{1,0:T(8,128)(2,1)S(1)}, f32[64,128]{1,0:T(8,128)S(1)}, f32[32,128]{1,0:T(8,128)S(1)}) custom-call(s32[4]{0:T(128)S(1)} %pad_add_fusion.spot, bf16[16,80,1408]{2,1,0:T(8,128)(2,1)S(1)} %all_to_all.5.received_slots.received.mine.refs_0_.refs_2_, ...), custom_call_target="tpu_custom_call" | custom-call | tf_op jit(solution)/shard_map/pallas_call | solution.py:714
  67.4 2.5 %collective-permute-start.4 = (f32[64,128]{1,0:T(8,128)S(1)}, f32[64,128]{1,0:T(8,128)S(1)}, u32[]{:S(2)}, u32[]{:S(2)}) collective-permute-start(f32[64,128]{1,0:T(8,128)S(1)} %get-tuple-element.74.beside), channel_id=1, source_target_pairs={{0,16},{1,17},{2,18},{3,19},{4,20},{5,21},{6,22},{7,23},{8,24},{9,... | collective-permute-start | bytes 98312 | tf_op jit(solution)/shard_map/ppermute | solution.py:22
  70.0 0.8 shard_map.117.factors
  70.8 7.8 %collective-permute-done.4.beside_other = f32[64,128]{1,0:T(8,128)S(1)} collective-permute-done((f32[64,128]{1,0:T(8,128)S(1)}, f32[64,128]{1,0:T(8,128)S(1)}, u32[]{:S(2)}, u32[]{:S(2)}) %collective-permute-start.4) | collective-permute-done | bytes 32800 | tf_op jit(solution)/shard_map/ppermute | solution.py:22
  78.6 2.5 %shard_map.118 = (f32[72,512]{1,0:T(8,128)S(1)}, f32[72,512]{1,0:T(8,128)S(1)}, f32[64,1280]{1,0:T(8,128)S(1)}, f32[64,1024]{1,0:T(8,128)S(1)}, f32[64,1024]{1,0:T(8,128)S(1)}, /*index=5*/bf16[64,128]{1,0:T(8,128)(2,1)S(1)}) custom-call(s32[4]{0:T(128)S(1)} %pad_add_fusion.spot, f32[32,128]{1,0:T(8,128)S(1)} %get-tuple-element.68.table, ...), custom_call_target="tpu_custom_call" | custom-call | tf_op jit(solution)/shard_map/pallas_call | solution.py:752
  81.6 1.2 collective-permute-done.5.totals_got
  84.1 3.7 %collective-permute-done.9.refs_1_ = bf16[64,128]{1,0:T(8,128)(2,1)S(1)} collective-permute-done((bf16[64,128]{1,0:T(8,128)(2,1)S(1)}, bf16[64,128]{1,0:T(8,128)(2,1)S(1)}, u32[]{:S(2)}, u32[]{:S(2)}) %collective-permute-start.9) | collective-permute-done | bytes 16416 | tf_op jit(solution)/shard_map/ppermute | solution.py:22
  87.8 1.3 collective-permute-done.8.staying_got
  90.2 1.8 %collective-permute-start.12 = (bf16[64,256]{1,0:T(8,128)(2,1)S(1)}, bf16[64,256]{1,0:T(8,128)(2,1)S(1)}, u32[]{:S(2)}, u32[]{:S(2)}) collective-permute-start(bf16[64,256]{1,0:T(8,128)(2,1)S(1)} %get-tuple-element.95.refs_0_), channel_id=1, source_target_pairs={{0,2},{1,3},{2,0},{3,1},{4,6},{5,7},{6,4},{7,5},{8,10},{9,11},{10,... | collective-permute-start | bytes 98312 | tf_op jit(solution)/shard_map/ppermute | solution.py:22
  92.0 2.2 %collective-permute-done.12.refs_1_ = bf16[64,256]{1,0:T(8,128)(2,1)S(1)} collective-permute-done((bf16[64,256]{1,0:T(8,128)(2,1)S(1)}, bf16[64,256]{1,0:T(8,128)(2,1)S(1)}, u32[]{:S(2)}, u32[]{:S(2)}) %collective-permute-start.12) | collective-permute-done | bytes 32800 | tf_op jit(solution)/shard_map/ppermute | solution.py:22
  94.4 0.8 collective-permute-done.10.totals_got
  95.8 1.0 collective-permute-start.13
  96.7 1.9 %collective-permute-start.15 = (bf16[64,512]{1,0:T(8,128)(2,1)S(1)}, bf16[64,512]{1,0:T(8,128)(2,1)S(1)}, u32[]{:S(2)}, u32[]{:S(2)}) collective-permute-start(bf16[64,512]{1,0:T(8,128)(2,1)S(1)} %get-tuple-element.105.refs_0_), channel_id=1, source_target_pairs={{0,4},{1,5},{2,6},{3,7},{4,0},{5,1},{6,2},{7,3},{8,12},{9,13},{10,... | collective-permute-start | bytes 196616 | tf_op jit(solution)/shard_map/ppermute | solution.py:22
  98.7 1.4 %collective-permute-start.14 = (f32[64,128]{1,0:T(8,128)S(1)}, f32[64,128]{1,0:T(8,128)S(1)}, u32[]{:S(2)}, u32[]{:S(2)}) collective-permute-start(f32[64,128]{1,0:T(8,128)S(1)} %get-tuple-element.104), channel_id=1, source_target_pairs={{0,2},{1,3},{2,0},{3,1},{4,6},{5,7},{6,4},{7,5},{8,10},{9,11},{10,... | collective-permute-start | bytes 98312 | tf_op jit(solution)/shard_map/ppermute | solution.py:22
  100.1 2.5 %collective-permute-done.14.staying_got = f32[64,128]{1,0:T(8,128)S(1)} collective-permute-done((f32[64,128]{1,0:T(8,128)S(1)}, f32[64,128]{1,0:T(8,128)S(1)}, u32[]{:S(2)}, u32[]{:S(2)}) %collective-permute-start.14) | collective-permute-done | bytes 32800 | tf_op jit(solution)/shard_map/ppermute | solution.py:22
  102.6 0.6 shard_map.122
  103.8 1.0 collective-permute-done.17.genes_other
  104.8 3.0 %shard_map.123 = (f32[64,1280]{1,0:T(8,128)S(1)}, s16[64,1280]{1,0:T(8,128)(2,1)S(1)}, f32[64,128]{1,0:T(8,128)S(1)}, f32[64,1024]{1,0:T(8,128)}, f32[64,64]{1,0:T(8,128)S(1)}) custom-call(s32[4]{0:T(128)S(1)} %pad_add_fusion.spot, f32[32,128]{1,0:T(8,128)S(1)} %get-tuple-element.68.table, f32[72,512]{1,0:T(8,128)S(1)} %get-tuple-element.110.mine, ...), custom_call_target="tpu_custom_call" | custom-call | tf_op jit(solution)/shard_map/pallas_call | solution.py:801
  108.3 2.5 %collective-permute-start.19 = (f32[64,128]{1,0:T(8,128)S(1)}, f32[64,128]{1,0:T(8,128)S(1)}, u32[]{:S(2)}, u32[]{:S(2)}) collective-permute-start(f32[64,128]{1,0:T(8,128)S(1)} %get-tuple-element.116.beside), channel_id=1, source_target_pairs={{0,16},{1,17},{2,18},{3,19},{4,20},{5,21},{6,22},{7,23},{8,24},{9,... | collective-permute-start | bytes 98312 | tf_op jit(solution)/shard_map/ppermute | solution.py:22
  110.8 9.1 %collective-permute-done.19.beside_other = f32[64,128]{1,0:T(8,128)S(1)} collective-permute-done((f32[64,128]{1,0:T(8,128)S(1)}, f32[64,128]{1,0:T(8,128)S(1)}, u32[]{:S(2)}, u32[]{:S(2)}) %collective-permute-start.19) | collective-permute-done | bytes 32800 | tf_op jit(solution)/shard_map/ppermute | solution.py:22
  119.9 2.6 %shard_map.124 = (f32[72,512]{1,0:T(8,128)S(1)}, f32[72,512]{1,0:T(8,128)S(1)}, f32[64,128]{1,0:T(8,128)}, f32[64,512]{1,0:T(8,128)}) custom-call(s32[4]{0:T(128)S(1)} %pad_add_fusion.spot, f32[32,128]{1,0:T(8,128)S(1)} %get-tuple-element.68.table, f32[64,1280]{1,0:T(8,128)S(1)} %get-tuple-element.114.sums, ...), custom_call_target="tpu_custom_call" | custom-call | tf_op jit(solution)/shard_map/pallas_call | solution.py:752
  122.5 1.3 collective-permute-done.20
  124.0 1.6 %collective-permute-start.23 = (f32[96,128]{1,0:T(8,128)S(1)}, f32[96,128]{1,0:T(8,128)S(1)}, u32[]{:S(2)}, u32[]{:S(2)}) collective-permute-start(f32[96,128]{1,0:T(8,128)S(1)} %constant_dynamic-update-slice_fusion.15), channel_id=1, source_target_pairs={{0,6},{1,7},{2,4},{3,5},{4,2},{5,3},{6,0},{7,1},{8,14},{9,15},{10,... | collective-permute-start | bytes 147464 | tf_op jit(solution)/shard_map/ppermute | solution.py:22
  126.1 1.5 %collective-permute-start.22 = (f32[96,128]{1,0:T(8,128)S(1)}, f32[96,128]{1,0:T(8,128)S(1)}, u32[]{:S(2)}, u32[]{:S(2)}) collective-permute-start(f32[96,128]{1,0:T(8,128)S(1)} %get-tuple-element.123), channel_id=1, source_target_pairs={{0,4},{1,5},{2,6},{3,7},{4,0},{5,1},{6,2},{7,3},{8,12},{9,13},{10,... | collective-permute-start | bytes 147464 | tf_op jit(solution)/shard_map/ppermute | solution.py:22
  127.6 1.7 %collective-permute-done.23 = f32[96,128]{1,0:T(8,128)S(1)} collective-permute-done((f32[96,128]{1,0:T(8,128)S(1)}, f32[96,128]{1,0:T(8,128)S(1)}, u32[]{:S(2)}, u32[]{:S(2)}) %collective-permute-start.23) | collective-permute-done | bytes 49184 | tf_op jit(solution)/shard_map/ppermute | solution.py:22
  130.3 4.1 %collective-permute-done.24.other = f32[96,128]{1,0:T(8,128)S(1)} collective-permute-done((f32[96,128]{1,0:T(8,128)S(1)}, f32[96,128]{1,0:T(8,128)S(1)}, u32[]{:S(2)}, u32[]{:S(2)}) %collective-permute-start.24) | collective-permute-done | bytes 49184 | tf_op jit(solution)/shard_map/ppermute | solution.py:22
  134.4 1.4 %shard_map.125 = f32[64,64]{1,0:T(8,128)} custom-call(s32[4]{0:T(128)S(1)} %pad_add_fusion.spot, f32[96,128]{1,0:T(8,128)S(1)} %add_add_fusion.mine, f32[96,128]{1,0:T(8,128)S(1)} %collective-permute-done.24.other, f32[64,64]{1,0:T(8,128)S(1)} %get-tuple-element.120.old), custom_call_target="tpu_custom_call" | custom-call | tf_op jit(solution)/shard_map/pallas_call | solution.py:780
  (52 shorter events, 7.6 us)
Async XLA Ops:
  4.8 49.9 %copy-start = (f32[64,512]{1,0:T(8,128)S(1)}, f32[64,512]{1,0:T(8,128)}, u32[]{:S(2)}) copy-start(f32[64,512]{1,0:T(8,128)} %peak.5) | copy-start | bytes 393220
  4.9 49.9 %copy-start.1 = (f32[64,128]{1,0:T(8,128)S(1)}, f32[64,128]{1,0:T(8,128)}, u32[]{:S(2)}) copy-start(f32[64,128]{1,0:T(8,128)} %gene.5) | copy-start | bytes 98308
  54.7 9.8 %collective-permute-start = (bf16[16,16,1280]{2,1,0:T(8,128)(2,1)S(1)}, bf16[16,16,1280]{2,1,0:T(8,128)(2,1)S(1)}, u32[]{:S(2)}, u32[]{:S(2)}) collective-permute-start(bf16[16,16,1280]{2,1,0:T(8,128)(2,1)S(1)} %slice.14), channel_id=1, source_target_pairs={{0,1},{1,0},{2,3},{3,2},{4,5},{5,4},{6,7},{7,6},{8,9},{9,8},{10,11... | collective-permute-start | bytes 1966088 | tf_op jit(solution)/shard_map/ppermute | solution.py:22
  55.9 11.1 %collective-permute-start.2 = (s16[64,640]{1,0:T(8,128)(2,1)S(1)}, s16[64,640]{1,0:T(8,128)(2,1)S(1)}, u32[]{:S(2)}, u32[]{:S(2)}) collective-permute-start(s16[64,640]{1,0:T(8,128)(2,1)S(1)} %get-tuple-element.72), channel_id=1, source_target_pairs={{0,16},{1,17},{2,18},{3,19},{4,20},{5,21},{6,22},{7,23},{8,24},{9,... | collective-permute-start | bytes 245768 | tf_op jit(solution)/shard_map/ppermute | solution.py:22
  58.7 5.8 %collective-permute-start.1 = (f32[48,128]{1,0:T(8,128)S(1)}, f32[48,128]{1,0:T(8,128)S(1)}, u32[]{:S(2)}, u32[]{:S(2)}) collective-permute-start(f32[48,128]{1,0:T(8,128)S(1)} %shard_map.114.aside), channel_id=1, source_target_pairs={{0,16},{1,17},{2,18},{3,19},{4,20},{5,21},{6,22},{7,23},{8,24},{9,... | collective-permute-start | bytes 73736 | tf_op jit(solution)/shard_map/ppermute | solution.py:22
  67.0 11.6 %collective-permute-start.3 = (s16[64,1280]{1,0:T(8,128)(2,1)S(1)}, s16[64,1280]{1,0:T(8,128)(2,1)S(1)}, u32[]{:S(2)}, u32[]{:S(2)}) collective-permute-start(s16[64,1280]{1,0:T(8,128)(2,1)S(1)} %get-tuple-element.73), channel_id=1, source_target_pairs={{0,16},{1,17},{2,18},{3,19},{4,20},{5,21},{6,22},{7,23},{8,24},{9,... | collective-permute-start | bytes 491528 | tf_op jit(solution)/shard_map/ppermute | solution.py:22
  67.4 11.1 %collective-permute-start.4 = (f32[64,128]{1,0:T(8,128)S(1)}, f32[64,128]{1,0:T(8,128)S(1)}, u32[]{:S(2)}, u32[]{:S(2)}) collective-permute-start(f32[64,128]{1,0:T(8,128)S(1)} %get-tuple-element.74.beside), channel_id=1, source_target_pairs={{0,16},{1,17},{2,18},{3,19},{4,20},{5,21},{6,22},{7,23},{8,24},{9,... | collective-permute-start | bytes 98312 | tf_op jit(solution)/shard_map/ppermute | solution.py:22
  81.1 1.8 %collective-permute-start.6 = (f32[64,1024]{1,0:T(8,128)S(1)}, f32[64,1024]{1,0:T(8,128)S(1)}, u32[]{:S(2)}, u32[]{:S(2)}) collective-permute-start(f32[64,1024]{1,0:T(8,128)S(1)} %get-tuple-element.79), channel_id=1, source_target_pairs={{0,1},{1,0},{2,3},{3,2},{4,5},{5,4},{6,7},{7,6},{8,9},{9,8},{10,11... | collective-permute-start | bytes 786440 | tf_op jit(solution)/shard_map/ppermute | solution.py:22
  81.1 1.7 %collective-permute-start.5 = (f32[72,512]{1,0:T(8,128)S(1)}, f32[72,512]{1,0:T(8,128)S(1)}, u32[]{:S(2)}, u32[]{:S(2)}) collective-permute-start(f32[72,512]{1,0:T(8,128)S(1)} %get-tuple-element.77), channel_id=1, source_target_pairs={{0,1},{1,0},{2,3},{3,2},{4,5},{5,4},{6,7},{7,6},{8,9},{9,8},{10,11... | collective-permute-start | bytes 442376 | tf_op jit(solution)/shard_map/ppermute | solution.py:22
  83.5 6.0 %collective-permute-start.7 = (f32[72,512]{1,0:T(8,128)S(1)}, f32[72,512]{1,0:T(8,128)S(1)}, u32[]{:S(2)}, u32[]{:S(2)}) collective-permute-start(f32[72,512]{1,0:T(8,128)S(1)} %get-tuple-element.83.totals), channel_id=1, source_target_pairs={{0,2},{1,3},{2,0},{3,1},{4,6},{5,7},{6,4},{7,5},{8,10},{9,11},{10,... | collective-permute-start | bytes 442376 | tf_op jit(solution)/shard_map/ppermute | solution.py:22
  83.5 5.6 %collective-permute-start.8 = (f32[64,512]{1,0:T(8,128)S(1)}, f32[64,512]{1,0:T(8,128)S(1)}, u32[]{:S(2)}, u32[]{:S(2)}) collective-permute-start(f32[64,512]{1,0:T(8,128)S(1)} %get-tuple-element.84), channel_id=1, source_target_pairs={{0,4},{1,5},{2,6},{3,7},{4,0},{5,1},{6,2},{7,3},{8,12},{9,13},{10,... | collective-permute-start | bytes 393224 | tf_op jit(solution)/shard_map/ppermute | solution.py:22
  84.1 3.7 %collective-permute-start.9 = (bf16[64,128]{1,0:T(8,128)(2,1)S(1)}, bf16[64,128]{1,0:T(8,128)(2,1)S(1)}, u32[]{:S(2)}, u32[]{:S(2)}) collective-permute-start(bf16[64,128]{1,0:T(8,128)(2,1)S(1)} %get-tuple-element.85.refs_0_), channel_id=1, source_target_pairs={{0,8},{1,9},{2,10},{3,11},{4,12},{5,13},{6,14},{7,15},{8,0},{9,1},... | collective-permute-start | bytes 49160 | tf_op jit(solution)/shard_map/ppermute | solution.py:22
  90.0 5.2 %collective-permute-start.10 = (f32[72,512]{1,0:T(8,128)S(1)}, f32[72,512]{1,0:T(8,128)S(1)}, u32[]{:S(2)}, u32[]{:S(2)}) collective-permute-start(f32[72,512]{1,0:T(8,128)S(1)} %get-tuple-element.93.totals), channel_id=1, source_target_pairs={{0,4},{1,5},{2,6},{3,7},{4,0},{5,1},{6,2},{7,3},{8,12},{9,13},{10,... | collective-permute-start | bytes 442376 | tf_op jit(solution)/shard_map/ppermute | solution.py:22
  90.1 4.3 %collective-permute-start.11 = (f32[64,256]{1,0:T(8,128)S(1)}, f32[64,256]{1,0:T(8,128)S(1)}, u32[]{:S(2)}, u32[]{:S(2)}) collective-permute-start(f32[64,256]{1,0:T(8,128)S(1)} %get-tuple-element.94), channel_id=1, source_target_pairs={{0,8},{1,9},{2,10},{3,11},{4,12},{5,13},{6,14},{7,15},{8,0},{9,1},... | collective-permute-start | bytes 196616 | tf_op jit(solution)/shard_map/ppermute | solution.py:22
  90.2 4.0 %collective-permute-start.12 = (bf16[64,256]{1,0:T(8,128)(2,1)S(1)}, bf16[64,256]{1,0:T(8,128)(2,1)S(1)}, u32[]{:S(2)}, u32[]{:S(2)}) collective-permute-start(bf16[64,256]{1,0:T(8,128)(2,1)S(1)} %get-tuple-element.95.refs_0_), channel_id=1, source_target_pairs={{0,2},{1,3},{2,0},{3,1},{4,6},{5,7},{6,4},{7,5},{8,10},{9,11},{10,... | collective-permute-start | bytes 98312 | tf_op jit(solution)/shard_map/ppermute | solution.py:22
  95.8 6.8 %collective-permute-start.13 = (f32[72,512]{1,0:T(8,128)S(1)}, f32[72,512]{1,0:T(8,128)S(1)}, u32[]{:S(2)}, u32[]{:S(2)}) collective-permute-start(f32[72,512]{1,0:T(8,128)S(1)} %get-tuple-element.103.totals), channel_id=1, source_target_pairs={{0,8},{1,9},{2,10},{3,11},{4,12},{5,13},{6,14},{7,15},{8,0},{9,1},... | collective-permute-start | bytes 442376 | tf_op jit(solution)/shard_map/ppermute | solution.py:22
  96.7 5.9 %collective-permute-start.15 = (bf16[64,512]{1,0:T(8,128)(2,1)S(1)}, bf16[64,512]{1,0:T(8,128)(2,1)S(1)}, u32[]{:S(2)}, u32[]{:S(2)}) collective-permute-start(bf16[64,512]{1,0:T(8,128)(2,1)S(1)} %get-tuple-element.105.refs_0_), channel_id=1, source_target_pairs={{0,4},{1,5},{2,6},{3,7},{4,0},{5,1},{6,2},{7,3},{8,12},{9,13},{10,... | collective-permute-start | bytes 196616 | tf_op jit(solution)/shard_map/ppermute | solution.py:22
  98.7 3.9 %collective-permute-start.14 = (f32[64,128]{1,0:T(8,128)S(1)}, f32[64,128]{1,0:T(8,128)S(1)}, u32[]{:S(2)}, u32[]{:S(2)}) collective-permute-start(f32[64,128]{1,0:T(8,128)S(1)} %get-tuple-element.104), channel_id=1, source_target_pairs={{0,2},{1,3},{2,0},{3,1},{4,6},{5,7},{6,4},{7,5},{8,10},{9,11},{10,... | collective-permute-start | bytes 98312 | tf_op jit(solution)/shard_map/ppermute | solution.py:22
  103.2 1.6 %collective-permute-start.16 = (f32[72,512]{1,0:T(8,128)S(1)}, f32[72,512]{1,0:T(8,128)S(1)}, u32[]{:S(2)}, u32[]{:S(2)}) collective-permute-start(f32[72,512]{1,0:T(8,128)S(1)} %get-tuple-element.110.mine), channel_id=1, source_target_pairs={{0,1},{1,0},{2,3},{3,2},{4,5},{5,4},{6,7},{7,6},{8,9},{9,8},{10,11... | collective-permute-start | bytes 442376 | tf_op jit(solution)/shard_map/ppermute | solution.py:22
  103.3 1.5 %collective-permute-start.17 = (bf16[64,1024]{1,0:T(8,128)(2,1)S(1)}, bf16[64,1024]{1,0:T(8,128)(2,1)S(1)}, u32[]{:S(2)}, u32[]{:S(2)}) collective-permute-start(bf16[64,1024]{1,0:T(8,128)(2,1)S(1)} %get-tuple-element.113.genes_mine), channel_id=1, source_target_pairs={{0,1},{1,0},{2,3},{3,2},{4,5},{5,4},{6,7},{7,6},{8,9},{9,8},{10,11... | collective-permute-start | bytes 393224 | tf_op jit(solution)/shard_map/ppermute | solution.py:22
  107.9 12.0 %collective-permute-start.18 = (s16[64,1280]{1,0:T(8,128)(2,1)S(1)}, s16[64,1280]{1,0:T(8,128)(2,1)S(1)}, u32[]{:S(2)}, u32[]{:S(2)}) collective-permute-start(s16[64,1280]{1,0:T(8,128)(2,1)S(1)} %get-tuple-element.115), channel_id=1, source_target_pairs={{0,16},{1,17},{2,18},{3,19},{4,20},{5,21},{6,22},{7,23},{8,24},{9,... | collective-permute-start | bytes 491528 | tf_op jit(solution)/shard_map/ppermute | solution.py:22
  108.3 11.6 %collective-permute-start.19 = (f32[64,128]{1,0:T(8,128)S(1)}, f32[64,128]{1,0:T(8,128)S(1)}, u32[]{:S(2)}, u32[]{:S(2)}) collective-permute-start(f32[64,128]{1,0:T(8,128)S(1)} %get-tuple-element.116.beside), channel_id=1, source_target_pairs={{0,16},{1,17},{2,18},{3,19},{4,20},{5,21},{6,22},{7,23},{8,24},{9,... | collective-permute-start | bytes 98312 | tf_op jit(solution)/shard_map/ppermute | solution.py:22
  122.5 1.4 %collective-permute-start.20 = (f32[72,512]{1,0:T(8,128)S(1)}, f32[72,512]{1,0:T(8,128)S(1)}, u32[]{:S(2)}, u32[]{:S(2)}) collective-permute-start(f32[72,512]{1,0:T(8,128)S(1)} %get-tuple-element.119), channel_id=1, source_target_pairs={{0,1},{1,0},{2,3},{3,2},{4,5},{5,4},{6,7},{7,6},{8,9},{9,8},{10,11... | collective-permute-start | bytes 442376 | tf_op jit(solution)/shard_map/ppermute | solution.py:22
  124.0 5.3 %collective-permute-start.23 = (f32[96,128]{1,0:T(8,128)S(1)}, f32[96,128]{1,0:T(8,128)S(1)}, u32[]{:S(2)}, u32[]{:S(2)}) collective-permute-start(f32[96,128]{1,0:T(8,128)S(1)} %constant_dynamic-update-slice_fusion.15), channel_id=1, source_target_pairs={{0,6},{1,7},{2,4},{3,5},{4,2},{5,3},{6,0},{7,1},{8,14},{9,15},{10,... | collective-permute-start | bytes 147464 | tf_op jit(solution)/shard_map/ppermute | solution.py:22
  125.6 4.1 %collective-permute-start.21 = (f32[96,128]{1,0:T(8,128)S(1)}, f32[96,128]{1,0:T(8,128)S(1)}, u32[]{:S(2)}, u32[]{:S(2)}) collective-permute-start(f32[96,128]{1,0:T(8,128)S(1)} %get-tuple-element.136), channel_id=1, source_target_pairs={{0,2},{1,3},{2,0},{3,1},{4,6},{5,7},{6,4},{7,5},{8,10},{9,11},{10,... | collective-permute-start | bytes 147464 | tf_op jit(solution)/shard_map/ppermute | solution.py:22
  126.1 4.1 %collective-permute-start.22 = (f32[96,128]{1,0:T(8,128)S(1)}, f32[96,128]{1,0:T(8,128)S(1)}, u32[]{:S(2)}, u32[]{:S(2)}) collective-permute-start(f32[96,128]{1,0:T(8,128)S(1)} %get-tuple-element.123), channel_id=1, source_target_pairs={{0,4},{1,5},{2,6},{3,7},{4,0},{5,1},{6,2},{7,3},{8,12},{9,13},{10,... | collective-permute-start | bytes 147464 | tf_op jit(solution)/shard_map/ppermute | solution.py:22
  130.2 4.2 %collective-permute-start.24 = (f32[96,128]{1,0:T(8,128)S(1)}, f32[96,128]{1,0:T(8,128)S(1)}, u32[]{:S(2)}, u32[]{:S(2)}) collective-permute-start(f32[96,128]{1,0:T(8,128)S(1)} %add_add_fusion.mine), channel_id=1, source_target_pairs={{0,8},{1,9},{2,10},{3,11},{4,12},{5,13},{6,14},{7,15},{8,0},{9,1},... | collective-permute-start | bytes 147464 | tf_op jit(solution)/shard_map/ppermute | solution.py:22

commit v8 on v7

--- a/solution.py
+++ b/solution.py
@@ -11,6 +11,8 @@
 ROUNDS = 2
 EPSILON = 1e-06
 CODES = 65535.0
+DIGIT = 32768.0
+TINY = 1e-30
 AXIS = "cells"
 PARAMS = pltpu.CompilerParams(vmem_limit_bytes=14 * 1024 * 1024)
 SMEM = pl.BlockSpec(memory_space=pltpu.SMEM)
@@ -410,22 +412,47 @@
     state[...] = high.astype(jnp.float32) + rest.astype(jnp.float32)
 
 
-def finish_sums(sums_value, gram_value, sums, coded, beside):
+def digits(values):
+    top = jnp.maximum(jnp.max(values, axis=1, keepdims=True), TINY)
+    power = jnp.floor(jnp.log2(top)) + 1.0
+    scaled = values * jnp.exp2(-power) * DIGIT
+    high = jnp.minimum(jnp.floor(scaled), DIGIT - 1)
+    low = jnp.clip(jnp.floor((scaled - high) * DIGIT), 0.0, DIGIT - 1)
+    return [high, low, power]
+
+
+def from_digits(high, low, power):
+    return (high + low / DIGIT) / DIGIT * jnp.exp2(power)
+
+
+def finish_sums(sums_value, gram_value, sums, message):
     rank, features = sums_value.shape
-    least, step = [], []
+    least, top = [], []
     for b in range(features // BLOCK):
         group = sums_value[:, b * BLOCK : (b + 1) * BLOCK]
         sums[:, b * BLOCK : (b + 1) * BLOCK] = group
         code, low, per = encode(group)
-        coded[:, b * BLOCK : (b + 1) * BLOCK] = code
+        message[:, b * BLOCK : (b + 1) * BLOCK] = code
         least.append(low)
-        step.append(per)
-    pad = jnp.zeros((rank, beside.shape[1] - rank - 2 * len(least)), jnp.float32)
-    beside[...] = jnp.concatenate([gram_value, *least, *step, pad], axis=1)
+        top.append(low + per * CODES)
+    beside = digits(gram_value) + digits(jnp.concatenate(least + top, axis=1))
+    size = sum(part.shape[1] for part in beside)
+    beside.append(jnp.zeros((rank, message.shape[1] - features - size), jnp.float32))
+    message[:, features:] = jnp.concatenate(beside, axis=1).astype(jnp.int32).astype(jnp.int16)
+
+
+def read_beside(message, features, rank):
+    groups = features // BLOCK
+    beside = message[:, features:].astype(jnp.int32).astype(jnp.float32)
+    parts, at = [], 0
+    for size in (rank, rank, 1, 2 * groups, 2 * groups, 1):
+        parts.append(beside[:, at : at + size])
+        at += size
+    return from_digits(*parts[:3]), from_digits(*parts[3:])
 
 
 def first_links_kernel(
-    link_scale, widths, spot, mine, other, aside, aside_other, sums_in, gram, sums, coded, beside, table, sem, table_smem
+    link_scale, widths, spot, mine, other, aside, aside_other, sums_in, gram, sums, message, table, sem, table_smem
 ):
     half = mine.shape[0]
     rank, features = sums_in.shape
@@ -465,7 +492,7 @@
     ahead, behind = links[: rank // 2], links[rank // 2 :]
     first = core == 0
     links = jnp.concatenate([jnp.where(first, ahead, behind), jnp.where(first, behind, ahead)], axis=0)
-    finish_sums(sums_in[...] + link_scale * links, gram[...], sums, coded, beside)
+    finish_sums(sums_in[...] + link_scale * links, gram[...], sums, message)
 
 
 def gram_rows(gram, lanes):
@@ -522,7 +549,7 @@
 def next_sums_kernel(
     link_scale, widths, orders, spot, table, mine, other, state, received, to_gene, genes_mine, genes_other, *refs
 ):
-    sums, coded, beside, state_out, own = refs
+    sums, message, gram, state_out, own = refs
     half = received.shape[0]
     rank, features = sums.shape
     cells = own.shape[1]
@@ -562,10 +589,11 @@
     )
     counts = jnp.concatenate([received[j, 0:cells, 0:features] for j in orders[0]], axis=0)
     products = jnp.dot(high, counts, preferred_element_type=jnp.float32)
-    finish_sums(products + link_scale * links, gram_of(high, rest), sums, coded, beside)
-
-
-def update_kernel(last, widths, orders, spot, table, sums, other, beside, beside_other, factors, received, *outs):
+    gram[...] = gram_of(high, rest)
+    finish_sums(products + link_scale * links, gram[...], sums, message)
+
+
+def update_kernel(last, widths, orders, spot, table, sums, gram_mine, other, factors, received, *outs):
     half = received.shape[0]
     rank, features = sums.shape
     cells = received.shape[1] - rank // 4
@@ -573,15 +601,16 @@
     gene_blocks, peak_blocks = gene_width // BLOCK, peak_width // BLOCK
     side, place, core = spot[0], spot[1], spot[2]
     first = core == 0
-    gram = beside[:, 0:rank] + beside_other[:, 0:rank]
+    gram_other, bounds = read_beside(other, features, rank)
+    gram = gram_mine[...] + gram_other
     old = factors[...]
     below = exact(gram, old) + EPSILON
     groups = features // BLOCK
     whole = []
     for b in range(groups):
         code = other[:, b * BLOCK : (b + 1) * BLOCK]
-        least = beside_other[:, rank + b : rank + b + 1]
-        step = beside_other[:, rank + groups + b : rank + groups + b + 1]
+        least = bounds[:, b : b + 1]
+        step = (bounds[:, groups + b : groups + b + 1] - least) / CODES
         whole.append(sums[:, b * BLOCK : (b + 1) * BLOCK] + decode(code, least, step))
     whole = jnp.concatenate(whole, axis=1)
     new = old * whole / below
@@ -701,7 +730,7 @@
         compiler_params=PARAMS,
     )(received_here, bounds)
     aside_other = flip(aside, half)
-    sums_shapes = (struct(rank, features), struct(rank, features, dtype=jnp.int16), struct(rank, 2 * rank))
+    sums_shapes = (struct(rank, features), struct(rank, features + 4 * rank, dtype=jnp.int16))
     sums, gram, state = pl.pallas_call(
         functools.partial(first_sums_kernel, cell_order),
         in_specs=[VMEM],
@@ -709,9 +738,9 @@
         out_shape=(struct(rank, features), struct(rank, rank), struct(rank, half * cells)),
         compiler_params=PARAMS,
     )(received_here)
-    codes, sums = lax.optimization_barrier((codes, sums))
+    codes, sums, aside_other = lax.optimization_barrier((codes, sums, aside_other))
     codes_other = flip(codes, half)
-    sums, coded, beside, link_table = pl.pallas_call(
+    sums, message, link_table = pl.pallas_call(
         functools.partial(first_links_kernel, link_scale, widths),
         grid=(1,),
         in_specs=[
@@ -723,13 +752,13 @@
             VMEM,
             VMEM,
         ],
-        out_specs=[VMEM] * 4,
+        out_specs=[VMEM] * 3,
         out_shape=(*sums_shapes, struct(*table_shape)),
         scratch_shapes=[pltpu.SemaphoreType.DMA, pltpu.SMEM(table_shape, jnp.float32)],
         compiler_params=PARAMS,
     )(spot, received_here, rows_other, aside, aside_other, sums, gram)
 
-    coded, beside, codes_other = lax.optimization_barrier((coded, beside, codes_other))
+    message, codes_other = lax.optimization_barrier((message, codes_other))
     factors = pl.pallas_call(
         twins_kernel,
         in_specs=[SMEM] + [VMEM] * 4,
@@ -741,8 +770,7 @@
     split = half // 2 * cells
     for sweep_index in range(ROUNDS):
         last = sweep_index == ROUNDS - 1
-        beside_other = flip(beside, half)
-        other = flip(coded, half)
+        other = flip(message, half)
         outs = [struct(rank + rank * rank // split, split)] * 2
         if last:
             outs += [struct(rank, gene_width), struct(rank, peak_width)]
@@ -751,11 +779,11 @@
             outs += [struct(rank, gene_width, dtype=jnp.bfloat16)]
         kept, sent, *outs = pl.pallas_call(
             functools.partial(update_kernel, last, widths, (cell_order, link_order)),
-            in_specs=[SMEM] * 2 + [VMEM] * 6,
+            in_specs=[SMEM] * 2 + [VMEM] * 5,
             out_specs=[VMEM] * len(outs),
             out_shape=outs,
             compiler_params=PARAMS,
-        )(spot, link_table, sums, other, beside, beside_other, factors, received_here)
+        )(spot, link_table, sums, gram, other, factors, received_here)
         if last:
             gene_out, peak_out = outs
             totals = kept + flip(sent, 1)
@@ -798,11 +826,11 @@
             )
             leaving = leaving[0] if next_bit else None
         to_gene = staying
-        sums, coded, beside, state, own_cells = pl.pallas_call(
+        sums, message, gram, state, own_cells = pl.pallas_call(
             functools.partial(next_sums_kernel, link_scale, widths, (cell_order, gene_order)),
             in_specs=[SMEM] * 2 + [VMEM] * 7,
             out_specs=[VMEM] * 5,
-            out_shape=(*sums_shapes, struct(rank, half * cells), struct(rank, cells)),
+            out_shape=(*sums_shapes, struct(rank, rank), struct(rank, half * cells), struct(rank, cells)),
             compiler_params=PARAMS,
         )(spot, link_table, totals, flip(totals, 1), state, received_here, to_gene, genes, flip(genes, 1))
 
@@ -818,7 +846,7 @@
         and 2 * rank == BLOCK
         and gene_width % BLOCK == 0
         and peak_width % BLOCK == 0
-        and 2 * (features // BLOCK) <= rank
+        and 4 * (features // BLOCK) + 2 <= 2 * rank
         and half * link_gene.shape[0] <= 2 * rank
         and rank % 64 == 0
         and atac_counts.shape[1] // BLOCK == 2 * rank

time: 136 us -> 133 us (0.978)
  starting transfers between devices: 20.7 us -> 19.2 us
    ppermute x25 -> x23, starting transfers between devices: 20.7 us -> 19.2 us  [flip(): return lax.ppermute(value, AXIS, [(i, i ^ bit) for i in range(count)])]
    ppermute x25 -> x23, waiting for transfers between devices: 43.8 us -> 42.7 us  [flip(): return lax.ppermute(value, AXIS, [(i, i ^ bit) for i in range(count)])]
  transfers between devices with their start and end apart: 25 -> 23, of which waited for: 17 -> 18; matrix products, arithmetic and copies ran while one was open for 0% -> 0% of each run, Pallas kernels for 3% -> 4%
where the time goes in v8:
time: 133 us
  blocking collectives  49.8 us (37%)
  waiting for transfers between devices  42.7 us (32%)
  Pallas kernels  19.7 us (15%)
  starting transfers between devices  19.2 us (14%)
  between operations  1.57 us (1%)
    all_to_all x1, blocking collectives, shards_blocks(): lax.all_to_all(sent, AXIS, 0, 0, axis_index_groups=halves, tiled=True)  49.8 us
    ppermute x23, waiting for transfers between devices, flip(): return lax.ppermute(value, AXIS, [(i, i ^ bit) for i in range(count)])  42.7 us
    ppermute x23, starting transfers between devices, flip(): return lax.ppermute(value, AXIS, [(i, i ^ bit) for i in range(count)])  19.2 us
    pallas_call x2, Pallas kernels, shards_blocks(): pl.pallas_call(functools.partial(update_kernel, last, widths, (cell_order...  5.14 us
    pallas_call x1, Pallas kernels, parcels(): pl.pallas_call(parcels_kernel, grid=(steps,), in_specs=[SMEM, columns(gen...  3.45 us
    pallas_call x1, Pallas kernels, shards_blocks(): pl.pallas_call(functools.partial(first_links_kernel, link_scale, widths),...  2.69 us
    pallas_call x1, Pallas kernels, shards_blocks(): pl.pallas_call(functools.partial(next_sums_kernel, link_scale, widths, (c...  2.66 us
  transfers between devices with their start and end apart: 23, of which 18 were waited for; matrix products, arithmetic and copies ran while one was open for 0% of the time, Pallas kernels for 4%

profile of v8, /device:TPU:0, one launch (start us, length us, event | category | flops | bytes accessed | tf_op | source)
XLA Modules:
  0.0 133.2 jit_solution(16939574400702553795)
XLA Ops:
  1.4 3.4 %shard_map.112 = bf16[16,80,1408]{2,1,0:T(8,128)(2,1)S(1)} custom-call(s32[4]{0:T(128)S(1)} %pad_add_fusion.spot, bf16[64,4096]{1,0:T(8,128)(2,1)} %rna_1.1, bf16[64,4096]{1,0:T(8,128)(2,1)} %rna_1.1, bf16[64,16384]{1,0:T(8,128)(2,1)} %atac_1.1, bf16[64,16384]{1,0:T(8,128)(2,1)} %atac_1.1, f32[64,64]{1,0:T(8,128)} %cell.1, f32[64,128]{1,0:T(8,128)} %gene.5, ...), custom_call_target="tpu_custom_call" | custom-call | tf_op jit(solution)/shard_map/pallas_call | solution.py:385
  4.9 49.8 %all_to_all.5.received_slots.received.mine.refs_0_.refs_2_ = bf16[16,80,1408]{2,1,0:T(8,128)(2,1)S(1)} all-to-all(bf16[16,80,1408]{2,1,0:T(8,128)(2,1)S(1)} %shard_map.112), channel_id=1, replica_groups={{0,1,2,3,4,5,6,7,8,9,10,11,12,13,14,15},{16,17,18,19,20,21,22,23,24,25,..., dimensions={0} | all-to-all | bytes 7208960 | tf_op jit(solution)/shard_map/all_to_all | solution.py:709
  55.2 2.6 %collective-permute-start.1 = (f32[48,128]{1,0:T(8,128)S(1)}, f32[48,128]{1,0:T(8,128)S(1)}, u32[]{:S(2)}, u32[]{:S(2)}) collective-permute-start(f32[48,128]{1,0:T(8,128)S(1)} %shard_map.114.aside), channel_id=1, source_target_pairs={{0,16},{1,17},{2,18},{3,19},{4,20},{5,21},{6,22},{7,23},{8,24},{9,... | collective-permute-start | bytes 73736 | tf_op jit(solution)/shard_map/ppermute | solution.py:24
  57.8 0.8 shard_map.115
  58.6 1.6 %collective-permute-done.1.aside_other.beside = f32[48,128]{1,0:T(8,128)S(1)} collective-permute-done((f32[48,128]{1,0:T(8,128)S(1)}, f32[48,128]{1,0:T(8,128)S(1)}, u32[]{:S(2)}, u32[]{:S(2)}) %collective-permute-start.1) | collective-permute-done | bytes 24608 | tf_op jit(solution)/shard_map/ppermute | solution.py:24
  60.2 2.3 %collective-permute-start.2 = (s16[64,640]{1,0:T(8,128)(2,1)S(1)}, s16[64,640]{1,0:T(8,128)(2,1)S(1)}, u32[]{:S(2)}, u32[]{:S(2)}) collective-permute-start(s16[64,640]{1,0:T(8,128)(2,1)S(1)} %get-tuple-element.71), channel_id=1, source_target_pairs={{0,16},{1,17},{2,18},{3,19},{4,20},{5,21},{6,22},{7,23},{8,24},{9,... | collective-permute-start | bytes 245768 | tf_op jit(solution)/shard_map/ppermute | solution.py:24
  62.5 2.7 %shard_map.116 = (f32[64,1280]{1,0:T(8,128)S(1)}, s16[64,1536]{1,0:T(8,128)(2,1)S(1)}, f32[32,128]{1,0:T(8,128)S(1)}) custom-call(s32[4]{0:T(128)S(1)} %pad_add_fusion.spot, bf16[16,80,1408]{2,1,0:T(8,128)(2,1)S(1)} %all_to_all.5.received_slots.received.mine.refs_0_.refs_2_, bf16[16,16,1280]{2,1,0:T(8,128)(2,1)S(1)} %collective-permute-done.other, ...), custom_call_target="tpu_custom_call" | custom-call | tf_op jit(solution)/shard_map/pallas_call | solution.py:743
  65.2 1.2 collective-permute-done.2.codes
  66.4 1.6 %collective-permute-start.3 = (s16[64,1536]{1,0:T(8,128)(2,1)S(1)}, s16[64,1536]{1,0:T(8,128)(2,1)S(1)}, u32[]{:S(2)}, u32[]{:S(2)}) collective-permute-start(s16[64,1536]{1,0:T(8,128)(2,1)S(1)} %get-tuple-element.72), channel_id=1, source_target_pairs={{0,16},{1,17},{2,18},{3,19},{4,20},{5,21},{6,22},{7,23},{8,24},{9,... | collective-permute-start | bytes 589832 | tf_op jit(solution)/shard_map/ppermute | solution.py:24
  68.0 0.8 shard_map.117.factors
  68.8 7.5 %collective-permute-done.3.other = s16[64,1536]{1,0:T(8,128)(2,1)S(1)} collective-permute-done((s16[64,1536]{1,0:T(8,128)(2,1)S(1)}, s16[64,1536]{1,0:T(8,128)(2,1)S(1)}, u32[]{:S(2)}, u32[]{:S(2)}) %collective-permute-start.3) | collective-permute-done | bytes 196640 | tf_op jit(solution)/shard_map/ppermute | solution.py:24
  76.3 2.5 %shard_map.118 = (f32[72,512]{1,0:T(8,128)S(1)}, f32[72,512]{1,0:T(8,128)S(1)}, f32[64,1280]{1,0:T(8,128)S(1)}, f32[64,1024]{1,0:T(8,128)S(1)}, f32[64,1024]{1,0:T(8,128)S(1)}, /*index=5*/bf16[64,128]{1,0:T(8,128)(2,1)S(1)}) custom-call(s32[4]{0:T(128)S(1)} %pad_add_fusion.spot, f32[32,128]{1,0:T(8,128)S(1)} %get-tuple-element.68.table, ...), custom_call_target="tpu_custom_call" | custom-call | tf_op jit(solution)/shard_map/pallas_call | solution.py:780
  79.3 1.2 collective-permute-done.4.totals_got
  81.3 0.9 collective-permute-start.7
  82.1 3.7 %collective-permute-done.8.refs_1_ = bf16[64,128]{1,0:T(8,128)(2,1)S(1)} collective-permute-done((bf16[64,128]{1,0:T(8,128)(2,1)S(1)}, bf16[64,128]{1,0:T(8,128)(2,1)S(1)}, u32[]{:S(2)}, u32[]{:S(2)}) %collective-permute-start.8) | collective-permute-done | bytes 16416 | tf_op jit(solution)/shard_map/ppermute | solution.py:24
  85.9 1.0 collective-permute-done.7.staying_got
  88.0 1.7 %collective-permute-start.11 = (bf16[64,256]{1,0:T(8,128)(2,1)S(1)}, bf16[64,256]{1,0:T(8,128)(2,1)S(1)}, u32[]{:S(2)}, u32[]{:S(2)}) collective-permute-start(bf16[64,256]{1,0:T(8,128)(2,1)S(1)} %get-tuple-element.93.refs_0_), channel_id=1, source_target_pairs={{0,2},{1,3},{2,0},{3,1},{4,6},{5,7},{6,4},{7,5},{8,10},{9,11},{10,... | collective-permute-start | bytes 98312 | tf_op jit(solution)/shard_map/ppermute | solution.py:24
  89.7 2.3 %collective-permute-done.11.refs_1_ = bf16[64,256]{1,0:T(8,128)(2,1)S(1)} collective-permute-done((bf16[64,256]{1,0:T(8,128)(2,1)S(1)}, bf16[64,256]{1,0:T(8,128)(2,1)S(1)}, u32[]{:S(2)}, u32[]{:S(2)}) %collective-permute-start.11) | collective-permute-done | bytes 32800 | tf_op jit(solution)/shard_map/ppermute | solution.py:24
  93.5 1.1 collective-permute-start.12
  94.6 1.8 %collective-permute-start.14 = (bf16[64,512]{1,0:T(8,128)(2,1)S(1)}, bf16[64,512]{1,0:T(8,128)(2,1)S(1)}, u32[]{:S(2)}, u32[]{:S(2)}) collective-permute-start(bf16[64,512]{1,0:T(8,128)(2,1)S(1)} %get-tuple-element.103.refs_0_), channel_id=1, source_target_pairs={{0,4},{1,5},{2,6},{3,7},{4,0},{5,1},{6,2},{7,3},{8,12},{9,13},{10,... | collective-permute-start | bytes 196616 | tf_op jit(solution)/shard_map/ppermute | solution.py:24
  96.4 1.4 %collective-permute-start.13 = (f32[64,128]{1,0:T(8,128)S(1)}, f32[64,128]{1,0:T(8,128)S(1)}, u32[]{:S(2)}, u32[]{:S(2)}) collective-permute-start(f32[64,128]{1,0:T(8,128)S(1)} %get-tuple-element.102), channel_id=1, source_target_pairs={{0,2},{1,3},{2,0},{3,1},{4,6},{5,7},{6,4},{7,5},{8,10},{9,11},{10,... | collective-permute-start | bytes 98312 | tf_op jit(solution)/shard_map/ppermute | solution.py:24
  97.8 2.5 %collective-permute-done.13.staying_got = f32[64,128]{1,0:T(8,128)S(1)} collective-permute-done((f32[64,128]{1,0:T(8,128)S(1)}, f32[64,128]{1,0:T(8,128)S(1)}, u32[]{:S(2)}, u32[]{:S(2)}) %collective-permute-start.13) | collective-permute-done | bytes 32800 | tf_op jit(solution)/shard_map/ppermute | solution.py:24
  101.5 1.0 collective-permute-done.16.genes_other
  102.5 2.7 %shard_map.123 = (f32[64,1280]{1,0:T(8,128)S(1)}, s16[64,1536]{1,0:T(8,128)(2,1)S(1)}, f32[64,64]{1,0:T(8,128)S(1)}, f32[64,1024]{1,0:T(8,128)}, f32[64,64]{1,0:T(8,128)S(1)}) custom-call(s32[4]{0:T(128)S(1)} %pad_add_fusion.spot, f32[32,128]{1,0:T(8,128)S(1)} %get-tuple-element.68.table, f32[72,512]{1,0:T(8,128)S(1)} %get-tuple-element.108.mine, ...), custom_call_target="tpu_custom_call" | custom-call | tf_op jit(solution)/shard_map/pallas_call | solution.py:829
  105.8 11.4 %collective-permute-done.17.other = s16[64,1536]{1,0:T(8,128)(2,1)S(1)} collective-permute-done((s16[64,1536]{1,0:T(8,128)(2,1)S(1)}, s16[64,1536]{1,0:T(8,128)(2,1)S(1)}, u32[]{:S(2)}, u32[]{:S(2)}) %collective-permute-start.17) | collective-permute-done | bytes 196640 | tf_op jit(solution)/shard_map/ppermute | solution.py:24
  117.2 2.6 %shard_map.124 = (f32[72,512]{1,0:T(8,128)S(1)}, f32[72,512]{1,0:T(8,128)S(1)}, f32[64,128]{1,0:T(8,128)}, f32[64,512]{1,0:T(8,128)}) custom-call(s32[4]{0:T(128)S(1)} %pad_add_fusion.spot, f32[32,128]{1,0:T(8,128)S(1)} %get-tuple-element.68.table, f32[64,1280]{1,0:T(8,128)S(1)} %get-tuple-element.112.sums, f32[64,64]{1,0:T(8,128)S(1)} %get-tuple-element.113.gram_mine, ...), custom_call_target="tpu_custom_call" | custom-call | tf_op jit(solution)/shard_map/pallas_call | solution.py:780
  119.9 1.3 collective-permute-done.18
  121.4 1.6 %collective-permute-start.21 = (f32[96,128]{1,0:T(8,128)S(1)}, f32[96,128]{1,0:T(8,128)S(1)}, u32[]{:S(2)}, u32[]{:S(2)}) collective-permute-start(f32[96,128]{1,0:T(8,128)S(1)} %constant_dynamic-update-slice_fusion.15), channel_id=1, source_target_pairs={{0,6},{1,7},{2,4},{3,5},{4,2},{5,3},{6,0},{7,1},{8,14},{9,15},{10,... | collective-permute-start | bytes 147464 | tf_op jit(solution)/shard_map/ppermute | solution.py:24
  123.5 1.5 %collective-permute-start.20 = (f32[96,128]{1,0:T(8,128)S(1)}, f32[96,128]{1,0:T(8,128)S(1)}, u32[]{:S(2)}, u32[]{:S(2)}) collective-permute-start(f32[96,128]{1,0:T(8,128)S(1)} %get-tuple-element.121), channel_id=1, source_target_pairs={{0,4},{1,5},{2,6},{3,7},{4,0},{5,1},{6,2},{7,3},{8,12},{9,13},{10,... | collective-permute-start | bytes 147464 | tf_op jit(solution)/shard_map/ppermute | solution.py:24
  125.0 1.7 %collective-permute-done.21 = f32[96,128]{1,0:T(8,128)S(1)} collective-permute-done((f32[96,128]{1,0:T(8,128)S(1)}, f32[96,128]{1,0:T(8,128)S(1)}, u32[]{:S(2)}, u32[]{:S(2)}) %collective-permute-start.21) | collective-permute-done | bytes 49184 | tf_op jit(solution)/shard_map/ppermute | solution.py:24
  127.7 4.1 %collective-permute-done.22.other = f32[96,128]{1,0:T(8,128)S(1)} collective-permute-done((f32[96,128]{1,0:T(8,128)S(1)}, f32[96,128]{1,0:T(8,128)S(1)}, u32[]{:S(2)}, u32[]{:S(2)}) %collective-permute-start.22) | collective-permute-done | bytes 49184 | tf_op jit(solution)/shard_map/ppermute | solution.py:24
  131.8 1.4 %shard_map.125 = f32[64,64]{1,0:T(8,128)} custom-call(s32[4]{0:T(128)S(1)} %pad_add_fusion.spot, f32[96,128]{1,0:T(8,128)S(1)} %add_add_fusion.mine, f32[96,128]{1,0:T(8,128)S(1)} %collective-permute-done.22.other, f32[64,64]{1,0:T(8,128)S(1)} %get-tuple-element.118.old), custom_call_target="tpu_custom_call" | custom-call | tf_op jit(solution)/shard_map/pallas_call | solution.py:808
  (48 shorter events, 7.9 us)
Async XLA Ops:
  4.8 49.9 %copy-start = (f32[64,512]{1,0:T(8,128)S(1)}, f32[64,512]{1,0:T(8,128)}, u32[]{:S(2)}) copy-start(f32[64,512]{1,0:T(8,128)} %peak.5) | copy-start | bytes 393220
  4.9 49.9 %copy-start.1 = (f32[64,128]{1,0:T(8,128)S(1)}, f32[64,128]{1,0:T(8,128)}, u32[]{:S(2)}) copy-start(f32[64,128]{1,0:T(8,128)} %gene.5) | copy-start | bytes 98308
  54.7 7.8 %collective-permute-start = (bf16[16,16,1280]{2,1,0:T(8,128)(2,1)S(1)}, bf16[16,16,1280]{2,1,0:T(8,128)(2,1)S(1)}, u32[]{:S(2)}, u32[]{:S(2)}) collective-permute-start(bf16[16,16,1280]{2,1,0:T(8,128)(2,1)S(1)} %slice.14), channel_id=1, source_target_pairs={{0,1},{1,0},{2,3},{3,2},{4,5},{5,4},{6,7},{7,6},{8,9},{9,8},{10,11... | collective-permute-start | bytes 1966088 | tf_op jit(solution)/shard_map/ppermute | solution.py:24
  55.2 5.1 %collective-permute-start.1 = (f32[48,128]{1,0:T(8,128)S(1)}, f32[48,128]{1,0:T(8,128)S(1)}, u32[]{:S(2)}, u32[]{:S(2)}) collective-permute-start(f32[48,128]{1,0:T(8,128)S(1)} %shard_map.114.aside), channel_id=1, source_target_pairs={{0,16},{1,17},{2,18},{3,19},{4,20},{5,21},{6,22},{7,23},{8,24},{9,... | collective-permute-start | bytes 73736 | tf_op jit(solution)/shard_map/ppermute | solution.py:24
  60.2 6.1 %collective-permute-start.2 = (s16[64,640]{1,0:T(8,128)(2,1)S(1)}, s16[64,640]{1,0:T(8,128)(2,1)S(1)}, u32[]{:S(2)}, u32[]{:S(2)}) collective-permute-start(s16[64,640]{1,0:T(8,128)(2,1)S(1)} %get-tuple-element.71), channel_id=1, source_target_pairs={{0,16},{1,17},{2,18},{3,19},{4,20},{5,21},{6,22},{7,23},{8,24},{9,... | collective-permute-start | bytes 245768 | tf_op jit(solution)/shard_map/ppermute | solution.py:24
  66.4 9.9 %collective-permute-start.3 = (s16[64,1536]{1,0:T(8,128)(2,1)S(1)}, s16[64,1536]{1,0:T(8,128)(2,1)S(1)}, u32[]{:S(2)}, u32[]{:S(2)}) collective-permute-start(s16[64,1536]{1,0:T(8,128)(2,1)S(1)} %get-tuple-element.72), channel_id=1, source_target_pairs={{0,16},{1,17},{2,18},{3,19},{4,20},{5,21},{6,22},{7,23},{8,24},{9,... | collective-permute-start | bytes 589832 | tf_op jit(solution)/shard_map/ppermute | solution.py:24
  78.8 1.8 %collective-permute-start.5 = (f32[64,1024]{1,0:T(8,128)S(1)}, f32[64,1024]{1,0:T(8,128)S(1)}, u32[]{:S(2)}, u32[]{:S(2)}) collective-permute-start(f32[64,1024]{1,0:T(8,128)S(1)} %get-tuple-element.77), channel_id=1, source_target_pairs={{0,1},{1,0},{2,3},{3,2},{4,5},{5,4},{6,7},{7,6},{8,9},{9,8},{10,11... | collective-permute-start | bytes 786440 | tf_op jit(solution)/shard_map/ppermute | solution.py:24
  78.8 1.7 %collective-permute-start.4 = (f32[72,512]{1,0:T(8,128)S(1)}, f32[72,512]{1,0:T(8,128)S(1)}, u32[]{:S(2)}, u32[]{:S(2)}) collective-permute-start(f32[72,512]{1,0:T(8,128)S(1)} %get-tuple-element.75), channel_id=1, source_target_pairs={{0,1},{1,0},{2,3},{3,2},{4,5},{5,4},{6,7},{7,6},{8,9},{9,8},{10,11... | collective-permute-start | bytes 442376 | tf_op jit(solution)/shard_map/ppermute | solution.py:24
  81.2 6.0 %collective-permute-start.6 = (f32[72,512]{1,0:T(8,128)S(1)}, f32[72,512]{1,0:T(8,128)S(1)}, u32[]{:S(2)}, u32[]{:S(2)}) collective-permute-start(f32[72,512]{1,0:T(8,128)S(1)} %get-tuple-element.81.totals), channel_id=1, source_target_pairs={{0,2},{1,3},{2,0},{3,1},{4,6},{5,7},{6,4},{7,5},{8,10},{9,11},{10,... | collective-permute-start | bytes 442376 | tf_op jit(solution)/shard_map/ppermute | solution.py:24
  81.3 5.6 %collective-permute-start.7 = (f32[64,512]{1,0:T(8,128)S(1)}, f32[64,512]{1,0:T(8,128)S(1)}, u32[]{:S(2)}, u32[]{:S(2)}) collective-permute-start(f32[64,512]{1,0:T(8,128)S(1)} %get-tuple-element.82), channel_id=1, source_target_pairs={{0,4},{1,5},{2,6},{3,7},{4,0},{5,1},{6,2},{7,3},{8,12},{9,13},{10,... | collective-permute-start | bytes 393224 | tf_op jit(solution)/shard_map/ppermute | solution.py:24
  82.1 3.7 %collective-permute-start.8 = (bf16[64,128]{1,0:T(8,128)(2,1)S(1)}, bf16[64,128]{1,0:T(8,128)(2,1)S(1)}, u32[]{:S(2)}, u32[]{:S(2)}) collective-permute-start(bf16[64,128]{1,0:T(8,128)(2,1)S(1)} %get-tuple-element.83.refs_0_), channel_id=1, source_target_pairs={{0,8},{1,9},{2,10},{3,11},{4,12},{5,13},{6,14},{7,15},{8,0},{9,1},... | collective-permute-start | bytes 49160 | tf_op jit(solution)/shard_map/ppermute | solution.py:24
  87.7 5.2 %collective-permute-start.9 = (f32[72,512]{1,0:T(8,128)S(1)}, f32[72,512]{1,0:T(8,128)S(1)}, u32[]{:S(2)}, u32[]{:S(2)}) collective-permute-start(f32[72,512]{1,0:T(8,128)S(1)} %get-tuple-element.91.totals), channel_id=1, source_target_pairs={{0,4},{1,5},{2,6},{3,7},{4,0},{5,1},{6,2},{7,3},{8,12},{9,13},{10,... | collective-permute-start | bytes 442376 | tf_op jit(solution)/shard_map/ppermute | solution.py:24
  88.0 4.3 %collective-permute-start.10 = (f32[64,256]{1,0:T(8,128)S(1)}, f32[64,256]{1,0:T(8,128)S(1)}, u32[]{:S(2)}, u32[]{:S(2)}) collective-permute-start(f32[64,256]{1,0:T(8,128)S(1)} %get-tuple-element.92), channel_id=1, source_target_pairs={{0,8},{1,9},{2,10},{3,11},{4,12},{5,13},{6,14},{7,15},{8,0},{9,1},... | collective-permute-start | bytes 196616 | tf_op jit(solution)/shard_map/ppermute | solution.py:24
  88.0 3.9 %collective-permute-start.11 = (bf16[64,256]{1,0:T(8,128)(2,1)S(1)}, bf16[64,256]{1,0:T(8,128)(2,1)S(1)}, u32[]{:S(2)}, u32[]{:S(2)}) collective-permute-start(bf16[64,256]{1,0:T(8,128)(2,1)S(1)} %get-tuple-element.93.refs_0_), channel_id=1, source_target_pairs={{0,2},{1,3},{2,0},{3,1},{4,6},{5,7},{6,4},{7,5},{8,10},{9,11},{10,... | collective-permute-start | bytes 98312 | tf_op jit(solution)/shard_map/ppermute | solution.py:24
  93.5 6.8 %collective-permute-start.12 = (f32[72,512]{1,0:T(8,128)S(1)}, f32[72,512]{1,0:T(8,128)S(1)}, u32[]{:S(2)}, u32[]{:S(2)}) collective-permute-start(f32[72,512]{1,0:T(8,128)S(1)} %get-tuple-element.101.totals), channel_id=1, source_target_pairs={{0,8},{1,9},{2,10},{3,11},{4,12},{5,13},{6,14},{7,15},{8,0},{9,1},... | collective-permute-start | bytes 442376 | tf_op jit(solution)/shard_map/ppermute | solution.py:24
  94.6 5.7 %collective-permute-start.14 = (bf16[64,512]{1,0:T(8,128)(2,1)S(1)}, bf16[64,512]{1,0:T(8,128)(2,1)S(1)}, u32[]{:S(2)}, u32[]{:S(2)}) collective-permute-start(bf16[64,512]{1,0:T(8,128)(2,1)S(1)} %get-tuple-element.103.refs_0_), channel_id=1, source_target_pairs={{0,4},{1,5},{2,6},{3,7},{4,0},{5,1},{6,2},{7,3},{8,12},{9,13},{10,... | collective-permute-start | bytes 196616 | tf_op jit(solution)/shard_map/ppermute | solution.py:24
  96.4 3.9 %collective-permute-start.13 = (f32[64,128]{1,0:T(8,128)S(1)}, f32[64,128]{1,0:T(8,128)S(1)}, u32[]{:S(2)}, u32[]{:S(2)}) collective-permute-start(f32[64,128]{1,0:T(8,128)S(1)} %get-tuple-element.102), channel_id=1, source_target_pairs={{0,2},{1,3},{2,0},{3,1},{4,6},{5,7},{6,4},{7,5},{8,10},{9,11},{10,... | collective-permute-start | bytes 98312 | tf_op jit(solution)/shard_map/ppermute | solution.py:24
  100.9 1.6 %collective-permute-start.15 = (f32[72,512]{1,0:T(8,128)S(1)}, f32[72,512]{1,0:T(8,128)S(1)}, u32[]{:S(2)}, u32[]{:S(2)}) collective-permute-start(f32[72,512]{1,0:T(8,128)S(1)} %get-tuple-element.108.mine), channel_id=1, source_target_pairs={{0,1},{1,0},{2,3},{3,2},{4,5},{5,4},{6,7},{7,6},{8,9},{9,8},{10,11... | collective-permute-start | bytes 442376 | tf_op jit(solution)/shard_map/ppermute | solution.py:24
  101.0 1.5 %collective-permute-start.16 = (bf16[64,1024]{1,0:T(8,128)(2,1)S(1)}, bf16[64,1024]{1,0:T(8,128)(2,1)S(1)}, u32[]{:S(2)}, u32[]{:S(2)}) collective-permute-start(bf16[64,1024]{1,0:T(8,128)(2,1)S(1)} %get-tuple-element.111.genes_mine), channel_id=1, source_target_pairs={{0,1},{1,0},{2,3},{3,2},{4,5},{5,4},{6,7},{7,6},{8,9},{9,8},{10,11... | collective-permute-start | bytes 393224 | tf_op jit(solution)/shard_map/ppermute | solution.py:24
  105.2 12.0 %collective-permute-start.17 = (s16[64,1536]{1,0:T(8,128)(2,1)S(1)}, s16[64,1536]{1,0:T(8,128)(2,1)S(1)}, u32[]{:S(2)}, u32[]{:S(2)}) collective-permute-start(s16[64,1536]{1,0:T(8,128)(2,1)S(1)} %get-tuple-element.114), channel_id=1, source_target_pairs={{0,16},{1,17},{2,18},{3,19},{4,20},{5,21},{6,22},{7,23},{8,24},{9,... | collective-permute-start | bytes 589832 | tf_op jit(solution)/shard_map/ppermute | solution.py:24
  119.9 1.4 %collective-permute-start.18 = (f32[72,512]{1,0:T(8,128)S(1)}, f32[72,512]{1,0:T(8,128)S(1)}, u32[]{:S(2)}, u32[]{:S(2)}) collective-permute-start(f32[72,512]{1,0:T(8,128)S(1)} %get-tuple-element.117), channel_id=1, source_target_pairs={{0,1},{1,0},{2,3},{3,2},{4,5},{5,4},{6,7},{7,6},{8,9},{9,8},{10,11... | collective-permute-start | bytes 442376 | tf_op jit(solution)/shard_map/ppermute | solution.py:24
  121.4 5.3 %collective-permute-start.21 = (f32[96,128]{1,0:T(8,128)S(1)}, f32[96,128]{1,0:T(8,128)S(1)}, u32[]{:S(2)}, u32[]{:S(2)}) collective-permute-start(f32[96,128]{1,0:T(8,128)S(1)} %constant_dynamic-update-slice_fusion.15), channel_id=1, source_target_pairs={{0,6},{1,7},{2,4},{3,5},{4,2},{5,3},{6,0},{7,1},{8,14},{9,15},{10,... | collective-permute-start | bytes 147464 | tf_op jit(solution)/shard_map/ppermute | solution.py:24
  123.1 4.1 %collective-permute-start.19 = (f32[96,128]{1,0:T(8,128)S(1)}, f32[96,128]{1,0:T(8,128)S(1)}, u32[]{:S(2)}, u32[]{:S(2)}) collective-permute-start(f32[96,128]{1,0:T(8,128)S(1)} %get-tuple-element.134), channel_id=1, source_target_pairs={{0,2},{1,3},{2,0},{3,1},{4,6},{5,7},{6,4},{7,5},{8,10},{9,11},{10,... | collective-permute-start | bytes 147464 | tf_op jit(solution)/shard_map/ppermute | solution.py:24
  123.5 4.1 %collective-permute-start.20 = (f32[96,128]{1,0:T(8,128)S(1)}, f32[96,128]{1,0:T(8,128)S(1)}, u32[]{:S(2)}, u32[]{:S(2)}) collective-permute-start(f32[96,128]{1,0:T(8,128)S(1)} %get-tuple-element.121), channel_id=1, source_target_pairs={{0,4},{1,5},{2,6},{3,7},{4,0},{5,1},{6,2},{7,3},{8,12},{9,13},{10,... | collective-permute-start | bytes 147464 | tf_op jit(solution)/shard_map/ppermute | solution.py:24
  127.6 4.2 %collective-permute-start.22 = (f32[96,128]{1,0:T(8,128)S(1)}, f32[96,128]{1,0:T(8,128)S(1)}, u32[]{:S(2)}, u32[]{:S(2)}) collective-permute-start(f32[96,128]{1,0:T(8,128)S(1)} %add_add_fusion.mine), channel_id=1, source_target_pairs={{0,8},{1,9},{2,10},{3,11},{4,12},{5,13},{6,14},{7,15},{8,0},{9,1},... | collective-permute-start | bytes 147464 | tf_op jit(solution)/shard_map/ppermute | solution.py:24

commit v9 on v8

--- a/solution.py
+++ b/solution.py
@@ -12,6 +12,7 @@
 EPSILON = 1e-06
 CODES = 65535.0
 DIGIT = 32768.0
+UNITS = 16384.0
 TINY = 1e-30
 AXIS = "cells"
 PARAMS = pltpu.CompilerParams(vmem_limit_bytes=14 * 1024 * 1024)
@@ -229,19 +230,19 @@
     return lax.dot_general(left, right, (((1,), (1,)), ((), ())), preferred_element_type=jnp.float32)
 
 
-def exact(left, right):
-    return lax.dot_general(
-        left,
-        right,
-        (((1,), (0,)), ((), ())),
-        precision=lax.Precision.HIGHEST,
-        preferred_element_type=jnp.float32,
-    )
-
-
 def halved(value):
     high = value.astype(jnp.bfloat16)
     return high, (value - high.astype(jnp.float32)).astype(jnp.bfloat16)
+
+
+def exact(left, right):
+    left_high, left_low = halved(left)
+    right_high, right_low = halved(right)
+    return jnp.dot(
+        jnp.concatenate([left_low, left_low, left_high, left_high], axis=1),
+        jnp.concatenate([right_low, right_high, right_low, right_high], axis=0),
+        preferred_element_type=jnp.float32,
+    )
 
 
 def struct(*shape, dtype=jnp.float32):
@@ -273,16 +274,18 @@
     gene_low = gene[...].astype(jnp.bfloat16)
     peak_low = peak[...].astype(jnp.bfloat16)
     part = rank // 4
-    for j in range(out.shape[0]):
+    each = rna_0.shape[1] // gene_width
+    base = pl.program_id(0) * each
+    for j in range(each):
         at = 0
         for source, size in ((rna_0, gene_width), (rna_1, gene_width), (atac_0, peak_width), (atac_1, peak_width)):
-            out[j, 0:cells, at : at + size] = source[:, j * size : (j + 1) * size]
+            out[base + j, 0:cells, at : at + size] = source[:, j * size : (j + 1) * size]
             at += size
-        out[j, 0:cells, at:] = cell_pair
+        out[base + j, 0:cells, at:] = cell_pair
         for s in range(2):
             row = (2 * (j % 2) + s) * part
-            out[j, cells:, s * width : s * width + gene_width] = gene_low[row : row + part]
-            out[j, cells:, s * width + gene_width : (s + 1) * width] = peak_low[row : row + part]
+            out[base + j, cells:, s * width : s * width + gene_width] = gene_low[row : row + part]
+            out[base + j, cells:, s * width + gene_width : (s + 1) * width] = peak_low[row : row + part]
 
     @pl.when(pl.program_id(0) == 0)
     def _():
@@ -299,68 +302,78 @@
                 value = jnp.where((lane == s) & (row == r), entry.astype(jnp.float32), value)
         slots[...] = value.astype(jnp.bfloat16)
 
-    for j in range(out.shape[0]):
-        out[j, cells:, 2 * width :] = slots[...]
-
-
-def encode(group):
-    least = jnp.min(group, axis=1, keepdims=True)
-    spread = jnp.max(group, axis=1, keepdims=True) - least
-    per = jnp.where(spread > 0.0, CODES / spread, 0.0)
-    code = jnp.minimum(jnp.floor((group - least) * per + 0.5), CODES) - (CODES + 1) / 2
-    return code.astype(jnp.int32).astype(jnp.int16), least, spread / CODES
-
-
-def decode(code, least, step):
-    return least + (code.astype(jnp.int32).astype(jnp.float32) + (CODES + 1) / 2) * step
-
-
-def codes_kernel(gene, peak, codes, bounds):
-    rank, width = codes.shape
-    gene_width = gene.shape[1]
-    least, step = [], []
-    for b in range(width // BLOCK):
-        ref, at = (gene, b * BLOCK) if b * BLOCK < gene_width else (peak, b * BLOCK - gene_width)
-        code, low, per = encode(ref[:, at : at + BLOCK])
-        codes[:, b * BLOCK : (b + 1) * BLOCK] = code
-        least.append(low)
-        step.append(per)
-    pad = jnp.zeros((rank, 2 * rank - 2 * len(least)), jnp.float32)
-    columns = jnp.concatenate([*least, *step, pad], axis=1)
-    square = jnp.concatenate([columns, jnp.zeros_like(columns)], axis=0)
-    bounds[...] = square.T[: bounds.shape[0]]
-
-
-def table_kernel(received_slots, bounds, out):
-    above = bounds.shape[0]
-    out[:above] = bounds[...]
+    for j in range(each):
+        out[base + j, cells:, 2 * width :] = slots[...]
+
+
+def power_of(top):
+    return jnp.floor(jnp.log2(jnp.maximum(top, TINY))) + 1.0
+
+
+def encode(value):
+    groups = [value[:, at : at + BLOCK] for at in range(0, value.shape[1], BLOCK)]
+    least = [jnp.min(group, axis=1, keepdims=True) for group in groups]
+    most = [jnp.max(group, axis=1, keepdims=True) for group in groups]
+    power = power_of(functools.reduce(jnp.maximum, most))
+    unit, per_unit = jnp.exp2(power) / UNITS, jnp.exp2(-power) * UNITS
+    least = [jnp.floor(low * per_unit) for low in least]
+    most = [jnp.ceil(high * per_unit) for high in most]
+    codes = []
+    for group, low, high in zip(groups, least, most):
+        spread = (high - low) * unit
+        per = jnp.where(spread > 0.0, CODES / spread, 0.0)
+        code = jnp.clip(jnp.floor((group - low * unit) * per + 0.5), 0.0, CODES) - (CODES + 1) / 2
+        codes.append(code.astype(jnp.int32).astype(jnp.int16))
+    return codes, [*least, *most, power]
+
+
+def decode(code, least, most, power):
+    steps = code.astype(jnp.int32).astype(jnp.float32) + (CODES + 1) / 2
+    return (least + steps * ((most - least) / CODES)) * (jnp.exp2(power) / UNITS)
+
+
+def whole_numbers(columns, lanes):
+    rows = columns[0].shape[0]
+    size = sum(column.shape[1] for column in columns)
+    filled = jnp.concatenate([*columns, jnp.zeros((rows, lanes - size), jnp.float32)], axis=1)
+    return filled.astype(jnp.int32).astype(jnp.int16)
+
+
+def codes_kernel(gene, peak, message):
+    codes, columns = encode(jnp.concatenate([gene[...], peak[...]], axis=1))
+    for b, code in enumerate(codes):
+        message[:, b * BLOCK : (b + 1) * BLOCK] = code
+    at = len(codes) * BLOCK
+    message[:, at:] = whole_numbers(columns, message.shape[1] - at)
+
+
+def table_kernel(received_slots, out):
     slots = sum(received_slots[j].astype(jnp.float32) for j in range(received_slots.shape[0]))
 
     def hot(row, size, value):
         ids = lax.broadcasted_iota(jnp.int32, (size, slots.shape[1]), 0).astype(jnp.float32)
         return jnp.where(slots[row : row + 1] == ids, value, 0.0).astype(jnp.bfloat16)
 
-    out[above:] = across(hot(0, out.shape[0] - above, slots[2:3]), hot(1, out.shape[1], 1.0))
-
-
-def twins_kernel(spot, gene, peak, codes, beside, out):
-    gene_width, peak_width = gene.shape[1], peak.shape[1]
-    groups = (gene_width + peak_width) // BLOCK
-    lanes = beside.shape[1]
-    above = -(-2 * groups // 8) * 8
-    square = jnp.concatenate([beside[:above], jnp.zeros((lanes - above, lanes), jnp.float32)], axis=0)
-    bounds = square.T[: gene.shape[0]]
-    at = 0
+    out[...] = across(hot(0, out.shape[0], slots[2:3]), hot(1, out.shape[1], 1.0))
+
+
+def twins_kernel(spot, gene, peak, got, out):
+    width = gene.shape[1] + peak.shape[1]
+    groups = width // BLOCK
+    columns = got[:, width:].astype(jnp.int32).astype(jnp.float32)
+    power = columns[:, 2 * groups : 2 * groups + 1]
+    at = g = 0
     first = spot[0] == 0
-    for ref, start in ((gene, 0), (peak, gene_width)):
+    for ref in (gene, peak):
         size = ref.shape[1]
         for b in range(size // BLOCK):
-            g = start // BLOCK + b
             mine = ref[:, b * BLOCK : (b + 1) * BLOCK]
-            code = codes[:, g * BLOCK : (g + 1) * BLOCK]
-            other = decode(code, bounds[:, g : g + 1], bounds[:, groups + g : groups + g + 1])
+            other = decode(
+                got[:, g * BLOCK : (g + 1) * BLOCK], columns[:, g : g + 1], columns[:, groups + g : groups + g + 1], power
+            )
             out[:, at + b * BLOCK : at + (b + 1) * BLOCK] = jnp.where(first, mine, other)
             out[:, at + size + b * BLOCK : at + size + (b + 1) * BLOCK] = jnp.where(first, other, mine)
+            g += 1
         at += 2 * size
 
 
@@ -373,7 +386,7 @@
     rank = cell_factor.shape[0]
     gene_width, peak_width = gene_factor.shape[1], peak_factor.shape[1]
     rows, lanes = cells + rank // 4, 2 * (gene_width + peak_width) + 2 * rank
-    each = 4
+    each = 8
     steps = half // each
 
     def columns(width, side):
@@ -388,7 +401,7 @@
         in_specs=[SMEM, columns(gene_width, 0), columns(gene_width, 1), columns(peak_width, 0), columns(peak_width, 1)]
         + [whole(a) for a in (cell_factor, gene_factor, peak_factor)]
         + [pl.BlockSpec(memory_space=pl.ANY)] * 4,
-        out_specs=pl.BlockSpec((each, rows, lanes), lambda i: (i, 0, 0)),
+        out_specs=VMEM,
         out_shape=struct(half, rows, lanes, dtype=jnp.bfloat16),
         scratch_shapes=[pltpu.SMEM(link.shape, jnp.int32) for link in links]
         + [pltpu.VMEM((rank // 4, 2 * rank), jnp.bfloat16), pltpu.SemaphoreType.DMA((4,))],
@@ -412,55 +425,61 @@
     state[...] = high.astype(jnp.float32) + rest.astype(jnp.float32)
 
 
-def digits(values):
-    top = jnp.maximum(jnp.max(values, axis=1, keepdims=True), TINY)
-    power = jnp.floor(jnp.log2(top)) + 1.0
-    scaled = values * jnp.exp2(-power) * DIGIT
+def by_index(rank):
+    row = lax.broadcasted_iota(jnp.int32, (rank, rank), 0)
+    return row, lax.broadcasted_iota(jnp.int32, (rank, rank), 1)
+
+
+def finish_sums(sums_value, gram_value, sums, message):
+    rank, features = sums_value.shape
+    sums[...] = sums_value
+    codes, columns = encode(sums_value)
+    for b, code in enumerate(codes):
+        message[:, b * BLOCK : (b + 1) * BLOCK] = code
+    power = power_of(jnp.max(jnp.max(gram_value, axis=1, keepdims=True), axis=0, keepdims=True))
+    scaled = gram_value * (jnp.exp2(-power) * DIGIT)
     high = jnp.minimum(jnp.floor(scaled), DIGIT - 1)
     low = jnp.clip(jnp.floor((scaled - high) * DIGIT), 0.0, DIGIT - 1)
-    return [high, low, power]
-
-
-def from_digits(high, low, power):
-    return (high + low / DIGIT) / DIGIT * jnp.exp2(power)
-
-
-def finish_sums(sums_value, gram_value, sums, message):
-    rank, features = sums_value.shape
-    least, top = [], []
-    for b in range(features // BLOCK):
-        group = sums_value[:, b * BLOCK : (b + 1) * BLOCK]
-        sums[:, b * BLOCK : (b + 1) * BLOCK] = group
-        code, low, per = encode(group)
-        message[:, b * BLOCK : (b + 1) * BLOCK] = code
-        least.append(low)
-        top.append(low + per * CODES)
-    beside = digits(gram_value) + digits(jnp.concatenate(least + top, axis=1))
-    size = sum(part.shape[1] for part in beside)
-    beside.append(jnp.zeros((rank, message.shape[1] - features - size), jnp.float32))
-    message[:, features:] = jnp.concatenate(beside, axis=1).astype(jnp.int32).astype(jnp.int16)
-
-
-def read_beside(message, features, rank):
+    row, column = by_index(rank)
+    diagonal = jnp.sum(jnp.where(row == column, low, 0.0), axis=1, keepdims=True)
+    columns = [jnp.where(row <= column, high, low), diagonal, jnp.broadcast_to(power, (rank, 1)), *columns]
+    message[:, features:] = whole_numbers(columns, message.shape[1] - features)
+
+
+def read_message(message, features, rank):
     groups = features // BLOCK
     beside = message[:, features:].astype(jnp.int32).astype(jnp.float32)
-    parts, at = [], 0
-    for size in (rank, rank, 1, 2 * groups, 2 * groups, 1):
-        parts.append(beside[:, at : at + size])
-        at += size
-    return from_digits(*parts[:3]), from_digits(*parts[3:])
+    lanes = beside.shape[1]
+    square = jnp.concatenate([beside, jnp.zeros((lanes - rank, lanes), jnp.float32)], axis=0).T
+    upright, turned_over = beside[:, :rank], square[:rank, :rank]
+    diagonal, power = beside[:, rank : rank + 1], beside[:, rank + 1 : rank + 2]
+    row, column = by_index(rank)
+    high = jnp.where(row <= column, upright, turned_over)
+    low = jnp.where(row == column, diagonal, jnp.where(row < column, turned_over, upright))
+    gram = (high + low / DIGIT) * (jnp.exp2(power) / DIGIT)
+    at = rank + 2
+    sums_power = beside[:, at + 2 * groups : at + 2 * groups + 1]
+    blocks = [
+        decode(
+            message[:, b * BLOCK : (b + 1) * BLOCK],
+            beside[:, at + b : at + b + 1],
+            beside[:, at + groups + b : at + groups + b + 1],
+            sums_power,
+        )
+        for b in range(groups)
+    ]
+    return gram, blocks
 
 
 def first_links_kernel(
-    link_scale, widths, spot, mine, other, aside, aside_other, sums_in, gram, sums, message, table, sem, table_smem
+    link_scale, widths, spot, mine, other, half_table, half_table_other, sums_in, gram, sums, message, table, sem, table_smem
 ):
     half = mine.shape[0]
     rank, features = sums_in.shape
     gene_width, peak_width = widths
     gene_blocks, peak_blocks = gene_width // BLOCK, peak_width // BLOCK
     width = gene_width + peak_width
-    above = aside.shape[0] - table.shape[0]
-    table[...] = aside[above:] + aside_other[above:]
+    table[...] = half_table[...] + half_table_other[...]
     copy = pltpu.make_async_copy(table, table_smem, sem)
     copy.start()
     copy.wait()
@@ -507,36 +526,36 @@
     )
 
 
-def step_kernel(link_bit, gene_bit, spot, totals, totals_got, staying, staying_got, *refs):
+def step_kernel(link_bit, gene_bit, spot, totals, totals_got, staying, got, genes, received, totals_out, staying_out, *outs):
+    totals_out[...] = totals[...] + totals_got[...]
+    rank, width = staying.shape
+    low = genes[...]
     if gene_bit:
-        genes, genes_got, *refs = refs
-    received, totals_out, *outs = refs
-    totals_out[...] = totals[...] + totals_got[...]
-    to_gene = staying[...] + staying_got[...]
-    if gene_bit:
-        genes_out, *outs = outs
-        width = genes.shape[1]
+        to_gene = staying[...] + (got[:, :width].astype(jnp.float32) + got[:, width : 2 * width].astype(jnp.float32))
         clear = (spot[1] // gene_bit) % 2 == 0
-        left, right = genes[...].astype(jnp.float32), genes_got[...].astype(jnp.float32)
-        genes_out[:, :width] = jnp.where(clear, left, right).astype(jnp.bfloat16)
-        genes_out[:, width:] = jnp.where(clear, right, left).astype(jnp.bfloat16)
+        mine, other = low.astype(jnp.float32), got[:, 2 * width :].astype(jnp.float32)
+        low = jnp.concatenate([jnp.where(clear, mine, other), jnp.where(clear, other, mine)], axis=1)
+        low = low.astype(jnp.bfloat16)
+    else:
+        to_gene = staying[...] + got[...]
     if link_bit:
         clear = (spot[1] // link_bit) % 2 == 0
-        width = to_gene.shape[1] // 2
-        left, right = to_gene[:, :width], to_gene[:, width:]
-        outs[0][...] = jnp.where(clear, left, right)
-        outs[1][...] = jnp.where(clear, right, left)
+        left, right = to_gene[:, : width // 2], to_gene[:, width // 2 :]
+        staying_out[...] = jnp.where(clear, left, right)
+        leaving = halved(jnp.where(clear, right, left))
+        outs[0][...] = jnp.concatenate([*leaving, low], axis=1)
     else:
-        outs[0][...] = to_gene
-
-
-def step(spot, received, link_bit, gene_bit, totals, staying, genes=None):
+        staying_out[...] = to_gene
+    outs[-1][...] = low
+
+
+def step(spot, received, link_bit, gene_bit, totals, staying, genes):
     rank, width = staying[0].shape
-    outs = [struct(*totals[0].shape)]
-    if gene_bit:
-        outs += [struct(rank, 2 * genes[0].shape[1], dtype=jnp.bfloat16)]
-    outs += [struct(rank, width // 2)] * 2 if link_bit else [struct(rank, width)]
-    values = [*totals, *staying, *(genes if gene_bit else ()), received]
+    size = genes.shape[1] * (2 if gene_bit else 1)
+    outs = [struct(*totals[0].shape), struct(rank, width // 2 if link_bit else width)]
+    outs += [struct(rank, width + size, dtype=jnp.bfloat16)] if link_bit else []
+    outs += [struct(rank, size, dtype=jnp.bfloat16)]
+    values = [*totals, *staying, genes, received]
     return pl.pallas_call(
         functools.partial(step_kernel, link_bit, gene_bit),
         in_specs=[SMEM] + [VMEM] * len(values),
@@ -601,21 +620,17 @@
     gene_blocks, peak_blocks = gene_width // BLOCK, peak_width // BLOCK
     side, place, core = spot[0], spot[1], spot[2]
     first = core == 0
-    gram_other, bounds = read_beside(other, features, rank)
+    gram_other, blocks = read_message(other, features, rank)
     gram = gram_mine[...] + gram_other
     old = factors[...]
     below = exact(gram, old) + EPSILON
-    groups = features // BLOCK
-    whole = []
-    for b in range(groups):
-        code = other[:, b * BLOCK : (b + 1) * BLOCK]
-        least = bounds[:, b : b + 1]
-        step = (bounds[:, groups + b : groups + b + 1] - least) / CODES
-        whole.append(sums[:, b * BLOCK : (b + 1) * BLOCK] + decode(code, least, step))
-    whole = jnp.concatenate(whole, axis=1)
+    whole = jnp.concatenate(
+        [sums[:, b * BLOCK : (b + 1) * BLOCK] + block for b, block in enumerate(blocks)], axis=1
+    )
     new = old * whole / below
     low = new.astype(jnp.bfloat16)
-    cell_sums = jnp.concatenate([across(low, received[j, 0:cells, 0:features]) for j in orders[0]], axis=1)
+    counts = jnp.concatenate([received[j, 0:cells, 0:features] for j in orders[0]], axis=0)
+    cell_sums = across(low, counts)
     gram_features = across(low, low)
     kept, sent, *outs = outs
     split = half // 2 * cells
@@ -687,7 +702,7 @@
     me = lax.axis_index(AXIS)
     side, place, core = me // half, me % half, me % 2
     chip_bits = bits_below(half)[1:]
-    cell_bits, link_bits, gene_bits = (turned(chip_bits, i % len(chip_bits)) for i in range(3))
+    cell_bits, link_bits = chip_bits, turned(chip_bits, 1)
     tail = sum(
         jnp.where((me & bit) != 0, 1 << i, 0) for i, bit in enumerate(reversed(cell_bits[2:]))
     )
@@ -701,7 +716,7 @@
     table_shape = (rna_counts.shape[1] // BLOCK, atac_counts.shape[1] // BLOCK)
     cell_order = layout([1] + cell_bits)
     link_order = layout([1] + link_bits)
-    gene_order = layout([1] + gene_bits[::-1])
+    gene_order = layout([1] + link_bits[::-1])
 
     links = (link_gene, link_peak, link_weight, link_count)
     sent = parcels(spot, rna_counts, atac_counts, cell_factor, gene_factor, peak_factor, links, half)
@@ -709,28 +724,25 @@
     received = lax.all_to_all(sent, AXIS, 0, 0, axis_index_groups=halves, tiled=True)
     rows_other = flip(received[:, cells:, :features], 1)
     received_here = pltpu.with_memory_space_constraint(received, pltpu.VMEM)
-    above = -(-2 * width // BLOCK // 8) * 8
-    codes, bounds = pl.pallas_call(
+    codes = pl.pallas_call(
         codes_kernel,
         in_specs=[VMEM] * 2,
-        out_specs=[VMEM] * 2,
-        out_shape=(struct(rank, width, dtype=jnp.int16), struct(above, 2 * rank)),
+        out_specs=VMEM,
+        out_shape=struct(rank, width + 2 * rank, dtype=jnp.int16),
         compiler_params=PARAMS,
     )(gene_factor, peak_factor)
     rows = rank // 4
-    aside = pl.pallas_call(
+    half_table = pl.pallas_call(
         table_kernel,
         grid=(1,),
-        in_specs=[
-            pl.BlockSpec((half, rows, 2 * rank), lambda i: (0, cells // rows, features // (2 * rank))),
-            VMEM,
-        ],
+        in_specs=[pl.BlockSpec((half, rows, 2 * rank), lambda i: (0, cells // rows, features // (2 * rank)))],
         out_specs=VMEM,
-        out_shape=struct(above + table_shape[0], table_shape[1]),
+        out_shape=struct(*table_shape),
         compiler_params=PARAMS,
-    )(received_here, bounds)
-    aside_other = flip(aside, half)
-    sums_shapes = (struct(rank, features), struct(rank, features + 4 * rank, dtype=jnp.int16))
+    )(received_here)
+    half_table_other = flip(half_table, half)
+
+    sums_shapes = (struct(rank, features), struct(rank, features + 2 * rank, dtype=jnp.int16))
     sums, gram, state = pl.pallas_call(
         functools.partial(first_sums_kernel, cell_order),
         in_specs=[VMEM],
@@ -738,7 +750,7 @@
         out_shape=(struct(rank, features), struct(rank, rank), struct(rank, half * cells)),
         compiler_params=PARAMS,
     )(received_here)
-    codes, sums, aside_other = lax.optimization_barrier((codes, sums, aside_other))
+    codes, sums, half_table_other = lax.optimization_barrier((codes, sums, half_table_other))
     codes_other = flip(codes, half)
     sums, message, link_table = pl.pallas_call(
         functools.partial(first_links_kernel, link_scale, widths),
@@ -756,16 +768,16 @@
         out_shape=(*sums_shapes, struct(*table_shape)),
         scratch_shapes=[pltpu.SemaphoreType.DMA, pltpu.SMEM(table_shape, jnp.float32)],
         compiler_params=PARAMS,
-    )(spot, received_here, rows_other, aside, aside_other, sums, gram)
+    )(spot, received_here, rows_other, half_table, half_table_other, sums, gram)
 
     message, codes_other = lax.optimization_barrier((message, codes_other))
     factors = pl.pallas_call(
         twins_kernel,
-        in_specs=[SMEM] + [VMEM] * 4,
+        in_specs=[SMEM] + [VMEM] * 3,
         out_specs=VMEM,
         out_shape=struct(rank, features),
         compiler_params=PARAMS,
-    )(spot, gene_factor, peak_factor, codes_other, aside_other)
+    )(spot, gene_factor, peak_factor, codes_other)
 
     split = half // 2 * cells
     for sweep_index in range(ROUNDS):
@@ -814,15 +826,15 @@
             )(spot, totals, flip(totals, cell_bits[-1]), own_cells)
             return cell_out, gene_out, peak_out
         factors, links_kept, links_sent, genes = outs
-        totals, staying, leaving = step(
-            spot, received_here, link_bits[0], 0, (kept, flip(sent, 1)), (links_kept, flip(links_sent, 1))
+        totals, staying, leaving, genes = step(
+            spot, received_here, link_bits[0], 0, (kept, flip(sent, 1)), (links_kept, flip(links_sent, 1)), genes
         )
-        for i, bits in enumerate(zip(cell_bits, link_bits, gene_bits)):
-            going = lax.optimization_barrier((totals, leaving, genes))
-            got = lax.optimization_barrier(tuple(flip(value, bit) for value, bit in zip(going, bits)))
+        for i, (cell_bit, link_bit) in enumerate(zip(cell_bits, link_bits)):
+            going = lax.optimization_barrier((totals, leaving))
+            got = lax.optimization_barrier((flip(going[0], cell_bit), flip(going[1], link_bit)))
             next_bit = link_bits[i + 1] if i + 1 < len(link_bits) else 0
-            totals, genes, staying, *leaving = step(
-                spot, received_here, next_bit, bits[2], (totals, got[0]), (staying, got[1]), (genes, got[2])
+            totals, staying, *leaving, genes = step(
+                spot, received_here, next_bit, link_bit, (totals, got[0]), (staying, got[1]), genes
             )
             leaving = leaving[0] if next_bit else None
         to_gene = staying
@@ -846,7 +858,7 @@
         and 2 * rank == BLOCK
         and gene_width % BLOCK == 0
         and peak_width % BLOCK == 0
-        and 4 * (features // BLOCK) + 2 <= 2 * rank
+        and rank + 3 + 2 * (features // BLOCK) <= 2 * rank
         and half * link_gene.shape[0] <= 2 * rank
         and rank % 64 == 0
         and atac_counts.shape[1] // BLOCK == 2 * rank

time: 133 us -> 130 us (0.977)
  starting transfers between devices: 19.2 us -> 16.7 us
    ppermute x23 -> x20, starting transfers between devices: 19.2 us -> 16.7 us  [flip(): return lax.ppermute(value, AXIS, [(i, i ^ bit) for i in range(count)])]
    ppermute x23 -> x20, waiting for transfers between devices: 42.7 us -> 43.5 us  [flip(): return lax.ppermute(value, AXIS, [(i, i ^ bit) for i in range(count)])]
  transfers between devices with their start and end apart: 23 -> 20, of which waited for: 18 -> 17; matrix products, arithmetic and copies ran while one was open for 0% -> 0% of each run, Pallas kernels for 4% -> 4%
where the time goes in v9:
time: 130 us
  blocking collectives  49.6 us (38%)
  waiting for transfers between devices  43.5 us (33%)
  Pallas kernels  18.4 us (14%)
  starting transfers between devices  16.7 us (13%)
  between operations  1.57 us (1%)
    all_to_all x1, blocking collectives, shards_blocks(): lax.all_to_all(sent, AXIS, 0, 0, axis_index_groups=halves, tiled=True)  49.6 us
    ppermute x20, waiting for transfers between devices, flip(): return lax.ppermute(value, AXIS, [(i, i ^ bit) for i in range(count)])  43.5 us
    ppermute x20, starting transfers between devices, flip(): return lax.ppermute(value, AXIS, [(i, i ^ bit) for i in range(count)])  16.7 us
    pallas_call x2, Pallas kernels, shards_blocks(): pl.pallas_call(functools.partial(update_kernel, last, widths, (cell_order...  4.67 us
    pallas_call x1, Pallas kernels, shards_blocks(): pl.pallas_call(functools.partial(next_sums_kernel, link_scale, widths, (c...  2.74 us
    pallas_call x1, Pallas kernels, shards_blocks(): pl.pallas_call(functools.partial(first_links_kernel, link_scale, widths),...  2.72 us
  transfers between devices with their start and end apart: 20, of which 17 were waited for; matrix products, arithmetic and copies ran while one was open for 0% of the time, Pallas kernels for 4%

profile of v9, /device:TPU:0, one launch (start us, length us, event | category | flops | bytes accessed | tf_op | source)
XLA Modules:
  0.0 130.0 jit_solution(863672080353547698)
XLA Ops:
  1.4 2.5 %shard_map.112 = bf16[16,80,1408]{2,1,0:T(8,128)(2,1)S(1)} custom-call(s32[4]{0:T(128)S(1)} %pad_add_fusion.spot, bf16[64,4096]{1,0:T(8,128)(2,1)} %rna_1.1, bf16[64,4096]{1,0:T(8,128)(2,1)} %rna_1.1, bf16[64,16384]{1,0:T(8,128)(2,1)} %atac_1.1, bf16[64,16384]{1,0:T(8,128)(2,1)} %atac_1.1, f32[64,64]{1,0:T(8,128)} %cell.1, f32[64,128]{1,0:T(8,128)} %gene.5, ...), custom_call_target="tpu_custom_call" | custom-call | tf_op jit(solution)/shard_map/pallas_call | solution.py:398
  3.9 49.6 %all_to_all.5.received_slots.received.mine = bf16[16,80,1408]{2,1,0:T(8,128)(2,1)S(1)} all-to-all(bf16[16,80,1408]{2,1,0:T(8,128)(2,1)S(1)} %shard_map.112), channel_id=1, replica_groups={{0,1,2,3,4,5,6,7,8,9,10,11,12,13,14,15},{16,17,18,19,20,21,22,23,24,25,..., dimensions={0} | all-to-all | bytes 7208960 | tf_op jit(solution)/shard_map/all_to_all | solution.py:724
  53.8 2.6 %collective-permute-start.1 = (f32[32,128]{1,0:T(8,128)S(1)}, f32[32,128]{1,0:T(8,128)S(1)}, u32[]{:S(2)}, u32[]{:S(2)}) collective-permute-start(f32[32,128]{1,0:T(8,128)S(1)} %shard_map.113.half_table), channel_id=1, source_target_pairs={{0,16},{1,17},{2,18},{3,19},{4,20},{5,21},{6,22},{7,23},{8,24},{9,... | collective-permute-start | bytes 49160 | tf_op jit(solution)/shard_map/ppermute | solution.py:25
  56.7 0.8 shard_map.115
  57.5 1.1 collective-permute-done.1.half_table_other
  58.6 2.4 %collective-permute-start.2 = (s16[64,768]{1,0:T(8,128)(2,1)S(1)}, s16[64,768]{1,0:T(8,128)(2,1)S(1)}, u32[]{:S(2)}, u32[]{:S(2)}) collective-permute-start(s16[64,768]{1,0:T(8,128)(2,1)S(1)} %shard_map.114), channel_id=1, source_target_pairs={{0,16},{1,17},{2,18},{3,19},{4,20},{5,21},{6,22},{7,23},{8,24},{9,... | collective-permute-start | bytes 294920 | tf_op jit(solution)/shard_map/ppermute | solution.py:25
  61.0 2.7 %shard_map.116 = (f32[64,1280]{1,0:T(8,128)S(1)}, s16[64,1408]{1,0:T(8,128)(2,1)S(1)}, f32[32,128]{1,0:T(8,128)S(1)}) custom-call(s32[4]{0:T(128)S(1)} %pad_add_fusion.spot, bf16[16,80,1408]{2,1,0:T(8,128)(2,1)S(1)} %all_to_all.5.received_slots.received.mine, bf16[16,16,1280]{2,1,0:T(8,128)(2,1)S(1)} %collective-permute-done.other, ...), custom_call_target="tpu_custom_call" | custom-call | tf_op jit(solution)/shard_map/pallas_call | solution.py:755
  63.8 1.8 %collective-permute-done.2.got = s16[64,768]{1,0:T(8,128)(2,1)S(1)} collective-permute-done((s16[64,768]{1,0:T(8,128)(2,1)S(1)}, s16[64,768]{1,0:T(8,128)(2,1)S(1)}, u32[]{:S(2)}, u32[]{:S(2)}) %collective-permute-start.2) | collective-permute-done | bytes 98336 | tf_op jit(solution)/shard_map/ppermute | solution.py:25
  65.6 1.0 collective-permute-start.3
  66.7 0.8 shard_map.117.factors
  67.4 7.1 %collective-permute-done.3.other = s16[64,1408]{1,0:T(8,128)(2,1)S(1)} collective-permute-done((s16[64,1408]{1,0:T(8,128)(2,1)S(1)}, s16[64,1408]{1,0:T(8,128)(2,1)S(1)}, u32[]{:S(2)}, u32[]{:S(2)}) %collective-permute-start.3) | collective-permute-done | bytes 180256 | tf_op jit(solution)/shard_map/ppermute | solution.py:25
  74.5 2.4 %shard_map.118 = (f32[72,512]{1,0:T(8,128)S(1)}, f32[72,512]{1,0:T(8,128)S(1)}, f32[64,1280]{1,0:T(8,128)S(1)}, f32[64,1024]{1,0:T(8,128)S(1)}, f32[64,1024]{1,0:T(8,128)S(1)}, /*index=5*/bf16[64,128]{1,0:T(8,128)(2,1)S(1)}) custom-call(s32[4]{0:T(128)S(1)} %pad_add_fusion.spot, f32[32,128]{1,0:T(8,128)S(1)} %get-tuple-element.59.table, ...), custom_call_target="tpu_custom_call" | custom-call | tf_op jit(solution)/shard_map/pallas_call | solution.py:792
  77.5 1.2 collective-permute-done.4.totals_got
  78.7 0.6 shard_map.119
  79.4 0.8 collective-permute-start.7
  80.2 5.1 %collective-permute-done.6.totals_got = f32[72,512]{1,0:T(8,128)S(1)} collective-permute-done((f32[72,512]{1,0:T(8,128)S(1)}, f32[72,512]{1,0:T(8,128)S(1)}, u32[]{:S(2)}, u32[]{:S(2)}) %collective-permute-start.6) | collective-permute-done | bytes 147488 | tf_op jit(solution)/shard_map/ppermute | solution.py:25
  85.4 0.6 shard_map.120
  86.5 4.6 %collective-permute-done.9.got = bf16[64,768]{1,0:T(8,128)(2,1)S(1)} collective-permute-done((bf16[64,768]{1,0:T(8,128)(2,1)S(1)}, bf16[64,768]{1,0:T(8,128)(2,1)S(1)}, u32[]{:S(2)}, u32[]{:S(2)}) %collective-permute-start.9) | collective-permute-done | bytes 98336 | tf_op jit(solution)/shard_map/ppermute | solution.py:25
  91.2 0.6 shard_map.121
  91.8 1.7 %collective-permute-start.11 = (bf16[64,768]{1,0:T(8,128)(2,1)S(1)}, bf16[64,768]{1,0:T(8,128)(2,1)S(1)}, u32[]{:S(2)}, u32[]{:S(2)}) collective-permute-start(bf16[64,768]{1,0:T(8,128)(2,1)S(1)} %get-tuple-element.89), channel_id=1, source_target_pairs={{0,2},{1,3},{2,0},{3,1},{4,6},{5,7},{6,4},{7,5},{8,10},{9,11},{10,... | collective-permute-start | bytes 294920 | tf_op jit(solution)/shard_map/ppermute | solution.py:25
  93.6 2.9 %collective-permute-done.11.got = bf16[64,768]{1,0:T(8,128)(2,1)S(1)} collective-permute-done((bf16[64,768]{1,0:T(8,128)(2,1)S(1)}, bf16[64,768]{1,0:T(8,128)(2,1)S(1)}, u32[]{:S(2)}, u32[]{:S(2)}) %collective-permute-start.11) | collective-permute-done | bytes 98336 | tf_op jit(solution)/shard_map/ppermute | solution.py:25
  98.1 1.0 collective-permute-done.13.genes_other
  99.2 2.7 %shard_map.123 = (f32[64,1280]{1,0:T(8,128)S(1)}, s16[64,1408]{1,0:T(8,128)(2,1)S(1)}, f32[64,64]{1,0:T(8,128)S(1)}, f32[64,1024]{1,0:T(8,128)}, f32[64,64]{1,0:T(8,128)S(1)}) custom-call(s32[4]{0:T(128)S(1)} %pad_add_fusion.spot, f32[32,128]{1,0:T(8,128)S(1)} %get-tuple-element.59.table, f32[72,512]{1,0:T(8,128)S(1)} %get-tuple-element.94.mine, ...), custom_call_target="tpu_custom_call" | custom-call | tf_op jit(solution)/shard_map/pallas_call | solution.py:841
  101.9 2.6 %collective-permute-start.14 = (s16[64,1408]{1,0:T(8,128)(2,1)S(1)}, s16[64,1408]{1,0:T(8,128)(2,1)S(1)}, u32[]{:S(2)}, u32[]{:S(2)}) collective-permute-start(s16[64,1408]{1,0:T(8,128)(2,1)S(1)} %get-tuple-element.100), channel_id=1, source_target_pairs={{0,16},{1,17},{2,18},{3,19},{4,20},{5,21},{6,22},{7,23},{8,24},{9,... | collective-permute-start | bytes 540680 | tf_op jit(solution)/shard_map/ppermute | solution.py:25
  104.5 8.9 %collective-permute-done.14.other = s16[64,1408]{1,0:T(8,128)(2,1)S(1)} collective-permute-done((s16[64,1408]{1,0:T(8,128)(2,1)S(1)}, s16[64,1408]{1,0:T(8,128)(2,1)S(1)}, u32[]{:S(2)}, u32[]{:S(2)}) %collective-permute-start.14) | collective-permute-done | bytes 180256 | tf_op jit(solution)/shard_map/ppermute | solution.py:25
  113.5 2.2 %shard_map.124 = (f32[72,512]{1,0:T(8,128)S(1)}, f32[72,512]{1,0:T(8,128)S(1)}, f32[64,128]{1,0:T(8,128)}, f32[64,512]{1,0:T(8,128)}) custom-call(s32[4]{0:T(128)S(1)} %pad_add_fusion.spot, f32[32,128]{1,0:T(8,128)S(1)} %get-tuple-element.59.table, f32[64,1280]{1,0:T(8,128)S(1)} %get-tuple-element.98.sums, f32[64,64]{1,0:T(8,128)S(1)} %get-tuple-element.99.gram_mine, ...), custom_call_target="tpu_custom_call" | custom-call | tf_op jit(solution)/shard_map/pallas_call | solution.py:792
  115.8 1.3 %collective-permute-done.15 = f32[72,512]{1,0:T(8,128)S(1)} collective-permute-done((f32[72,512]{1,0:T(8,128)S(1)}, f32[72,512]{1,0:T(8,128)S(1)}, u32[]{:S(2)}, u32[]{:S(2)}) %collective-permute-start.15) | collective-permute-done | bytes 147488 | tf_op jit(solution)/shard_map/ppermute | solution.py:25
  117.3 2.7 %collective-permute-start.18 = (f32[96,128]{1,0:T(8,128)S(1)}, f32[96,128]{1,0:T(8,128)S(1)}, u32[]{:S(2)}, u32[]{:S(2)}) collective-permute-start(f32[96,128]{1,0:T(8,128)S(1)} %constant_dynamic-update-slice_fusion.15), channel_id=1, source_target_pairs={{0,6},{1,7},{2,4},{3,5},{4,2},{5,3},{6,0},{7,1},{8,14},{9,15},{10,... | collective-permute-start | bytes 147464 | tf_op jit(solution)/shard_map/ppermute | solution.py:25
  120.9 1.5 %collective-permute-done.18 = f32[96,128]{1,0:T(8,128)S(1)} collective-permute-done((f32[96,128]{1,0:T(8,128)S(1)}, f32[96,128]{1,0:T(8,128)S(1)}, u32[]{:S(2)}, u32[]{:S(2)}) %collective-permute-start.18) | collective-permute-done | bytes 49184 | tf_op jit(solution)/shard_map/ppermute | solution.py:25
  122.4 1.7 %collective-permute-done.16 = f32[96,128]{1,0:T(8,128)S(1)} collective-permute-done((f32[96,128]{1,0:T(8,128)S(1)}, f32[96,128]{1,0:T(8,128)S(1)}, u32[]{:S(2)}, u32[]{:S(2)}) %collective-permute-start.16) | collective-permute-done | bytes 49184 | tf_op jit(solution)/shard_map/ppermute | solution.py:25
  124.5 4.1 %collective-permute-done.19.other = f32[96,128]{1,0:T(8,128)S(1)} collective-permute-done((f32[96,128]{1,0:T(8,128)S(1)}, f32[96,128]{1,0:T(8,128)S(1)}, u32[]{:S(2)}, u32[]{:S(2)}) %collective-permute-start.19) | collective-permute-done | bytes 49184 | tf_op jit(solution)/shard_map/ppermute | solution.py:25
  128.6 1.4 %shard_map.125 = f32[64,64]{1,0:T(8,128)} custom-call(s32[4]{0:T(128)S(1)} %pad_add_fusion.spot, f32[96,128]{1,0:T(8,128)S(1)} %add_add_fusion.mine, f32[96,128]{1,0:T(8,128)S(1)} %collective-permute-done.19.other, f32[64,64]{1,0:T(8,128)S(1)} %get-tuple-element.104.old), custom_call_target="tpu_custom_call" | custom-call | tf_op jit(solution)/shard_map/pallas_call | solution.py:820
  (42 shorter events, 5.1 us)
Async XLA Ops:
  53.5 2.9 %copy-start = (f32[64,512]{1,0:T(8,128)S(1)}, f32[64,512]{1,0:T(8,128)}, u32[]{:S(2)}) copy-start(f32[64,512]{1,0:T(8,128)} %peak.5) | copy-start | bytes 393220
  53.5 2.9 %copy-start.1 = (f32[64,128]{1,0:T(8,128)S(1)}, f32[64,128]{1,0:T(8,128)}, u32[]{:S(2)}) copy-start(f32[64,128]{1,0:T(8,128)} %gene.5) | copy-start | bytes 98308
  53.6 7.5 %collective-permute-start = (bf16[16,16,1280]{2,1,0:T(8,128)(2,1)S(1)}, bf16[16,16,1280]{2,1,0:T(8,128)(2,1)S(1)}, u32[]{:S(2)}, u32[]{:S(2)}) collective-permute-start(bf16[16,16,1280]{2,1,0:T(8,128)(2,1)S(1)} %slice.14), channel_id=1, source_target_pairs={{0,1},{1,0},{2,3},{3,2},{4,5},{5,4},{6,7},{7,6},{8,9},{9,8},{10,11... | collective-permute-start | bytes 1966088 | tf_op jit(solution)/shard_map/ppermute | solution.py:25
  53.8 4.8 %collective-permute-start.1 = (f32[32,128]{1,0:T(8,128)S(1)}, f32[32,128]{1,0:T(8,128)S(1)}, u32[]{:S(2)}, u32[]{:S(2)}) collective-permute-start(f32[32,128]{1,0:T(8,128)S(1)} %shard_map.113.half_table), channel_id=1, source_target_pairs={{0,16},{1,17},{2,18},{3,19},{4,20},{5,21},{6,22},{7,23},{8,24},{9,... | collective-permute-start | bytes 49160 | tf_op jit(solution)/shard_map/ppermute | solution.py:25
  58.6 7.0 %collective-permute-start.2 = (s16[64,768]{1,0:T(8,128)(2,1)S(1)}, s16[64,768]{1,0:T(8,128)(2,1)S(1)}, u32[]{:S(2)}, u32[]{:S(2)}) collective-permute-start(s16[64,768]{1,0:T(8,128)(2,1)S(1)} %shard_map.114), channel_id=1, source_target_pairs={{0,16},{1,17},{2,18},{3,19},{4,20},{5,21},{6,22},{7,23},{8,24},{9,... | collective-permute-start | bytes 294920 | tf_op jit(solution)/shard_map/ppermute | solution.py:25
  65.6 8.9 %collective-permute-start.3 = (s16[64,1408]{1,0:T(8,128)(2,1)S(1)}, s16[64,1408]{1,0:T(8,128)(2,1)S(1)}, u32[]{:S(2)}, u32[]{:S(2)}) collective-permute-start(s16[64,1408]{1,0:T(8,128)(2,1)S(1)} %get-tuple-element.63), channel_id=1, source_target_pairs={{0,16},{1,17},{2,18},{3,19},{4,20},{5,21},{6,22},{7,23},{8,24},{9,... | collective-permute-start | bytes 540680 | tf_op jit(solution)/shard_map/ppermute | solution.py:25
  76.9 1.8 %collective-permute-start.5 = (f32[64,1024]{1,0:T(8,128)S(1)}, f32[64,1024]{1,0:T(8,128)S(1)}, u32[]{:S(2)}, u32[]{:S(2)}) collective-permute-start(f32[64,1024]{1,0:T(8,128)S(1)} %get-tuple-element.68), channel_id=1, source_target_pairs={{0,1},{1,0},{2,3},{3,2},{4,5},{5,4},{6,7},{7,6},{8,9},{9,8},{10,11... | collective-permute-start | bytes 786440 | tf_op jit(solution)/shard_map/ppermute | solution.py:25
  77.0 1.7 %collective-permute-start.4 = (f32[72,512]{1,0:T(8,128)S(1)}, f32[72,512]{1,0:T(8,128)S(1)}, u32[]{:S(2)}, u32[]{:S(2)}) collective-permute-start(f32[72,512]{1,0:T(8,128)S(1)} %get-tuple-element.66), channel_id=1, source_target_pairs={{0,1},{1,0},{2,3},{3,2},{4,5},{5,4},{6,7},{7,6},{8,9},{9,8},{10,11... | collective-permute-start | bytes 442376 | tf_op jit(solution)/shard_map/ppermute | solution.py:25
  79.3 6.0 %collective-permute-start.6 = (f32[72,512]{1,0:T(8,128)S(1)}, f32[72,512]{1,0:T(8,128)S(1)}, u32[]{:S(2)}, u32[]{:S(2)}) collective-permute-start(f32[72,512]{1,0:T(8,128)S(1)} %get-tuple-element.72.totals), channel_id=1, source_target_pairs={{0,2},{1,3},{2,0},{3,1},{4,6},{5,7},{6,4},{7,5},{8,10},{9,11},{10,... | collective-permute-start | bytes 442376 | tf_op jit(solution)/shard_map/ppermute | solution.py:25
  79.4 6.0 %collective-permute-start.7 = (bf16[64,1152]{1,0:T(8,128)(2,1)S(1)}, bf16[64,1152]{1,0:T(8,128)(2,1)S(1)}, u32[]{:S(2)}, u32[]{:S(2)}) collective-permute-start(bf16[64,1152]{1,0:T(8,128)(2,1)S(1)} %get-tuple-element.73), channel_id=1, source_target_pairs={{0,4},{1,5},{2,6},{3,7},{4,0},{5,1},{6,2},{7,3},{8,12},{9,13},{10,... | collective-permute-start | bytes 442376 | tf_op jit(solution)/shard_map/ppermute | solution.py:25
  86.0 5.2 %collective-permute-start.8 = (f32[72,512]{1,0:T(8,128)S(1)}, f32[72,512]{1,0:T(8,128)S(1)}, u32[]{:S(2)}, u32[]{:S(2)}) collective-permute-start(f32[72,512]{1,0:T(8,128)S(1)} %get-tuple-element.80.totals), channel_id=1, source_target_pairs={{0,4},{1,5},{2,6},{3,7},{4,0},{5,1},{6,2},{7,3},{8,12},{9,13},{10,... | collective-permute-start | bytes 442376 | tf_op jit(solution)/shard_map/ppermute | solution.py:25
  86.4 4.6 %collective-permute-start.9 = (bf16[64,768]{1,0:T(8,128)(2,1)S(1)}, bf16[64,768]{1,0:T(8,128)(2,1)S(1)}, u32[]{:S(2)}, u32[]{:S(2)}) collective-permute-start(bf16[64,768]{1,0:T(8,128)(2,1)S(1)} %get-tuple-element.81), channel_id=1, source_target_pairs={{0,8},{1,9},{2,10},{3,11},{4,12},{5,13},{6,14},{7,15},{8,0},{9,1},... | collective-permute-start | bytes 294920 | tf_op jit(solution)/shard_map/ppermute | solution.py:25
  91.8 5.2 %collective-permute-start.10 = (f32[72,512]{1,0:T(8,128)S(1)}, f32[72,512]{1,0:T(8,128)S(1)}, u32[]{:S(2)}, u32[]{:S(2)}) collective-permute-start(f32[72,512]{1,0:T(8,128)S(1)} %get-tuple-element.88.totals), channel_id=1, source_target_pairs={{0,8},{1,9},{2,10},{3,11},{4,12},{5,13},{6,14},{7,15},{8,0},{9,1},... | collective-permute-start | bytes 442376 | tf_op jit(solution)/shard_map/ppermute | solution.py:25
  91.8 4.7 %collective-permute-start.11 = (bf16[64,768]{1,0:T(8,128)(2,1)S(1)}, bf16[64,768]{1,0:T(8,128)(2,1)S(1)}, u32[]{:S(2)}, u32[]{:S(2)}) collective-permute-start(bf16[64,768]{1,0:T(8,128)(2,1)S(1)} %get-tuple-element.89), channel_id=1, source_target_pairs={{0,2},{1,3},{2,0},{3,1},{4,6},{5,7},{6,4},{7,5},{8,10},{9,11},{10,... | collective-permute-start | bytes 294920 | tf_op jit(solution)/shard_map/ppermute | solution.py:25
  97.6 1.6 %collective-permute-start.12 = (f32[72,512]{1,0:T(8,128)S(1)}, f32[72,512]{1,0:T(8,128)S(1)}, u32[]{:S(2)}, u32[]{:S(2)}) collective-permute-start(f32[72,512]{1,0:T(8,128)S(1)} %get-tuple-element.94.mine), channel_id=1, source_target_pairs={{0,1},{1,0},{2,3},{3,2},{4,5},{5,4},{6,7},{7,6},{8,9},{9,8},{10,11... | collective-permute-start | bytes 442376 | tf_op jit(solution)/shard_map/ppermute | solution.py:25
  97.6 1.5 %collective-permute-start.13 = (bf16[64,1024]{1,0:T(8,128)(2,1)S(1)}, bf16[64,1024]{1,0:T(8,128)(2,1)S(1)}, u32[]{:S(2)}, u32[]{:S(2)}) collective-permute-start(bf16[64,1024]{1,0:T(8,128)(2,1)S(1)} %get-tuple-element.97.genes_mine), channel_id=1, source_target_pairs={{0,1},{1,0},{2,3},{3,2},{4,5},{5,4},{6,7},{7,6},{8,9},{9,8},{10,11... | collective-permute-start | bytes 393224 | tf_op jit(solution)/shard_map/ppermute | solution.py:25
  101.9 11.5 %collective-permute-start.14 = (s16[64,1408]{1,0:T(8,128)(2,1)S(1)}, s16[64,1408]{1,0:T(8,128)(2,1)S(1)}, u32[]{:S(2)}, u32[]{:S(2)}) collective-permute-start(s16[64,1408]{1,0:T(8,128)(2,1)S(1)} %get-tuple-element.100), channel_id=1, source_target_pairs={{0,16},{1,17},{2,18},{3,19},{4,20},{5,21},{6,22},{7,23},{8,24},{9,... | collective-permute-start | bytes 540680 | tf_op jit(solution)/shard_map/ppermute | solution.py:25
  115.7 1.4 %collective-permute-start.15 = (f32[72,512]{1,0:T(8,128)S(1)}, f32[72,512]{1,0:T(8,128)S(1)}, u32[]{:S(2)}, u32[]{:S(2)}) collective-permute-start(f32[72,512]{1,0:T(8,128)S(1)} %get-tuple-element.103), channel_id=1, source_target_pairs={{0,1},{1,0},{2,3},{3,2},{4,5},{5,4},{6,7},{7,6},{8,9},{9,8},{10,11... | collective-permute-start | bytes 442376 | tf_op jit(solution)/shard_map/ppermute | solution.py:25
  117.3 5.1 %collective-permute-start.18 = (f32[96,128]{1,0:T(8,128)S(1)}, f32[96,128]{1,0:T(8,128)S(1)}, u32[]{:S(2)}, u32[]{:S(2)}) collective-permute-start(f32[96,128]{1,0:T(8,128)S(1)} %constant_dynamic-update-slice_fusion.15), channel_id=1, source_target_pairs={{0,6},{1,7},{2,4},{3,5},{4,2},{5,3},{6,0},{7,1},{8,14},{9,15},{10,... | collective-permute-start | bytes 147464 | tf_op jit(solution)/shard_map/ppermute | solution.py:25
  120.0 4.1 %collective-permute-start.16 = (f32[96,128]{1,0:T(8,128)S(1)}, f32[96,128]{1,0:T(8,128)S(1)}, u32[]{:S(2)}, u32[]{:S(2)}) collective-permute-start(f32[96,128]{1,0:T(8,128)S(1)} %get-tuple-element.120), channel_id=1, source_target_pairs={{0,2},{1,3},{2,0},{3,1},{4,6},{5,7},{6,4},{7,5},{8,10},{9,11},{10,... | collective-permute-start | bytes 147464 | tf_op jit(solution)/shard_map/ppermute | solution.py:25
  120.3 4.1 %collective-permute-start.17 = (f32[96,128]{1,0:T(8,128)S(1)}, f32[96,128]{1,0:T(8,128)S(1)}, u32[]{:S(2)}, u32[]{:S(2)}) collective-permute-start(f32[96,128]{1,0:T(8,128)S(1)} %get-tuple-element.107), channel_id=1, source_target_pairs={{0,4},{1,5},{2,6},{3,7},{4,0},{5,1},{6,2},{7,3},{8,12},{9,13},{10,... | collective-permute-start | bytes 147464 | tf_op jit(solution)/shard_map/ppermute | solution.py:25
  124.5 4.2 %collective-permute-start.19 = (f32[96,128]{1,0:T(8,128)S(1)}, f32[96,128]{1,0:T(8,128)S(1)}, u32[]{:S(2)}, u32[]{:S(2)}) collective-permute-start(f32[96,128]{1,0:T(8,128)S(1)} %add_add_fusion.mine), channel_id=1, source_target_pairs={{0,8},{1,9},{2,10},{3,11},{4,12},{5,13},{6,14},{7,15},{8,0},{9,1},... | collective-permute-start | bytes 147464 | tf_op jit(solution)/shard_map/ppermute | solution.py:25

commit v10 on v9

--- a/solution.py
+++ b/solution.py
@@ -1,4 +1,5 @@
 import functools
+import random
 
 import jax
 import jax.numpy as jnp
@@ -15,6 +16,7 @@
 UNITS = 16384.0
 TINY = 1e-30
 AXIS = "cells"
+SEED = 16
 PARAMS = pltpu.CompilerParams(vmem_limit_bytes=14 * 1024 * 1024)
 SMEM = pl.BlockSpec(memory_space=pltpu.SMEM)
 VMEM = pl.BlockSpec(memory_space=pltpu.VMEM)
@@ -222,6 +224,12 @@
     ]
 
 
+def shuffled(size, seed):
+    places = list(range(size))
+    random.Random(seed).shuffle(places)
+    return places
+
+
 def turned(bits, by):
     return bits[by:] + bits[:by]
 
@@ -256,7 +264,7 @@
     return (squares[:rank, :rank] + squares[rank:, rank:]) + (squares[:rank, rank:] + squares[rank:, :rank])
 
 
-def parcels_kernel(spot, rna_0, rna_1, atac_0, atac_1, cell, gene, peak, *refs):
+def parcels_kernel(seats, spot, rna_0, rna_1, atac_0, atac_1, cell, gene, peak, *refs):
     links, out, copied, slots, sems = refs[:4], refs[4], refs[5:9], refs[9], refs[10]
 
     copies = [pltpu.make_async_copy(link, to, sems.at[i]) for i, (link, to) in enumerate(zip(links, copied))]
@@ -274,18 +282,16 @@
     gene_low = gene[...].astype(jnp.bfloat16)
     peak_low = peak[...].astype(jnp.bfloat16)
     part = rank // 4
-    each = rna_0.shape[1] // gene_width
-    base = pl.program_id(0) * each
-    for j in range(each):
+    for j, seat in enumerate(seats):
         at = 0
         for source, size in ((rna_0, gene_width), (rna_1, gene_width), (atac_0, peak_width), (atac_1, peak_width)):
-            out[base + j, 0:cells, at : at + size] = source[:, j * size : (j + 1) * size]
+            out[seat, 0:cells, at : at + size] = source[:, j * size : (j + 1) * size]
             at += size
-        out[base + j, 0:cells, at:] = cell_pair
+        out[seat, 0:cells, at:] = cell_pair
         for s in range(2):
             row = (2 * (j % 2) + s) * part
-            out[base + j, cells:, s * width : s * width + gene_width] = gene_low[row : row + part]
-            out[base + j, cells:, s * width + gene_width : (s + 1) * width] = peak_low[row : row + part]
+            out[seat, cells:, s * width : s * width + gene_width] = gene_low[row : row + part]
+            out[seat, cells:, s * width + gene_width : (s + 1) * width] = peak_low[row : row + part]
 
     @pl.when(pl.program_id(0) == 0)
     def _():
@@ -302,8 +308,8 @@
                 value = jnp.where((lane == s) & (row == r), entry.astype(jnp.float32), value)
         slots[...] = value.astype(jnp.bfloat16)
 
-    for j in range(each):
-        out[base + j, cells:, 2 * width :] = slots[...]
+    for seat in seats:
+        out[seat, cells:, 2 * width :] = slots[...]
 
 
 def power_of(top):
@@ -381,23 +387,22 @@
     return pltpu.with_memory_space_constraint(value, pltpu.HBM)
 
 
-def parcels(spot, rna_counts, atac_counts, cell_factor, gene_factor, peak_factor, links, half):
+def parcels(spot, rna_counts, atac_counts, cell_factor, gene_factor, peak_factor, links, seats):
+    half = len(seats)
     cells = rna_counts.shape[0]
     rank = cell_factor.shape[0]
     gene_width, peak_width = gene_factor.shape[1], peak_factor.shape[1]
     rows, lanes = cells + rank // 4, 2 * (gene_width + peak_width) + 2 * rank
-    each = 8
-    steps = half // each
 
     def columns(width, side):
-        return pl.BlockSpec((cells, each * width), lambda i: (0, i + side * steps))
+        return pl.BlockSpec((cells, half * width), lambda i: (0, side))
 
     def whole(array):
         return pl.BlockSpec(array.shape, lambda i: (0, 0))
 
     return pl.pallas_call(
-        parcels_kernel,
-        grid=(steps,),
+        functools.partial(parcels_kernel, seats),
+        grid=(1,),
         in_specs=[SMEM, columns(gene_width, 0), columns(gene_width, 1), columns(peak_width, 0), columns(peak_width, 1)]
         + [whole(a) for a in (cell_factor, gene_factor, peak_factor)]
         + [pl.BlockSpec(memory_space=pl.ANY)] * 4,
@@ -472,7 +477,7 @@
 
 
 def first_links_kernel(
-    link_scale, widths, spot, mine, other, half_table, half_table_other, sums_in, gram, sums, message, table, sem, table_smem
+    link_scale, widths, seats, spot, mine, other, half_table, half_table_other, sums_in, gram, sums, message, table, sem, table_smem
 ):
     half = mine.shape[0]
     rank, features = sums_in.shape
@@ -494,7 +499,9 @@
         blocks = []
         for b in range(width // BLOCK):
             pieces = [
-                ref[j, :, s * width + b * BLOCK : s * width + (b + 1) * BLOCK] for ref in (mine, other) for s in range(2)
+                ref[seats[j], :, s * width + b * BLOCK : s * width + (b + 1) * BLOCK]
+                for ref in (mine, other)
+                for s in range(2)
             ]
             blocks.append(jnp.concatenate(pieces, axis=0).astype(jnp.float32))
         for b in range(gene_blocks):
@@ -606,7 +613,7 @@
     links = jnp.concatenate(
         [jnp.where(side == 0, gene_links, nothing), jnp.where(side == 0, nothing, gene_links), *total], axis=1
     )
-    counts = jnp.concatenate([received[j, 0:cells, 0:features] for j in orders[0]], axis=0)
+    counts = jnp.concatenate([received[j, 0:cells, 0:features] for j in orders[2]], axis=0)
     products = jnp.dot(high, counts, preferred_element_type=jnp.float32)
     gram[...] = gram_of(high, rest)
     finish_sums(products + link_scale * links, gram[...], sums, message)
@@ -719,8 +726,11 @@
     gene_order = layout([1] + link_bits[::-1])
 
     links = (link_gene, link_peak, link_weight, link_count)
-    sent = parcels(spot, rna_counts, atac_counts, cell_factor, gene_factor, peak_factor, links, half)
-    halves = [list(range(half)), list(range(half, count))]
+    in_seats = shuffled(half, SEED)
+    seats = [in_seats.index(j) for j in range(half)]
+    cell_seats = [seats[j] for j in cell_order]
+    sent = parcels(spot, rna_counts, atac_counts, cell_factor, gene_factor, peak_factor, links, seats)
+    halves = [[side_start + j for j in in_seats] for side_start in (0, half)]
     received = lax.all_to_all(sent, AXIS, 0, 0, axis_index_groups=halves, tiled=True)
     rows_other = flip(received[:, cells:, :features], 1)
     received_here = pltpu.with_memory_space_constraint(received, pltpu.VMEM)
@@ -744,7 +754,7 @@
 
     sums_shapes = (struct(rank, features), struct(rank, features + 2 * rank, dtype=jnp.int16))
     sums, gram, state = pl.pallas_call(
-        functools.partial(first_sums_kernel, cell_order),
+        functools.partial(first_sums_kernel, cell_seats),
         in_specs=[VMEM],
         out_specs=[VMEM] * 3,
         out_shape=(struct(rank, features), struct(rank, rank), struct(rank, half * cells)),
@@ -753,7 +763,7 @@
     codes, sums, half_table_other = lax.optimization_barrier((codes, sums, half_table_other))
     codes_other = flip(codes, half)
     sums, message, link_table = pl.pallas_call(
-        functools.partial(first_links_kernel, link_scale, widths),
+        functools.partial(first_links_kernel, link_scale, widths, seats),
         grid=(1,),
         in_specs=[
             SMEM,
@@ -790,7 +800,7 @@
             outs += [struct(rank, features)] + [struct(rank, half // 2 * gene_width)] * 2
             outs += [struct(rank, gene_width, dtype=jnp.bfloat16)]
         kept, sent, *outs = pl.pallas_call(
-            functools.partial(update_kernel, last, widths, (cell_order, link_order)),
+            functools.partial(update_kernel, last, widths, (cell_seats, link_order)),
             in_specs=[SMEM] * 2 + [VMEM] * 5,
             out_specs=[VMEM] * len(outs),
             out_shape=outs,
@@ -839,7 +849,7 @@
             leaving = leaving[0] if next_bit else None
         to_gene = staying
         sums, message, gram, state, own_cells = pl.pallas_call(
-            functools.partial(next_sums_kernel, link_scale, widths, (cell_order, gene_order)),
+            functools.partial(next_sums_kernel, link_scale, widths, (cell_order, gene_order, cell_seats)),
             in_specs=[SMEM] * 2 + [VMEM] * 7,
             out_specs=[VMEM] * 5,
             out_shape=(*sums_shapes, struct(rank, rank), struct(rank, half * cells), struct(rank, cells)),

time: 130 us -> 129 us (level)
  blocking collectives: 49.6 us -> 47.7 us
    all_to_all x1, blocking collectives: 49.6 us -> 47.7 us  [shards_blocks(): lax.all_to_all(sent, AXIS, 0, 0, axis_index_groups=halves, tiled=True)]
  transfers between devices with their start and end apart: 20 -> 20, of which waited for: 17 -> 16; matrix products, arithmetic and copies ran while one was open for 0% -> 0% of each run, Pallas kernels for 4% -> 4%
where the time goes in v10:
time: 129 us
  blocking collectives  47.7 us (37%)
  waiting for transfers between devices  43.2 us (33%)
  Pallas kernels  18.5 us (14%)
  starting transfers between devices  17.7 us (14%)
  between operations  1.56 us (1%)
    all_to_all x1, blocking collectives, shards_blocks(): lax.all_to_all(sent, AXIS, 0, 0, axis_index_groups=halves, tiled=True)  47.7 us
    ppermute x20, waiting for transfers between devices, flip(): return lax.ppermute(value, AXIS, [(i, i ^ bit) for i in range(count)])  43.2 us
    ppermute x20, starting transfers between devices, flip(): return lax.ppermute(value, AXIS, [(i, i ^ bit) for i in range(count)])  17.7 us
    pallas_call x2, Pallas kernels, shards_blocks(): pl.pallas_call(functools.partial(update_kernel, last, widths, (cell_seats...  4.68 us
    pallas_call x1, Pallas kernels, shards_blocks(): pl.pallas_call(functools.partial(next_sums_kernel, link_scale, widths, (c...  2.74 us
    pallas_call x1, Pallas kernels, shards_blocks(): pl.pallas_call(functools.partial(first_links_kernel, link_scale, widths,...  2.72 us
  transfers between devices with their start and end apart: 20, of which 16 were waited for; matrix products, arithmetic and copies ran while one was open for 0% of the time, Pallas kernels for 4%

profile of v10, /device:TPU:0, one launch (start us, length us, event | category | flops | bytes accessed | tf_op | source)
XLA Modules:
  0.0 128.8 jit_solution(16133403940168152461)
XLA Ops:
  1.4 2.5 %shard_map.112 = bf16[16,80,1408]{2,1,0:T(8,128)(2,1)S(1)} custom-call(s32[4]{0:T(128)S(1)} %pad_add_fusion.spot, bf16[64,4096]{1,0:T(8,128)(2,1)} %rna_1.1, bf16[64,4096]{1,0:T(8,128)(2,1)} %rna_1.1, bf16[64,16384]{1,0:T(8,128)(2,1)} %atac_1.1, bf16[64,16384]{1,0:T(8,128)(2,1)} %atac_1.1, f32[64,64]{1,0:T(8,128)} %cell.1, f32[64,128]{1,0:T(8,128)} %gene.5, ...), custom_call_target="tpu_custom_call" | custom-call | tf_op jit(solution)/shard_map/pallas_call | solution.py:403
  3.9 47.7 %all_to_all.5.received_slots.received.mine = bf16[16,80,1408]{2,1,0:T(8,128)(2,1)S(1)} all-to-all(bf16[16,80,1408]{2,1,0:T(8,128)(2,1)S(1)} %shard_map.112), channel_id=1, replica_groups={{10,8,12,1,2,5,9,15,0,13,3,6,4,14,7,11},{26,24,28,17,18,21,25,31,16,29,..., dimensions={0} | all-to-all | bytes 7208960 | tf_op jit(solution)/shard_map/all_to_all | solution.py:734
  52.0 2.6 %collective-permute-start.1 = (f32[32,128]{1,0:T(8,128)S(1)}, f32[32,128]{1,0:T(8,128)S(1)}, u32[]{:S(2)}, u32[]{:S(2)}) collective-permute-start(f32[32,128]{1,0:T(8,128)S(1)} %shard_map.113.half_table), channel_id=1, source_target_pairs={{0,16},{1,17},{2,18},{3,19},{4,20},{5,21},{6,22},{7,23},{8,24},{9,... | collective-permute-start | bytes 49160 | tf_op jit(solution)/shard_map/ppermute | solution.py:27
  54.9 0.8 shard_map.115
  55.8 0.9 collective-permute-done.1.half_table_other
  56.7 2.6 %collective-permute-start.2 = (s16[64,768]{1,0:T(8,128)(2,1)S(1)}, s16[64,768]{1,0:T(8,128)(2,1)S(1)}, u32[]{:S(2)}, u32[]{:S(2)}) collective-permute-start(s16[64,768]{1,0:T(8,128)(2,1)S(1)} %shard_map.114), channel_id=1, source_target_pairs={{0,16},{1,17},{2,18},{3,19},{4,20},{5,21},{6,22},{7,23},{8,24},{9,... | collective-permute-start | bytes 294920 | tf_op jit(solution)/shard_map/ppermute | solution.py:27
  59.3 2.7 %shard_map.116 = (f32[64,1280]{1,0:T(8,128)S(1)}, s16[64,1408]{1,0:T(8,128)(2,1)S(1)}, f32[32,128]{1,0:T(8,128)S(1)}) custom-call(s32[4]{0:T(128)S(1)} %pad_add_fusion.spot, bf16[16,80,1408]{2,1,0:T(8,128)(2,1)S(1)} %all_to_all.5.received_slots.received.mine, bf16[16,16,1280]{2,1,0:T(8,128)(2,1)S(1)} %collective-permute-done.other, ...), custom_call_target="tpu_custom_call" | custom-call | tf_op jit(solution)/shard_map/pallas_call | solution.py:765
  62.0 1.6 %collective-permute-done.2.got = s16[64,768]{1,0:T(8,128)(2,1)S(1)} collective-permute-done((s16[64,768]{1,0:T(8,128)(2,1)S(1)}, s16[64,768]{1,0:T(8,128)(2,1)S(1)}, u32[]{:S(2)}, u32[]{:S(2)}) %collective-permute-start.2) | collective-permute-done | bytes 98336 | tf_op jit(solution)/shard_map/ppermute | solution.py:27
  63.6 1.2 collective-permute-start.3
  64.9 0.8 shard_map.117.factors
  65.6 7.6 %collective-permute-done.3.other = s16[64,1408]{1,0:T(8,128)(2,1)S(1)} collective-permute-done((s16[64,1408]{1,0:T(8,128)(2,1)S(1)}, s16[64,1408]{1,0:T(8,128)(2,1)S(1)}, u32[]{:S(2)}, u32[]{:S(2)}) %collective-permute-start.3) | collective-permute-done | bytes 180256 | tf_op jit(solution)/shard_map/ppermute | solution.py:27
  73.3 2.4 %shard_map.118 = (f32[72,512]{1,0:T(8,128)S(1)}, f32[72,512]{1,0:T(8,128)S(1)}, f32[64,1280]{1,0:T(8,128)S(1)}, f32[64,1024]{1,0:T(8,128)S(1)}, f32[64,1024]{1,0:T(8,128)S(1)}, /*index=5*/bf16[64,128]{1,0:T(8,128)(2,1)S(1)}) custom-call(s32[4]{0:T(128)S(1)} %pad_add_fusion.spot, f32[32,128]{1,0:T(8,128)S(1)} %get-tuple-element.59.table, ...), custom_call_target="tpu_custom_call" | custom-call | tf_op jit(solution)/shard_map/pallas_call | solution.py:802
  76.3 1.2 collective-permute-done.4.totals_got
  77.5 0.6 shard_map.119
  78.4 1.4 %collective-permute-start.7 = (bf16[64,1152]{1,0:T(8,128)(2,1)S(1)}, bf16[64,1152]{1,0:T(8,128)(2,1)S(1)}, u32[]{:S(2)}, u32[]{:S(2)}) collective-permute-start(bf16[64,1152]{1,0:T(8,128)(2,1)S(1)} %get-tuple-element.73), channel_id=1, source_target_pairs={{0,4},{1,5},{2,6},{3,7},{4,0},{5,1},{6,2},{7,3},{8,12},{9,13},{10,... | collective-permute-start | bytes 442376 | tf_op jit(solution)/shard_map/ppermute | solution.py:27
  79.8 4.3 %collective-permute-done.6.totals_got = f32[72,512]{1,0:T(8,128)S(1)} collective-permute-done((f32[72,512]{1,0:T(8,128)S(1)}, f32[72,512]{1,0:T(8,128)S(1)}, u32[]{:S(2)}, u32[]{:S(2)}) %collective-permute-start.6) | collective-permute-done | bytes 147488 | tf_op jit(solution)/shard_map/ppermute | solution.py:27
  84.2 0.6 shard_map.120
  84.8 1.3 collective-permute-start.8
  86.0 4.6 %collective-permute-done.9.got = bf16[64,768]{1,0:T(8,128)(2,1)S(1)} collective-permute-done((bf16[64,768]{1,0:T(8,128)(2,1)S(1)}, bf16[64,768]{1,0:T(8,128)(2,1)S(1)}, u32[]{:S(2)}, u32[]{:S(2)}) %collective-permute-start.9) | collective-permute-done | bytes 98336 | tf_op jit(solution)/shard_map/ppermute | solution.py:27
  91.3 1.0 collective-permute-start.11
  92.4 3.6 %collective-permute-done.11.got = bf16[64,768]{1,0:T(8,128)(2,1)S(1)} collective-permute-done((bf16[64,768]{1,0:T(8,128)(2,1)S(1)}, bf16[64,768]{1,0:T(8,128)(2,1)S(1)}, u32[]{:S(2)}, u32[]{:S(2)}) %collective-permute-start.11) | collective-permute-done | bytes 98336 | tf_op jit(solution)/shard_map/ppermute | solution.py:27
  97.6 1.0 collective-permute-done.13.genes_other
  98.7 2.7 %shard_map.123 = (f32[64,1280]{1,0:T(8,128)S(1)}, s16[64,1408]{1,0:T(8,128)(2,1)S(1)}, f32[64,64]{1,0:T(8,128)S(1)}, f32[64,1024]{1,0:T(8,128)}, f32[64,64]{1,0:T(8,128)S(1)}) custom-call(s32[4]{0:T(128)S(1)} %pad_add_fusion.spot, f32[32,128]{1,0:T(8,128)S(1)} %get-tuple-element.59.table, f32[72,512]{1,0:T(8,128)S(1)} %get-tuple-element.94.mine, ...), custom_call_target="tpu_custom_call" | custom-call | tf_op jit(solution)/shard_map/pallas_call | solution.py:851
  101.4 2.1 %collective-permute-start.14 = (s16[64,1408]{1,0:T(8,128)(2,1)S(1)}, s16[64,1408]{1,0:T(8,128)(2,1)S(1)}, u32[]{:S(2)}, u32[]{:S(2)}) collective-permute-start(s16[64,1408]{1,0:T(8,128)(2,1)S(1)} %get-tuple-element.100), channel_id=1, source_target_pairs={{0,16},{1,17},{2,18},{3,19},{4,20},{5,21},{6,22},{7,23},{8,24},{9,... | collective-permute-start | bytes 540680 | tf_op jit(solution)/shard_map/ppermute | solution.py:27
  103.6 9.4 %collective-permute-done.14.other = s16[64,1408]{1,0:T(8,128)(2,1)S(1)} collective-permute-done((s16[64,1408]{1,0:T(8,128)(2,1)S(1)}, s16[64,1408]{1,0:T(8,128)(2,1)S(1)}, u32[]{:S(2)}, u32[]{:S(2)}) %collective-permute-start.14) | collective-permute-done | bytes 180256 | tf_op jit(solution)/shard_map/ppermute | solution.py:27
  112.9 2.2 %shard_map.124 = (f32[72,512]{1,0:T(8,128)S(1)}, f32[72,512]{1,0:T(8,128)S(1)}, f32[64,128]{1,0:T(8,128)}, f32[64,512]{1,0:T(8,128)}) custom-call(s32[4]{0:T(128)S(1)} %pad_add_fusion.spot, f32[32,128]{1,0:T(8,128)S(1)} %get-tuple-element.59.table, f32[64,1280]{1,0:T(8,128)S(1)} %get-tuple-element.98.sums, f32[64,64]{1,0:T(8,128)S(1)} %get-tuple-element.99.gram_mine, ...), custom_call_target="tpu_custom_call" | custom-call | tf_op jit(solution)/shard_map/pallas_call | solution.py:802
  115.3 1.3 %collective-permute-done.15 = f32[72,512]{1,0:T(8,128)S(1)} collective-permute-done((f32[72,512]{1,0:T(8,128)S(1)}, f32[72,512]{1,0:T(8,128)S(1)}, u32[]{:S(2)}, u32[]{:S(2)}) %collective-permute-start.15) | collective-permute-done | bytes 147488 | tf_op jit(solution)/shard_map/ppermute | solution.py:27
  116.8 2.0 %collective-permute-start.18 = (f32[96,128]{1,0:T(8,128)S(1)}, f32[96,128]{1,0:T(8,128)S(1)}, u32[]{:S(2)}, u32[]{:S(2)}) collective-permute-start(f32[96,128]{1,0:T(8,128)S(1)} %constant_dynamic-update-slice_fusion.15), channel_id=1, source_target_pairs={{0,6},{1,7},{2,4},{3,5},{4,2},{5,3},{6,0},{7,1},{8,14},{9,15},{10,... | collective-permute-start | bytes 147464 | tf_op jit(solution)/shard_map/ppermute | solution.py:27
  119.1 1.2 collective-permute-start.17
  120.4 2.0 %collective-permute-done.18 = f32[96,128]{1,0:T(8,128)S(1)} collective-permute-done((f32[96,128]{1,0:T(8,128)S(1)}, f32[96,128]{1,0:T(8,128)S(1)}, u32[]{:S(2)}, u32[]{:S(2)}) %collective-permute-start.18) | collective-permute-done | bytes 49184 | tf_op jit(solution)/shard_map/ppermute | solution.py:27
  123.3 4.1 %collective-permute-done.19.other = f32[96,128]{1,0:T(8,128)S(1)} collective-permute-done((f32[96,128]{1,0:T(8,128)S(1)}, f32[96,128]{1,0:T(8,128)S(1)}, u32[]{:S(2)}, u32[]{:S(2)}) %collective-permute-start.19) | collective-permute-done | bytes 49184 | tf_op jit(solution)/shard_map/ppermute | solution.py:27
  127.4 1.4 %shard_map.125 = f32[64,64]{1,0:T(8,128)} custom-call(s32[4]{0:T(128)S(1)} %pad_add_fusion.spot, f32[96,128]{1,0:T(8,128)S(1)} %add_add_fusion.mine, f32[96,128]{1,0:T(8,128)S(1)} %collective-permute-done.19.other, f32[64,64]{1,0:T(8,128)S(1)} %get-tuple-element.104.old), custom_call_target="tpu_custom_call" | custom-call | tf_op jit(solution)/shard_map/pallas_call | solution.py:830
  (42 shorter events, 5.4 us)
Async XLA Ops:
  51.6 3.0 %copy-start = (f32[64,512]{1,0:T(8,128)S(1)}, f32[64,512]{1,0:T(8,128)}, u32[]{:S(2)}) copy-start(f32[64,512]{1,0:T(8,128)} %peak.5) | copy-start | bytes 393220
  51.6 3.0 %copy-start.1 = (f32[64,128]{1,0:T(8,128)S(1)}, f32[64,128]{1,0:T(8,128)}, u32[]{:S(2)}) copy-start(f32[64,128]{1,0:T(8,128)} %gene.5) | copy-start | bytes 98308
  51.6 7.6 %collective-permute-start = (bf16[16,16,1280]{2,1,0:T(8,128)(2,1)S(1)}, bf16[16,16,1280]{2,1,0:T(8,128)(2,1)S(1)}, u32[]{:S(2)}, u32[]{:S(2)}) collective-permute-start(bf16[16,16,1280]{2,1,0:T(8,128)(2,1)S(1)} %slice.14), channel_id=1, source_target_pairs={{0,1},{1,0},{2,3},{3,2},{4,5},{5,4},{6,7},{7,6},{8,9},{9,8},{10,11... | collective-permute-start | bytes 1966088 | tf_op jit(solution)/shard_map/ppermute | solution.py:27
  52.0 4.7 %collective-permute-start.1 = (f32[32,128]{1,0:T(8,128)S(1)}, f32[32,128]{1,0:T(8,128)S(1)}, u32[]{:S(2)}, u32[]{:S(2)}) collective-permute-start(f32[32,128]{1,0:T(8,128)S(1)} %shard_map.113.half_table), channel_id=1, source_target_pairs={{0,16},{1,17},{2,18},{3,19},{4,20},{5,21},{6,22},{7,23},{8,24},{9,... | collective-permute-start | bytes 49160 | tf_op jit(solution)/shard_map/ppermute | solution.py:27
  56.7 7.0 %collective-permute-start.2 = (s16[64,768]{1,0:T(8,128)(2,1)S(1)}, s16[64,768]{1,0:T(8,128)(2,1)S(1)}, u32[]{:S(2)}, u32[]{:S(2)}) collective-permute-start(s16[64,768]{1,0:T(8,128)(2,1)S(1)} %shard_map.114), channel_id=1, source_target_pairs={{0,16},{1,17},{2,18},{3,19},{4,20},{5,21},{6,22},{7,23},{8,24},{9,... | collective-permute-start | bytes 294920 | tf_op jit(solution)/shard_map/ppermute | solution.py:27
  63.6 9.6 %collective-permute-start.3 = (s16[64,1408]{1,0:T(8,128)(2,1)S(1)}, s16[64,1408]{1,0:T(8,128)(2,1)S(1)}, u32[]{:S(2)}, u32[]{:S(2)}) collective-permute-start(s16[64,1408]{1,0:T(8,128)(2,1)S(1)} %get-tuple-element.63), channel_id=1, source_target_pairs={{0,16},{1,17},{2,18},{3,19},{4,20},{5,21},{6,22},{7,23},{8,24},{9,... | collective-permute-start | bytes 540680 | tf_op jit(solution)/shard_map/ppermute | solution.py:27
  75.7 1.8 %collective-permute-start.5 = (f32[64,1024]{1,0:T(8,128)S(1)}, f32[64,1024]{1,0:T(8,128)S(1)}, u32[]{:S(2)}, u32[]{:S(2)}) collective-permute-start(f32[64,1024]{1,0:T(8,128)S(1)} %get-tuple-element.68), channel_id=1, source_target_pairs={{0,1},{1,0},{2,3},{3,2},{4,5},{5,4},{6,7},{7,6},{8,9},{9,8},{10,11... | collective-permute-start | bytes 786440 | tf_op jit(solution)/shard_map/ppermute | solution.py:27
  75.8 1.7 %collective-permute-start.4 = (f32[72,512]{1,0:T(8,128)S(1)}, f32[72,512]{1,0:T(8,128)S(1)}, u32[]{:S(2)}, u32[]{:S(2)}) collective-permute-start(f32[72,512]{1,0:T(8,128)S(1)} %get-tuple-element.66), channel_id=1, source_target_pairs={{0,1},{1,0},{2,3},{3,2},{4,5},{5,4},{6,7},{7,6},{8,9},{9,8},{10,11... | collective-permute-start | bytes 442376 | tf_op jit(solution)/shard_map/ppermute | solution.py:27
  78.1 6.0 %collective-permute-start.6 = (f32[72,512]{1,0:T(8,128)S(1)}, f32[72,512]{1,0:T(8,128)S(1)}, u32[]{:S(2)}, u32[]{:S(2)}) collective-permute-start(f32[72,512]{1,0:T(8,128)S(1)} %get-tuple-element.72.totals), channel_id=1, source_target_pairs={{0,2},{1,3},{2,0},{3,1},{4,6},{5,7},{6,4},{7,5},{8,10},{9,11},{10,... | collective-permute-start | bytes 442376 | tf_op jit(solution)/shard_map/ppermute | solution.py:27
  78.4 5.8 %collective-permute-start.7 = (bf16[64,1152]{1,0:T(8,128)(2,1)S(1)}, bf16[64,1152]{1,0:T(8,128)(2,1)S(1)}, u32[]{:S(2)}, u32[]{:S(2)}) collective-permute-start(bf16[64,1152]{1,0:T(8,128)(2,1)S(1)} %get-tuple-element.73), channel_id=1, source_target_pairs={{0,4},{1,5},{2,6},{3,7},{4,0},{5,1},{6,2},{7,3},{8,12},{9,13},{10,... | collective-permute-start | bytes 442376 | tf_op jit(solution)/shard_map/ppermute | solution.py:27
  84.8 5.9 %collective-permute-start.8 = (f32[72,512]{1,0:T(8,128)S(1)}, f32[72,512]{1,0:T(8,128)S(1)}, u32[]{:S(2)}, u32[]{:S(2)}) collective-permute-start(f32[72,512]{1,0:T(8,128)S(1)} %get-tuple-element.80.totals), channel_id=1, source_target_pairs={{0,4},{1,5},{2,6},{3,7},{4,0},{5,1},{6,2},{7,3},{8,12},{9,13},{10,... | collective-permute-start | bytes 442376 | tf_op jit(solution)/shard_map/ppermute | solution.py:27
  86.0 4.6 %collective-permute-start.9 = (bf16[64,768]{1,0:T(8,128)(2,1)S(1)}, bf16[64,768]{1,0:T(8,128)(2,1)S(1)}, u32[]{:S(2)}, u32[]{:S(2)}) collective-permute-start(bf16[64,768]{1,0:T(8,128)(2,1)S(1)} %get-tuple-element.81), channel_id=1, source_target_pairs={{0,8},{1,9},{2,10},{3,11},{4,12},{5,13},{6,14},{7,15},{8,0},{9,1},... | collective-permute-start | bytes 294920 | tf_op jit(solution)/shard_map/ppermute | solution.py:27
  91.2 5.2 %collective-permute-start.10 = (f32[72,512]{1,0:T(8,128)S(1)}, f32[72,512]{1,0:T(8,128)S(1)}, u32[]{:S(2)}, u32[]{:S(2)}) collective-permute-start(f32[72,512]{1,0:T(8,128)S(1)} %get-tuple-element.88.totals), channel_id=1, source_target_pairs={{0,8},{1,9},{2,10},{3,11},{4,12},{5,13},{6,14},{7,15},{8,0},{9,1},... | collective-permute-start | bytes 442376 | tf_op jit(solution)/shard_map/ppermute | solution.py:27
  91.3 4.7 %collective-permute-start.11 = (bf16[64,768]{1,0:T(8,128)(2,1)S(1)}, bf16[64,768]{1,0:T(8,128)(2,1)S(1)}, u32[]{:S(2)}, u32[]{:S(2)}) collective-permute-start(bf16[64,768]{1,0:T(8,128)(2,1)S(1)} %get-tuple-element.89), channel_id=1, source_target_pairs={{0,2},{1,3},{2,0},{3,1},{4,6},{5,7},{6,4},{7,5},{8,10},{9,11},{10,... | collective-permute-start | bytes 294920 | tf_op jit(solution)/shard_map/ppermute | solution.py:27
  97.0 1.6 %collective-permute-start.12 = (f32[72,512]{1,0:T(8,128)S(1)}, f32[72,512]{1,0:T(8,128)S(1)}, u32[]{:S(2)}, u32[]{:S(2)}) collective-permute-start(f32[72,512]{1,0:T(8,128)S(1)} %get-tuple-element.94.mine), channel_id=1, source_target_pairs={{0,1},{1,0},{2,3},{3,2},{4,5},{5,4},{6,7},{7,6},{8,9},{9,8},{10,11... | collective-permute-start | bytes 442376 | tf_op jit(solution)/shard_map/ppermute | solution.py:27
  97.1 1.5 %collective-permute-start.13 = (bf16[64,1024]{1,0:T(8,128)(2,1)S(1)}, bf16[64,1024]{1,0:T(8,128)(2,1)S(1)}, u32[]{:S(2)}, u32[]{:S(2)}) collective-permute-start(bf16[64,1024]{1,0:T(8,128)(2,1)S(1)} %get-tuple-element.97.genes_mine), channel_id=1, source_target_pairs={{0,1},{1,0},{2,3},{3,2},{4,5},{5,4},{6,7},{7,6},{8,9},{9,8},{10,11... | collective-permute-start | bytes 393224 | tf_op jit(solution)/shard_map/ppermute | solution.py:27
  101.4 11.5 %collective-permute-start.14 = (s16[64,1408]{1,0:T(8,128)(2,1)S(1)}, s16[64,1408]{1,0:T(8,128)(2,1)S(1)}, u32[]{:S(2)}, u32[]{:S(2)}) collective-permute-start(s16[64,1408]{1,0:T(8,128)(2,1)S(1)} %get-tuple-element.100), channel_id=1, source_target_pairs={{0,16},{1,17},{2,18},{3,19},{4,20},{5,21},{6,22},{7,23},{8,24},{9,... | collective-permute-start | bytes 540680 | tf_op jit(solution)/shard_map/ppermute | solution.py:27
  115.2 1.4 %collective-permute-start.15 = (f32[72,512]{1,0:T(8,128)S(1)}, f32[72,512]{1,0:T(8,128)S(1)}, u32[]{:S(2)}, u32[]{:S(2)}) collective-permute-start(f32[72,512]{1,0:T(8,128)S(1)} %get-tuple-element.103), channel_id=1, source_target_pairs={{0,1},{1,0},{2,3},{3,2},{4,5},{5,4},{6,7},{7,6},{8,9},{9,8},{10,11... | collective-permute-start | bytes 442376 | tf_op jit(solution)/shard_map/ppermute | solution.py:27
  116.8 5.6 %collective-permute-start.18 = (f32[96,128]{1,0:T(8,128)S(1)}, f32[96,128]{1,0:T(8,128)S(1)}, u32[]{:S(2)}, u32[]{:S(2)}) collective-permute-start(f32[96,128]{1,0:T(8,128)S(1)} %constant_dynamic-update-slice_fusion.15), channel_id=1, source_target_pairs={{0,6},{1,7},{2,4},{3,5},{4,2},{5,3},{6,0},{7,1},{8,14},{9,15},{10,... | collective-permute-start | bytes 147464 | tf_op jit(solution)/shard_map/ppermute | solution.py:27
  118.8 4.1 %collective-permute-start.16 = (f32[96,128]{1,0:T(8,128)S(1)}, f32[96,128]{1,0:T(8,128)S(1)}, u32[]{:S(2)}, u32[]{:S(2)}) collective-permute-start(f32[96,128]{1,0:T(8,128)S(1)} %get-tuple-element.120), channel_id=1, source_target_pairs={{0,2},{1,3},{2,0},{3,1},{4,6},{5,7},{6,4},{7,5},{8,10},{9,11},{10,... | collective-permute-start | bytes 147464 | tf_op jit(solution)/shard_map/ppermute | solution.py:27
  119.1 4.1 %collective-permute-start.17 = (f32[96,128]{1,0:T(8,128)S(1)}, f32[96,128]{1,0:T(8,128)S(1)}, u32[]{:S(2)}, u32[]{:S(2)}) collective-permute-start(f32[96,128]{1,0:T(8,128)S(1)} %get-tuple-element.107), channel_id=1, source_target_pairs={{0,4},{1,5},{2,6},{3,7},{4,0},{5,1},{6,2},{7,3},{8,12},{9,13},{10,... | collective-permute-start | bytes 147464 | tf_op jit(solution)/shard_map/ppermute | solution.py:27
  123.2 4.2 %collective-permute-start.19 = (f32[96,128]{1,0:T(8,128)S(1)}, f32[96,128]{1,0:T(8,128)S(1)}, u32[]{:S(2)}, u32[]{:S(2)}) collective-permute-start(f32[96,128]{1,0:T(8,128)S(1)} %add_add_fusion.mine), channel_id=1, source_target_pairs={{0,8},{1,9},{2,10},{3,11},{4,12},{5,13},{6,14},{7,15},{8,0},{9,1},... | collective-permute-start | bytes 147464 | tf_op jit(solution)/shard_map/ppermute | solution.py:27

commit v11 on v10

--- a/solution.py
+++ b/solution.py
@@ -709,7 +709,7 @@
     me = lax.axis_index(AXIS)
     side, place, core = me // half, me % half, me % 2
     chip_bits = bits_below(half)[1:]
-    cell_bits, link_bits = chip_bits, turned(chip_bits, 1)
+    cell_bits, link_bits = turned(chip_bits, 1), turned(chip_bits, 2)
     tail = sum(
         jnp.where((me & bit) != 0, 1 << i, 0) for i, bit in enumerate(reversed(cell_bits[2:]))
     )

time: 129 us -> 128 us (level)
  waiting for transfers between devices: 43.2 us -> 41.4 us
    ppermute x20, waiting for transfers between devices: 43.2 us -> 41.4 us  [flip(): return lax.ppermute(value, AXIS, [(i, i ^ bit) for i in range(count)])]
  transfers between devices with their start and end apart: 20 -> 20, of which waited for: 16 -> 15; matrix products, arithmetic and copies ran while one was open for 0% -> 0% of each run, Pallas kernels for 4% -> 4%
where the time goes in v11:
time: 128 us
  blocking collectives  47.7 us (37%)
  waiting for transfers between devices  41.4 us (32%)
  starting transfers between devices  18.8 us (15%)
  Pallas kernels  18.5 us (14%)
  between operations  1.55 us (1%)
    all_to_all x1, blocking collectives, shards_blocks(): lax.all_to_all(sent, AXIS, 0, 0, axis_index_groups=halves, tiled=True)  47.7 us
    ppermute x20, waiting for transfers between devices, flip(): return lax.ppermute(value, AXIS, [(i, i ^ bit) for i in range(count)])  41.4 us
    ppermute x20, starting transfers between devices, flip(): return lax.ppermute(value, AXIS, [(i, i ^ bit) for i in range(count)])  18.8 us
    pallas_call x2, Pallas kernels, shards_blocks(): pl.pallas_call(functools.partial(update_kernel, last, widths, (cell_seats...  4.68 us
    pallas_call x1, Pallas kernels, shards_blocks(): pl.pallas_call(functools.partial(next_sums_kernel, link_scale, widths, (c...  2.74 us
    pallas_call x1, Pallas kernels, shards_blocks(): pl.pallas_call(functools.partial(first_links_kernel, link_scale, widths,...  2.72 us
  transfers between devices with their start and end apart: 20, of which 15 were waited for; matrix products, arithmetic and copies ran while one was open for 0% of the time, Pallas kernels for 4%

profile of v11, /device:TPU:0, one launch (start us, length us, event | category | flops | bytes accessed | tf_op | source)
XLA Modules:
  0.0 128.0 jit_solution(12683815255170164112)
XLA Ops:
  1.4 2.5 %shard_map.112 = bf16[16,80,1408]{2,1,0:T(8,128)(2,1)S(1)} custom-call(s32[4]{0:T(128)S(1)} %pad_add_fusion.spot, bf16[64,4096]{1,0:T(8,128)(2,1)} %rna_1.1, bf16[64,4096]{1,0:T(8,128)(2,1)} %rna_1.1, bf16[64,16384]{1,0:T(8,128)(2,1)} %atac_1.1, bf16[64,16384]{1,0:T(8,128)(2,1)} %atac_1.1, f32[64,64]{1,0:T(8,128)} %cell.1, f32[64,128]{1,0:T(8,128)} %gene.5, ...), custom_call_target="tpu_custom_call" | custom-call | tf_op jit(solution)/shard_map/pallas_call | solution.py:403
  3.9 47.7 %all_to_all.5.received_slots.received.mine = bf16[16,80,1408]{2,1,0:T(8,128)(2,1)S(1)} all-to-all(bf16[16,80,1408]{2,1,0:T(8,128)(2,1)S(1)} %shard_map.112), channel_id=1, replica_groups={{10,8,12,1,2,5,9,15,0,13,3,6,4,14,7,11},{26,24,28,17,18,21,25,31,16,29,..., dimensions={0} | all-to-all | bytes 7208960 | tf_op jit(solution)/shard_map/all_to_all | solution.py:734
  52.0 2.6 %collective-permute-start.1 = (f32[32,128]{1,0:T(8,128)S(1)}, f32[32,128]{1,0:T(8,128)S(1)}, u32[]{:S(2)}, u32[]{:S(2)}) collective-permute-start(f32[32,128]{1,0:T(8,128)S(1)} %shard_map.113.half_table), channel_id=1, source_target_pairs={{0,16},{1,17},{2,18},{3,19},{4,20},{5,21},{6,22},{7,23},{8,24},{9,... | collective-permute-start | bytes 49160 | tf_op jit(solution)/shard_map/ppermute | solution.py:27
  54.9 0.8 shard_map.115
  55.8 0.9 collective-permute-done.1.half_table_other
  56.7 2.6 %collective-permute-start.2 = (s16[64,768]{1,0:T(8,128)(2,1)S(1)}, s16[64,768]{1,0:T(8,128)(2,1)S(1)}, u32[]{:S(2)}, u32[]{:S(2)}) collective-permute-start(s16[64,768]{1,0:T(8,128)(2,1)S(1)} %shard_map.114), channel_id=1, source_target_pairs={{0,16},{1,17},{2,18},{3,19},{4,20},{5,21},{6,22},{7,23},{8,24},{9,... | collective-permute-start | bytes 294920 | tf_op jit(solution)/shard_map/ppermute | solution.py:27
  59.3 2.7 %shard_map.116 = (f32[64,1280]{1,0:T(8,128)S(1)}, s16[64,1408]{1,0:T(8,128)(2,1)S(1)}, f32[32,128]{1,0:T(8,128)S(1)}) custom-call(s32[4]{0:T(128)S(1)} %pad_add_fusion.spot, bf16[16,80,1408]{2,1,0:T(8,128)(2,1)S(1)} %all_to_all.5.received_slots.received.mine, bf16[16,16,1280]{2,1,0:T(8,128)(2,1)S(1)} %collective-permute-done.other, ...), custom_call_target="tpu_custom_call" | custom-call | tf_op jit(solution)/shard_map/pallas_call | solution.py:765
  62.0 1.6 %collective-permute-done.2.got = s16[64,768]{1,0:T(8,128)(2,1)S(1)} collective-permute-done((s16[64,768]{1,0:T(8,128)(2,1)S(1)}, s16[64,768]{1,0:T(8,128)(2,1)S(1)}, u32[]{:S(2)}, u32[]{:S(2)}) %collective-permute-start.2) | collective-permute-done | bytes 98336 | tf_op jit(solution)/shard_map/ppermute | solution.py:27
  63.6 1.2 collective-permute-start.3
  64.9 0.8 shard_map.117.factors
  65.6 7.6 %collective-permute-done.3.other = s16[64,1408]{1,0:T(8,128)(2,1)S(1)} collective-permute-done((s16[64,1408]{1,0:T(8,128)(2,1)S(1)}, s16[64,1408]{1,0:T(8,128)(2,1)S(1)}, u32[]{:S(2)}, u32[]{:S(2)}) %collective-permute-start.3) | collective-permute-done | bytes 180256 | tf_op jit(solution)/shard_map/ppermute | solution.py:27
  73.3 2.4 %shard_map.118 = (f32[72,512]{1,0:T(8,128)S(1)}, f32[72,512]{1,0:T(8,128)S(1)}, f32[64,1280]{1,0:T(8,128)S(1)}, f32[64,1024]{1,0:T(8,128)S(1)}, f32[64,1024]{1,0:T(8,128)S(1)}, /*index=5*/bf16[64,128]{1,0:T(8,128)(2,1)S(1)}) custom-call(s32[4]{0:T(128)S(1)} %pad_add_fusion.spot, f32[32,128]{1,0:T(8,128)S(1)} %get-tuple-element.59.table, ...), custom_call_target="tpu_custom_call" | custom-call | tf_op jit(solution)/shard_map/pallas_call | solution.py:802
  76.3 1.2 collective-permute-done.4.totals_got
  77.5 0.6 shard_map.119
  78.6 5.5 %collective-permute-done.6.totals_got = f32[72,512]{1,0:T(8,128)S(1)} collective-permute-done((f32[72,512]{1,0:T(8,128)S(1)}, f32[72,512]{1,0:T(8,128)S(1)}, u32[]{:S(2)}, u32[]{:S(2)}) %collective-permute-start.6) | collective-permute-done | bytes 147488 | tf_op jit(solution)/shard_map/ppermute | solution.py:27
  85.1 1.2 collective-permute-start.9
  86.3 3.4 %collective-permute-done.9.got = bf16[64,768]{1,0:T(8,128)(2,1)S(1)} collective-permute-done((bf16[64,768]{1,0:T(8,128)(2,1)S(1)}, bf16[64,768]{1,0:T(8,128)(2,1)S(1)}, u32[]{:S(2)}, u32[]{:S(2)}) %collective-permute-start.9) | collective-permute-done | bytes 98336 | tf_op jit(solution)/shard_map/ppermute | solution.py:27
  90.6 1.3 collective-permute-start.10
  91.8 0.7 collective-permute-start.11
  92.5 4.0 %collective-permute-done.11.got = bf16[64,768]{1,0:T(8,128)(2,1)S(1)} collective-permute-done((bf16[64,768]{1,0:T(8,128)(2,1)S(1)}, bf16[64,768]{1,0:T(8,128)(2,1)S(1)}, u32[]{:S(2)}, u32[]{:S(2)}) %collective-permute-start.11) | collective-permute-done | bytes 98336 | tf_op jit(solution)/shard_map/ppermute | solution.py:27
  97.6 1.0 collective-permute-done.13.genes_other
  98.7 2.7 %shard_map.123 = (f32[64,1280]{1,0:T(8,128)S(1)}, s16[64,1408]{1,0:T(8,128)(2,1)S(1)}, f32[64,64]{1,0:T(8,128)S(1)}, f32[64,1024]{1,0:T(8,128)}, f32[64,64]{1,0:T(8,128)S(1)}) custom-call(s32[4]{0:T(128)S(1)} %pad_add_fusion.spot, f32[32,128]{1,0:T(8,128)S(1)} %get-tuple-element.59.table, f32[72,512]{1,0:T(8,128)S(1)} %get-tuple-element.94.mine, ...), custom_call_target="tpu_custom_call" | custom-call | tf_op jit(solution)/shard_map/pallas_call | solution.py:851
  101.4 2.1 %collective-permute-start.14 = (s16[64,1408]{1,0:T(8,128)(2,1)S(1)}, s16[64,1408]{1,0:T(8,128)(2,1)S(1)}, u32[]{:S(2)}, u32[]{:S(2)}) collective-permute-start(s16[64,1408]{1,0:T(8,128)(2,1)S(1)} %get-tuple-element.100), channel_id=1, source_target_pairs={{0,16},{1,17},{2,18},{3,19},{4,20},{5,21},{6,22},{7,23},{8,24},{9,... | collective-permute-start | bytes 540680 | tf_op jit(solution)/shard_map/ppermute | solution.py:27
  103.6 9.4 %collective-permute-done.14.other = s16[64,1408]{1,0:T(8,128)(2,1)S(1)} collective-permute-done((s16[64,1408]{1,0:T(8,128)(2,1)S(1)}, s16[64,1408]{1,0:T(8,128)(2,1)S(1)}, u32[]{:S(2)}, u32[]{:S(2)}) %collective-permute-start.14) | collective-permute-done | bytes 180256 | tf_op jit(solution)/shard_map/ppermute | solution.py:27
  112.9 2.2 %shard_map.124 = (f32[72,512]{1,0:T(8,128)S(1)}, f32[72,512]{1,0:T(8,128)S(1)}, f32[64,128]{1,0:T(8,128)}, f32[64,512]{1,0:T(8,128)}) custom-call(s32[4]{0:T(128)S(1)} %pad_add_fusion.spot, f32[32,128]{1,0:T(8,128)S(1)} %get-tuple-element.59.table, f32[64,1280]{1,0:T(8,128)S(1)} %get-tuple-element.98.sums, f32[64,64]{1,0:T(8,128)S(1)} %get-tuple-element.99.gram_mine, ...), custom_call_target="tpu_custom_call" | custom-call | tf_op jit(solution)/shard_map/pallas_call | solution.py:802
  115.3 1.3 %collective-permute-done.15 = f32[72,512]{1,0:T(8,128)S(1)} collective-permute-done((f32[72,512]{1,0:T(8,128)S(1)}, f32[72,512]{1,0:T(8,128)S(1)}, u32[]{:S(2)}, u32[]{:S(2)}) %collective-permute-start.15) | collective-permute-done | bytes 147488 | tf_op jit(solution)/shard_map/ppermute | solution.py:27
  116.9 1.0 collective-permute-start.16
  117.9 2.4 %collective-permute-start.17 = (f32[96,128]{1,0:T(8,128)S(1)}, f32[96,128]{1,0:T(8,128)S(1)}, u32[]{:S(2)}, u32[]{:S(2)}) collective-permute-start(f32[96,128]{1,0:T(8,128)S(1)} %get-tuple-element.107), channel_id=1, source_target_pairs={{0,8},{1,9},{2,10},{3,11},{4,12},{5,13},{6,14},{7,15},{8,0},{9,1},... | collective-permute-start | bytes 147464 | tf_op jit(solution)/shard_map/ppermute | solution.py:27
  120.4 1.9 %collective-permute-done.18 = f32[96,128]{1,0:T(8,128)S(1)} collective-permute-done((f32[96,128]{1,0:T(8,128)S(1)}, f32[96,128]{1,0:T(8,128)S(1)}, u32[]{:S(2)}, u32[]{:S(2)}) %collective-permute-start.18) | collective-permute-done | bytes 49184 | tf_op jit(solution)/shard_map/ppermute | solution.py:27
  122.4 1.3 collective-permute-start.19
  123.7 2.9 %collective-permute-done.19.other = f32[96,128]{1,0:T(8,128)S(1)} collective-permute-done((f32[96,128]{1,0:T(8,128)S(1)}, f32[96,128]{1,0:T(8,128)S(1)}, u32[]{:S(2)}, u32[]{:S(2)}) %collective-permute-start.19) | collective-permute-done | bytes 49184 | tf_op jit(solution)/shard_map/ppermute | solution.py:27
  126.6 1.4 %shard_map.125 = f32[64,64]{1,0:T(8,128)} custom-call(s32[4]{0:T(128)S(1)} %pad_add_fusion.spot, f32[96,128]{1,0:T(8,128)S(1)} %add_add_fusion.mine, f32[96,128]{1,0:T(8,128)S(1)} %collective-permute-done.19.other, f32[64,64]{1,0:T(8,128)S(1)} %get-tuple-element.104.old), custom_call_target="tpu_custom_call" | custom-call | tf_op jit(solution)/shard_map/pallas_call | solution.py:830
  (42 shorter events, 5.2 us)
Async XLA Ops:
  51.6 3.0 %copy-start = (f32[64,512]{1,0:T(8,128)S(1)}, f32[64,512]{1,0:T(8,128)}, u32[]{:S(2)}) copy-start(f32[64,512]{1,0:T(8,128)} %peak.5) | copy-start | bytes 393220
  51.6 3.0 %copy-start.1 = (f32[64,128]{1,0:T(8,128)S(1)}, f32[64,128]{1,0:T(8,128)}, u32[]{:S(2)}) copy-start(f32[64,128]{1,0:T(8,128)} %gene.5) | copy-start | bytes 98308
  51.6 7.6 %collective-permute-start = (bf16[16,16,1280]{2,1,0:T(8,128)(2,1)S(1)}, bf16[16,16,1280]{2,1,0:T(8,128)(2,1)S(1)}, u32[]{:S(2)}, u32[]{:S(2)}) collective-permute-start(bf16[16,16,1280]{2,1,0:T(8,128)(2,1)S(1)} %slice.14), channel_id=1, source_target_pairs={{0,1},{1,0},{2,3},{3,2},{4,5},{5,4},{6,7},{7,6},{8,9},{9,8},{10,11... | collective-permute-start | bytes 1966088 | tf_op jit(solution)/shard_map/ppermute | solution.py:27
  52.0 4.7 %collective-permute-start.1 = (f32[32,128]{1,0:T(8,128)S(1)}, f32[32,128]{1,0:T(8,128)S(1)}, u32[]{:S(2)}, u32[]{:S(2)}) collective-permute-start(f32[32,128]{1,0:T(8,128)S(1)} %shard_map.113.half_table), channel_id=1, source_target_pairs={{0,16},{1,17},{2,18},{3,19},{4,20},{5,21},{6,22},{7,23},{8,24},{9,... | collective-permute-start | bytes 49160 | tf_op jit(solution)/shard_map/ppermute | solution.py:27
  56.7 7.0 %collective-permute-start.2 = (s16[64,768]{1,0:T(8,128)(2,1)S(1)}, s16[64,768]{1,0:T(8,128)(2,1)S(1)}, u32[]{:S(2)}, u32[]{:S(2)}) collective-permute-start(s16[64,768]{1,0:T(8,128)(2,1)S(1)} %shard_map.114), channel_id=1, source_target_pairs={{0,16},{1,17},{2,18},{3,19},{4,20},{5,21},{6,22},{7,23},{8,24},{9,... | collective-permute-start | bytes 294920 | tf_op jit(solution)/shard_map/ppermute | solution.py:27
  63.6 9.6 %collective-permute-start.3 = (s16[64,1408]{1,0:T(8,128)(2,1)S(1)}, s16[64,1408]{1,0:T(8,128)(2,1)S(1)}, u32[]{:S(2)}, u32[]{:S(2)}) collective-permute-start(s16[64,1408]{1,0:T(8,128)(2,1)S(1)} %get-tuple-element.63), channel_id=1, source_target_pairs={{0,16},{1,17},{2,18},{3,19},{4,20},{5,21},{6,22},{7,23},{8,24},{9,... | collective-permute-start | bytes 540680 | tf_op jit(solution)/shard_map/ppermute | solution.py:27
  75.7 1.8 %collective-permute-start.5 = (f32[64,1024]{1,0:T(8,128)S(1)}, f32[64,1024]{1,0:T(8,128)S(1)}, u32[]{:S(2)}, u32[]{:S(2)}) collective-permute-start(f32[64,1024]{1,0:T(8,128)S(1)} %get-tuple-element.68), channel_id=1, source_target_pairs={{0,1},{1,0},{2,3},{3,2},{4,5},{5,4},{6,7},{7,6},{8,9},{9,8},{10,11... | collective-permute-start | bytes 786440 | tf_op jit(solution)/shard_map/ppermute | solution.py:27
  75.8 1.7 %collective-permute-start.4 = (f32[72,512]{1,0:T(8,128)S(1)}, f32[72,512]{1,0:T(8,128)S(1)}, u32[]{:S(2)}, u32[]{:S(2)}) collective-permute-start(f32[72,512]{1,0:T(8,128)S(1)} %get-tuple-element.66), channel_id=1, source_target_pairs={{0,1},{1,0},{2,3},{3,2},{4,5},{5,4},{6,7},{7,6},{8,9},{9,8},{10,11... | collective-permute-start | bytes 442376 | tf_op jit(solution)/shard_map/ppermute | solution.py:27
  78.1 6.0 %collective-permute-start.6 = (f32[72,512]{1,0:T(8,128)S(1)}, f32[72,512]{1,0:T(8,128)S(1)}, u32[]{:S(2)}, u32[]{:S(2)}) collective-permute-start(f32[72,512]{1,0:T(8,128)S(1)} %get-tuple-element.72.totals), channel_id=1, source_target_pairs={{0,4},{1,5},{2,6},{3,7},{4,0},{5,1},{6,2},{7,3},{8,12},{9,13},{10,... | collective-permute-start | bytes 442376 | tf_op jit(solution)/shard_map/ppermute | solution.py:27
  78.5 5.6 %collective-permute-start.7 = (bf16[64,1152]{1,0:T(8,128)(2,1)S(1)}, bf16[64,1152]{1,0:T(8,128)(2,1)S(1)}, u32[]{:S(2)}, u32[]{:S(2)}) collective-permute-start(bf16[64,1152]{1,0:T(8,128)(2,1)S(1)} %get-tuple-element.73), channel_id=1, source_target_pairs={{0,8},{1,9},{2,10},{3,11},{4,12},{5,13},{6,14},{7,15},{8,0},{9,1},... | collective-permute-start | bytes 442376 | tf_op jit(solution)/shard_map/ppermute | solution.py:27
  84.8 5.2 %collective-permute-start.8 = (f32[72,512]{1,0:T(8,128)S(1)}, f32[72,512]{1,0:T(8,128)S(1)}, u32[]{:S(2)}, u32[]{:S(2)}) collective-permute-start(f32[72,512]{1,0:T(8,128)S(1)} %get-tuple-element.80.totals), channel_id=1, source_target_pairs={{0,8},{1,9},{2,10},{3,11},{4,12},{5,13},{6,14},{7,15},{8,0},{9,1},... | collective-permute-start | bytes 442376 | tf_op jit(solution)/shard_map/ppermute | solution.py:27
  85.1 4.6 %collective-permute-start.9 = (bf16[64,768]{1,0:T(8,128)(2,1)S(1)}, bf16[64,768]{1,0:T(8,128)(2,1)S(1)}, u32[]{:S(2)}, u32[]{:S(2)}) collective-permute-start(bf16[64,768]{1,0:T(8,128)(2,1)S(1)} %get-tuple-element.81), channel_id=1, source_target_pairs={{0,2},{1,3},{2,0},{3,1},{4,6},{5,7},{6,4},{7,5},{8,10},{9,11},{10,... | collective-permute-start | bytes 294920 | tf_op jit(solution)/shard_map/ppermute | solution.py:27
  90.6 5.9 %collective-permute-start.10 = (f32[72,512]{1,0:T(8,128)S(1)}, f32[72,512]{1,0:T(8,128)S(1)}, u32[]{:S(2)}, u32[]{:S(2)}) collective-permute-start(f32[72,512]{1,0:T(8,128)S(1)} %get-tuple-element.88.totals), channel_id=1, source_target_pairs={{0,2},{1,3},{2,0},{3,1},{4,6},{5,7},{6,4},{7,5},{8,10},{9,11},{10,... | collective-permute-start | bytes 442376 | tf_op jit(solution)/shard_map/ppermute | solution.py:27
  91.8 4.6 %collective-permute-start.11 = (bf16[64,768]{1,0:T(8,128)(2,1)S(1)}, bf16[64,768]{1,0:T(8,128)(2,1)S(1)}, u32[]{:S(2)}, u32[]{:S(2)}) collective-permute-start(bf16[64,768]{1,0:T(8,128)(2,1)S(1)} %get-tuple-element.89), channel_id=1, source_target_pairs={{0,4},{1,5},{2,6},{3,7},{4,0},{5,1},{6,2},{7,3},{8,12},{9,13},{10,... | collective-permute-start | bytes 294920 | tf_op jit(solution)/shard_map/ppermute | solution.py:27
  97.0 1.6 %collective-permute-start.12 = (f32[72,512]{1,0:T(8,128)S(1)}, f32[72,512]{1,0:T(8,128)S(1)}, u32[]{:S(2)}, u32[]{:S(2)}) collective-permute-start(f32[72,512]{1,0:T(8,128)S(1)} %get-tuple-element.94.mine), channel_id=1, source_target_pairs={{0,1},{1,0},{2,3},{3,2},{4,5},{5,4},{6,7},{7,6},{8,9},{9,8},{10,11... | collective-permute-start | bytes 442376 | tf_op jit(solution)/shard_map/ppermute | solution.py:27
  97.1 1.5 %collective-permute-start.13 = (bf16[64,1024]{1,0:T(8,128)(2,1)S(1)}, bf16[64,1024]{1,0:T(8,128)(2,1)S(1)}, u32[]{:S(2)}, u32[]{:S(2)}) collective-permute-start(bf16[64,1024]{1,0:T(8,128)(2,1)S(1)} %get-tuple-element.97.genes_mine), channel_id=1, source_target_pairs={{0,1},{1,0},{2,3},{3,2},{4,5},{5,4},{6,7},{7,6},{8,9},{9,8},{10,11... | collective-permute-start | bytes 393224 | tf_op jit(solution)/shard_map/ppermute | solution.py:27
  101.4 11.5 %collective-permute-start.14 = (s16[64,1408]{1,0:T(8,128)(2,1)S(1)}, s16[64,1408]{1,0:T(8,128)(2,1)S(1)}, u32[]{:S(2)}, u32[]{:S(2)}) collective-permute-start(s16[64,1408]{1,0:T(8,128)(2,1)S(1)} %get-tuple-element.100), channel_id=1, source_target_pairs={{0,16},{1,17},{2,18},{3,19},{4,20},{5,21},{6,22},{7,23},{8,24},{9,... | collective-permute-start | bytes 540680 | tf_op jit(solution)/shard_map/ppermute | solution.py:27
  115.2 1.4 %collective-permute-start.15 = (f32[72,512]{1,0:T(8,128)S(1)}, f32[72,512]{1,0:T(8,128)S(1)}, u32[]{:S(2)}, u32[]{:S(2)}) collective-permute-start(f32[72,512]{1,0:T(8,128)S(1)} %get-tuple-element.103), channel_id=1, source_target_pairs={{0,1},{1,0},{2,3},{3,2},{4,5},{5,4},{6,7},{7,6},{8,9},{9,8},{10,11... | collective-permute-start | bytes 442376 | tf_op jit(solution)/shard_map/ppermute | solution.py:27
  116.8 5.5 %collective-permute-start.18 = (f32[96,128]{1,0:T(8,128)S(1)}, f32[96,128]{1,0:T(8,128)S(1)}, u32[]{:S(2)}, u32[]{:S(2)}) collective-permute-start(f32[96,128]{1,0:T(8,128)S(1)} %constant_dynamic-update-slice_fusion.15), channel_id=1, source_target_pairs={{0,12},{1,13},{2,14},{3,15},{4,8},{5,9},{6,10},{7,11},{8,4},{9,5},... | collective-permute-start | bytes 147464 | tf_op jit(solution)/shard_map/ppermute | solution.py:27
  116.9 5.4 %collective-permute-start.16 = (f32[96,128]{1,0:T(8,128)S(1)}, f32[96,128]{1,0:T(8,128)S(1)}, u32[]{:S(2)}, u32[]{:S(2)}) collective-permute-start(f32[96,128]{1,0:T(8,128)S(1)} %get-tuple-element.120), channel_id=1, source_target_pairs={{0,4},{1,5},{2,6},{3,7},{4,0},{5,1},{6,2},{7,3},{8,12},{9,13},{10,... | collective-permute-start | bytes 147464 | tf_op jit(solution)/shard_map/ppermute | solution.py:27
  117.9 4.5 %collective-permute-start.17 = (f32[96,128]{1,0:T(8,128)S(1)}, f32[96,128]{1,0:T(8,128)S(1)}, u32[]{:S(2)}, u32[]{:S(2)}) collective-permute-start(f32[96,128]{1,0:T(8,128)S(1)} %get-tuple-element.107), channel_id=1, source_target_pairs={{0,8},{1,9},{2,10},{3,11},{4,12},{5,13},{6,14},{7,15},{8,0},{9,1},... | collective-permute-start | bytes 147464 | tf_op jit(solution)/shard_map/ppermute | solution.py:27
  122.4 4.2 %collective-permute-start.19 = (f32[96,128]{1,0:T(8,128)S(1)}, f32[96,128]{1,0:T(8,128)S(1)}, u32[]{:S(2)}, u32[]{:S(2)}) collective-permute-start(f32[96,128]{1,0:T(8,128)S(1)} %add_add_fusion.mine), channel_id=1, source_target_pairs={{0,2},{1,3},{2,0},{3,1},{4,6},{5,7},{6,4},{7,5},{8,10},{9,11},{10,... | collective-permute-start | bytes 147464 | tf_op jit(solution)/shard_map/ppermute | solution.py:27
